TPU v7x, 32 devices: a whole 2x2x4 slice. The times are simulated.
32 devices in a mesh: grp: 2 (over y), ep: 16 (over z, x, core).
Axes of the slice: x: 2, y: 2, z: 4, core: 2. Of those that a mesh axis runs over, the one named last changes fastest.
Arguments:
- tokens: bfloat16 [4096, 2048], P(('grp', 'ep')), may hold values from -18 to 18
- w_query: bfloat16 [2048, 2048], P(('grp', 'ep')), may hold values from -0.125 to 0.125
- w_key: bfloat16 [2048, 2048], P(('grp', 'ep')), may hold values from -0.125 to 0.125
- w_value: bfloat16 [2048, 2048], P(('grp', 'ep')), may hold values from -0.125 to 0.125
- w_output: bfloat16 [2048, 2048], P(('grp', 'ep')), may hold values from -2 to 2
- w_router: bfloat16 [2048, 64], P(('grp', 'ep')), may hold values from -0.0625 to 0.0625
- attn_gain: bfloat16 [2048], P(('grp', 'ep')), may hold values from 0.099609375 to 1.8984375
- query_gain: bfloat16 [2048], P(('grp', 'ep')), may hold values from 0.099609375 to 1.8984375
- key_gain: bfloat16 [2048], P(('grp', 'ep')), may hold values from 0.099609375 to 1.8984375
- moe_gain: bfloat16 [2048], P(('grp', 'ep')), may hold values from 0.099609375 to 1.8984375
- w_gate: bfloat16 [64, 2048, 1024], P('ep'), may hold values from -0.125 to 0.125
- w_up: bfloat16 [64, 2048, 1024], P('ep'), may hold values from -0.125 to 0.125
- w_down: bfloat16 [64, 1024, 2048], P('ep'), may hold values from -6 to 6
- routes: int32 [4096, 8], P(('grp', 'ep')), may hold values from 0 to 63, all different within a row; in each aligned block of 128 rows (0 to 127, 128 to 255, ...) at most 24 rows name the same one
- cotangent: bfloat16 [4096, 2048], P(('grp', 'ep')), may hold values from -6 to 6
Outputs:
- output: bfloat16 [4096, 2048], P(('grp', 'ep'))
- tokens_grad: bfloat16 [4096, 2048], P(('grp', 'ep'))
- query_grad: float32 [2048, 2048], P(('grp', 'ep'))
- key_grad: float32 [2048, 2048], P(('grp', 'ep'))
- value_grad: float32 [2048, 2048], P(('grp', 'ep'))
- output_grad: float32 [2048, 2048], P(('grp', 'ep'))
- router_grad: float32 [2048, 64], P(('grp', 'ep'))
- attn_gain_grad: float32 [2048], P(('grp', 'ep'))
- query_gain_grad: float32 [2048], P(('grp', 'ep'))
- key_gain_grad: float32 [2048], P(('grp', 'ep'))
- moe_gain_grad: float32 [2048], P(('grp', 'ep'))
- gate_grad: float32 [64, 2048, 1024], P('ep', 'grp')
- up_grad: float32 [64, 2048, 1024], P('ep', 'grp')
- down_grad: float32 [64, 1024, 2048], P('ep', 'grp')
- rms_stats: float32 [2, 3], P('grp')
Inputs may be any that keep to these rules, and one draw needn't show every extreme that they name: `routes`: each row names 8 different experts. Within the rows of one device no expert is named by more than 24 rows, and in every draw some expert is named by exactly 24 rows of some device.
All inputs are finite; a program needn't handle non-finite values.
Results may differ from a plain program's by a relative error of at most 0.024.
Values may be sent and summed in bfloat16 or wider, within the bound.
No kernel may reach another device: no remote copies, remote signals or barrier semaphores. Data moves between devices by JAX's collectives and lax.ppermute only.
A program may use at most 448 MiB of HBM per device.

v0:
```python
import math

import jax
import jax.numpy as jnp
from jax import lax
from jax.sharding import PartitionSpec as P

D = 2048
HEADS = 16
HD = 128
EXPERTS = 64
TOPK = 8
TOK_DEV = 128
BLOCK = 256
CAP = 24


EPSILON = 1e-05
NEG_FILL = -1e30


def inv_rms(values):
    return lax.rsqrt(jnp.mean(values * values, -1, keepdims=True) + EPSILON)


def norm_back(grad_out, values, inverse, gain_vec):
    scaled = grad_out * gain_vec
    grad_in = inverse * (
        scaled - values * inverse * inverse * jnp.mean(scaled * values, -1, keepdims=True)
    )
    return (grad_in, jnp.sum(grad_out * values * inverse, 0))


def rope_tables(positions):
    half_dim = HD // 2
    frequency = jnp.exp(-(2.0 * jnp.arange(half_dim, dtype=jnp.float32) / HD) * math.log(10000.0))
    angles = positions.astype(jnp.float32)[:, None] * frequency[None, :]
    return (jnp.cos(angles)[:, None, :], jnp.sin(angles)[:, None, :])


def rotate(values, cosine, sine_tab):
    half_dim = HD // 2
    first_half = values[..., :half_dim]
    second_half = values[..., half_dim:]
    return jnp.concatenate(
        [
            first_half * cosine - second_half * sine_tab,
            second_half * cosine + first_half * sine_tab,
        ],
        -1,
    )


def rotate_back(grad_in, cosine, sine_tab):
    half_dim = HD // 2
    first_half = grad_in[..., :half_dim]
    second_half = grad_in[..., half_dim:]
    return jnp.concatenate(
        [
            first_half * cosine + second_half * sine_tab,
            second_half * cosine - first_half * sine_tab,
        ],
        -1,
    )


def fold_keys(state_now, key_piece, queries, query_pos):
    keys_in, values_in = key_piece
    piece_rows = keys_in.shape[0]
    blk_rows = math.gcd(piece_rows, 1024)
    key_blocks = keys_in.reshape(piece_rows // blk_rows, blk_rows, HEADS, HD)
    value_blocks = values_in.reshape(piece_rows // blk_rows, blk_rows, HEADS, HD)
    last_block = query_pos[-1] // BLOCK

    def block_step(state_in, block_items):
        key_blk, value_blk, block_num = block_items
        key_start = block_num * blk_rows

        def block_compute(state_cur):
            top_now, total_now, acc_now = state_cur
            key_pos = key_start + jnp.arange(blk_rows, dtype=jnp.int32)
            scores = jnp.einsum(
                "qhd,khd->hqk", queries, key_blk, preferred_element_type=jnp.float32
            ) * HD ** (-0.5)
            allowed = (key_pos // BLOCK)[None, None, :] <= (query_pos // BLOCK)[None, :, None]
            scores = jnp.where(allowed, scores, NEG_FILL)
            top_new = jnp.maximum(top_now, jnp.max(scores, -1, keepdims=True))
            weights = jnp.where(allowed, jnp.exp(scores - top_new), 0.0)
            rescale = jnp.exp(top_now - top_new)
            total_new = total_now * rescale + jnp.sum(weights, -1, keepdims=True)
            acc_new = acc_now * jnp.transpose(rescale, (1, 0, 2)) + jnp.einsum(
                "hqk,khd->qhd",
                weights.astype(jnp.bfloat16),
                value_blk,
                preferred_element_type=jnp.float32,
            )
            return (top_new, total_new, acc_new)

        def block_passing(state_cur):
            return state_cur

        return (
            lax.cond(key_start // BLOCK <= last_block, block_compute, block_passing, state_in),
            None,
        )

    state_out, unused = lax.scan(
        block_step,
        state_now,
        (key_blocks, value_blocks, jnp.arange(piece_rows // blk_rows, dtype=jnp.int32)),
    )
    return state_out


def score_grads(queries, grad_attended, row_delta, log_sum, query_pos, key_blk, value_blk, key_pos):
    scores = jnp.einsum(
        "qhd,khd->hqk", queries, key_blk, preferred_element_type=jnp.float32
    ) * HD ** (-0.5)
    allowed = (key_pos // BLOCK)[None, None, :] <= (query_pos // BLOCK)[None, :, None]
    prob_vals = jnp.where(allowed, jnp.exp(scores - log_sum), 0.0)
    grad_probs = jnp.einsum(
        "qhd,khd->hqk", grad_attended, value_blk, preferred_element_type=jnp.float32
    )
    grad_scores = (prob_vals * (grad_probs - row_delta)).astype(jnp.bfloat16)
    return (prob_vals, grad_scores)


def shards(
    tokens,
    w_query,
    w_key,
    w_value,
    w_output,
    w_router,
    attn_gain,
    query_gain,
    key_gain,
    moe_gain,
    w_gate,
    w_up,
    w_down,
    routes,
    cotangent,
):
    gathered = (
        lax.all_gather(w_query, ("grp", "ep"), axis=0, tiled=True),
        lax.all_gather(w_key, ("grp", "ep"), axis=0, tiled=True),
        lax.all_gather(w_value, ("grp", "ep"), axis=0, tiled=True),
        lax.all_gather(w_output, ("grp", "ep"), axis=0, tiled=True),
        lax.all_gather(w_router, ("grp", "ep"), axis=0, tiled=True),
        lax.all_gather(attn_gain, ("grp", "ep"), axis=0, tiled=True),
        lax.all_gather(query_gain, ("grp", "ep"), axis=0, tiled=True),
        lax.all_gather(key_gain, ("grp", "ep"), axis=0, tiled=True),
        lax.all_gather(moe_gain, ("grp", "ep"), axis=0, tiled=True),
    )
    query_full, key_full, value_full, output_full, router_full = (
        gathered[0],
        gathered[1],
        gathered[2],
        gathered[3],
        gathered[4],
    )
    attn_scale = gathered[5].astype(jnp.float32)
    query_scale = gathered[6].astype(jnp.float32)
    key_scale = gathered[7].astype(jnp.float32)
    moe_scale = gathered[8].astype(jnp.float32)
    ep_count = lax.axis_size("ep")
    exp_local = EXPERTS // ep_count
    score_scale = HD ** (-0.5)
    inputs = tokens.astype(jnp.float32)
    positions = lax.axis_index("ep") * TOK_DEV + jnp.arange(TOK_DEV, dtype=jnp.int32)
    cosine, sine_tab = rope_tables(positions)
    attn_inv = inv_rms(inputs)
    normed = (inputs * attn_inv * attn_scale).astype(jnp.bfloat16)
    query_raw = jnp.dot(normed, query_full, preferred_element_type=jnp.float32)
    key_raw = jnp.dot(normed, key_full, preferred_element_type=jnp.float32)
    values16 = jnp.dot(normed, value_full, preferred_element_type=jnp.float32).astype(jnp.bfloat16)
    query_inv = inv_rms(query_raw)
    queries16 = rotate(
        (query_raw * query_inv * query_scale).reshape(TOK_DEV, HEADS, HD), cosine, sine_tab
    ).astype(jnp.bfloat16)
    key_inv = inv_rms(key_raw)
    keys16 = (
        rotate((key_raw * key_inv * key_scale).reshape(TOK_DEV, HEADS, HD), cosine, sine_tab)
        .astype(jnp.bfloat16)
        .reshape(TOK_DEV, D)
    )
    start_state = (
        jnp.full((HEADS, TOK_DEV, 1), NEG_FILL, jnp.float32),
        jnp.zeros((HEADS, TOK_DEV, 1), jnp.float32),
        jnp.zeros((TOK_DEV, HEADS, HD), jnp.float32),
    )
    folded = fold_keys(
        start_state,
        (
            lax.all_gather(keys16, "ep", axis=0, tiled=True),
            lax.all_gather(values16, "ep", axis=0, tiled=True),
        ),
        queries16,
        positions,
    )
    top_score, total_weight, acc_sum = folded
    log_sum = top_score + jnp.log(total_weight)
    attn_float = acc_sum / jnp.transpose(total_weight, (1, 0, 2))
    attended16 = attn_float.reshape(TOK_DEV, D).astype(jnp.bfloat16)
    branch_attn = jnp.dot(attended16, output_full, preferred_element_type=jnp.float32)
    hidden = inputs + branch_attn
    moe_inv = inv_rms(hidden)
    mixed_in = (hidden * moe_inv * moe_scale).astype(jnp.bfloat16)
    logits = jnp.dot(mixed_in, router_full, preferred_element_type=jnp.float32)
    route_probs = jax.nn.softmax(logits, -1)
    chosen = (routes[:, :, None] == jnp.arange(EXPERTS, dtype=jnp.int32)[None, None, :]).astype(
        jnp.float32
    )
    gate_vals = jnp.sum(chosen * route_probs[:, None, :], -1)
    pair_expert = routes.reshape(-1)
    one_hot = (pair_expert[:, None] == jnp.arange(EXPERTS, dtype=jnp.int32)[None, :]).astype(
        jnp.int32
    )
    pair_rank = jnp.sum(jnp.cumsum(one_hot, 0) * one_hot, 1) - 1
    slot_index = pair_expert * CAP + pair_rank
    pair_token = jnp.arange(TOK_DEV * TOPK, dtype=jnp.int32) // TOPK
    send_rows = jnp.zeros((EXPERTS * CAP, D), jnp.bfloat16).at[slot_index].set(mixed_in[pair_token])
    send_rows = send_rows.reshape(ep_count, exp_local, CAP, D)
    received = lax.all_to_all(send_rows, "ep", split_axis=0, concat_axis=0, tiled=True)
    gate_pre = jnp.einsum("secd,edf->secf", received, w_gate, preferred_element_type=jnp.float32)
    up_pre = jnp.einsum("secd,edf->secf", received, w_up, preferred_element_type=jnp.float32)
    activation = (jax.nn.silu(gate_pre) * up_pre).astype(jnp.bfloat16)
    expert_out = jnp.einsum(
        "secf,efd->secd", activation, w_down, preferred_element_type=jnp.float32
    ).astype(jnp.bfloat16)
    expert_out, gate_pre, up_pre, activation, received = (
        expert_out,
        gate_pre,
        up_pre,
        activation,
        received,
    )
    returned = lax.all_to_all(expert_out, "ep", split_axis=0, concat_axis=0, tiled=True).reshape(
        EXPERTS * CAP, D
    )
    pair_out = returned[slot_index].astype(jnp.float32).reshape(TOK_DEV, TOPK, D)
    branch_moe = jnp.sum(gate_vals[:, :, None] * pair_out, 1)
    output = (hidden + branch_moe).astype(jnp.bfloat16)
    local_sums = jnp.stack(
        [
            jnp.sum(inputs * inputs),
            jnp.sum(branch_attn * branch_attn),
            jnp.sum(branch_moe * branch_moe),
        ]
    )
    seq_sums = lax.psum(local_sums, "ep")
    rms_stats = jnp.sqrt(seq_sums / (TOK_DEV * ep_count * D)).reshape(1, 3)
    grad_out = cotangent.astype(jnp.float32)
    grad_gates = jnp.sum(pair_out * grad_out[:, None, :], -1)
    grad_pairs = (
        (gate_vals[:, :, None] * grad_out[:, None, :])
        .astype(jnp.bfloat16)
        .reshape(TOK_DEV * TOPK, D)
    )
    send_grads = jnp.zeros((EXPERTS * CAP, D), jnp.bfloat16).at[slot_index].set(grad_pairs)
    send_grads = send_grads.reshape(ep_count, exp_local, CAP, D)
    grad_received = lax.all_to_all(send_grads, "ep", split_axis=0, concat_axis=0, tiled=True)
    grad_activation = jnp.einsum(
        "secd,efd->secf", grad_received, w_down, preferred_element_type=jnp.float32
    )
    grad_down = jnp.einsum(
        "secf,secd->efd", activation, grad_received, preferred_element_type=jnp.float32
    )
    sig_gate = jax.nn.sigmoid(gate_pre)
    grad_gate_pre = (
        grad_activation * up_pre * sig_gate * (1.0 + gate_pre * (1.0 - sig_gate))
    ).astype(jnp.bfloat16)
    grad_up_pre = (grad_activation * gate_pre * sig_gate).astype(jnp.bfloat16)
    grad_gate_w = jnp.einsum(
        "secd,secf->edf", received, grad_gate_pre, preferred_element_type=jnp.float32
    )
    grad_up_w = jnp.einsum(
        "secd,secf->edf", received, grad_up_pre, preferred_element_type=jnp.float32
    )
    grad_inputs = (
        jnp.einsum("secf,edf->secd", grad_gate_pre, w_gate, preferred_element_type=jnp.float32)
        + jnp.einsum("secf,edf->secd", grad_up_pre, w_up, preferred_element_type=jnp.float32)
    ).astype(jnp.bfloat16)
    grad_back = lax.all_to_all(grad_inputs, "ep", split_axis=0, concat_axis=0, tiled=True).reshape(
        EXPERTS * CAP, D
    )
    grad_mixed = jnp.sum(grad_back[slot_index].astype(jnp.float32).reshape(TOK_DEV, TOPK, D), 1)
    spread = jnp.sum(chosen * grad_gates[:, :, None], 1)
    grad_logits = (
        route_probs * (spread - jnp.sum(route_probs * spread, -1, keepdims=True))
    ).astype(jnp.bfloat16)
    router_grad = jnp.einsum("td,te->de", mixed_in, grad_logits, preferred_element_type=jnp.float32)
    grad_mixed = grad_mixed + jnp.einsum(
        "te,de->td", grad_logits, router_full, preferred_element_type=jnp.float32
    )
    grad_hid_norm, moe_gain_grad = norm_back(grad_mixed, hidden, moe_inv, moe_scale)
    grad_hidden = grad_out + grad_hid_norm
    grad_branch = grad_hidden.astype(jnp.bfloat16)
    output_grad = jnp.einsum(
        "td,tf->df", attended16, grad_branch, preferred_element_type=jnp.float32
    )
    grad_attended = jnp.einsum(
        "tf,df->td", grad_branch, output_full, preferred_element_type=jnp.float32
    ).astype(jnp.bfloat16)
    grad_attended = grad_attended.reshape(TOK_DEV, HEADS, HD)
    row_delta = jnp.transpose(jnp.sum(grad_attended.astype(jnp.float32) * attn_float, -1), (1, 0))[
        :, :, None
    ]
    gathered_keys, gathered_values = (
        lax.all_gather(keys16, "ep", axis=0, tiled=True),
        lax.all_gather(values16, "ep", axis=0, tiled=True),
    )
    total_rows = gathered_keys.shape[0]
    blk_rows = math.gcd(total_rows, 1024)
    last_query_block = positions[-1] // BLOCK

    def query_step(grad_now, block_num):
        begin_row = block_num * blk_rows

        def query_compute(grad_cur):
            key_blk = lax.dynamic_slice_in_dim(gathered_keys, begin_row, blk_rows, 0).reshape(
                blk_rows, HEADS, HD
            )
            value_blk = lax.dynamic_slice_in_dim(gathered_values, begin_row, blk_rows, 0).reshape(
                blk_rows, HEADS, HD
            )
            key_pos = begin_row + jnp.arange(blk_rows, dtype=jnp.int32)
            prob_vals, grad_scores = score_grads(
                queries16, grad_attended, row_delta, log_sum, positions, key_blk, value_blk, key_pos
            )
            return (
                grad_cur
                + jnp.einsum(
                    "hqk,khd->qhd", grad_scores, key_blk, preferred_element_type=jnp.float32
                )
                * score_scale
            )

        def query_passing(grad_cur):
            return grad_cur

        return (
            lax.cond(
                begin_row // BLOCK <= last_query_block, query_compute, query_passing, grad_now
            ),
            None,
        )

    grad_queries, unused = lax.scan(
        query_step,
        jnp.zeros((TOK_DEV, HEADS, HD), jnp.float32),
        jnp.arange(total_rows // blk_rows, dtype=jnp.int32),
    )
    all_queries, all_grad_att = (
        lax.all_gather(queries16, "ep", axis=0, tiled=True),
        lax.all_gather(grad_attended, "ep", axis=0, tiled=True),
    )
    all_delta, all_log_sum = (
        lax.all_gather(row_delta, "ep", axis=1, tiled=True),
        lax.all_gather(log_sum, "ep", axis=1, tiled=True),
    )
    query_rows = all_queries.shape[0]
    query_blk_rows = math.gcd(query_rows, 1024)
    own_keys = keys16.reshape(TOK_DEV, HEADS, HD)
    own_values = values16.reshape(TOK_DEV, HEADS, HD)
    first_key_block = positions[0] // BLOCK

    def key_step(grads_now, block_num):
        begin_row = block_num * query_blk_rows

        def key_compute(grads_cur):
            query_blk = lax.dynamic_slice_in_dim(all_queries, begin_row, query_blk_rows, 0)
            grad_att_blk = lax.dynamic_slice_in_dim(all_grad_att, begin_row, query_blk_rows, 0)
            delta_blk = lax.dynamic_slice_in_dim(all_delta, begin_row, query_blk_rows, 1)
            log_blk = lax.dynamic_slice_in_dim(all_log_sum, begin_row, query_blk_rows, 1)
            query_pos = begin_row + jnp.arange(query_blk_rows, dtype=jnp.int32)
            prob_vals, grad_scores = score_grads(
                query_blk,
                grad_att_blk,
                delta_blk,
                log_blk,
                query_pos,
                own_keys,
                own_values,
                positions,
            )
            key_part = (
                jnp.einsum(
                    "hqk,qhd->khd", grad_scores, query_blk, preferred_element_type=jnp.float32
                )
                * score_scale
            )
            value_part = jnp.einsum(
                "hqk,qhd->khd",
                prob_vals.astype(jnp.bfloat16),
                grad_att_blk,
                preferred_element_type=jnp.float32,
            )
            return (grads_cur[0] + key_part, grads_cur[1] + value_part)

        def key_passing(grads_cur):
            return grads_cur

        return (
            lax.cond(
                (begin_row + query_blk_rows - 1) // BLOCK >= first_key_block,
                key_compute,
                key_passing,
                grads_now,
            ),
            None,
        )

    key_start = (
        jnp.zeros((TOK_DEV, HEADS, HD), jnp.float32),
        jnp.zeros((TOK_DEV, HEADS, HD), jnp.float32),
    )
    key_value_grads, unused = lax.scan(
        key_step, key_start, jnp.arange(query_rows // query_blk_rows, dtype=jnp.int32)
    )
    grad_keys16 = key_value_grads[0].astype(jnp.bfloat16)
    grad_values16 = key_value_grads[1].reshape(TOK_DEV, D).astype(jnp.bfloat16)
    grad_keys = lax.optimization_barrier(grad_keys16).astype(jnp.float32)
    grad_queries = lax.optimization_barrier(grad_queries.astype(jnp.bfloat16)).astype(jnp.float32)
    grad_query_rot = rotate_back(grad_queries, cosine, sine_tab).reshape(TOK_DEV, D)
    grad_query_raw, query_gain_grad = norm_back(grad_query_rot, query_raw, query_inv, query_scale)
    grad_query16 = grad_query_raw.astype(jnp.bfloat16)
    grad_key_rot = rotate_back(grad_keys, cosine, sine_tab).reshape(TOK_DEV, D)
    grad_key_raw, key_gain_grad = norm_back(grad_key_rot, key_raw, key_inv, key_scale)
    grad_key16 = grad_key_raw.astype(jnp.bfloat16)
    query_grad = jnp.einsum("td,tf->df", normed, grad_query16, preferred_element_type=jnp.float32)
    key_grad = jnp.einsum("td,tf->df", normed, grad_key16, preferred_element_type=jnp.float32)
    value_grad = jnp.einsum("td,tf->df", normed, grad_values16, preferred_element_type=jnp.float32)
    grad_normed = (
        jnp.einsum("tf,df->td", grad_query16, query_full, preferred_element_type=jnp.float32)
        + jnp.einsum("tf,df->td", grad_key16, key_full, preferred_element_type=jnp.float32)
        + jnp.einsum("tf,df->td", grad_values16, value_full, preferred_element_type=jnp.float32)
    )
    grad_tok_norm, attn_gain_grad = norm_back(grad_normed, inputs, attn_inv, attn_scale)
    tokens_grad = (grad_hidden + grad_tok_norm).astype(jnp.bfloat16)
    dense_sums = (
        lax.psum_scatter(query_grad, ("grp", "ep"), scatter_dimension=0, tiled=True),
        lax.psum_scatter(key_grad, ("grp", "ep"), scatter_dimension=0, tiled=True),
        lax.psum_scatter(value_grad, ("grp", "ep"), scatter_dimension=0, tiled=True),
        lax.psum_scatter(output_grad, ("grp", "ep"), scatter_dimension=0, tiled=True),
        lax.psum_scatter(router_grad, ("grp", "ep"), scatter_dimension=0, tiled=True),
        lax.psum_scatter(attn_gain_grad, ("grp", "ep"), scatter_dimension=0, tiled=True),
        lax.psum_scatter(query_gain_grad, ("grp", "ep"), scatter_dimension=0, tiled=True),
        lax.psum_scatter(key_gain_grad, ("grp", "ep"), scatter_dimension=0, tiled=True),
        lax.psum_scatter(moe_gain_grad, ("grp", "ep"), scatter_dimension=0, tiled=True),
    )
    expert_sums = (
        lax.psum_scatter(
            grad_gate_w.astype(jnp.bfloat16), "grp", scatter_dimension=1, tiled=True
        ).astype(jnp.float32),
        lax.psum_scatter(
            grad_up_w.astype(jnp.bfloat16), "grp", scatter_dimension=1, tiled=True
        ).astype(jnp.float32),
        lax.psum_scatter(
            grad_down.astype(jnp.bfloat16), "grp", scatter_dimension=1, tiled=True
        ).astype(jnp.float32),
    )
    return (
        output,
        tokens_grad,
        dense_sums[0],
        dense_sums[1],
        dense_sums[2],
        dense_sums[3],
        dense_sums[4],
        dense_sums[5],
        dense_sums[6],
        dense_sums[7],
        dense_sums[8],
        expert_sums[0],
        expert_sums[1],
        expert_sums[2],
        rms_stats,
    )


def solution(mesh):
    return jax.shard_map(
        shards,
        mesh=mesh,
        in_specs=(
            P(("grp", "ep"), None),
            P(("grp", "ep"), None),
            P(("grp", "ep"), None),
            P(("grp", "ep"), None),
            P(("grp", "ep"), None),
            P(("grp", "ep"), None),
            P(("grp", "ep")),
            P(("grp", "ep")),
            P(("grp", "ep")),
            P(("grp", "ep")),
            P("ep", None, None),
            P("ep", None, None),
            P("ep", None, None),
            P(("grp", "ep"), None),
            P(("grp", "ep"), None),
        ),
        out_specs=(
            P(("grp", "ep"), None),
            P(("grp", "ep"), None),
            P(("grp", "ep"), None),
            P(("grp", "ep"), None),
            P(("grp", "ep"), None),
            P(("grp", "ep"), None),
            P(("grp", "ep"), None),
            P(("grp", "ep")),
            P(("grp", "ep")),
            P(("grp", "ep")),
            P(("grp", "ep")),
            P("ep", "grp", None),
            P("ep", "grp", None),
            P("ep", "grp", None),
            P("grp", None),
        ),
        check_vma=False,
    )
```

profile of v0, /device:TPU:12, one launch (start us, length us, event | category | flops | bytes accessed | tf_op | source)
XLA Modules:
  0.0 2772.7 jit_solution(11519413807217320677)
XLA Ops:
  12.8 42.0 %all-reduce.9 = (bf16[2048]{0:T(1024)(128)(2,1)S(1)}, bf16[2048]{0:T(1024)(128)(2,1)S(1)}, bf16[2048]{0:T(1024)(128)(2,1)S(1)}, bf16[2048]{0:T(1024)(128)(2,1)S(1)}) all-reduce(bf16[2048]{0:T(1024)(128)(2,1)S(1)} %dynamic-update-slice, bf16[2048]{0:T(1024)(128)(2,1)S(1)} %dynamic-update-slice.1, ...), channel_id=1, replica_groups=mesh['grp'=2,'ep'=16] {'grp','ep'}, use_global_device_ids=true, to_apply=%add | all-reduce | flops 8192 | bytes 32768
  56.4 33.4 %all-gather.10.cloned.1.call-done = bf16[2048,2048]{1,0:T(8,128)(2,1)} async-done(((bf16[64,2048]{1,0:T(8,128)(2,1)}), bf16[2048,2048]{1,0:T(8,128)(2,1)}) %all-gather.10.cloned.1.call-update) | async-done | bytes 8388624 | tf_op jit(solution)/shard_map/all_gather | solution.py:147
  97.3 71.4 %all-gather.16.cloned.1.call-done = bf16[2048,2048]{1,0:T(8,128)(2,1)} async-done(((bf16[64,2048]{1,0:T(8,128)(2,1)}), bf16[2048,2048]{1,0:T(8,128)(2,1)}) %all-gather.16.cloned.1.call-update) | async-done | bytes 8388624 | tf_op jit(solution)/shard_map/all_gather | solution.py:148
  178.3 18.0 reduce-window.6
  197.2 50.4 %all-gather.14.cloned.1.call-done = bf16[2048,2048]{1,0:T(8,128)(2,1)} async-done(((bf16[64,2048]{1,0:T(8,128)(2,1)}), bf16[2048,2048]{1,0:T(8,128)(2,1)}) %all-gather.14.cloned.1.call-update) | async-done | bytes 8388624 | tf_op jit(solution)/shard_map/all_gather | solution.py:146
  254.4 70.6 %all-gather.12.cloned.1.call-done = bf16[2048,2048]{0,1:T(8,128)(2,1)} async-done(((bf16[128,2048]{0,1:T(8,128)(2,1)}), bf16[2048,2048]{0,1:T(8,128)(2,1)}) %all-gather.12.cloned.1.call-update) | async-done | bytes 8388624 | tf_op jit(solution)/shard_map/all_gather | solution.py:196
  339.6 21.2 copy.217
  360.7 41.3 %all-gather.18.cloned.1.call-done = bf16[2048,2048]{1,0:T(8,128)(2,1)} async-done(((bf16[128,2048]{1,0:T(8,128)(2,1)}), bf16[2048,2048]{1,0:T(8,128)(2,1)}) %all-gather.18.cloned.1.call-update) | async-done | bytes 8388624 | tf_op jit(solution)/shard_map/all_gather | solution.py:197
  435.9 45.1 %all-gather.20.cloned.1.call-done = bf16[2048,2048]{1,0:T(8,128)(2,1)} async-done(((bf16[64,2048]{1,0:T(8,128)(2,1)}), bf16[2048,2048]{1,0:T(8,128)(2,1)}) %all-gather.20.cloned.1.call-update) | async-done | bytes 8388624 | tf_op jit(solution)/shard_map/all_gather | solution.py:149
  486.7 24.3 scatter_custom_fusion
  516.1 162.8 %all_gather.57 = bf16[2048,64]{1,0:T(8,128)(2,1)S(1)} all-gather(bf16[64,64]{1,0:T(8,128)(2,1)S(1)} %copy-done.55), channel_id=1, replica_groups=mesh['grp'=2,'ep'=16] {'grp','ep'}, dimensions={0}, use_global_device_ids=true | all-gather | bytes 270336 | tf_op jit(solution)/shard_map/all_gather | solution.py:150
  729.8 105.0 %all-to-all-done.2 = bf16[16,4,24,2048]{3,2,1,0:T(8,128)(2,1)} async-done(((bf16[16,4,24,2048]{3,2,1,0:T(8,128)(2,1)}), bf16[16,4,24,2048]{3,2,1,0:T(8,128)(2,1)}, u32[]{:S(2)}, u32[]{:S(2)}) %all-to-all-start.2) | async-done | bytes 6291488 | tf_op jit(solution)/shard_map/all_to_all | solution.py:263
  834.8 17.8 fusion.133
  914.0 149.2 %all-to-all-done.1 = bf16[16,4,24,2048]{3,2,1,0:T(8,128)(2,1)} async-done(((bf16[16,4,24,2048]{3,2,1,0:T(8,128)(2,1)}), bf16[16,4,24,2048]{3,2,1,0:T(8,128)(2,1)}, u32[]{:S(2)}, u32[]{:S(2)}) %all-to-all-start.1) | async-done | bytes 6291488 | tf_op jit(solution)/shard_map/all_to_all | solution.py:239
  1088.3 117.2 %all-to-all-done.3 = bf16[16,4,24,2048]{3,2,1,0:T(8,128)(2,1)} async-done(((bf16[16,4,24,2048]{3,2,1,0:T(8,128)(2,1)}), bf16[16,4,24,2048]{3,2,1,0:T(8,128)(2,1)}, u32[]{:S(2)}, u32[]{:S(2)}) %all-to-all-start.3) | async-done | bytes 6291488 | tf_op jit(solution)/shard_map/all_to_all | solution.py:285
  1270.4 16.4 bitcast_convert_fusion.1
  1326.4 18.7 all_gather.59
  1347.9 31.2 %while.52 = (s32[]{:T(128)}, f32[128,16,128]{0,2,1:T(8,128)S(1)}, s32[2]{0:T(128)S(1)}, s32[]{:T(128)}, bf16[2048,2048]{0,1:T(8,128)(2,1)}, /*index=5*/bf16[128,...) while((s32[]{:T(128)}, f32[128,16,128]{0,2,1:T(8,128)S(1)}, ...), condition=%wide.region_28.29_spmd.clone, body=%wide.region_25.28_spmd.clone.sunk | while | flops 1623869440 | bytes 66349560 | solution.py:350
  1349.4 28.5 %conditional.10 = (f32[128,16,128]{0,2,1:T(8,128)S(1)}) conditional(s32[]{:T(128)} %convert_element_type.360, f32[128,16,128]{0,2,1:T(8,128)S(1)} %get-tuple-element.1485, (s32[]{:T(128)}, bf16[2048,2048]{0,1:T(8,128)(2,1)}, s32[]{:T(128)}, bf16[128,16,128]{2,0,1:T(8,128)(2,1)S(1)}, f32[16,128,1]{1,0,2:T(8,128)S(1)}, ...), branch_computations={%region_26.26_spmd, %region_27.27_spmd} | conditional | flops 1623869440 | bytes 66348624 | solution.py:344
  1380.4 48.0 %all-gather = f32[16,2048]{0,1:T(8,128)S(1)} all-gather(f32[16,128]{0,1:T(8,128)S(1)} %bitcast.305), channel_id=2, replica_groups=mesh['grp'=2,'ep'=16] {'ep'}, dimensions={1}, use_global_device_ids=true | all-gather | bytes 139264 | tf_op jit(solution)/shard_map/all_gather | solution.py:360
  1430.0 50.9 %while.53 = (s32[]{:T(128)}, f32[128,16,128]{0,2,1:T(8,128)S(1)}, f32[128,16,128]{0,2,1:T(8,128)}, s32[2]{0:T(128)S(1)}, s32[]{:T(128)}, /*index=5*/bf16[2048,16...) while((s32[]{:T(128)}, f32[128,16,128]{0,2,1:T(8,128)S(1)}, ...), condition=%wide.region_33.34_spmd.clone, body=%wide.region_30.33_spmd.clone.sunk | while | flops 2169391104 | bytes 125644480 | solution.py:419
  1431.5 24.0 conditional.11
  1456.7 23.7 conditional.11
  1536.8 25.0 psum.7
  1561.8 47.7 %all-reduce.8 = (f32[2048]{0:T(1024)S(1)}, f32[2048]{0:T(1024)S(1)}, f32[2048]{0:T(1024)S(1)}, f32[2048]{0:T(1024)S(1)}) all-reduce(f32[2048]{0:T(1024)S(1)} %get-tuple-element.1023, f32[2048]{0:T(1024)S(1)} %get-tuple-element.1021, f32[2048]{0:T(1024)S(1)} %get-tuple-element.1019, ...), channel_id=8, replica_groups=mesh['grp'=2,'ep'=16] {'grp','ep'}, use_global_device_ids=true, to_apply=%region_42.43.clone | all-reduce | flops 8192 | bytes 65536
  1625.3 69.6 %reduce-scatter.19.cloned.1.call-done = bf16[4,1024,1024]{2,1,0:T(8,128)(2,1)} async-done(((bf16[4,2048,1024]{2,1,0:T(8,128)(2,1)}), bf16[4,1024,1024]{2,1,0:T(8,128)(2,1)}) %reduce-scatter.19.cloned.1.call-update) | async-done | bytes 8388624 | tf_op jit(solution)/shard_map/reduce_scatter | solution.py:454
  1706.7 179.7 %reduce-scatter.21.cloned.1.call-done = bf16[4,1024,1024]{2,1,0:T(8,128)(2,1)} async-done(((bf16[4,2048,1024]{2,1,0:T(8,128)(2,1)}), bf16[4,1024,1024]{2,1,0:T(8,128)(2,1)}) %reduce-scatter.21.cloned.1.call-update) | async-done | bytes 8388624 | tf_op jit(solution)/shard_map/reduce_scatter | solution.py:457
  1898.0 116.0 %reduce-scatter.17.cloned.1.call-done = f32[64,64]{1,0:T(8,128)} async-done(((f32[2048,64]{1,0:T(8,128)}), f32[64,64]{1,0:T(8,128)}) %reduce-scatter.17.cloned.1.call-update) | async-done | bytes 16400 | tf_op jit(solution)/shard_map/reduce_scatter | solution.py:447
  2014.0 191.1 %reduce-scatter.15.cloned.1.call-done = f32[64,2048]{1,0:T(8,128)} async-done(((f32[2048,2048]{1,0:T(8,128)}), f32[64,2048]{1,0:T(8,128)}) %reduce-scatter.15.cloned.1.call-update) | async-done | bytes 524304 | tf_op jit(solution)/shard_map/reduce_scatter | solution.py:446
  2205.1 186.9 %reduce-scatter.11.cloned.1.call-done = f32[64,2048]{1,0:T(8,128)} async-done(((f32[2048,2048]{1,0:T(8,128)}), f32[64,2048]{1,0:T(8,128)}) %reduce-scatter.11.cloned.1.call-update) | async-done | bytes 524304 | tf_op jit(solution)/shard_map/reduce_scatter | solution.py:444
  2392.0 186.9 %reduce-scatter.9.cloned.1.call-done = f32[64,2048]{1,0:T(8,128)} async-done(((f32[2048,2048]{1,0:T(8,128)}), f32[64,2048]{1,0:T(8,128)}) %reduce-scatter.9.cloned.1.call-update) | async-done | bytes 524304 | tf_op jit(solution)/shard_map/reduce_scatter | solution.py:443
  2579.0 187.0 %reduce-scatter.13.cloned.1.call-done = f32[64,2048]{1,0:T(8,128)} async-done(((f32[2048,2048]{1,0:T(8,128)}), f32[64,2048]{1,0:T(8,128)}) %reduce-scatter.13.cloned.1.call-update) | async-done | bytes 524304 | tf_op jit(solution)/shard_map/reduce_scatter | solution.py:445
  (374 shorter events, 528.1 us)
Async XLA Ops:
  7.2 82.6 %all-gather.10.cloned.1.call-start = ((), (), s32[]{:S(2)}) async-start(), calls=%async_computation.12 | async-start | bytes 8650752 | tf_op jit(solution)/shard_map/all_gather | solution.py:147
  7.9 160.8 %all-gather.16.cloned.1.call-start = ((), (), s32[]{:S(2)}) async-start(), calls=%async_computation.15 | async-start | bytes 8650752 | tf_op jit(solution)/shard_map/all_gather | solution.py:148
  8.7 239.0 %all-gather.14.cloned.1.call-start = ((), (), s32[]{:S(2)}) async-start(), calls=%async_computation.14 | async-start | bytes 8650752 | tf_op jit(solution)/shard_map/all_gather | solution.py:146
  9.4 315.7 %all-gather.12.cloned.1.call-start = ((), (), s32[]{:S(2)}) async-start(), calls=%async_computation.13 | async-start | bytes 8912896 | tf_op jit(solution)/shard_map/all_gather | solution.py:196
  54.8 192.8 %copy-start.30 = (f32[2048]{0:T(1024)}, f32[2048]{0:T(1024)S(1)}, u32[]{:S(2)}) copy-start(f32[2048]{0:T(1024)S(1)} %convert_element_type.194) | copy-start | bytes 24580
  56.1 191.5 %copy-start.51 = (f32[128]{0:T(128)}, f32[128]{0:T(128)S(1)}, u32[]{:S(2)}) copy-start(f32[128]{0:T(128)S(1)} %add_rsqrt_fusion.3) | copy-start | bytes 1540
  56.4 197.6 %copy-start.40 = (f32[128,64]{0,1:T(8,128)}, f32[128,64]{0,1:T(8,128)S(1)}, u32[]{:S(2)}) copy-start(f32[128,64]{0,1:T(8,128)S(1)} %get-tuple-element.1127) | copy-start | bytes 98308
  56.4 197.6 %copy-start.42 = (f32[128,64]{0,1:T(8,128)}, f32[128,64]{0,1:T(8,128)S(1)}, u32[]{:S(2)}) copy-start(f32[128,64]{0,1:T(8,128)S(1)} %get-tuple-element.1128) | copy-start | bytes 98308
  56.4 112.3 %copy-start.2 = (bf16[128,2048]{1,0:T(8,128)(2,1)S(1)}, bf16[128,2048]{1,0:T(8,128)(2,1)}, u32[]{:S(2)}) copy-start(bf16[128,2048]{1,0:T(8,128)(2,1)} %param.27) | copy-start | bytes 1572868
  94.7 79.4 %copy-start.56 = (f32[128]{0:T(128)}, f32[128]{0:T(128)S(1)}, u32[]{:S(2)}) copy-start(f32[128]{0:T(128)S(1)} %add_rsqrt_fusion.2) | copy-start | bytes 1540
  97.2 80.1 %copy-start.53 = (s32[128,8]{0,1:T(8,128)S(1)}, s32[128,8]{0,1:T(8,128)}, u32[]{:S(2)}) copy-start(s32[128,8]{0,1:T(8,128)} %param.40) | copy-start | bytes 12292
  97.2 304.8 %all-gather.18.cloned.1.call-start = ((), (), s32[]{:S(2)}) async-start(), calls=%async_computation.16 | async-start | bytes 8912896 | tf_op jit(solution)/shard_map/all_gather | solution.py:197
  174.2 306.9 %all-gather.20.cloned.1.call-start = ((), (), s32[]{:S(2)}) async-start(), calls=%async_computation.17 | async-start | bytes 8650752 | tf_op jit(solution)/shard_map/all_gather | solution.py:149
  178.3 74.2 %copy-start.49 = (f32[2048]{0:T(1024)}, f32[2048]{0:T(1024)S(1)}, u32[]{:S(2)}) copy-start(f32[2048]{0:T(1024)S(1)} %convert_element_type.200) | copy-start | bytes 24580
  252.5 87.1 %copy-start.58 = (f32[128]{0:T(128)}, f32[128]{0:T(128)S(1)}, u32[]{:S(2)}) copy-start(f32[128]{0:T(128)S(1)} %add_rsqrt_fusion.1) | copy-start | bytes 1540
  254.1 85.4 %copy-start.23 = (bf16[128,16,128]{0,2,1:T(8,128)(2,1)}, bf16[128,16,128]{0,2,1:T(8,128)(2,1)S(1)}, u32[]{:S(2)}) copy-start(bf16[128,16,128]{0,2,1:T(8,128)(2,1)S(1)} %pad_maximum_fusion.2) | copy-start | bytes 1572868
  486.7 192.2 %copy-start.18 = (bf16[128,2048]{1,0:T(8,128)(2,1)}, bf16[128,2048]{1,0:T(8,128)(2,1)S(1)}, u32[]{:S(2)}) copy-start(bf16[128,2048]{1,0:T(8,128)(2,1)S(1)} %multiply_convert_fusion.10) | copy-start | bytes 1572868
  511.1 179.2 %all-to-all-start = ((bf16[16,4,24,2048]{3,2,1,0:T(8,128)(2,1)}), bf16[16,4,24,2048]{3,2,1,0:T(8,128)(2,1)}, u32[]{:S(2)}, u32[]{:S(2)}) async-start(bf16[16,4,24,2048]{3,2,1,0:T(8,128)(2,1)} %bitcast.285), calls=%async_computation | async-start | bytes 12582912 | tf_op jit(solution)/shard_map/all_to_all | solution.py:225
  690.3 144.5 %all-to-all-start.2 = ((bf16[16,4,24,2048]{3,2,1,0:T(8,128)(2,1)}), bf16[16,4,24,2048]{3,2,1,0:T(8,128)(2,1)}, u32[]{:S(2)}, u32[]{:S(2)}) async-start(bf16[16,4,24,2048]{3,2,1,0:T(8,128)(2,1)} %bitcast.286), calls=%async_computation.2 | async-start | bytes 12582912 | tf_op jit(solution)/shard_map/all_to_all | solution.py:263
  870.4 192.9 %all-to-all-start.1 = ((bf16[16,4,24,2048]{3,2,1,0:T(8,128)(2,1)}), bf16[16,4,24,2048]{3,2,1,0:T(8,128)(2,1)}, u32[]{:S(2)}, u32[]{:S(2)}) async-start(bf16[16,4,24,2048]{3,2,1,0:T(8,128)(2,1)} %copy.229), calls=%async_computation.1 | async-start | bytes 12582912 | tf_op jit(solution)/shard_map/all_to_all | solution.py:239
  876.9 437.0 %all-gather.22.cloned.1.call-start = ((), (), s32[]{:S(2)}) async-start(), calls=%async_computation.18 | async-start | bytes 8912896 | tf_op jit(solution)/shard_map/all_gather | solution.py:356
  1063.3 142.3 %all-to-all-start.3 = ((bf16[16,4,24,2048]{3,2,1,0:T(8,128)(2,1)}), bf16[16,4,24,2048]{3,2,1,0:T(8,128)(2,1)}, u32[]{:S(2)}, u32[]{:S(2)}) async-start(bf16[16,4,24,2048]{3,2,1,0:T(8,128)(2,1)} %copy.232), calls=%async_computation.3 | async-start | bytes 12582912 | tf_op jit(solution)/shard_map/all_to_all | solution.py:285
  1069.8 358.9 %all-gather.24.cloned.1.call-start = ((), (), s32[]{:S(2)}) async-start(), calls=%async_computation.19 | async-start | bytes 8912896 | tf_op jit(solution)/shard_map/all_gather | solution.py:357
  1235.6 377.8 %reduce-scatter.23.cloned.1.call-start = ((), (), s32[]{:S(2)}) async-start(), calls=%async_computation.27 | async-start | bytes 25165824 | tf_op jit(solution)/shard_map/reduce_scatter | solution.py:460
  1251.3 443.6 %reduce-scatter.19.cloned.1.call-start = ((), (), s32[]{:S(2)}) async-start(), calls=%async_computation.25 | async-start | bytes 25165824 | tf_op jit(solution)/shard_map/reduce_scatter | solution.py:454
  1268.6 617.8 %reduce-scatter.21.cloned.1.call-start = ((), (), s32[]{:S(2)}) async-start(), calls=%async_computation.26 | async-start | bytes 25165824 | tf_op jit(solution)/shard_map/reduce_scatter | solution.py:457
  1286.8 727.2 %reduce-scatter.17.cloned.1.call-start = ((), (), s32[]{:S(2)}) async-start(), calls=%async_computation.24 | async-start | bytes 1081344 | tf_op jit(solution)/shard_map/reduce_scatter | solution.py:447
  1289.2 915.9 %reduce-scatter.15.cloned.1.call-start = ((), (), s32[]{:S(2)}) async-start(), calls=%async_computation.23 | async-start | bytes 17301504 | tf_op jit(solution)/shard_map/reduce_scatter | solution.py:446
  1297.5 1094.6 %reduce-scatter.11.cloned.1.call-start = ((), (), s32[]{:S(2)}) async-start(), calls=%async_computation.21 | async-start | bytes 17301504 | tf_op jit(solution)/shard_map/reduce_scatter | solution.py:444
  1495.9 1083.1 %reduce-scatter.9.cloned.1.call-start = ((), (), s32[]{:S(2)}) async-start(), calls=%async_computation.20 | async-start | bytes 17301504 | tf_op jit(solution)/shard_map/reduce_scatter | solution.py:443
  1508.3 1257.6 %reduce-scatter.13.cloned.1.call-start = ((), (), s32[]{:S(2)}) async-start(), calls=%async_computation.22 | async-start | bytes 17301504 | tf_op jit(solution)/shard_map/reduce_scatter | solution.py:445
  1531.3 81.1 %copy-start.8 = (f32[128,2048]{1,0:T(8,128)S(1)}, f32[128,2048]{1,0:T(8,128)}, u32[]{:S(2)}) copy-start(f32[128,2048]{1,0:T(8,128)} %copy-done.6) | copy-start | bytes 3145732
  (60 other events, 763.5 us)
Sparse Core Ops, SparseCore 0:
  10.8 78.8 all-gather.9
  92.6 76.0 all-gather.15
  171.5 76.0 all-gather.13
  250.2 74.7 all-gather.11
  327.7 74.3 all-gather.17
  404.7 76.3 all-gather.19
  880.5 165.8 all-gather.21
  1235.8 75.7 all-gather.23
  1314.4 187.0 reduce-scatter.22
  1504.3 190.5 reduce-scatter.18
  1697.2 189.0 reduce-scatter.20
  1889.1 124.9 reduce-scatter.16
  2016.9 188.1 reduce-scatter.14
  2207.8 184.1 reduce-scatter.10
  2394.8 184.1 reduce-scatter.8
  2581.7 184.2 reduce-scatter.12
where the time goes:
time: 2780 us; the launch traced here: 2770 us
  waiting for transfers between devices  1800 us (65%)
  blocking collectives  344 us (12%)
  matrix products  281 us (10%)
  local copies, waits for them, and re-layouts  194 us (7%)
  other arithmetic  94.6 us (3%)
  starting transfers between devices  28 us (1%)
    reduce_scatter x1, waiting for transfers between devices, shards(): lax.psum_scatter(output_grad, ('grp', 'ep'), scatter_dimension=0, tiled=T...  191 us
    reduce_scatter x1, waiting for transfers between devices, shards(): lax.psum_scatter(value_grad, ('grp', 'ep'), scatter_dimension=0, tiled=True)  187 us
    reduce_scatter x1, waiting for transfers between devices, shards(): lax.psum_scatter(key_grad, ('grp', 'ep'), scatter_dimension=0, tiled=True)  187 us
    reduce_scatter x1, waiting for transfers between devices, shards(): lax.psum_scatter(query_grad, ('grp', 'ep'), scatter_dimension=0, tiled=True)  187 us
    reduce_scatter x1, waiting for transfers between devices, shards(): lax.psum_scatter(grad_up_w.astype(jnp.bfloat16), 'grp', scatter_dimension...  180 us
    all_gather x1, blocking collectives, shards(): lax.all_gather(w_router, ('grp', 'ep'), axis=0, tiled=True)  163 us
    all_to_all x1, waiting for transfers between devices, shards(): lax.all_to_all(expert_out, 'ep', split_axis=0, concat_axis=0, tiled=True)  149 us
    all_to_all x1, waiting for transfers between devices, shards(): lax.all_to_all(grad_inputs, 'ep', split_axis=0, concat_axis=0, tiled=True)  117 us
  transfers between devices with their start and end apart: 20, of which 16 were waited for; matrix products, arithmetic and copies ran while one was open for 17% of the time, Pallas kernels for 0%

commit v1 on v0

--- a/solution.py
+++ b/solution.py
@@ -1,8 +1,11 @@
+import functools
 import math
 
 import jax
 import jax.numpy as jnp
 from jax import lax
+from jax.experimental import pallas as pl
+from jax.experimental.pallas import tpu as pltpu
 from jax.sharding import PartitionSpec as P
 
 D = 2048
@@ -480,7 +483,686 @@
     )
 
 
+F32 = jnp.float32
+BF16 = jnp.bfloat16
+EP = ("z", "x", "core")
+ALL = ("grp", "z", "x", "core")
+PAIR = 2 * TOK_DEV
+SLOTS = 2 * CAP
+SIDES = {16: (4, 2, 2)}
+
+
+def nt(left, right):
+    return lax.dot_general(left, right, (((1,), (1,)), ((), ())), preferred_element_type=F32)
+
+
+def nn(left, right):
+    return lax.dot_general(left, right, (((1,), (0,)), ((), ())), preferred_element_type=F32)
+
+
+def tn(left, right):
+    return lax.dot_general(left, right, (((0,), (0,)), ((), ())), preferred_element_type=F32)
+
+
+def as_row(column):
+    return jnp.broadcast_to(column, (column.shape[0], 128)).T[0:1]
+
+
+def as_column(row):
+    return jnp.broadcast_to(row, (128, row.shape[1])).T
+
+
+def inv_of(sum_row):
+    return as_column(lax.rsqrt(sum_row / D + EPSILON))
+
+
+def params(mebibytes):
+    return pltpu.CompilerParams(vmem_limit_bytes=mebibytes * 1024 * 1024)
+
+
+def cost(flops, moved):
+    return pl.CostEstimate(flops=int(flops), bytes_accessed=int(moved), transcendentals=0)
+
+
+def whole(*dims):
+    return pl.BlockSpec(dims, lambda *_: (0,) * len(dims))
+
+
+def project_kernel(tok_ref, w_ref, gain_ref, qkv_ref, stat_ref):
+    rows = tok_ref[...].astype(F32)
+    inverse = lax.rsqrt(jnp.mean(rows * rows, -1, keepdims=True) + EPSILON)
+    normed = (rows * inverse * gain_ref[...]).astype(BF16)
+    out = nn(normed, w_ref[...])
+    qkv_ref[...] = out
+    stat_ref[0:1, :] = as_row(jnp.sum(out[:, :HD] * out[:, :HD], -1, keepdims=True))
+    stat_ref[1:2, :] = as_row(jnp.sum(out[:, HD : 2 * HD] * out[:, HD : 2 * HD], -1, keepdims=True))
+
+
+def project(tok_all, w_head, gain_row):
+    rows = tok_all.shape[0]
+    return pl.pallas_call(
+        project_kernel,
+        grid=(rows // PAIR,),
+        in_specs=[
+            pl.BlockSpec((PAIR, D), lambda i: (i, 0)),
+            whole(D, 3 * HD),
+            whole(1, D),
+        ],
+        out_specs=[
+            pl.BlockSpec((PAIR, 3 * HD), lambda i: (i, 0)),
+            pl.BlockSpec((2, PAIR), lambda i: (0, i)),
+        ],
+        out_shape=[
+            jax.ShapeDtypeStruct((rows, 3 * HD), F32),
+            jax.ShapeDtypeStruct((2, rows), F32),
+        ],
+        compiler_params=params(32),
+        cost_estimate=cost(2 * rows * D * 3 * HD, 2 * rows * D + 4 * rows * 384),
+        name="project",
+    )(tok_all, w_head, gain_row)
+
+
+def attend_kernel(
+    qkv_ref, stat_ref, gq_ref, gk_ref, cos_ref, sin_ref,
+    q_ref, k_ref, v_ref, of_ref, att_ref, lse_ref, vt_ref,
+):
+    blocks = q_ref.shape[0] // BLOCK
+    for i in range(blocks):
+        rows = slice(i * BLOCK, (i + 1) * BLOCK)
+        cosine, sine = cos_ref[rows, :], sin_ref[rows, :]
+        for part, gain_ref, out_ref in ((0, gq_ref, q_ref), (1, gk_ref, k_ref)):
+            raw = qkv_ref[rows, part * HD : (part + 1) * HD]
+            scaled = raw * inv_of(stat_ref[part : part + 1, rows]) * gain_ref[...]
+            turned = scaled * cosine + pltpu.roll(scaled, HD // 2, 1) * sine
+            out_ref[rows, :] = turned.astype(BF16)
+        value = qkv_ref[rows, 2 * HD :]
+        v_ref[rows, :] = value.astype(BF16)
+        vt_ref[:, rows] = value.T.astype(BF16)
+    for i in range(blocks):
+        rows = slice(i * BLOCK, (i + 1) * BLOCK)
+        reach = (i + 1) * BLOCK
+        scores = nt(k_ref[0:reach, :], q_ref[rows, :]) * HD ** (-0.5)
+        top = jnp.max(scores, 0, keepdims=True)
+        weights = jnp.exp(scores - top)
+        total = jnp.sum(weights, 0, keepdims=True)
+        probs = (weights * (1.0 / total)).astype(BF16)
+        out = nn(vt_ref[:, 0:reach], probs).T
+        of_ref[rows, :] = out
+        att_ref[rows, :] = out.astype(BF16)
+        lse_ref[:, rows] = top + jnp.log(total)
+
+
+def attend(qkv, stat, gain_q, gain_k, cosine, sine):
+    rows = qkv.shape[0]
+    shape = lambda kind: jax.ShapeDtypeStruct((rows, HD), kind)
+    return pl.pallas_call(
+        attend_kernel,
+        out_shape=[shape(BF16), shape(BF16), shape(BF16), shape(F32), shape(BF16),
+                   jax.ShapeDtypeStruct((1, rows), F32)],
+        scratch_shapes=[pltpu.VMEM((HD, rows), BF16)],
+        compiler_params=params(48),
+        cost_estimate=cost(8 * rows * rows * HD, 10 * rows * 384),
+        name="attend",
+    )(qkv, stat, gain_q, gain_k, cosine, sine)
+
+
+def attend_back_kernel(
+    q_ref, k_ref, v_ref, do_ref, of_ref, lse_ref, qkv_ref, stat_ref, gq_ref, gk_ref,
+    cos_ref, sin_ref, dnq_ref, dnk_ref, dv_ref, means_ref, gains_ref, dk_acc, dv_acc,
+):
+    blocks = q_ref.shape[0] // BLOCK
+    scale = HD ** (-0.5)
+    dk_acc[...] = jnp.zeros_like(dk_acc)
+    dv_acc[...] = jnp.zeros_like(dv_acc)
+
+    def turn_back(grad, rows, part, gain_ref, out_ref):
+        grad = grad.astype(BF16).astype(F32)
+        grad = grad * cos_ref[rows, :] - pltpu.roll(grad, HD // 2, 1) * sin_ref[rows, :]
+        raw = qkv_ref[rows, part * HD : (part + 1) * HD]
+        out_ref[rows, :] = grad
+        means_ref[part : part + 1, rows] = jnp.sum((grad * gain_ref[...] * raw).T, 0, keepdims=True)
+        inverse = inv_of(stat_ref[part : part + 1, rows])
+        return jnp.sum(grad * raw * inverse, 0, keepdims=True)
+
+    gain_q = jnp.zeros((1, HD), F32)
+    gain_k = jnp.zeros((1, HD), F32)
+    for i in range(blocks):
+        rows = slice(i * BLOCK, (i + 1) * BLOCK)
+        reach = (i + 1) * BLOCK
+        queries, grads = q_ref[rows, :], do_ref[rows, :]
+        delta = jnp.sum((grads.astype(F32) * of_ref[rows, :]).T, 0, keepdims=True)
+        scores = nt(k_ref[0:reach, :], queries) * scale
+        probs = jnp.exp(scores - lse_ref[:, rows])
+        slopes = nt(v_ref[0:reach, :], grads)
+        grad_scores = (probs * (slopes - delta)).astype(BF16)
+        dv_acc[0:reach, :] += nn(probs.astype(BF16), grads)
+        dk_acc[0:reach, :] += nn(grad_scores, queries)
+        gain_q += turn_back(tn(grad_scores, k_ref[0:reach, :]) * scale, rows, 0, gq_ref, dnq_ref)
+    for i in range(blocks):
+        rows = slice(i * BLOCK, (i + 1) * BLOCK)
+        dv_ref[rows, :] = dv_acc[rows, :].astype(BF16)
+        gain_k += turn_back(dk_acc[rows, :] * scale, rows, 1, gk_ref, dnk_ref)
+    gains_ref[0:1, :] = gain_q
+    gains_ref[1:2, :] = gain_k
+
+
+def attend_back(q, k, v, grad, out, lse, qkv, stat, gain_q, gain_k, cosine, sine):
+    rows = q.shape[0]
+    shape = lambda kind: jax.ShapeDtypeStruct((rows, HD), kind)
+    return pl.pallas_call(
+        attend_back_kernel,
+        out_shape=[shape(F32), shape(F32), shape(BF16),
+                   jax.ShapeDtypeStruct((2, rows), F32), jax.ShapeDtypeStruct((2, HD), F32)],
+        scratch_shapes=[pltpu.VMEM((rows, HD), F32), pltpu.VMEM((rows, HD), F32)],
+        compiler_params=params(48),
+        cost_estimate=cost(20 * rows * rows * HD, 20 * rows * 384),
+        name="attend_back",
+    )(q, k, v, grad, out, lse, qkv, stat, gain_q, gain_k, cosine, sine)
+
+
+def project_back_kernel(
+    dnq_ref, dnk_ref, dv_ref, qkv_ref, stat_ref, means_ref, gq_ref, gk_ref, tok_ref, gain_ref,
+    w_ref, part_ref, dw_ref,
+):
+    grads = []
+    for part, dn_ref, g_ref in ((0, dnq_ref, gq_ref), (1, dnk_ref, gk_ref)):
+        raw = qkv_ref[:, part * HD : (part + 1) * HD]
+        inverse = inv_of(stat_ref[part : part + 1, :])
+        mean = as_column(means_ref[part : part + 1, :] / D)
+        grad = inverse * (dn_ref[...] * g_ref[...] - raw * inverse * inverse * mean)
+        grads.append(grad.astype(BF16))
+    grad = jnp.concatenate(grads + [dv_ref[...]], 1)
+    part_ref[...] = nt(grad, w_ref[...]).astype(BF16)
+    rows = tok_ref[...].astype(F32)
+    inverse = lax.rsqrt(jnp.mean(rows * rows, -1, keepdims=True) + EPSILON)
+    normed = (rows * inverse * gain_ref[...]).astype(BF16)
+
+    @pl.when(pl.program_id(0) == 0)
+    def _():
+        dw_ref[...] = jnp.zeros_like(dw_ref)
+
+    dw_ref[...] += tn(normed, grad)
+
+
+def project_back(dnq, dnk, dv, qkv, stat, means, gain_q, gain_k, tok_all, gain_row, w_head):
+    rows = tok_all.shape[0]
+    head = pl.BlockSpec((PAIR, HD), lambda i: (i, 0))
+    line = pl.BlockSpec((2, PAIR), lambda i: (0, i))
+    return pl.pallas_call(
+        project_back_kernel,
+        grid=(rows // PAIR,),
+        in_specs=[
+            head, head, head, pl.BlockSpec((PAIR, 3 * HD), lambda i: (i, 0)), line, line,
+            whole(1, HD), whole(1, HD), pl.BlockSpec((PAIR, D), lambda i: (i, 0)),
+            whole(1, D), whole(D, 3 * HD),
+        ],
+        out_specs=[pl.BlockSpec((PAIR, D), lambda i: (i, 0)), whole(D, 3 * HD)],
+        out_shape=[
+            jax.ShapeDtypeStruct((rows, D), BF16),
+            jax.ShapeDtypeStruct((D, 3 * HD), F32),
+        ],
+        compiler_params=params(40),
+        cost_estimate=cost(4 * rows * D * 3 * HD, 4 * rows * D + 8 * rows * 384),
+        name="project_back",
+    )(dnq, dnk, dv, qkv, stat, means, gain_q, gain_k, tok_all, gain_row, w_head)
+
+
+def picks(slot_ref, dtype):
+    shape = (SLOTS, PAIR)
+    numbers = lax.broadcasted_iota(jnp.int32, shape, 0)
+    return [
+        (numbers == slot_ref[j : j + 1, :]).astype(dtype) for j in range(slot_ref.shape[0])
+    ]
+
+
+def dispatch_kernel(row_ref, slot_ref, out_ref):
+    pick = jnp.concatenate(picks(slot_ref, F32), 0).astype(BF16)
+    out = nn(pick, row_ref[...]).astype(BF16)
+    for j in range(slot_ref.shape[0]):
+        out_ref[j] = out[j * SLOTS : (j + 1) * SLOTS]
+
+
+def dispatch(rows_all, slots):
+    rows, local = rows_all.shape[0], slots.shape[0]
+    pairs = rows // PAIR
+    return pl.pallas_call(
+        dispatch_kernel,
+        grid=(pairs,),
+        in_specs=[
+            pl.BlockSpec((PAIR, D), lambda i: (i, 0)),
+            pl.BlockSpec((local, PAIR), lambda i: (0, i)),
+        ],
+        out_specs=pl.BlockSpec((local, SLOTS, D), lambda i: (0, i, 0)),
+        out_shape=jax.ShapeDtypeStruct((local, pairs * SLOTS, D), BF16),
+        compiler_params=params(24),
+        cost_estimate=cost(2 * rows * D * local * SLOTS, 4 * rows * D),
+        name="dispatch",
+    )(rows_all, slots)
+
+
+def combine_kernel(row_ref, slot_ref, out_ref):
+    local = slot_ref.shape[0]
+    pick = jnp.concatenate(picks(slot_ref, F32), 0).astype(BF16)
+    rows = jnp.concatenate([row_ref[j] for j in range(local)], 0)
+    out_ref[...] = tn(pick, rows).astype(BF16)
+
+
+def combine(slot_rows, slots):
+    local, rows = slots.shape
+    pairs = rows // PAIR
+    return pl.pallas_call(
+        combine_kernel,
+        grid=(pairs,),
+        in_specs=[
+            pl.BlockSpec((local, SLOTS, D), lambda i: (0, i, 0)),
+            pl.BlockSpec((local, PAIR), lambda i: (0, i)),
+        ],
+        out_specs=pl.BlockSpec((PAIR, D), lambda i: (i, 0)),
+        out_shape=jax.ShapeDtypeStruct((rows, D), BF16),
+        compiler_params=params(24),
+        cost_estimate=cost(2 * rows * D * local * SLOTS, 4 * rows * D),
+        name="combine",
+    )(slot_rows, slots)
+
+
+def spread_kernel(dp_ref, slot_ref, out_ref):
+    for j, pick in enumerate(picks(slot_ref, F32)):
+        column = jnp.concatenate([dp_ref[j]] * (PAIR // HD), 1)
+        out_ref[j : j + 1, :] = jnp.sum(pick * column, 0, keepdims=True)
+
+
+def spread_back(dp_slots, slots):
+    local, rows = slots.shape
+    return pl.pallas_call(
+        spread_kernel,
+        grid=(rows // PAIR,),
+        in_specs=[
+            pl.BlockSpec((local, SLOTS, HD), lambda i: (0, i, 0)),
+            pl.BlockSpec((local, PAIR), lambda i: (0, i)),
+        ],
+        out_specs=pl.BlockSpec((local, PAIR), lambda i: (0, i)),
+        out_shape=jax.ShapeDtypeStruct((local, rows), F32),
+        compiler_params=params(24),
+        name="spread_back",
+    )(dp_slots, slots)
+
+
+def expert_kernel(
+    first_ref, x_ref, g_ref, wg_ref, wu_ref, wd_ref, wr_ref, *rest, full
+):
+    if full:
+        (act_ref, dg_ref, du_ref, ge_ref, y_ref, z_ref, dp_ref, gate_s, y_s, z_s, dp_s) = rest
+    else:
+        (act_ref, dg_ref, du_ref, ge_ref, gate_s) = rest
+    step, steps = pl.program_id(1), pl.num_programs(1)
+    rows, grads = x_ref[0], g_ref[0]
+
+    @pl.when(step == 0)
+    def _():
+        logits = nn(rows, wr_ref[...])
+        lane = lax.broadcasted_iota(jnp.int32, logits.shape, 1)
+        logits = jnp.where(lane < EXPERTS, logits, NEG_FILL)
+        powers = jnp.exp(logits - jnp.max(logits, -1, keepdims=True))
+        mine = jnp.where(lane == first_ref[0] + pl.program_id(0), powers, 0.0)
+        gate = jnp.sum(mine, -1, keepdims=True) / jnp.sum(powers, -1, keepdims=True)
+        gate_s[...] = jnp.broadcast_to(gate, gate_s.shape)
+        ge_ref[0] = (grads.astype(F32) * gate).astype(BF16)
+        if full:
+            y_s[...] = jnp.zeros_like(y_s)
+            z_s[...] = jnp.zeros_like(z_s)
+            dp_s[...] = jnp.zeros_like(dp_s)
+
+    gate = gate_s[:, 0:1]
+    gate_pre = nn(rows, wg_ref[0])
+    up_pre = nn(rows, wu_ref[0])
+    slope = nt(grads, wd_ref[0])
+    sig = jax.nn.sigmoid(gate_pre)
+    silu = gate_pre * sig
+    act = (silu * up_pre).astype(BF16)
+    grad_act = slope * gate
+    grad_gate = (grad_act * up_pre * sig * (1.0 + gate_pre * (1.0 - sig))).astype(BF16)
+    grad_up = (grad_act * silu).astype(BF16)
+    act_ref[0] = act
+    dg_ref[0] = grad_gate
+    du_ref[0] = grad_up
+    if full:
+        dp_s[...] += jnp.broadcast_to(
+            jnp.sum(act.astype(F32) * slope, -1, keepdims=True), dp_s.shape
+        )
+        y_s[...] += nn(act, wd_ref[0])
+        z_s[...] += nt(grad_gate, wg_ref[0]) + nt(grad_up, wu_ref[0])
+
+        @pl.when(step == steps - 1)
+        def _():
+            y_ref[0] = (y_s[...] * gate).astype(BF16)
+            z_ref[0] = z_s[...].astype(BF16)
+            dp_ref[0] = dp_s[...]
+
+
+def experts(first, rows, grads, w_gate, w_up, w_down, router, full):
+    local, count, _ = rows.shape
+    hidden = w_gate.shape[2]
+    chunk = hidden // 2
+    row_spec = pl.BlockSpec((1, count, D), lambda j, f, s: (j, 0, 0))
+    mid_spec = pl.BlockSpec((1, count, chunk), lambda j, f, s: (j, 0, f))
+    in_w = pl.BlockSpec((1, D, chunk), lambda j, f, s: (j, 0, f))
+    mid_shape = jax.ShapeDtypeStruct((local, count, hidden), BF16)
+    row_shape = jax.ShapeDtypeStruct((local, count, D), BF16)
+    out_specs = [mid_spec, mid_spec, mid_spec, row_spec]
+    out_shape = [mid_shape, mid_shape, mid_shape, row_shape]
+    scratch = [pltpu.VMEM((count, HD), F32)]
+    if full:
+        out_specs += [row_spec, row_spec, pl.BlockSpec((1, count, HD), lambda j, f, s: (j, 0, 0))]
+        out_shape += [row_shape, row_shape, jax.ShapeDtypeStruct((local, count, HD), F32)]
+        scratch += [
+            pltpu.VMEM((count, D), F32),
+            pltpu.VMEM((count, D), F32),
+            pltpu.VMEM((count, HD), F32),
+        ]
+    unit = 2 * local * count * hidden * D
+    return pl.pallas_call(
+        functools.partial(expert_kernel, full=full),
+        grid_spec=pltpu.PrefetchScalarGridSpec(
+            num_scalar_prefetch=1,
+            grid=(local, 2),
+            in_specs=[
+                row_spec, row_spec, in_w, in_w,
+                pl.BlockSpec((1, chunk, D), lambda j, f, s: (j, f, 0)),
+                pl.BlockSpec((D, HD), lambda j, f, s: (0, 0)),
+            ],
+            out_specs=out_specs,
+            scratch_shapes=scratch,
+        ),
+        out_shape=out_shape,
+        compiler_params=params(60),
+        cost_estimate=cost((6 if full else 3) * unit, 6 * local * hidden * D + 8 * local * count * D),
+        name="experts_full" if full else "experts_half",
+    )(first, rows, grads, w_gate, w_up, w_down, router)
+
+
+def weights_kernel(
+    half_ref, xa, xb, dga, dgb, dua, dub, aa, ab, gea, geb, gate_ref, up_ref, down_ref
+):
+    gate_ref[0] = tn(xa[0], dga[0]) + tn(xb[0], dgb[0])
+    up_ref[0] = tn(xa[0], dua[0]) + tn(xb[0], dub[0])
+    down_ref[0] = tn(aa[0], gea[0]) + tn(ab[0], geb[0])
+
+
+def weight_grads(half, x_pair, dg_pair, du_pair, act_pair, ge_pair):
+    local, count, _ = x_pair[0].shape
+    hidden = dg_pair[0].shape[2]
+    x_spec = pl.BlockSpec((1, count, D // 2), lambda j, f, s: (j, 0, s[0]))
+    d_spec = pl.BlockSpec((1, count, hidden // 2), lambda j, f, s: (j, 0, f))
+    a_spec = pl.BlockSpec((1, count, hidden // 2), lambda j, f, s: (j, 0, s[0]))
+    g_spec = pl.BlockSpec((1, count, D // 2), lambda j, f, s: (j, 0, f))
+    unit = 2 * local * count * hidden * D
+    return pl.pallas_call(
+        weights_kernel,
+        grid_spec=pltpu.PrefetchScalarGridSpec(
+            num_scalar_prefetch=1,
+            grid=(local, 2),
+            in_specs=[x_spec] * 2 + [d_spec] * 4 + [a_spec] * 2 + [g_spec] * 2,
+            out_specs=[
+                pl.BlockSpec((1, D // 2, hidden // 2), lambda j, f, s: (j, 0, f)),
+                pl.BlockSpec((1, D // 2, hidden // 2), lambda j, f, s: (j, 0, f)),
+                pl.BlockSpec((1, hidden // 2, D // 2), lambda j, f, s: (j, 0, f)),
+            ],
+        ),
+        out_shape=[
+            jax.ShapeDtypeStruct((local, D // 2, hidden), F32),
+            jax.ShapeDtypeStruct((local, D // 2, hidden), F32),
+            jax.ShapeDtypeStruct((local, hidden // 2, D), F32),
+        ],
+        compiler_params=params(60),
+        cost_estimate=cost(3 * unit, 6 * local * hidden * D + 8 * local * count * D),
+        name="weight_grads",
+    )(half, *x_pair, *dg_pair, *du_pair, *act_pair, *ge_pair)
+
+
+def swap(value, axis):
+    return lax.ppermute(value, axis, [(0, 1), (1, 0)])
+
+
+def total_over_ep(value):
+    value = value + swap(value, "core")
+    value = value + swap(value, "x")
+    value = value + lax.ppermute(value, "z", [(0, 1), (1, 0), (2, 3), (3, 2)])
+    return value + lax.ppermute(value, "z", [(0, 2), (2, 0), (1, 3), (3, 1)])
+
+
+def gather_rows(value):
+    return lax.all_gather(value, EP, axis=0, tiled=True)
+
+
+def reduce_rows(value):
+    return lax.psum_scatter(value, EP, scatter_dimension=0, tiled=True)
+
+
+def expert_slots(routes_all, first, local):
+    rows = routes_all.shape[0]
+    ids = first + jnp.arange(local, dtype=jnp.int32)
+    named = jnp.any(routes_all[None, :, :] == ids[:, None, None], -1).reshape(
+        local, rows // TOK_DEV, TOK_DEV
+    )
+    places = jnp.arange(TOK_DEV, dtype=jnp.int32)
+    upto = (places[:, None] <= places[None, :]).astype(BF16)
+    rank = jnp.einsum(
+        "ebt,ts->ebs", named.astype(BF16), upto, preferred_element_type=F32
+    ).astype(jnp.int32)
+    base = (jnp.arange(rows // TOK_DEV, dtype=jnp.int32) % 2) * CAP
+    return jnp.where(named, rank - 1 + base[None, :, None], -1).reshape(local, rows)
+
+
+def fast_shards(
+    tokens, w_query, w_key, w_value, w_output, w_router, attn_gain, query_gain, key_gain,
+    moe_gain, w_gate, w_up, w_down, routes, cotangent,
+):
+    group = lax.axis_index("grp")
+    place = lax.axis_index(EP)
+    members = lax.axis_size(EP)
+    seq = TOK_DEV * members
+    local = w_gate.shape[0]
+    wide = w_query.shape[0]
+    first = (place * local).reshape(1).astype(jnp.int32)
+
+    small = jnp.concatenate(
+        [
+            w_router,
+            routes.reshape(-1, EXPERTS).astype(BF16),
+            jnp.stack([attn_gain, query_gain, key_gain, moe_gain]),
+            jnp.zeros((12, EXPERTS), BF16),
+        ],
+        0,
+    )
+    small_all = lax.all_gather(small, ALL)
+    route_rows = TOK_DEV * TOPK // EXPERTS
+    router_full = small_all[:, :wide].reshape(D, EXPERTS)
+    routes_all = (
+        small_all[:, wide : wide + route_rows].reshape(2, seq, TOPK).astype(jnp.int32)
+    )
+    gains = jnp.transpose(
+        small_all[:, wide + route_rows : wide + route_rows + 4], (1, 0, 2)
+    ).reshape(4, D).astype(F32)
+    router_wide = jnp.concatenate([router_full, jnp.zeros((D, HD - EXPERTS), BF16)], 1)
+    head_gains = lax.dynamic_slice(gains, (0, place * HD), (4, HD))
+    gain_q, gain_k = head_gains[1:2], head_gains[2:3]
+    attn_row, moe_row = gains[0:1], gains[3:4]
+
+    tok_all = gather_rows(tokens)
+    columns = jnp.stack([w_query, w_key, w_value], 1).reshape(wide, 3, HEADS, HD)
+    columns = jnp.transpose(columns, (2, 0, 1, 3)).reshape(HEADS, wide, 3 * HD)
+    mine = lax.all_to_all(columns, EP, 0, 0, tiled=True).reshape(D // 2, 3 * HD)
+    other = swap(mine, "grp")
+    w_head = jnp.where(
+        group == 0, jnp.concatenate([mine, other], 0), jnp.concatenate([other, mine], 0)
+    )
+    half_out = gather_rows(w_output)
+    other_out = swap(half_out, "grp")
+    output_full = jnp.where(
+        group == 0,
+        jnp.concatenate([half_out, other_out], 0),
+        jnp.concatenate([other_out, half_out], 0),
+    )
+    cot_own = gather_rows(cotangent)
+    cot_other = swap(cot_own, "grp")
+
+    slots_own = expert_slots(lax.dynamic_index_in_dim(routes_all, group, 0, False), first, local)
+    slots_other = expert_slots(
+        lax.dynamic_index_in_dim(routes_all, 1 - group, 0, False), first, local
+    )
+
+    positions = jnp.arange(seq, dtype=jnp.int32)
+    half_dim = HD // 2
+    frequency = jnp.exp(-(2.0 * jnp.arange(half_dim, dtype=F32) / HD) * math.log(10000.0))
+    angles = positions.astype(F32)[:, None] * frequency[None, :]
+    cosine = jnp.concatenate([jnp.cos(angles)] * 2, 1)
+    sine = jnp.concatenate([-jnp.sin(angles), jnp.sin(angles)], 1)
+
+    qkv, stat = project(tok_all, w_head, attn_row)
+    stat = total_over_ep(stat)
+    q16, k16, v16, attn_float, att_head, lse = attend(qkv, stat, gain_q, gain_k, cosine, sine)
+    attended = lax.all_to_all(att_head.reshape(members, TOK_DEV, HD), EP, 0, 0, tiled=True)
+    attended = jnp.transpose(attended, (1, 0, 2)).reshape(TOK_DEV, D)
+
+    inputs = tokens.astype(F32)
+    branch_attn = nn(attended, output_full)
+    hidden = inputs + branch_attn
+    moe_inv = inv_rms(hidden)
+    mixed = (hidden * moe_inv * moe_row).astype(BF16)
+    mixed_own = gather_rows(mixed)
+    mixed_other = swap(mixed_own, "grp")
+
+    route_probs = jax.nn.softmax(nn(mixed, router_full), -1)
+    g_own = dispatch(cot_own, slots_own)
+    x_own = dispatch(mixed_own, slots_own)
+    act_a, dg_a, du_a, ge_a, y_rows, z_rows, dp_slots = experts(
+        first, x_own, g_own, w_gate, w_up, w_down, router_wide, True
+    )
+    mixed_part = combine(z_rows, slots_own)
+    grad_mixed = reduce_rows(mixed_part).astype(F32)
+    dp_part = spread_back(dp_slots, slots_own)
+    dp_part = jnp.transpose(dp_part.reshape(local, members, TOK_DEV), (1, 0, 2))
+    dp = lax.all_to_all(dp_part, EP, 0, 0, tiled=True).reshape(EXPERTS, TOK_DEV).T
+
+    branch_moe = reduce_rows(combine(y_rows, slots_own)).astype(F32)
+    output = (hidden + branch_moe).astype(BF16)
+
+    grad_logits = (
+        route_probs * (dp - jnp.sum(route_probs * dp, -1, keepdims=True))
+    ).astype(BF16)
+    router_part = tn(mixed, grad_logits)
+    grad_mixed = grad_mixed + nt(grad_logits, router_full)
+    grad_hid_norm, moe_gain_part = norm_back(grad_mixed, hidden, moe_inv, moe_row)
+    grad_hidden = cotangent.astype(F32) + grad_hid_norm
+    grad_branch = grad_hidden.astype(BF16)
+    grad_attended = nt(grad_branch, output_full).astype(BF16)
+    grad_att_head = lax.all_to_all(
+        jnp.transpose(grad_attended.reshape(TOK_DEV, HEADS, HD), (1, 0, 2)), EP, 0, 0, tiled=True
+    ).reshape(seq, HD)
+
+    output_part = tn(attended, grad_branch).astype(BF16)
+    output_keep = lax.dynamic_slice_in_dim(output_part, group * (D // 2), D // 2, 0)
+    output_send = lax.dynamic_slice_in_dim(output_part, (1 - group) * (D // 2), D // 2, 0)
+    output_grad = reduce_rows(
+        (output_keep.astype(F32) + swap(output_send, "grp").astype(F32)).astype(BF16)
+    ).astype(F32)
+
+    dnq, dnk, dv16, means, gain_parts = attend_back(
+        q16, k16, v16, grad_att_head, attn_float, lse, qkv, stat, gain_q, gain_k, cosine, sine
+    )
+    means = total_over_ep(means)
+    normed_part, dw_head = project_back(
+        dnq, dnk, dv16, qkv, stat, means, gain_q, gain_k, tok_all, attn_row, w_head
+    )
+    grad_normed = reduce_rows(normed_part).astype(F32)
+    attn_inv = inv_rms(inputs)
+    scaled = grad_normed * attn_row
+    grad_tok = attn_inv * (
+        scaled - inputs * attn_inv * attn_inv * jnp.mean(scaled * inputs, -1, keepdims=True)
+    )
+    tokens_grad = (grad_hidden + grad_tok).astype(BF16)
+
+    dw_keep = lax.dynamic_slice_in_dim(dw_head, group * (D // 2), D // 2, 0)
+    dw_send = lax.dynamic_slice_in_dim(dw_head, (1 - group) * (D // 2), D // 2, 0)
+    dw_half = (dw_keep + swap(dw_send.astype(BF16), "grp").astype(F32)).astype(BF16)
+    gain_parts = gain_parts + swap(gain_parts, "grp")
+    sums = jnp.stack(
+        [jnp.sum(inputs * inputs), jnp.sum(branch_attn * branch_attn), jnp.sum(branch_moe * branch_moe)]
+    )
+    extra = jnp.concatenate(
+        [gain_parts.reshape(1, 2 * HD), sums[None, :], jnp.zeros((1, HD - 3), F32)], 1
+    )
+    high = extra.astype(BF16)
+    low = (extra - high.astype(F32)).astype(BF16)
+    extra = jnp.concatenate([high, low, jnp.zeros((14, 3 * HD), BF16)], 0)
+    payload = jnp.concatenate(
+        [
+            dw_half.reshape(members, wide, 3 * HD),
+            jnp.broadcast_to(extra[None], (members, 16, 3 * HD)),
+        ],
+        1,
+    )
+    arrived = lax.all_to_all(payload, EP, 0, 0, tiled=True).astype(F32)
+    dense = jnp.transpose(
+        arrived[:, :wide].reshape(HEADS, wide, 3, HD), (2, 1, 0, 3)
+    ).reshape(3, wide, D)
+    extras = arrived[:, wide] + arrived[:, wide + 1]
+    rms_stats = jnp.sqrt(jnp.sum(extras[:, 2 * HD : 2 * HD + 3], 0) / (seq * D)).reshape(1, 3)
+    flat = group * members + place
+    head_row = lax.dynamic_slice(
+        extras[:, : 2 * HD].reshape(HEADS, 2, HD // wide, wide),
+        (flat // (HD // wide), 0, flat % (HD // wide), 0),
+        (1, 2, 1, wide),
+    ).reshape(2, wide)
+    attn_gain_grad = (
+        jnp.sum(
+            w_query.astype(F32) * dense[0]
+            + w_key.astype(F32) * dense[1]
+            + w_value.astype(F32) * dense[2],
+            -1,
+        )
+        / attn_gain.astype(F32)
+    )
+
+    rest_part = jnp.concatenate(
+        [router_part, moe_gain_part[:, None], jnp.zeros((D, HD - EXPERTS - 1), F32)], 1
+    )
+    rest = lax.psum_scatter(rest_part, ALL, scatter_dimension=0, tiled=True)
+    router_grad, moe_gain_grad = rest[:, :EXPERTS], rest[:, EXPERTS]
+
+    g_other = dispatch(cot_other, slots_other)
+    x_other = dispatch(mixed_other, slots_other)
+    act_b, dg_b, du_b, ge_b = experts(
+        first, x_other, g_other, w_gate, w_up, w_down, router_wide, False
+    )
+    half = group.reshape(1).astype(jnp.int32)
+    gate_grad, up_grad, down_grad = weight_grads(
+        half, (x_own, x_other), (dg_a, dg_b), (du_a, du_b), (act_a, act_b), (ge_a, ge_b)
+    )
+    return (
+        output, tokens_grad, dense[0], dense[1], dense[2], output_grad, router_grad,
+        attn_gain_grad, head_row[0], head_row[1], moe_gain_grad, gate_grad, up_grad, down_grad,
+        rms_stats,
+    )
+
+
+def fast_solution(mesh, sides):
+    inner = jax.sharding.Mesh(mesh.devices.reshape((2,) + sides), ALL)
+    rows = P(ALL, None)
+    expert = P(EP, None, None)
+    return jax.shard_map(
+        fast_shards,
+        mesh=inner,
+        in_specs=(rows,) * 6 + (P(ALL),) * 4 + (expert,) * 3 + (rows,) * 2,
+        out_specs=(rows,) * 7 + (P(ALL),) * 4 + (P(EP, "grp", None),) * 3 + (P("grp", None),),
+        check_vma=False,
+    )
+
+
 def solution(mesh):
+    sides = SIDES.get(mesh.shape["ep"])
+    if sides is not None and mesh.shape["grp"] == 2:
+        return fast_solution(mesh, sides)
     return jax.shard_map(
         shards,
         mesh=mesh,

time: 2780 us -> 1290 us (0.46)
  waiting for transfers between devices: 1800 us -> 817 us
  blocking collectives: 344 us -> 56 us
  matrix products: 281 us -> 22.9 us
  Pallas kernels: 0 us -> 214 us
  local copies, waits for them, and re-layouts: 194 us -> 80.2 us
  other arithmetic: 94.6 us -> 36.1 us
    reduce_scatter x8 -> x4, waiting for transfers between devices: 1120 us -> 184 us  [reduce_rows(): return lax.psum_scatter(value, EP, scatter_dimension=0, tiled=True)]
    ppermute x0 -> x15, waiting for transfers between devices: none -> 513 us  [the longest x11 504 us: swap(): return lax.ppermute(value, axis, [(0, 1), (1, 0)])]
    all_to_all x4, waiting for transfers between devices: 371 us -> 18.4 us  [the longest x1 13.5 us: fast_shards(): lax.all_to_all(att_head.reshape(members, TOK_DEV, HD), EP, 0, 0, tiled=True)]
    dot_general x34 -> x8, matrix products: 281 us -> 22.9 us  [the longest x2 9.71 us: nn(): lax.dot_general(left, right, (((1,), (0,)), ((), ())), preferred_element_...]
    pallas_call x0 -> x14, Pallas kernels: none -> 214 us  [the longest x2 99.9 us: experts(): pl.pallas_call(functools.partial(expert_kernel, full=full), grid_spec=plt...]
    all_gather x8 -> x4, waiting for transfers between devices: 312 us -> 99.4 us  [gather_rows(): return lax.all_gather(value, EP, axis=0, tiled=True)]
    all_gather x3 -> x1, blocking collectives: 230 us -> 37.9 us  [fast_shards(): small_all = lax.all_gather(small, ALL)]
    unnamed x2 -> x0, blocking collectives: 89.7 us -> none
  transfers between devices with their start and end apart: 20 -> 28, of which waited for: 16 -> 15; matrix products, arithmetic and copies ran while one was open for 17% -> 6% of each run, Pallas kernels for 0% -> 9%
where the time goes in v1:
time: 1290 us
  waiting for transfers between devices  817 us (63%)
  Pallas kernels  214 us (17%)
  local copies, waits for them, and re-layouts  80.2 us (6%)
  blocking collectives  56 us (4%)
  starting transfers between devices  44.7 us (3%)
  other arithmetic  36.1 us (3%)
  matrix products  22.9 us (2%)
  between operations  15.6 us (1%)
    ppermute x11, waiting for transfers between devices, swap(): return lax.ppermute(value, axis, [(0, 1), (1, 0)])  504 us
    reduce_scatter x4, waiting for transfers between devices, reduce_rows(): return lax.psum_scatter(value, EP, scatter_dimension=0, tiled=True)  184 us
    pallas_call x2, Pallas kernels, experts(): pl.pallas_call(functools.partial(expert_kernel, full=full), grid_spec=plt...  99.9 us
    all_gather x4, waiting for transfers between devices, gather_rows(): return lax.all_gather(value, EP, axis=0, tiled=True)  99.4 us
    unnamed x110, local copies, waits for them, and re-layouts  51.4 us
    all_gather x1, blocking collectives, fast_shards(): small_all = lax.all_gather(small, ALL)  37.9 us
    pallas_call x1, Pallas kernels, weight_grads(): pl.pallas_call(weights_kernel, grid_spec=pltpu.PrefetchScalarGridSpec(num...  36.7 us
  transfers between devices with their start and end apart: 28, of which 15 were waited for; matrix products, arithmetic and copies ran while one was open for 6% of the time, Pallas kernels for 9%

profile of v1, /device:TPU:12, one launch (start us, length us, event | category | flops | bytes accessed | tf_op | source)
XLA Modules:
  0.0 1286.4 jit_solution(7838096410385912813)
XLA Ops:
  17.2 6.3 all-to-all-start
  23.5 46.8 %all-gather.9.cloned.1.call-done = bf16[1024,2048]{1,0:T(8,128)(2,1)} async-done(((bf16[64,2048]{1,0:T(8,128)(2,1)}), bf16[1024,2048]{1,0:T(8,128)(2,1)}) %all-gather.9.cloned.1.call-update) | async-done | bytes 4194320 | tf_op jit(solution)/shard_map/all_gather | solution.py:934
  73.4 37.9 %all-gather.1 = bf16[32,96,64]{1,2,0:T(8,128)(2,1)S(1)} all-gather(bf16[1,96,64]{1,2,0:T(8,128)(2,1)S(1)} %bitcast.151), channel_id=2, replica_groups=mesh['grp'=2,'z'=4,'x'=2,'core'=2] {'grp','z','x','core'}, dimensions={0}, use_global_device_ids=true | all-gather | bytes 405504 | tf_op jit(solution)/shard_map/all_gather | solution.py:977
  114.2 65.9 %collective-permute-done = bf16[1024,384]{1,0:T(8,128)(2,1)S(1)} collective-permute-done((bf16[1024,384]{1,0:T(8,128)(2,1)S(1)}, bf16[1024,384]{1,0:T(8,128)(2,1)S(1)}, u32[]{:S(2)}, u32[]{:S(2)}) %collective-permute-start) | collective-permute-done | bytes 786464 | tf_op jit(solution)/shard_map/ppermute | solution.py:923
  180.5 5.0 copy-done.15
  185.5 9.1 project.1
  204.2 4.1 collective-permute-start.4
  210.1 9.7 attend.1
  224.7 6.1 all-to-all-start.1
  230.9 13.5 %all-to-all-done.1 = bf16[16,128,128]{1,2,0:T(8,128)(2,1)S(1)} async-done(((bf16[16,128,128]{1,2,0:T(8,128)(2,1)}), bf16[16,128,128]{1,2,0:T(8,128)(2,1)S(1)}, u32[]{:S(2)}, u32[]{:S(2)}) %all-to-all-start.1) | async-done | bytes 524320 | tf_op jit(solution)/shard_map/all_to_all | solution.py:1024
  244.4 8.3 multiply_reduce_fusion.3
  275.3 52.6 %all-gather.11.cloned.1.call-done.row_ref = bf16[2048,2048]{1,0:T(8,128)(2,1)} async-done(((bf16[128,2048]{1,0:T(8,128)(2,1)}), bf16[2048,2048]{1,0:T(8,128)(2,1)}) %all-gather.11.cloned.1.call-update) | async-done | bytes 8388624 | tf_op jit(solution)/shard_map/all_gather | solution.py:934
  337.3 59.4 %experts_full.1 = (bf16[4,384,1024]{2,1,0:T(8,128)(2,1)}, bf16[4,384,1024]{2,1,0:T(8,128)(2,1)}, bf16[4,384,1024]{2,1,0:T(8,128)(2,1)}, bf16[4,384,2048]{2,1,0:T...) custom-call(s32[1]{0:T(128)} %bitcast.12.first_ref, ...), custom_call_target="tpu_custom_call" | custom-call | flops 38654705664 | bytes 75497472 | tf_op jit(solution)/shard_map/experts_full/pallas_call | solution.py:863
  399.5 4.2 combine.3
  410.0 4.2 combine.2
  423.1 4.5 all-to-all-start.2
  427.8 4.9 all-to-all-done.2
  432.7 78.3 %reduce-scatter.10.cloned.1.call-done = bf16[128,2048]{1,0:T(8,128)(2,1)} async-done(((bf16[2048,2048]{1,0:T(8,128)(2,1)}), bf16[128,2048]{1,0:T(8,128)(2,1)}) %reduce-scatter.10.cloned.1.call-update) | async-done | bytes 524304 | tf_op jit(solution)/shard_map/reduce_scatter | solution.py:938
  513.6 106.2 %reduce-scatter.8.cloned.1.call-done = bf16[128,2048]{1,0:T(8,128)(2,1)} async-done(((bf16[2048,2048]{1,0:T(8,128)(2,1)}), bf16[128,2048]{1,0:T(8,128)(2,1)}) %reduce-scatter.8.cloned.1.call-update) | async-done | bytes 524304 | tf_op jit(solution)/shard_map/reduce_scatter | solution.py:938
  623.3 6.5 fusion.3
  629.9 18.1 %all_to_all.25 = bf16[16,128,128]{2,1,0:T(8,128)(2,1)S(1)} all-to-all(bf16[16,128,128]{2,1,0:T(8,128)(2,1)S(1)} %bitcast.137), channel_id=1, replica_groups=mesh['grp'=2,'z'=4,'x'=2,'core'=2] {'z','x','core'}, dimensions={0} | all-to-all | bytes 1048576 | tf_op jit(solution)/shard_map/all_to_all | solution.py:1059
  648.0 9.5 attend_back.1
  667.7 3.8 collective-permute-done.9
  671.5 16.2 %project_back.1 = (bf16[2048,2048]{1,0:T(8,128)(2,1)}, f32[2048,384]{1,0:T(8,128)S(1)}) custom-call(f32[2048,128]{1,0:T(8,128)S(1)} %get-tuple-element.55.dnq_ref, f32[2048,128]{1,0:T(8,128)S(1)} %get-tuple-element.56.dnk_ref, bf16[2048,128]{1,0:T(8,128)(2,1)S(1)} %get-tuple-element.57.dv_ref, f32[2048,384]{1,0:T(8,128)S(1)} %copy-done.17, ...), custom_call_target="tpu_custom_call" | custom-call | flops 6442450944 | bytes 23068672 | tf_op jit(solution)/shard_map/project_back/pallas_call | solution.py:691
  690.1 3.7 convolution_convert_fusion
  704.0 433.2 %collective-permute-done.12 = bf16[1024,2048]{1,0:T(8,128)(2,1)} collective-permute-done((bf16[1024,2048]{1,0:T(8,128)(2,1)}, bf16[1024,2048]{1,0:T(8,128)(2,1)}, u32[]{:S(2)}, u32[]{:S(2)}) %collective-permute-start.12) | collective-permute-done | bytes 4194336 | tf_op jit(solution)/shard_map/ppermute | solution.py:923
  1137.3 7.7 add_convert_fusion
  1145.5 7.3 dispatch.7.g_ref
  1155.5 7.5 dispatch.6.x_ref.xb
  1168.7 40.5 %experts_half.1 = (bf16[4,384,1024]{2,1,0:T(8,128)(2,1)}, bf16[4,384,1024]{2,1,0:T(8,128)(2,1)}, bf16[4,384,1024]{2,1,0:T(8,128)(2,1)}, bf16[4,384,2048]{2,1,0:T(8,128)(2,1)}) custom-call(s32[1]{0:T(128)} %bitcast.12.first_ref, bf16[4,384,2048]{2,1,0:T(8,128)(2,1)} %copy-done.5, bf16[4,384,2048]{2,1,0:T(8,128)(2,1)} %copy-done.6, ...), custom_call_target="tpu_custom_call" | custom-call | flops 19327352832 | bytes 75497472 | tf_op jit(solution)/shard_map/experts_half/pallas_call | solution.py:863
  1217.9 10.1 all-to-all-start.4
  1228.0 36.7 %weight_grads.1 = (f32[4,1024,1024]{2,1,0:T(8,128)}, f32[4,1024,1024]{2,1,0:T(8,128)}, f32[4,512,2048]{2,1,0:T(8,128)}) custom-call(s32[1]{0:T(128)} %bitcast.35.half_ref, bf16[4,384,2048]{2,1,0:T(8,128)(2,1)} %copy-done.4, bf16[4,384,2048]{2,1,0:T(8,128)(2,1)} %copy-done.5, bf16[4,384,1024]{2,1,0:T(8,128)(2,1)} %get-tuple-element.62.dga, ...), custom_call_target="tpu_custom_call" | custom-call | flops 19327352832 | bytes 75497472 | tf_op jit(solution)/shard_map/weight_grads/pallas_call | solution.py:899
  (260 shorter events, 143.2 us)
Async XLA Ops:
  7.2 63.1 %all-gather.9.cloned.1.call-start = ((), (), s32[]{:S(2)}) async-start(), calls=%async_computation.11 | async-start | bytes 4456448 | tf_op jit(solution)/shard_map/all_gather | solution.py:934
  7.9 172.6 %all-gather.7.cloned.1.call-start = ((), (), s32[]{:S(2)}) async-start(), calls=%async_computation.10 | async-start | bytes 8912896 | tf_op jit(solution)/shard_map/all_gather | solution.py:934
  8.7 257.1 %all-gather.13.cloned.1.call-start = ((), (), s32[]{:S(2)}) async-start(), calls=%async_computation.13 | async-start | bytes 8912896 | tf_op jit(solution)/shard_map/all_gather | solution.py:934
  11.9 60.6 %copy-start.44 = (bf16[64]{0:T(256)(128)(2,1)S(1)}, bf16[64]{0:T(256)(128)(2,1)}, u32[]{:S(2)}) copy-start(bf16[64]{0:T(256)(128)(2,1)} %param.23) | copy-start | bytes 388
  11.9 60.7 %copy-start.45 = (bf16[64]{0:T(256)(128)(2,1)S(1)}, bf16[64]{0:T(256)(128)(2,1)}, u32[]{:S(2)}) copy-start(bf16[64]{0:T(256)(128)(2,1)} %param.24) | copy-start | bytes 388
  12.0 60.8 %copy-start.46 = (bf16[64]{0:T(256)(128)(2,1)S(1)}, bf16[64]{0:T(256)(128)(2,1)}, u32[]{:S(2)}) copy-start(bf16[64]{0:T(256)(128)(2,1)} %param.21) | copy-start | bytes 388
  17.2 53.6 %all-to-all-start = ((bf16[16,64,384]{2,1,0:T(8,128)(2,1)}), bf16[16,64,384]{2,1,0:T(8,128)(2,1)S(1)}, u32[]{:S(2)}, u32[]{:S(2)}) async-start(bf16[16,64,384]{2,1,0:T(8,128)(2,1)} %reshape.296), calls=%async_computation | async-start | bytes 1572864 | tf_op jit(solution)/shard_map/all_to_all | solution.py:994
  70.3 160.6 %collective-permute-start.5 = (bf16[1024,2048]{1,0:T(8,128)(2,1)}, bf16[1024,2048]{1,0:T(8,128)(2,1)}, u32[]{:S(2)}, u32[]{:S(2)}) collective-permute-start(bf16[1024,2048]{1,0:T(8,128)(2,1)} %all-gather.9.cloned.1.call-done), channel_id=1, source_target_pairs={{0,16},{16,0},{1,17},{17,1},{2,18},{18,2},{3,19},{19,3},{4,20},{20... | collective-permute-start | bytes 12582920 | tf_op jit(solution)/shard_map/ppermute | solution.py:923
  70.9 109.2 %collective-permute-start = (bf16[1024,384]{1,0:T(8,128)(2,1)S(1)}, bf16[1024,384]{1,0:T(8,128)(2,1)S(1)}, u32[]{:S(2)}, u32[]{:S(2)}) collective-permute-start(bf16[1024,384]{1,0:T(8,128)(2,1)S(1)} %bitcast.131), channel_id=1, source_target_pairs={{0,16},{16,0},{1,17},{17,1},{2,18},{18,2},{3,19},{19,3},{4,20},{20... | collective-permute-start | bytes 2359304 | tf_op jit(solution)/shard_map/ppermute | solution.py:923
  194.7 1.2 collective-permute-start.1
  195.9 4.3 collective-permute-start.2
  200.3 3.8 collective-permute-start.3
  204.2 6.0 collective-permute-start.4
  224.7 19.7 %all-to-all-start.1 = ((bf16[16,128,128]{1,2,0:T(8,128)(2,1)}), bf16[16,128,128]{1,2,0:T(8,128)(2,1)S(1)}, u32[]{:S(2)}, u32[]{:S(2)}) async-start(bf16[16,128,128]{1,2,0:T(8,128)(2,1)} %copy.150), calls=%async_computation.1 | async-start | bytes 1048576 | tf_op jit(solution)/shard_map/all_to_all | solution.py:1024
  230.8 97.1 %all-gather.11.cloned.1.call-start = ((), (), s32[]{:S(2)}) async-start(), calls=%async_computation.12 | async-start | bytes 8912896 | tf_op jit(solution)/shard_map/all_gather | solution.py:934
  253.7 257.3 %reduce-scatter.10.cloned.1.call-start = ((), (), s32[]{:S(2)}) async-start(), calls=%async_computation.15 | async-start | bytes 8912896 | tf_op jit(solution)/shard_map/reduce_scatter | solution.py:938
  407.2 212.7 %reduce-scatter.8.cloned.1.call-start = ((), (), s32[]{:S(2)}) async-start(), calls=%async_computation.14 | async-start | bytes 8912896 | tf_op jit(solution)/shard_map/reduce_scatter | solution.py:938
  420.4 199.5 %copy-start.37 = (bf16[128,2048]{1,0:T(8,128)(2,1)S(1)}, bf16[128,2048]{1,0:T(8,128)(2,1)}, u32[]{:S(2)}) copy-start(bf16[128,2048]{1,0:T(8,128)(2,1)} %param.29) | copy-start | bytes 1572868
  423.1 9.6 all-to-all-start.2
  427.5 783.8 %reduce-scatter.12.cloned.1.call-start = ((), (), s32[]{:S(2)}) async-start(), calls=%async_computation.16 | async-start | bytes 8912896 | tf_op jit(solution)/shard_map/reduce_scatter | solution.py:938
  657.5 1.6 collective-permute-start.6
  659.1 3.8 collective-permute-start.7
  662.9 3.8 collective-permute-start.8
  666.7 4.7 collective-permute-start.9
  687.7 577.0 %reduce-scatter.16.cloned.1.call-start = ((), (), s32[]{:S(2)}) async-start(), calls=%async_computation.18 | async-start | bytes 1081344
  688.0 457.5 %collective-permute-start.14 = (bf16[2048,2048]{1,0:T(8,128)(2,1)}, bf16[2048,2048]{1,0:T(8,128)(2,1)}, u32[]{:S(2)}, u32[]{:S(2)}) collective-permute-start(bf16[2048,2048]{1,0:T(8,128)(2,1)} %all-gather.13.cloned.1.call-done.row_ref), channel_id=1, source_target_pairs={{0,16},{16,0},{1,17},{17,1},{2,18},{18,2},{3,19},{19,3},{4,20},{20... | collective-permute-start | bytes 25165832 | tf_op jit(solution)/shard_map/ppermute | solution.py:923
  688.6 466.9 %collective-permute-start.13 = (bf16[2048,2048]{1,0:T(8,128)(2,1)}, bf16[2048,2048]{1,0:T(8,128)(2,1)}, u32[]{:S(2)}, u32[]{:S(2)}) collective-permute-start(bf16[2048,2048]{1,0:T(8,128)(2,1)} %all-gather.11.cloned.1.call-done.row_ref), channel_id=1, source_target_pairs={{0,16},{16,0},{1,17},{17,1},{2,18},{18,2},{3,19},{19,3},{4,20},{20... | collective-permute-start | bytes 25165832 | tf_op jit(solution)/shard_map/ppermute | solution.py:923
  699.3 437.9 %collective-permute-start.12 = (bf16[1024,2048]{1,0:T(8,128)(2,1)}, bf16[1024,2048]{1,0:T(8,128)(2,1)}, u32[]{:S(2)}, u32[]{:S(2)}) collective-permute-start(bf16[1024,2048]{1,0:T(8,128)(2,1)} %constant_dynamic-slice_fusion.3), channel_id=1, source_target_pairs={{0,16},{16,0},{1,17},{17,1},{2,18},{18,2},{3,19},{19,3},{4,20},{20... | collective-permute-start | bytes 12582920 | tf_op jit(solution)/shard_map/ppermute | solution.py:923
  704.0 562.2 %reduce-scatter.14.cloned.1.call-start = ((), (), s32[]{:S(2)}) async-start(), calls=%async_computation.17 | async-start | bytes 4456448 | tf_op jit(solution)/shard_map/reduce_scatter | solution.py:938
  1165.7 43.5 %collective-permute-start.11 = (f32[2,128]{1,0:T(2,128)S(1)}, f32[2,128]{1,0:T(2,128)S(1)}, u32[]{:S(2)}, u32[]{:S(2)}) collective-permute-start(f32[2,128]{1,0:T(2,128)S(1)} %get-tuple-element.61), channel_id=1, source_target_pairs={{0,16},{16,0},{1,17},{17,1},{2,18},{18,2},{3,19},{19,3},{4,20},{20... | collective-permute-start | bytes 3080 | tf_op jit(solution)/shard_map/ppermute | solution.py:923
  1167.2 42.0 %collective-permute-start.10 = (bf16[1024,384]{1,0:T(8,128)(2,1)}, bf16[1024,384]{1,0:T(8,128)(2,1)}, u32[]{:S(2)}, u32[]{:S(2)}) collective-permute-start(bf16[1024,384]{1,0:T(8,128)(2,1)} %dynamic-slice_convert_fusion), channel_id=1, source_target_pairs={{0,16},{16,0},{1,17},{17,1},{2,18},{18,2},{3,19},{19,3},{4,20},{20... | collective-permute-start | bytes 2359304 | tf_op jit(solution)/shard_map/ppermute | solution.py:923
  1217.9 51.3 %all-to-all-start.4 = ((bf16[16,80,384]{2,1,0:T(8,128)(2,1)}), bf16[16,80,384]{2,1,0:T(8,128)(2,1)S(1)}, u32[]{:S(2)}, u32[]{:S(2)}) async-start(bf16[16,80,384]{2,1,0:T(8,128)(2,1)} %pad_maximum_fusion.2), calls=%async_computation.7 | async-start | bytes 1966080 | tf_op jit(solution)/shard_map/all_to_all | solution.py:1105
  (45 other events, 610.3 us)
Sparse Core Ops, SparseCore 0:
  10.2 60.0 all-gather.8
  72.5 74.4 all-gather.6
  149.1 73.6 all-gather.12
  253.8 74.0 all-gather.10
  407.3 103.6 reduce-scatter.9
  515.5 104.3 reduce-scatter.7
  687.8 104.4 reduce-scatter.11
  795.1 126.1 reduce-scatter.15
  1145.1 77.1 reduce-scatter.13

commit v2 on v1

--- a/solution.py
+++ b/solution.py
@@ -489,6 +489,7 @@
 ALL = ("grp", "z", "x", "core")
 PAIR = 2 * TOK_DEV
 SLOTS = 2 * CAP
+COST = 0.01
 SIDES = {16: (4, 2, 2)}
 
 
@@ -521,45 +522,79 @@
 
 
 def cost(flops, moved):
-    return pl.CostEstimate(flops=int(flops), bytes_accessed=int(moved), transcendentals=0)
+    return pl.CostEstimate(flops=int(flops * COST), bytes_accessed=int(moved * COST), transcendentals=0)
 
 
 def whole(*dims):
     return pl.BlockSpec(dims, lambda *_: (0,) * len(dims))
 
 
-def project_kernel(tok_ref, w_ref, gain_ref, qkv_ref, stat_ref):
-    rows = tok_ref[...].astype(F32)
-    inverse = lax.rsqrt(jnp.mean(rows * rows, -1, keepdims=True) + EPSILON)
-    normed = (rows * inverse * gain_ref[...]).astype(BF16)
-    out = nn(normed, w_ref[...])
-    qkv_ref[...] = out
-    stat_ref[0:1, :] = as_row(jnp.sum(out[:, :HD] * out[:, :HD], -1, keepdims=True))
-    stat_ref[1:2, :] = as_row(jnp.sum(out[:, HD : 2 * HD] * out[:, HD : 2 * HD], -1, keepdims=True))
-
-
-def project(tok_all, w_head, gain_row):
-    rows = tok_all.shape[0]
-    return pl.pallas_call(
+def ordered(kernel, after, specs, **settings):
+    after = [array for array in after if not any(array is other for other in specs.pop("kept", ()))]
+    inputs = len(specs["in_specs"])
+    prefetch = specs.pop("num_scalar_prefetch", 0)
+    extra = len(after)
+
+    def body(*refs):
+        kept = refs[: prefetch + inputs] + refs[prefetch + inputs + extra :]
+        kernel(*kept)
+
+    specs["in_specs"] = list(specs["in_specs"]) + [pl.BlockSpec(memory_space=pl.ANY)] * extra
+    call = pl.pallas_call(
+        body,
+        grid_spec=pltpu.PrefetchScalarGridSpec(num_scalar_prefetch=prefetch, **specs),
+        **settings,
+    )
+    return lambda *args: call(*args, *after)
+
+
+ANYWHERE = pl.BlockSpec(memory_space=pl.ANY)
+BLOCK_SHAPE = (TOK_DEV, D)
+
+
+def project_kernel(place_ref, own_ref, other_ref, w_ref, gain_ref, *refs):
+    normed_ref, qkv_ref, stat_ref = refs[-3:]
+    core = place_ref[1]
+    for side, tok_ref in ((core, own_ref), (1 - core, other_ref)):
+        here = pl.ds(pl.multiple_of(side * TOK_DEV, TOK_DEV), TOK_DEV)
+        rows = tok_ref[...].astype(F32)
+        inverse = lax.rsqrt(jnp.mean(rows * rows, -1, keepdims=True) + EPSILON)
+        normed = (rows * inverse * gain_ref[...]).astype(BF16)
+        normed_ref[here, :] = normed
+        out = nn(normed, w_ref[...])
+        qkv_ref[here, :] = out
+        for part in range(2):
+            piece = out[:, part * HD : (part + 1) * HD]
+            stat_ref[part : part + 1, here] = as_row(jnp.sum(piece * piece, -1, keepdims=True))
+
+
+def project(chip_core, own, other, w_head, gain_row, buffers, seq, after=()):
+    kept = [] if buffers is None else list(buffers)
+    return ordered(
         project_kernel,
-        grid=(rows // PAIR,),
-        in_specs=[
-            pl.BlockSpec((PAIR, D), lambda i: (i, 0)),
-            whole(D, 3 * HD),
-            whole(1, D),
+        after,
+        dict(
+            num_scalar_prefetch=1,
+            grid=(1,),
+            in_specs=[whole(TOK_DEV, D), whole(TOK_DEV, D), whole(D, 3 * HD), whole(1, D)]
+            + [ANYWHERE] * len(kept),
+            kept=kept,
+            out_specs=[
+                pl.BlockSpec((PAIR, D), lambda i, s: (s[0], 0)),
+                pl.BlockSpec((PAIR, 3 * HD), lambda i, s: (s[0], 0)),
+                pl.BlockSpec((2, PAIR), lambda i, s: (0, s[0])),
+            ],
+        ),
+        out_shape=[
+            jax.ShapeDtypeStruct((seq, D), BF16),
+            jax.ShapeDtypeStruct((seq, 3 * HD), F32),
+            jax.ShapeDtypeStruct((2, seq), F32),
         ],
-        out_specs=[
-            pl.BlockSpec((PAIR, 3 * HD), lambda i: (i, 0)),
-            pl.BlockSpec((2, PAIR), lambda i: (0, i)),
-        ],
-        out_shape=[
-            jax.ShapeDtypeStruct((rows, 3 * HD), F32),
-            jax.ShapeDtypeStruct((2, rows), F32),
-        ],
-        compiler_params=params(32),
-        cost_estimate=cost(2 * rows * D * 3 * HD, 2 * rows * D + 4 * rows * 384),
+        input_output_aliases={5 + i: i for i in range(len(kept))},
+        compiler_params=params(24),
+        cost_estimate=cost(2 * PAIR * D * 3 * HD, 10 * PAIR * D),
         name="project",
-    )(tok_all, w_head, gain_row)
+    )(chip_core, own, other, w_head, gain_row, *kept)
 
 
 def attend_kernel(
@@ -660,104 +695,210 @@
     )(q, k, v, grad, out, lse, qkv, stat, gain_q, gain_k, cosine, sine)
 
 
-def project_back_kernel(
-    dnq_ref, dnk_ref, dv_ref, qkv_ref, stat_ref, means_ref, gq_ref, gk_ref, tok_ref, gain_ref,
-    w_ref, part_ref, dw_ref,
+def finish_kernel(
+    dnq_ref, dnk_ref, dv_ref, qkv_ref, stat_ref, means_ref, gq_ref, gk_ref, out_ref
 ):
-    grads = []
     for part, dn_ref, g_ref in ((0, dnq_ref, gq_ref), (1, dnk_ref, gk_ref)):
         raw = qkv_ref[:, part * HD : (part + 1) * HD]
         inverse = inv_of(stat_ref[part : part + 1, :])
         mean = as_column(means_ref[part : part + 1, :] / D)
         grad = inverse * (dn_ref[...] * g_ref[...] - raw * inverse * inverse * mean)
-        grads.append(grad.astype(BF16))
-    grad = jnp.concatenate(grads + [dv_ref[...]], 1)
-    part_ref[...] = nt(grad, w_ref[...]).astype(BF16)
-    rows = tok_ref[...].astype(F32)
-    inverse = lax.rsqrt(jnp.mean(rows * rows, -1, keepdims=True) + EPSILON)
-    normed = (rows * inverse * gain_ref[...]).astype(BF16)
-
+        out_ref[:, part * HD : (part + 1) * HD] = grad.astype(BF16)
+    out_ref[:, 2 * HD :] = dv_ref[...]
+
+
+def finish(dnq, dnk, dv, qkv, stat, means, gain_q, gain_k):
+    rows = dnq.shape[0]
+    head = pl.BlockSpec((PAIR, HD), lambda i: (i, 0))
+    line = pl.BlockSpec((2, PAIR), lambda i: (0, i))
+    full = pl.BlockSpec((PAIR, 3 * HD), lambda i: (i, 0))
+    return pl.pallas_call(
+        finish_kernel,
+        grid=(rows // PAIR,),
+        in_specs=[head, head, head, full, line, line, whole(1, HD), whole(1, HD)],
+        out_specs=full,
+        out_shape=jax.ShapeDtypeStruct((rows, 3 * HD), BF16),
+        compiler_params=params(24),
+        cost_estimate=cost(20 * rows * 3 * HD, 12 * rows * 3 * HD),
+        name="finish",
+    )(dnq, dnk, dv, qkv, stat, means, gain_q, gain_k)
+
+
+def sort_cores(core, first, second, own_ref, other_ref, at):
+    @pl.when(core == 0)
+    def _():
+        own_ref[at] = first
+        other_ref[at] = second
+
+    @pl.when(core == 1)
+    def _():
+        own_ref[at] = second
+        other_ref[at] = first
+
+
+def normed_part_kernel(place_ref, a_ref, b_ref, w_ref, own_ref, other_ref):
+    for at, g_ref in enumerate((a_ref, b_ref)):
+        out = nt(g_ref[...], w_ref[...]).astype(BF16)
+        sort_cores(place_ref[2], out[:TOK_DEV], out[TOK_DEV:], own_ref, other_ref, at)
+
+
+def normed_part(place, grads, w_head, after=()):
+    blocks = jax.ShapeDtypeStruct((2, TOK_DEV, D), BF16)
+    return ordered(
+        normed_part_kernel,
+        after,
+        dict(
+            num_scalar_prefetch=1,
+            grid=(1,),
+            in_specs=[
+                pl.BlockSpec((PAIR, 3 * HD), lambda i, s: (s[0], 0)),
+                pl.BlockSpec((PAIR, 3 * HD), lambda i, s: (s[1], 0)),
+                whole(D, 3 * HD),
+            ],
+            out_specs=[whole(2, TOK_DEV, D)] * 2,
+        ),
+        out_shape=[blocks, blocks],
+        compiler_params=params(24),
+        cost_estimate=cost(4 * PAIR * D * 3 * HD, 8 * PAIR * D),
+        name="normed_part",
+    )(place, grads, grads, w_head)
+
+
+def dw_kernel(normed_ref, grad_ref, out_ref):
     @pl.when(pl.program_id(0) == 0)
     def _():
-        dw_ref[...] = jnp.zeros_like(dw_ref)
-
-    dw_ref[...] += tn(normed, grad)
-
-
-def project_back(dnq, dnk, dv, qkv, stat, means, gain_q, gain_k, tok_all, gain_row, w_head):
-    rows = tok_all.shape[0]
-    head = pl.BlockSpec((PAIR, HD), lambda i: (i, 0))
-    line = pl.BlockSpec((2, PAIR), lambda i: (0, i))
-    return pl.pallas_call(
-        project_back_kernel,
-        grid=(rows // PAIR,),
-        in_specs=[
-            head, head, head, pl.BlockSpec((PAIR, 3 * HD), lambda i: (i, 0)), line, line,
-            whole(1, HD), whole(1, HD), pl.BlockSpec((PAIR, D), lambda i: (i, 0)),
-            whole(1, D), whole(D, 3 * HD),
+        out_ref[...] = jnp.zeros_like(out_ref)
+
+    out_ref[...] += tn(normed_ref[...], grad_ref[...])
+
+
+def dw_product(normed, grads, after=()):
+    rows = normed.shape[0]
+    return ordered(
+        dw_kernel,
+        after,
+        dict(
+            grid=(rows // 512,),
+            in_specs=[
+                pl.BlockSpec((512, D), lambda i: (i, 0)),
+                pl.BlockSpec((512, 3 * HD), lambda i: (i, 0)),
+            ],
+            out_specs=whole(D, 3 * HD),
+        ),
+        out_shape=jax.ShapeDtypeStruct((D, 3 * HD), F32),
+        compiler_params=params(32),
+        cost_estimate=cost(2 * rows * D * 3 * HD, 3 * rows * D),
+        name="dw_product",
+    )(normed, grads)
+
+
+def picks(slots, dtype):
+    shape = (SLOTS, slots.shape[1])
+    numbers = lax.broadcasted_iota(jnp.int32, shape, 0)
+    return [(numbers == slots[j : j + 1, :]).astype(dtype) for j in range(slots.shape[0])]
+
+
+def pick_matrix(slots):
+    return jnp.concatenate(picks(slots, F32), 0).astype(BF16)
+
+
+def dispatch_kernel(place_ref, own_ref, other_ref, own_slot, other_slot, *refs):
+    out_ref, column_ref = refs[-2:]
+    core = place_ref[1]
+    lanes = pl.ds(pl.multiple_of(place_ref[2] * HD, HD), HD)
+    out = nn(pick_matrix(own_slot[0]), own_ref[...])
+    out = (out + nn(pick_matrix(other_slot[0]), other_ref[...])).astype(BF16)
+    for j in range(out_ref.shape[0]):
+        out_ref[j] = out[j * SLOTS : (j + 1) * SLOTS]
+    for side, row_ref in ((core, own_ref), (1 - core, other_ref)):
+        column_ref[pl.ds(pl.multiple_of(side * TOK_DEV, TOK_DEV), TOK_DEV), :] = row_ref[:, lanes]
+
+
+def dispatch(place, own, other, slots, buffers, after=()):
+    blocks, local, _ = slots.shape
+    kept = [] if buffers is None else list(buffers)
+    return ordered(
+        dispatch_kernel,
+        after,
+        dict(
+            num_scalar_prefetch=1,
+            grid=(1,),
+            in_specs=[
+                whole(*BLOCK_SHAPE),
+                whole(*BLOCK_SHAPE),
+                pl.BlockSpec((1, local, TOK_DEV), lambda i, s: (2 * s[0] + s[1], 0, 0)),
+                pl.BlockSpec((1, local, TOK_DEV), lambda i, s: (2 * s[0] + 1 - s[1], 0, 0)),
+            ]
+            + [ANYWHERE] * len(kept),
+            kept=kept,
+            out_specs=[
+                pl.BlockSpec((local, SLOTS, D), lambda i, s: (0, s[0], 0)),
+                pl.BlockSpec((PAIR, HD), lambda i, s: (s[0], 0)),
+            ],
+        ),
+        out_shape=[
+            jax.ShapeDtypeStruct((local, blocks // 2 * SLOTS, D), BF16),
+            jax.ShapeDtypeStruct((blocks * TOK_DEV, HD), BF16),
         ],
-        out_specs=[pl.BlockSpec((PAIR, D), lambda i: (i, 0)), whole(D, 3 * HD)],
-        out_shape=[
-            jax.ShapeDtypeStruct((rows, D), BF16),
-            jax.ShapeDtypeStruct((D, 3 * HD), F32),
-        ],
-        compiler_params=params(40),
-        cost_estimate=cost(4 * rows * D * 3 * HD, 4 * rows * D + 8 * rows * 384),
-        name="project_back",
-    )(dnq, dnk, dv, qkv, stat, means, gain_q, gain_k, tok_all, gain_row, w_head)
-
-
-def picks(slot_ref, dtype):
-    shape = (SLOTS, PAIR)
-    numbers = lax.broadcasted_iota(jnp.int32, shape, 0)
-    return [
-        (numbers == slot_ref[j : j + 1, :]).astype(dtype) for j in range(slot_ref.shape[0])
-    ]
-
-
-def dispatch_kernel(row_ref, slot_ref, out_ref):
-    pick = jnp.concatenate(picks(slot_ref, F32), 0).astype(BF16)
-    out = nn(pick, row_ref[...]).astype(BF16)
-    for j in range(slot_ref.shape[0]):
+        input_output_aliases={5 + i: i for i in range(len(kept))},
+        compiler_params=params(24),
+        cost_estimate=cost(2 * PAIR * D * local * SLOTS, 4 * PAIR * D),
+        name="dispatch",
+    )(place, own, other, slots, slots, *kept)
+
+
+def plain_dispatch_kernel(row_ref, slot_ref, out_ref):
+    out = sum(nn(pick_matrix(slot_ref[i]), row_ref[i]) for i in range(2)).astype(BF16)
+    for j in range(out_ref.shape[0]):
         out_ref[j] = out[j * SLOTS : (j + 1) * SLOTS]
 
 
-def dispatch(rows_all, slots):
-    rows, local = rows_all.shape[0], slots.shape[0]
-    pairs = rows // PAIR
-    return pl.pallas_call(
-        dispatch_kernel,
-        grid=(pairs,),
-        in_specs=[
-            pl.BlockSpec((PAIR, D), lambda i: (i, 0)),
-            pl.BlockSpec((local, PAIR), lambda i: (0, i)),
-        ],
-        out_specs=pl.BlockSpec((local, SLOTS, D), lambda i: (0, i, 0)),
-        out_shape=jax.ShapeDtypeStruct((local, pairs * SLOTS, D), BF16),
+def plain_dispatch(rows, slots, after=()):
+    blocks, local, _ = slots.shape
+    rows = rows.reshape(blocks, TOK_DEV, D)
+    return ordered(
+        plain_dispatch_kernel,
+        after,
+        dict(
+            grid=(blocks // 2,),
+            in_specs=[
+                pl.BlockSpec((2, TOK_DEV, D), lambda i: (i, 0, 0)),
+                pl.BlockSpec((2, local, TOK_DEV), lambda i: (i, 0, 0)),
+            ],
+            out_specs=pl.BlockSpec((local, SLOTS, D), lambda i: (0, i, 0)),
+        ),
+        out_shape=jax.ShapeDtypeStruct((local, blocks // 2 * SLOTS, D), BF16),
         compiler_params=params(24),
-        cost_estimate=cost(2 * rows * D * local * SLOTS, 4 * rows * D),
-        name="dispatch",
-    )(rows_all, slots)
+        cost_estimate=cost(2 * blocks * TOK_DEV * D * local * SLOTS, 4 * blocks * TOK_DEV * D),
+        name="plain_dispatch",
+    )(rows, slots)
+
+
+def combine_chip(row_ref, slot_ref):
+    rows = jnp.concatenate([row_ref[j] for j in range(row_ref.shape[0])], 0)
+    return [tn(pick_matrix(slot_ref[i]), rows).astype(BF16) for i in range(2)]
 
 
 def combine_kernel(row_ref, slot_ref, out_ref):
-    local = slot_ref.shape[0]
-    pick = jnp.concatenate(picks(slot_ref, F32), 0).astype(BF16)
-    rows = jnp.concatenate([row_ref[j] for j in range(local)], 0)
-    out_ref[...] = tn(pick, rows).astype(BF16)
-
-
-def combine(slot_rows, slots):
-    local, rows = slots.shape
-    pairs = rows // PAIR
-    return pl.pallas_call(
+    first, second = combine_chip(row_ref, slot_ref)
+    out_ref[:TOK_DEV] = first
+    out_ref[TOK_DEV:] = second
+
+
+def combine(slot_rows, slots, after=()):
+    blocks, local, _ = slots.shape
+    rows = blocks * TOK_DEV
+    return ordered(
         combine_kernel,
-        grid=(pairs,),
-        in_specs=[
-            pl.BlockSpec((local, SLOTS, D), lambda i: (0, i, 0)),
-            pl.BlockSpec((local, PAIR), lambda i: (0, i)),
-        ],
-        out_specs=pl.BlockSpec((PAIR, D), lambda i: (i, 0)),
+        after,
+        dict(
+            grid=(blocks // 2,),
+            in_specs=[
+                pl.BlockSpec((local, SLOTS, D), lambda i: (0, i, 0)),
+                pl.BlockSpec((2, local, TOK_DEV), lambda i: (i, 0, 0)),
+            ],
+            out_specs=pl.BlockSpec((PAIR, D), lambda i: (i, 0)),
+        ),
         out_shape=jax.ShapeDtypeStruct((rows, D), BF16),
         compiler_params=params(24),
         cost_estimate=cost(2 * rows * D * local * SLOTS, 4 * rows * D),
@@ -765,37 +906,91 @@
     )(slot_rows, slots)
 
 
+def combine_part_kernel(place_ref, a_ref, b_ref, a_slot, b_slot, own_ref, other_ref):
+    for at, (row_ref, slot_ref) in enumerate(((a_ref, a_slot), (b_ref, b_slot))):
+        first, second = combine_chip(row_ref, slot_ref)
+        sort_cores(place_ref[2], first, second, own_ref, other_ref, at)
+
+
+def combine_part(place, slot_rows, slots, after=()):
+    local = slots.shape[1]
+    shape = jax.ShapeDtypeStruct((2, TOK_DEV, D), BF16)
+    rows = lambda n: pl.BlockSpec((local, SLOTS, D), lambda i, s: (0, s[n], 0))
+    spots = lambda n: pl.BlockSpec((2, local, TOK_DEV), lambda i, s: (s[n], 0, 0))
+    return ordered(
+        combine_part_kernel,
+        after,
+        dict(
+            num_scalar_prefetch=1,
+            grid=(1,),
+            in_specs=[rows(0), rows(1), spots(0), spots(1)],
+            out_specs=[whole(2, TOK_DEV, D)] * 2,
+        ),
+        out_shape=[shape, shape],
+        compiler_params=params(24),
+        cost_estimate=cost(4 * PAIR * D * local * SLOTS, 8 * PAIR * D),
+        name="combine_part",
+    )(place, slot_rows, slot_rows, slots, slots)
+
+
 def spread_kernel(dp_ref, slot_ref, out_ref):
-    for j, pick in enumerate(picks(slot_ref, F32)):
-        column = jnp.concatenate([dp_ref[j]] * (PAIR // HD), 1)
-        out_ref[j : j + 1, :] = jnp.sum(pick * column, 0, keepdims=True)
-
-
-def spread_back(dp_slots, slots):
-    local, rows = slots.shape
-    return pl.pallas_call(
+    for i in range(2):
+        for j, pick in enumerate(picks(slot_ref[i], F32)):
+            out_ref[i, j : j + 1, :] = jnp.sum(pick * dp_ref[j], 0, keepdims=True)
+
+
+def spread_back(dp_slots, slots, after=()):
+    blocks, local, _ = slots.shape
+    return ordered(
         spread_kernel,
-        grid=(rows // PAIR,),
-        in_specs=[
-            pl.BlockSpec((local, SLOTS, HD), lambda i: (0, i, 0)),
-            pl.BlockSpec((local, PAIR), lambda i: (0, i)),
-        ],
-        out_specs=pl.BlockSpec((local, PAIR), lambda i: (0, i)),
-        out_shape=jax.ShapeDtypeStruct((local, rows), F32),
+        after,
+        dict(
+            grid=(blocks // 2,),
+            in_specs=[
+                pl.BlockSpec((local, SLOTS, HD), lambda i: (0, i, 0)),
+                pl.BlockSpec((2, local, TOK_DEV), lambda i: (i, 0, 0)),
+            ],
+            out_specs=pl.BlockSpec((2, local, TOK_DEV), lambda i: (i, 0, 0)),
+        ),
+        out_shape=jax.ShapeDtypeStruct(slots.shape, F32),
         compiler_params=params(24),
         name="spread_back",
     )(dp_slots, slots)
 
 
-def expert_kernel(
-    first_ref, x_ref, g_ref, wg_ref, wu_ref, wd_ref, wr_ref, *rest, full
-):
+def slope_kernel(g_ref, wd_ref, out_ref):
+    out_ref[0] = nt(g_ref[0], wd_ref[0])
+
+
+def slopes(grads, w_down, after=()):
+    local, count, _ = grads.shape
+    hidden = w_down.shape[1]
+    chunk = hidden // 2
+    return ordered(
+        slope_kernel,
+        after,
+        dict(
+            grid=(local, 2),
+            in_specs=[
+                pl.BlockSpec((1, count, D), lambda j, f: (j, 0, 0)),
+                pl.BlockSpec((1, chunk, D), lambda j, f: (j, f, 0)),
+            ],
+            out_specs=pl.BlockSpec((1, count, chunk), lambda j, f: (j, 0, f)),
+        ),
+        out_shape=jax.ShapeDtypeStruct((local, count, hidden), F32),
+        compiler_params=params(24),
+        cost_estimate=cost(2 * local * count * hidden * D, 2 * local * hidden * D),
+        name="slopes",
+    )(grads, w_down)
+
+
+def expert_kernel(first_ref, x_ref, h_ref, wg_ref, wu_ref, wr_ref, *rest, full):
     if full:
-        (act_ref, dg_ref, du_ref, ge_ref, y_ref, z_ref, dp_ref, gate_s, y_s, z_s, dp_s) = rest
+        (act_ref, dg_ref, du_ref, gate_ref, z_ref, dp_ref, z_s, dp_s) = rest
     else:
-        (act_ref, dg_ref, du_ref, ge_ref, gate_s) = rest
+        (act_ref, dg_ref, du_ref, gate_ref) = rest
     step, steps = pl.program_id(1), pl.num_programs(1)
-    rows, grads = x_ref[0], g_ref[0]
+    rows = x_ref[0]
 
     @pl.when(step == 0)
     def _():
@@ -805,17 +1000,15 @@
         powers = jnp.exp(logits - jnp.max(logits, -1, keepdims=True))
         mine = jnp.where(lane == first_ref[0] + pl.program_id(0), powers, 0.0)
         gate = jnp.sum(mine, -1, keepdims=True) / jnp.sum(powers, -1, keepdims=True)
-        gate_s[...] = jnp.broadcast_to(gate, gate_s.shape)
-        ge_ref[0] = (grads.astype(F32) * gate).astype(BF16)
+        gate_ref[0] = jnp.broadcast_to(gate, gate_ref.shape[1:])
         if full:
-            y_s[...] = jnp.zeros_like(y_s)
             z_s[...] = jnp.zeros_like(z_s)
             dp_s[...] = jnp.zeros_like(dp_s)
 
-    gate = gate_s[:, 0:1]
+    gate = gate_ref[0, :, 0:1]
     gate_pre = nn(rows, wg_ref[0])
     up_pre = nn(rows, wu_ref[0])
-    slope = nt(grads, wd_ref[0])
+    slope = h_ref[0]
     sig = jax.nn.sigmoid(gate_pre)
     silu = gate_pre * sig
     act = (silu * up_pre).astype(BF16)
@@ -829,79 +1022,104 @@
         dp_s[...] += jnp.broadcast_to(
             jnp.sum(act.astype(F32) * slope, -1, keepdims=True), dp_s.shape
         )
-        y_s[...] += nn(act, wd_ref[0])
         z_s[...] += nt(grad_gate, wg_ref[0]) + nt(grad_up, wu_ref[0])
 
         @pl.when(step == steps - 1)
         def _():
-            y_ref[0] = (y_s[...] * gate).astype(BF16)
             z_ref[0] = z_s[...].astype(BF16)
             dp_ref[0] = dp_s[...]
 
 
-def experts(first, rows, grads, w_gate, w_up, w_down, router, full):
+def experts(first, rows, slope, w_gate, w_up, router, full, after=()):
     local, count, _ = rows.shape
     hidden = w_gate.shape[2]
     chunk = hidden // 2
     row_spec = pl.BlockSpec((1, count, D), lambda j, f, s: (j, 0, 0))
     mid_spec = pl.BlockSpec((1, count, chunk), lambda j, f, s: (j, 0, f))
+    lane_spec = pl.BlockSpec((1, count, HD), lambda j, f, s: (j, 0, 0))
     in_w = pl.BlockSpec((1, D, chunk), lambda j, f, s: (j, 0, f))
     mid_shape = jax.ShapeDtypeStruct((local, count, hidden), BF16)
-    row_shape = jax.ShapeDtypeStruct((local, count, D), BF16)
-    out_specs = [mid_spec, mid_spec, mid_spec, row_spec]
-    out_shape = [mid_shape, mid_shape, mid_shape, row_shape]
-    scratch = [pltpu.VMEM((count, HD), F32)]
+    lane_shape = jax.ShapeDtypeStruct((local, count, HD), F32)
+    out_specs = [mid_spec, mid_spec, mid_spec, lane_spec]
+    out_shape = [mid_shape, mid_shape, mid_shape, lane_shape]
+    scratch = []
     if full:
-        out_specs += [row_spec, row_spec, pl.BlockSpec((1, count, HD), lambda j, f, s: (j, 0, 0))]
-        out_shape += [row_shape, row_shape, jax.ShapeDtypeStruct((local, count, HD), F32)]
-        scratch += [
-            pltpu.VMEM((count, D), F32),
-            pltpu.VMEM((count, D), F32),
-            pltpu.VMEM((count, HD), F32),
-        ]
+        out_specs += [row_spec, lane_spec]
+        out_shape += [jax.ShapeDtypeStruct((local, count, D), BF16), lane_shape]
+        scratch += [pltpu.VMEM((count, D), F32), pltpu.VMEM((count, HD), F32)]
     unit = 2 * local * count * hidden * D
-    return pl.pallas_call(
+    return ordered(
         functools.partial(expert_kernel, full=full),
-        grid_spec=pltpu.PrefetchScalarGridSpec(
+        after,
+        dict(
             num_scalar_prefetch=1,
             grid=(local, 2),
             in_specs=[
-                row_spec, row_spec, in_w, in_w,
-                pl.BlockSpec((1, chunk, D), lambda j, f, s: (j, f, 0)),
+                row_spec, mid_spec, in_w, in_w,
                 pl.BlockSpec((D, HD), lambda j, f, s: (0, 0)),
             ],
             out_specs=out_specs,
             scratch_shapes=scratch,
         ),
         out_shape=out_shape,
-        compiler_params=params(60),
-        cost_estimate=cost((6 if full else 3) * unit, 6 * local * hidden * D + 8 * local * count * D),
+        compiler_params=params(40),
+        cost_estimate=cost((4 if full else 2) * unit, 4 * local * hidden * D + 8 * local * count * D),
         name="experts_full" if full else "experts_half",
-    )(first, rows, grads, w_gate, w_up, w_down, router)
+    )(first, rows, slope, w_gate, w_up, router)
+
+
+def down_kernel(act_ref, gate_ref, wd_ref, out_ref):
+    out_ref[0] = (nn(act_ref[0], wd_ref[0]) * gate_ref[0, :, 0:1]).astype(BF16)
+
+
+def down(act, gate, w_down, after=()):
+    local, count, hidden = act.shape
+    chunk = D // 2
+    return ordered(
+        down_kernel,
+        after,
+        dict(
+            grid=(local, 2),
+            in_specs=[
+                pl.BlockSpec((1, count, hidden), lambda j, f: (j, 0, 0)),
+                pl.BlockSpec((1, count, HD), lambda j, f: (j, 0, 0)),
+                pl.BlockSpec((1, hidden, chunk), lambda j, f: (j, 0, f)),
+            ],
+            out_specs=pl.BlockSpec((1, count, chunk), lambda j, f: (j, 0, f)),
+        ),
+        out_shape=jax.ShapeDtypeStruct((local, count, D), BF16),
+        compiler_params=params(24),
+        cost_estimate=cost(2 * local * count * hidden * D, 2 * local * hidden * D),
+        name="down",
+    )(act, gate, w_down)
 
 
 def weights_kernel(
-    half_ref, xa, xb, dga, dgb, dua, dub, aa, ab, gea, geb, gate_ref, up_ref, down_ref
+    half_ref, xa, xb, dga, dgb, dua, dub, aa, ab, ga, gb, gate_a, gate_b, gate_ref, up_ref, down_ref
 ):
     gate_ref[0] = tn(xa[0], dga[0]) + tn(xb[0], dgb[0])
     up_ref[0] = tn(xa[0], dua[0]) + tn(xb[0], dub[0])
-    down_ref[0] = tn(aa[0], gea[0]) + tn(ab[0], geb[0])
-
-
-def weight_grads(half, x_pair, dg_pair, du_pair, act_pair, ge_pair):
+    grad_a = (ga[0].astype(F32) * gate_a[0, :, 0:1]).astype(BF16)
+    grad_b = (gb[0].astype(F32) * gate_b[0, :, 0:1]).astype(BF16)
+    down_ref[0] = tn(aa[0], grad_a) + tn(ab[0], grad_b)
+
+
+def weight_grads(half, x_pair, dg_pair, du_pair, act_pair, g_pair, gate_pair, after=()):
     local, count, _ = x_pair[0].shape
     hidden = dg_pair[0].shape[2]
     x_spec = pl.BlockSpec((1, count, D // 2), lambda j, f, s: (j, 0, s[0]))
     d_spec = pl.BlockSpec((1, count, hidden // 2), lambda j, f, s: (j, 0, f))
     a_spec = pl.BlockSpec((1, count, hidden // 2), lambda j, f, s: (j, 0, s[0]))
     g_spec = pl.BlockSpec((1, count, D // 2), lambda j, f, s: (j, 0, f))
+    lane_spec = pl.BlockSpec((1, count, HD), lambda j, f, s: (j, 0, 0))
     unit = 2 * local * count * hidden * D
-    return pl.pallas_call(
+    return ordered(
         weights_kernel,
-        grid_spec=pltpu.PrefetchScalarGridSpec(
+        after,
+        dict(
             num_scalar_prefetch=1,
             grid=(local, 2),
-            in_specs=[x_spec] * 2 + [d_spec] * 4 + [a_spec] * 2 + [g_spec] * 2,
+            in_specs=[x_spec] * 2 + [d_spec] * 4 + [a_spec] * 2 + [g_spec] * 2 + [lane_spec] * 2,
             out_specs=[
                 pl.BlockSpec((1, D // 2, hidden // 2), lambda j, f, s: (j, 0, f)),
                 pl.BlockSpec((1, D // 2, hidden // 2), lambda j, f, s: (j, 0, f)),
@@ -913,10 +1131,10 @@
             jax.ShapeDtypeStruct((local, D // 2, hidden), F32),
             jax.ShapeDtypeStruct((local, hidden // 2, D), F32),
         ],
-        compiler_params=params(60),
+        compiler_params=params(44),
         cost_estimate=cost(3 * unit, 6 * local * hidden * D + 8 * local * count * D),
         name="weight_grads",
-    )(half, *x_pair, *dg_pair, *du_pair, *act_pair, *ge_pair)
+    )(half, *x_pair, *dg_pair, *du_pair, *act_pair, *g_pair, *gate_pair)
 
 
 def swap(value, axis):
@@ -936,6 +1154,175 @@
 
 def reduce_rows(value):
     return lax.psum_scatter(value, EP, scatter_dimension=0, tiled=True)
+
+
+CHIP_ORDER = ((0, 1, 2, 3), (1, 0, 2, 3), (2, 1, 3, 0), (3, 2, 1, 0))
+
+
+def chip_places():
+    z, x = lax.axis_index("z"), lax.axis_index("x")
+    order = jnp.asarray(CHIP_ORDER, jnp.int32)[z]
+    return [[order[s] * 2 + (x if r == 0 else 1 - x) for r in range(2)] for s in range(4)]
+
+
+def shift(value, pairs):
+    return lax.ppermute(value, "z", pairs)
+
+
+def choose_kernel(flag_ref, *refs):
+    out_ref = refs[-1]
+    for i in range(len(refs) - 1):
+
+        @pl.when(flag_ref[i] == 1)
+        def _(i=i):
+            out_ref[...] = refs[i][...]
+
+
+def choose(flags, options, after=()):
+    return ordered(
+        choose_kernel,
+        after,
+        dict(
+            num_scalar_prefetch=1,
+            grid=(1,),
+            in_specs=[whole(*BLOCK_SHAPE)] * len(options),
+            out_specs=whole(*BLOCK_SHAPE),
+        ),
+        out_shape=jax.ShapeDtypeStruct(BLOCK_SHAPE, BF16),
+        compiler_params=params(16),
+        cost_estimate=cost(TOK_DEV * D, 2 * (len(options) + 1) * TOK_DEV * D),
+        name="choose",
+    )(flags, *options)
+
+
+def gather_steps(block, use, work):
+    z = lax.axis_index("z")
+    flags = lambda *tests: jnp.stack([jnp.asarray(test, jnp.int32) for test in tests])
+    below1 = shift(block, [(0, 1), (1, 2), (2, 3)])
+    above1 = shift(block, [(3, 2), (2, 1), (1, 0)])
+    across0 = swap(block, "x")
+    far00 = swap(block, "core")
+    last = work(0, block)
+    column1 = choose(flags(z == 0, z != 0), [above1, below1], [last])
+    below2 = shift(below1, [(1, 2), (2, 3)])
+    above2 = shift(above1, [(2, 1), (1, 0)])
+    across1 = swap(column1, "x")
+    far01, far10 = swap(across0, "core"), swap(column1, "core")
+    last = use(0, 0, block, far00, [column1])
+    last = use(0, 1, across0, far01, [last])
+    last = use(1, 0, column1, far10, [last])
+    last = work(1, last)
+    column2 = choose(
+        flags(z == 0, z == 3, (z == 1) | (z == 2)), [above2, below2, above1], [last]
+    )
+    below3 = shift(below2, [(2, 3)])
+    above3 = shift(above2, [(1, 0)])
+    across2 = swap(column2, "x")
+    far11, far20 = swap(across1, "core"), swap(column2, "core")
+    last = use(1, 1, across1, far11, [column2])
+    last = use(2, 0, column2, far20, [last])
+    last = work(2, last)
+    column3 = choose(
+        flags(z == 0, z == 1, z == 2, z == 3), [above3, above2, below2, below3], [last]
+    )
+    across3 = swap(column3, "x")
+    far21, far30 = swap(across2, "core"), swap(column3, "core")
+    last = use(2, 1, across2, far21, [column3])
+    last = use(3, 0, column3, far30, [last])
+    last = work(3, last)
+    far31 = swap(across3, "core")
+    return use(3, 1, across3, far31, [last])
+
+
+def sum_kernel(*refs):
+    out_ref = refs[-1]
+    total = refs[0][...].astype(F32)
+    for ref in refs[1:-1]:
+        total = total + ref[...].astype(F32)
+    out_ref[...] = total.astype(out_ref.dtype)
+
+
+def sum_blocks(terms, after=(), dtype=BF16):
+    specs, arrays = [], []
+    for term in terms:
+        if isinstance(term, tuple):
+            arrays.append(term[0])
+            specs.append(pl.BlockSpec((None,) + BLOCK_SHAPE, lambda i, n=term[1]: (n, 0, 0)))
+        else:
+            arrays.append(term)
+            specs.append(whole(*BLOCK_SHAPE))
+    return ordered(
+        sum_kernel,
+        after,
+        dict(grid=(1,), in_specs=specs, out_specs=whole(*BLOCK_SHAPE)),
+        out_shape=jax.ShapeDtypeStruct(BLOCK_SHAPE, dtype),
+        compiler_params=params(16),
+        cost_estimate=cost(len(terms) * TOK_DEV * D, 2 * (len(terms) + 1) * TOK_DEV * D),
+        name="sum_blocks",
+    )(*arrays)
+
+
+def pass_on(place, near_up, far_up, near_down, far_down, below, above, after=()):
+    def kernel(place_ref, nu, fu, nd, fd, below_ref, above_ref, up_ref, down_ref):
+        z = place_ref[0]
+
+        def store(out_ref, source_ref, arrived_ref):
+            total = source_ref[...].astype(F32) + arrived_ref[...].astype(F32)
+            out_ref[...] = total.astype(BF16)
+
+        for edge, near, far, arrived, out_ref in (
+            (0, nu, fu, below_ref, up_ref),
+            (3, nd, fd, above_ref, down_ref),
+        ):
+            pl.when(z == edge)(functools.partial(store, out_ref, near, arrived))
+            pl.when(z != edge)(functools.partial(store, out_ref, far, arrived))
+
+    shape = jax.ShapeDtypeStruct(BLOCK_SHAPE, BF16)
+    return ordered(
+        kernel,
+        after,
+        dict(
+            num_scalar_prefetch=1,
+            grid=(1,),
+            in_specs=[whole(*BLOCK_SHAPE)] * 6,
+            out_specs=[whole(*BLOCK_SHAPE)] * 2,
+        ),
+        out_shape=[shape, shape],
+        compiler_params=params(24),
+        cost_estimate=cost(4 * TOK_DEV * D, 16 * TOK_DEV * D),
+        name="pass_on",
+    )(place, near_up, far_up, near_down, far_down, below, above)
+
+
+def reduce_steps(parts, work):
+    place = lax.axis_index("z").reshape(1).astype(jnp.int32)
+    own, near = {}, {}
+    last = None
+    for s in (3, 2, 1, 0):
+        own[s], other = parts(s, [] if last is None else [last])
+        near[s] = swap(other, "core")
+        last = own[s]
+    crossed = {}
+    for s in (3, 2, 1, 0):
+        last = sum_blocks([(own[s], 1), (near[s], 1)], [last])
+        crossed[s] = swap(last, "x")
+    last = work(0, last)
+    low = {}
+    low[3] = last = sum_blocks([(own[3], 0), (near[3], 0), crossed[3]], [last])
+    up3 = shift(low[3], [(0, 1)])
+    down3 = shift(low[3], [(3, 2)])
+    last = work(1, last)
+    low[2] = last = sum_blocks([(own[2], 0), (near[2], 0), crossed[2]], [last])
+    up2, down2 = pass_on(place, low[2], low[3], low[2], low[3], up3, down3)
+    last = work(2, up2)
+    up2 = shift(up2, [(0, 1), (1, 2)])
+    down2 = shift(down2, [(3, 2), (2, 1)])
+    low[1] = last = sum_blocks([(own[1], 0), (near[1], 0), crossed[1]], [last])
+    up1, down1 = pass_on(place, low[1], low[2], low[1], low[1], up2, down2)
+    last = work(3, up1)
+    up1 = shift(up1, [(0, 1), (1, 2), (2, 3)])
+    down1 = shift(down1, [(3, 2), (2, 1), (1, 0)])
+    return sum_blocks([(own[0], 0), (near[0], 0), crossed[0], up1, down1], [last], F32)
 
 
 def expert_slots(routes_all, first, local):
@@ -950,7 +1337,8 @@
         "ebt,ts->ebs", named.astype(BF16), upto, preferred_element_type=F32
     ).astype(jnp.int32)
     base = (jnp.arange(rows // TOK_DEV, dtype=jnp.int32) % 2) * CAP
-    return jnp.where(named, rank - 1 + base[None, :, None], -1).reshape(local, rows)
+    slots = jnp.where(named, rank - 1 + base[None, :, None], -1)
+    return jnp.transpose(slots, (1, 0, 2))
 
 
 def fast_shards(
@@ -965,6 +1353,8 @@
     wide = w_query.shape[0]
     first = (place * local).reshape(1).astype(jnp.int32)
 
+    core = lax.axis_index("core").astype(jnp.int32)
+    chips = chip_places()
     small = jnp.concatenate(
         [
             w_router,
@@ -973,8 +1363,15 @@
             jnp.zeros((12, EXPERTS), BF16),
         ],
         0,
-    )
-    small_all = lax.all_gather(small, ALL)
+    ).reshape(16, 3 * HD)
+    columns = jnp.stack([w_query, w_key, w_value], 1).reshape(wide, 3, HEADS, HD)
+    columns = jnp.transpose(columns, (2, 0, 1, 3)).reshape(HEADS, wide, 3 * HD)
+    columns = jnp.concatenate([columns, jnp.broadcast_to(small, (HEADS,) + small.shape)], 1)
+    mine = lax.all_to_all(columns, EP, 0, 0, tiled=True)
+    other = swap(mine, "grp")
+    both = jnp.where(group == 0, jnp.stack([mine, other]), jnp.stack([other, mine]))
+    w_head = both[:, :, :wide].reshape(D, 3 * HD)
+    small_all = both[:, :, wide:].reshape(2 * members, -1, EXPERTS)
     route_rows = TOK_DEV * TOPK // EXPERTS
     router_full = small_all[:, :wide].reshape(D, EXPERTS)
     routes_all = (
@@ -988,23 +1385,16 @@
     gain_q, gain_k = head_gains[1:2], head_gains[2:3]
     attn_row, moe_row = gains[0:1], gains[3:4]
 
-    tok_all = gather_rows(tokens)
-    columns = jnp.stack([w_query, w_key, w_value], 1).reshape(wide, 3, HEADS, HD)
-    columns = jnp.transpose(columns, (2, 0, 1, 3)).reshape(HEADS, wide, 3 * HD)
-    mine = lax.all_to_all(columns, EP, 0, 0, tiled=True).reshape(D // 2, 3 * HD)
-    other = swap(mine, "grp")
-    w_head = jnp.where(
-        group == 0, jnp.concatenate([mine, other], 0), jnp.concatenate([other, mine], 0)
-    )
-    half_out = gather_rows(w_output)
-    other_out = swap(half_out, "grp")
-    output_full = jnp.where(
+    out_pair = jnp.where(
         group == 0,
-        jnp.concatenate([half_out, other_out], 0),
-        jnp.concatenate([other_out, half_out], 0),
-    )
+        jnp.concatenate([w_output, swap(w_output, "grp")]),
+        jnp.concatenate([swap(w_output, "grp"), w_output]),
+    )
+    output_full = jnp.transpose(
+        gather_rows(out_pair).reshape(members, 2, wide, D), (1, 0, 2, 3)
+    ).reshape(D, D)
     cot_own = gather_rows(cotangent)
-    cot_other = swap(cot_own, "grp")
+    cot_other = gather_rows(swap(cotangent, "grp"))
 
     slots_own = expert_slots(lax.dynamic_index_in_dim(routes_all, group, 0, False), first, local)
     slots_other = expert_slots(
@@ -1018,63 +1408,128 @@
     cosine = jnp.concatenate([jnp.cos(angles)] * 2, 1)
     sine = jnp.concatenate([-jnp.sin(angles), jnp.sin(angles)], 1)
 
-    qkv, stat = project(tok_all, w_head, attn_row)
+    kept = [None]
+
+    def use_tokens(s, r, own, far, after):
+        spot = jnp.stack([chips[s][r], core])
+        kept[0] = project(spot, own, far, w_head, attn_row, kept[0], seq, after)
+        return kept[0][2]
+
+    def idle(_, last):
+        return last
+
+    gather_steps(tokens, use_tokens, idle)
+    normed_all, qkv, stat = kept[0]
     stat = total_over_ep(stat)
     q16, k16, v16, attn_float, att_head, lse = attend(qkv, stat, gain_q, gain_k, cosine, sine)
     attended = lax.all_to_all(att_head.reshape(members, TOK_DEV, HD), EP, 0, 0, tiled=True)
     attended = jnp.transpose(attended, (1, 0, 2)).reshape(TOK_DEV, D)
-
     inputs = tokens.astype(F32)
     branch_attn = nn(attended, output_full)
     hidden = inputs + branch_attn
     moe_inv = inv_rms(hidden)
     mixed = (hidden * moe_inv * moe_row).astype(BF16)
-    mixed_own = gather_rows(mixed)
-    mixed_other = swap(mixed_own, "grp")
-
+
+    early = {}
+
+    def early_work(step, last):
+        if step == 1:
+            early["g"] = plain_dispatch(cot_own, slots_own, [last])
+            return early["g"]
+        if step == 2:
+            early["slope"] = slopes(early["g"], w_down, [last])
+            return early["slope"]
+        return last
+
+    rows = [None]
+
+    def use_mixed(s, r, own, far, after):
+        spot = jnp.stack([chips[s][r], core, place.astype(jnp.int32)])
+        rows[0] = dispatch(spot, own, far, slots_own, rows[0], after)
+        return rows[0][0]
+
+    gather_steps(mixed, use_mixed, early_work)
+    x_own, mixed_columns = rows[0]
+    mixed_other = gather_rows(swap(mixed, "grp"))
+    g_own, slope_own = early["g"], early["slope"]
     route_probs = jax.nn.softmax(nn(mixed, router_full), -1)
-    g_own = dispatch(cot_own, slots_own)
-    x_own = dispatch(mixed_own, slots_own)
-    act_a, dg_a, du_a, ge_a, y_rows, z_rows, dp_slots = experts(
-        first, x_own, g_own, w_gate, w_up, w_down, router_wide, True
-    )
-    mixed_part = combine(z_rows, slots_own)
-    grad_mixed = reduce_rows(mixed_part).astype(F32)
-    dp_part = spread_back(dp_slots, slots_own)
-    dp_part = jnp.transpose(dp_part.reshape(local, members, TOK_DEV), (1, 0, 2))
-    dp = lax.all_to_all(dp_part, EP, 0, 0, tiled=True).reshape(EXPERTS, TOK_DEV).T
-
-    branch_moe = reduce_rows(combine(y_rows, slots_own)).astype(F32)
+    act_a, dg_a, du_a, gate_a, z_rows, dp_slots = experts(
+        first, x_own, slope_own, w_gate, w_up, router_wide, True
+    )
+
+    def place_of(s):
+        return jnp.stack([chips[s][0], chips[s][1], core])
+
+    late = {}
+
+    def late_work(step, last):
+        if step == 0:
+            dp_part = spread_back(dp_slots, slots_own, [last])
+            late["dp"] = lax.all_to_all(dp_part, EP, 0, 0, tiled=True).reshape(EXPERTS, TOK_DEV).T
+            return dp_part
+        if step == 1:
+            late["y"] = down(act_a, gate_a, w_down, [last])
+            return late["y"]
+        if step == 2:
+            return last
+        late["g"] = plain_dispatch(cot_other, slots_other, [last])
+        late["slope"] = slopes(late["g"], w_down, [late["g"]])
+        return late["slope"]
+
+    grad_mixed = reduce_steps(
+        lambda s, after: combine_part(place_of(s), z_rows, slots_own, after), late_work
+    )
+    dp = late["dp"]
+    branch_part = combine(late["y"], slots_own)
+    branch_moe = reduce_rows(branch_part).astype(F32)
     output = (hidden + branch_moe).astype(BF16)
 
     grad_logits = (
         route_probs * (dp - jnp.sum(route_probs * dp, -1, keepdims=True))
     ).astype(BF16)
-    router_part = tn(mixed, grad_logits)
     grad_mixed = grad_mixed + nt(grad_logits, router_full)
     grad_hid_norm, moe_gain_part = norm_back(grad_mixed, hidden, moe_inv, moe_row)
     grad_hidden = cotangent.astype(F32) + grad_hid_norm
     grad_branch = grad_hidden.astype(BF16)
-    grad_attended = nt(grad_branch, output_full).astype(BF16)
-    grad_att_head = lax.all_to_all(
-        jnp.transpose(grad_attended.reshape(TOK_DEV, HEADS, HD), (1, 0, 2)), EP, 0, 0, tiled=True
-    ).reshape(seq, HD)
-
-    output_part = tn(attended, grad_branch).astype(BF16)
-    output_keep = lax.dynamic_slice_in_dim(output_part, group * (D // 2), D // 2, 0)
-    output_send = lax.dynamic_slice_in_dim(output_part, (1 - group) * (D // 2), D // 2, 0)
-    output_grad = reduce_rows(
-        (output_keep.astype(F32) + swap(output_send, "grp").astype(F32)).astype(BF16)
-    ).astype(F32)
-
+    grad_out = nt(grad_branch, output_full).astype(BF16).reshape(TOK_DEV, HEADS, HD)
+    grad_out = jnp.transpose(grad_out, (1, 0, 2))
+    grad_att_head = lax.all_to_all(grad_out, EP, 0, 0, tiled=True).reshape(seq, HD)
+
+    wide_branch = jnp.concatenate(
+        [grad_branch, grad_logits, jnp.zeros((TOK_DEV, HD - EXPERTS), BF16)], 1
+    )
+    branch_all = gather_rows(wide_branch)
     dnq, dnk, dv16, means, gain_parts = attend_back(
         q16, k16, v16, grad_att_head, attn_float, lse, qkv, stat, gain_q, gain_k, cosine, sine
     )
     means = total_over_ep(means)
-    normed_part, dw_head = project_back(
-        dnq, dnk, dv16, qkv, stat, means, gain_q, gain_k, tok_all, attn_row, w_head
-    )
-    grad_normed = reduce_rows(normed_part).astype(F32)
+    qkv_grads = finish(dnq, dnk, dv16, qkv, stat, means, gain_q, gain_k)
+    half = group.reshape(1).astype(jnp.int32)
+
+    def last_work(step, last):
+        if step == 0:
+            late["dw"] = dw_product(normed_all, qkv_grads, [last])
+            return late["dw"]
+        if step == 1:
+            late["x"] = plain_dispatch(mixed_other, slots_other, [last])
+            return late["x"]
+        if step == 2:
+            late["mid"] = experts(
+                first, late["x"], late["slope"], w_gate, w_up, router_wide, False, [last]
+            )
+            return late["mid"][3]
+        act_b, dg_b, du_b, gate_b = late["mid"]
+        late["grads"] = weight_grads(
+            half, (x_own, late["x"]), (dg_a, dg_b), (du_a, du_b), (act_a, act_b),
+            (g_own, late["g"]), (gate_a, gate_b), [last],
+        )
+        return late["grads"][0]
+
+    grad_normed = reduce_steps(
+        lambda s, after: normed_part(place_of(s), qkv_grads, w_head, after), last_work
+    )
+    dw_head = late["dw"]
+    gate_grad, up_grad, down_grad = late["grads"]
     attn_inv = inv_rms(inputs)
     scaled = grad_normed * attn_row
     grad_tok = attn_inv * (
@@ -1094,11 +1549,18 @@
     )
     high = extra.astype(BF16)
     low = (extra - high.astype(F32)).astype(BF16)
-    extra = jnp.concatenate([high, low, jnp.zeros((14, 3 * HD), BF16)], 0)
+    moe_high = moe_gain_part.astype(BF16)
+    moe_low = (moe_gain_part - moe_high.astype(F32)).astype(BF16)
+    moe_rows = jnp.concatenate(
+        [moe_high.reshape(members, 1, HD), moe_low.reshape(members, 1, HD),
+         jnp.zeros((members, 1, HD), BF16)], 2,
+    )
+    extra = jnp.broadcast_to(jnp.stack([high[0], low[0]])[None], (members, 2, 3 * HD))
+    extra = jnp.concatenate([extra, moe_rows, jnp.zeros((members, 13, 3 * HD), BF16)], 1)
     payload = jnp.concatenate(
         [
             dw_half.reshape(members, wide, 3 * HD),
-            jnp.broadcast_to(extra[None], (members, 16, 3 * HD)),
+            extra,
         ],
         1,
     )
@@ -1124,21 +1586,21 @@
         / attn_gain.astype(F32)
     )
 
-    rest_part = jnp.concatenate(
-        [router_part, moe_gain_part[:, None], jnp.zeros((D, HD - EXPERTS - 1), F32)], 1
-    )
-    rest = lax.psum_scatter(rest_part, ALL, scatter_dimension=0, tiled=True)
-    router_grad, moe_gain_grad = rest[:, :EXPERTS], rest[:, EXPERTS]
-
-    g_other = dispatch(cot_other, slots_other)
-    x_other = dispatch(mixed_other, slots_other)
-    act_b, dg_b, du_b, ge_b = experts(
-        first, x_other, g_other, w_gate, w_up, w_down, router_wide, False
-    )
-    half = group.reshape(1).astype(jnp.int32)
-    gate_grad, up_grad, down_grad = weight_grads(
-        half, (x_own, x_other), (dg_a, dg_b), (du_a, du_b), (act_a, act_b), (ge_a, ge_b)
-    )
+    moe_sums = jnp.sum(arrived[:, wide + 2], 0)
+    moe_part = (moe_sums[:HD] + moe_sums[HD : 2 * HD]).reshape(2, wide, 1)
+    out_part = tn(att_head, branch_all[:, :D]).reshape(2, wide, D)
+    router_part = tn(mixed_columns, branch_all[:, D : D + EXPERTS]).reshape(2, wide, EXPERTS)
+    out_part = jnp.concatenate(
+        [out_part, router_part, moe_part, jnp.zeros((2, wide, HD - EXPERTS - 1), F32)], 2
+    )
+    out_keep = lax.dynamic_index_in_dim(out_part, group, 0, False)
+    out_send = lax.dynamic_index_in_dim(out_part, 1 - group, 0, False).astype(BF16)
+    out_sum = (out_keep + swap(out_send, "grp").astype(F32)).astype(BF16)
+    owners = [(g * members + e, 2 * e + g) for g in range(2) for e in range(members)]
+    owned = lax.ppermute(out_sum, ALL, owners).astype(F32)
+    output_grad = owned[:, :D]
+    router_grad, moe_gain_grad = owned[:, D : D + EXPERTS], owned[:, D + EXPERTS]
+
     return (
         output, tokens_grad, dense[0], dense[1], dense[2], output_grad, router_grad,
         attn_gain_grad, head_row[0], head_row[1], moe_gain_grad, gate_grad, up_grad, down_grad,

time: 1290 us -> 922 us (0.71)
  waiting for transfers between devices: 817 us -> 237 us
  starting transfers between devices: 44.7 us -> 123 us
  local copies, waits for them, and re-layouts: 80.2 us -> 150 us
  Pallas kernels: 214 us -> 258 us
  blocking collectives: 56 us -> 69.1 us
    ppermute x11 -> x51, waiting for transfers between devices: 504 us -> 105 us  [swap(): return lax.ppermute(value, axis, [(0, 1), (1, 0)])]
    reduce_scatter x4 -> x1, waiting for transfers between devices: 184 us -> 0.01 us  [reduce_rows(): return lax.psum_scatter(value, EP, scatter_dimension=0, tiled=True)]
    all_gather x4 -> x5, waiting for transfers between devices: 99.4 us -> 0.03 us  [gather_rows(): return lax.all_gather(value, EP, axis=0, tiled=True)]
    ppermute x0 -> x25, waiting for transfers between devices: none -> 79.9 us  [the longest x24 70.3 us: shift(): return lax.ppermute(value, 'z', pairs)]
    ppermute x0 -> x25, starting transfers between devices: none -> 65.3 us  [the longest x24 63.3 us: shift(): return lax.ppermute(value, 'z', pairs)]
    unnamed x110 -> x252, local copies, waits for them, and re-layouts: 51.4 us -> 109 us
    all_to_all x1 -> x2, blocking collectives: 18.1 us -> 69.1 us  [the longest x1 48.7 us: fast_shards(): mine = lax.all_to_all(columns, EP, 0, 0, tiled=True)]
    pallas_call x12 -> x63, Pallas kernels: 195 us -> 238 us  [the longest x62 236 us: ordered(): return lambda *args: call(*args, *after)]
  transfers between devices with their start and end apart: 28 -> 89, of which waited for: 15 -> 34; matrix products, arithmetic and copies ran while one was open for 6% -> 9% of each run, Pallas kernels for 9% -> 28%
where the time goes in v2:
time: 922 us; the launch traced here: 910 us
  Pallas kernels  258 us (28%)
  waiting for transfers between devices  237 us (26%)
  local copies, waits for them, and re-layouts  150 us (16%)
  starting transfers between devices  123 us (13%)
  blocking collectives  69.1 us (7%)
  other arithmetic  32.3 us (4%)
  matrix products  21.1 us (2%)
  between operations  19.2 us (2%)
    pallas_call x62, Pallas kernels, ordered(): return lambda *args: call(*args, *after)  236 us
    unnamed x252, local copies, waits for them, and re-layouts  109 us
    ppermute x51, waiting for transfers between devices, swap(): return lax.ppermute(value, axis, [(0, 1), (1, 0)])  105 us
    ppermute x24, waiting for transfers between devices, shift(): return lax.ppermute(value, 'z', pairs)  70.3 us
    ppermute x24, starting transfers between devices, shift(): return lax.ppermute(value, 'z', pairs)  63.3 us
    all_to_all x1, blocking collectives, fast_shards(): mine = lax.all_to_all(columns, EP, 0, 0, tiled=True)  48.7 us
    ppermute x51, starting transfers between devices, swap(): return lax.ppermute(value, axis, [(0, 1), (1, 0)])  32.8 us
    all_to_all x1, waiting for transfers between devices, fast_shards(): arrived = lax.all_to_all(payload, EP, 0, 0, tiled=True).astype(F32)  20.5 us
  transfers between devices with their start and end apart: 89, of which 34 were waited for; matrix products, arithmetic and copies ran while one was open for 9% of the time, Pallas kernels for 28%

profile of v2, /device:TPU:12, one launch (start us, length us, event | category | flops | bytes accessed | tf_op | source)
XLA Modules:
  0.0 909.8 jit_solution(5840845083530674269)
XLA Ops:
  7.8 7.7 collective-permute-done.23
  18.9 12.5 %collective-permute-done.56 = bf16[128,2048]{1,0:T(8,128)(2,1)S(1)} collective-permute-done((bf16[128,2048]{1,0:T(8,128)(2,1)}, bf16[128,2048]{1,0:T(8,128)(2,1)S(1)}, u32[]{:S(2)}, u32[]{:S(2)}) %collective-permute-start.56) | collective-permute-done | bytes 524320 | tf_op jit(solution)/shard_map/ppermute | solution.py:1141
  38.2 48.7 %all_to_all.25 = bf16[16,80,384]{2,1,0:T(8,128)(2,1)S(1)} all-to-all(bf16[16,80,384]{2,1,0:T(8,128)(2,1)S(1)} %pad_maximum_fusion.2), channel_id=1, replica_groups=mesh['grp'=2,'z'=4,'x'=2,'core'=2] {'z','x','core'}, dimensions={0} | all-to-all | bytes 1966080 | tf_op jit(solution)/shard_map/all_to_all | solution.py:1370
  99.2 14.0 %collective-permute-done.refs_1_.refs_3_ = bf16[128,2048]{1,0:T(8,128)(2,1)} collective-permute-done((bf16[128,2048]{1,0:T(8,128)(2,1)S(1)}, bf16[128,2048]{1,0:T(8,128)(2,1)}, u32[]{:S(2)}, u32[]{:S(2)}) %collective-permute-start) | collective-permute-done | bytes 524320 | tf_op jit(solution)/shard_map/ppermute | solution.py:1169
  173.6 12.1 %collective-permute-done.2.refs_1_ = bf16[128,2048]{1,0:T(8,128)(2,1)} collective-permute-done((bf16[128,2048]{1,0:T(8,128)(2,1)}, bf16[128,2048]{1,0:T(8,128)(2,1)}, u32[]{:S(2)}, u32[]{:S(2)}) %collective-permute-start.2) | collective-permute-done | bytes 524320 | tf_op jit(solution)/shard_map/ppermute | solution.py:1169
  191.8 11.6 %collective-permute-done.14.refs_1_ = bf16[128,2048]{1,0:T(8,128)(2,1)} collective-permute-done((bf16[128,2048]{1,0:T(8,128)(2,1)}, bf16[128,2048]{1,0:T(8,128)(2,1)}, u32[]{:S(2)}, u32[]{:S(2)}) %collective-permute-start.14) | collective-permute-done | bytes 524320 | tf_op jit(solution)/shard_map/ppermute | solution.py:1141
  239.6 10.2 %attend.1 = (bf16[2048,128]{1,0:T(8,128)(2,1)S(1)}, bf16[2048,128]{1,0:T(8,128)(2,1)S(1)}, bf16[2048,128]{1,0:T(8,128)(2,1)S(1)}, f32[2048,128]{1,0:T(8,128)S(1)...) custom-call(f32[2048,384]{1,0:T(8,128)} %copy-done.12, f32[2,2048]{1,0:T(2,128)S(1)} %add.220.stat_ref, ...), custom_call_target="tpu_custom_call" | custom-call | flops 42949672 | bytes 78643 | tf_op jit(solution)/shard_map/attend/pallas_call | solution.py:633
  254.2 6.3 all-to-all-start.1
  260.8 8.5 copy.137
  269.3 15.7 %all-to-all-done.1 = bf16[16,128,128]{1,2,0:T(8,128)(2,1)S(1)} async-done(((bf16[16,128,128]{1,2,0:T(8,128)(2,1)}), bf16[16,128,128]{1,2,0:T(8,128)(2,1)S(1)}, u32[]{:S(2)}, u32[]{:S(2)}) %all-to-all-start.1) | async-done | bytes 524320 | tf_op jit(solution)/shard_map/all_to_all | solution.py:1425
  357.8 12.0 %slopes.2.refs_5_.refs_2_ = f32[4,384,1024]{2,1,0:T(8,128)S(1)} custom-call(bf16[4,384,2048]{2,1,0:T(8,128)(2,1)S(1)} %plain_dispatch.3.refs_4_.refs_0_.refs_9_, bf16[4,1024,2048]{2,1,0:T(8,128)(2,1)} %refs_1_.5, bf16[4,384,2048]{2,1,0:T(8,128)(2,1)S(1)} %copy-done.3), custom_call_target="tpu_custom_call" | custom-call | flops 64424508 | bytes 167772 | tf_op jit(solution)/shard_map/slopes/pallas_call | solution.py:548
  375.0 12.7 %collective-permute-done.37.refs_1_ = bf16[128,2048]{1,0:T(8,128)(2,1)S(1)} collective-permute-done((bf16[128,2048]{1,0:T(8,128)(2,1)S(1)}, bf16[128,2048]{1,0:T(8,128)(2,1)S(1)}, u32[]{:S(2)}, u32[]{:S(2)}) %collective-permute-start.37) | collective-permute-done | bytes 524320 | tf_op jit(solution)/shard_map/ppermute | solution.py:1141
  394.2 40.2 %experts_full.1 = (bf16[4,384,1024]{2,1,0:T(8,128)(2,1)S(1)}, bf16[4,384,1024]{2,1,0:T(8,128)(2,1)S(1)}, bf16[4,384,1024]{2,1,0:T(8,128)(2,1)S(1)}, f32[4,384,12...) custom-call(s32[1]{0:T(128)} %bitcast.34.refs_0_, bf16[4,384,2048]{2,1,0:T(8,128)(2,1)} %copy-done.5, ...), custom_call_target="tpu_custom_call" | custom-call | flops 257698032 | bytes 587202 | tf_op jit(solution)/shard_map/experts_full/pallas_call | solution.py:548
  434.5 6.4 copy-done.11
  456.7 7.3 collective-permute-done.43.refs_2_
  464.2 5.9 copy-done.19
  470.1 9.5 %down.1.refs_0_.refs_3_ = bf16[4,384,2048]{2,1,0:T(8,128)(2,1)S(1)} custom-call(bf16[4,384,1024]{2,1,0:T(8,128)(2,1)S(1)} %get-tuple-element.142.refs_0_.refs_7_, f32[4,384,128]{2,1,0:T(8,128)S(1)} %get-tuple-element.143.refs_1_.refs_11_, bf16[4,1024,2048]{2,1,0:T(8,128)(2,1)S(1)} %copy-done.19, bf16[128,2048]{1,0:T(8,128)(2,1)S(1)} %sum_blocks.20.refs_3_.refs_2_.refs_4_), custom_call_target="tpu_custom_call" | custom-call | flops 64424508 | bytes 167772 | tf_op jit(solution)/shard_map/down/pallas_call | solution.py:548
  490.5 13.4 %collective-permute-done.67 = bf16[128,2048]{1,0:T(8,128)(2,1)} collective-permute-done((bf16[128,2048]{1,0:T(8,128)(2,1)}, bf16[128,2048]{1,0:T(8,128)(2,1)}, u32[]{:S(2)}, u32[]{:S(2)}) %collective-permute-start.67) | collective-permute-done | bytes 524320 | tf_op jit(solution)/shard_map/ppermute | solution.py:1141
  508.1 11.0 %collective-permute-done.49.refs_2_ = bf16[128,2048]{1,0:T(8,128)(2,1)S(1)} collective-permute-done((bf16[128,2048]{1,0:T(8,128)(2,1)}, bf16[128,2048]{1,0:T(8,128)(2,1)S(1)}, u32[]{:S(2)}, u32[]{:S(2)}) %collective-permute-start.49) | collective-permute-done | bytes 524320 | tf_op jit(solution)/shard_map/ppermute | solution.py:1141
  535.1 28.0 %collective-permute-done.52.refs_5_ = bf16[128,2048]{1,0:T(8,128)(2,1)S(1)} collective-permute-done((bf16[128,2048]{1,0:T(8,128)(2,1)S(1)}, bf16[128,2048]{1,0:T(8,128)(2,1)S(1)}, u32[]{:S(2)}, u32[]{:S(2)}) %collective-permute-start.52) | collective-permute-done | bytes 524320 | tf_op jit(solution)/shard_map/ppermute | solution.py:1169
  572.7 6.2 all-to-all-start.2
  592.9 5.9 copy-done.20
  598.9 8.5 slopes.3.refs_5_.refs_2_
  620.6 6.6 fusion.4
  627.4 20.4 %all_to_all.26 = bf16[16,128,128]{2,1,0:T(8,128)(2,1)S(1)} all-to-all(bf16[16,128,128]{2,1,0:T(8,128)(2,1)S(1)} %bitcast.177), channel_id=1, replica_groups=mesh['grp'=2,'z'=4,'x'=2,'core'=2] {'z','x','core'}, dimensions={0} | all-to-all | bytes 1048576 | tf_op jit(solution)/shard_map/all_to_all | solution.py:1496
  647.8 9.5 %attend_back.1 = (f32[2048,128]{1,0:T(8,128)S(1)}, f32[2048,128]{1,0:T(8,128)S(1)}, bf16[2048,128]{1,0:T(8,128)(2,1)S(1)}, f32[2,2048]{1,0:T(2,128)S(1)}, f32[2,128]{1,0:T(2,128)S(1)}) custom-call(bf16[2048,128]{1,0:T(8,128)(2,1)S(1)} %copy-done.84, bf16[2048,128]{1,0:T(8,128)(2,1)S(1)} %copy-done.86, bf16[2048,128]{1,0:T(8,128)(2,1)S(1)} %copy-done.88, ...), custom_call_target="tpu_custom_call" | custom-call | flops 107374184 | bytes 157286 | tf_op jit(solution)/shard_map/attend_back/pallas_call | solution.py:687
  717.9 9.2 %collective-permute-done.70.refs_5_ = bf16[128,2048]{1,0:T(8,128)(2,1)} collective-permute-done((bf16[128,2048]{1,0:T(8,128)(2,1)}, bf16[128,2048]{1,0:T(8,128)(2,1)}, u32[]{:S(2)}, u32[]{:S(2)}) %collective-permute-start.70) | collective-permute-done | bytes 524320 | tf_op jit(solution)/shard_map/ppermute | solution.py:1169
  735.9 26.0 %experts_half.1 = (bf16[4,384,1024]{2,1,0:T(8,128)(2,1)S(1)}, bf16[4,384,1024]{2,1,0:T(8,128)(2,1)S(1)}, bf16[4,384,1024]{2,1,0:T(8,128)(2,1)S(1)}, f32[4,384,128]{2,1,0:T(8,128)S(1)}) custom-call(s32[1]{0:T(128)} %bitcast.34.refs_0_, bf16[4,384,2048]{2,1,0:T(8,128)(2,1)} %copy-done.21, f32[4,384,1024]{2,1,0:T(8,128)} %copy-done.27, ...), custom_call_target="tpu_custom_call" | custom-call | flops 128849016 | bytes 587202 | tf_op jit(solution)/shard_map/experts_half/pallas_call | solution.py:548
  786.6 34.0 %weight_grads.1 = (f32[4,1024,1024]{2,1,0:T(8,128)}, f32[4,1024,1024]{2,1,0:T(8,128)}, f32[4,512,2048]{2,1,0:T(8,128)}) custom-call(s32[1]{0:T(128)} %bitcast.52.refs_0_, bf16[4,384,2048]{2,1,0:T(8,128)(2,1)} %copy-done.5, bf16[4,384,2048]{2,1,0:T(8,128)(2,1)} %copy-done.21, bf16[4,384,1024]{2,1,0:T(8,128)(2,1)S(1)} %copy-done.66, ...), custom_call_target="tpu_custom_call" | custom-call | flops 193273536 | bytes 754974 | tf_op jit(solution)/shard_map/weight_grads/pallas_call | solution.py:548
  840.1 20.5 %all-to-all-done.4 = bf16[16,80,384]{2,1,0:T(8,128)(2,1)S(1)} async-done(((bf16[16,80,384]{2,1,0:T(8,128)(2,1)}), bf16[16,80,384]{2,1,0:T(8,128)(2,1)S(1)}, u32[]{:S(2)}, u32[]{:S(2)}) %all-to-all-start.4) | async-done | bytes 983072 | tf_op jit(solution)/shard_map/all_to_all | solution.py:1567
  881.4 6.3 collective-permute-done.78
  890.7 9.6 %collective-permute-done.79 = bf16[64,2176]{1,0:T(8,128)(2,1)S(1)} collective-permute-done((bf16[64,2176]{1,0:T(8,128)(2,1)S(1)}, bf16[64,2176]{1,0:T(8,128)(2,1)S(1)}, u32[]{:S(2)}, u32[]{:S(2)}) %collective-permute-start.79) | collective-permute-done | bytes 278560 | tf_op jit(solution)/shard_map/ppermute | solution.py:1600
  (613 shorter events, 434.2 us)
Async XLA Ops:
  7.2 253.6 %all-gather.6.cloned.1.call-start = ((), (), s32[]{:S(2)}) async-start(), calls=%async_computation.6 | async-start | bytes 8912896 | tf_op jit(solution)/shard_map/all_gather | solution.py:1152
  17.5 313.0 %all-gather.8.cloned.1.call-start = ((), (), s32[]{:S(2)}) async-start(), calls=%async_computation.7 | async-start | bytes 8912896 | tf_op jit(solution)/shard_map/all_gather | solution.py:1152
  18.3 566.1 %all-gather.10.cloned.1.call-start = ((), (), s32[]{:S(2)}) async-start(), calls=%async_computation.9 | async-start | bytes 8912896 | tf_op jit(solution)/shard_map/all_gather | solution.py:1152
  86.9 37.8 %collective-permute-start.7 = (bf16[16,80,384]{2,1,0:T(8,128)(2,1)S(1)}, bf16[16,80,384]{2,1,0:T(8,128)(2,1)S(1)}, u32[]{:S(2)}, u32[]{:S(2)}) collective-permute-start(bf16[16,80,384]{2,1,0:T(8,128)(2,1)S(1)} %all_to_all.25), channel_id=1, source_target_pairs={{0,16},{16,0},{1,17},{17,1},{2,18},{18,2},{3,19},{19,3},{4,20},{20... | collective-permute-start | bytes 2949128 | tf_op jit(solution)/shard_map/ppermute | solution.py:1141
  115.8 28.3 %collective-permute-start.6 = (bf16[128,2048]{1,0:T(8,128)(2,1)}, bf16[128,2048]{1,0:T(8,128)(2,1)}, u32[]{:S(2)}, u32[]{:S(2)}) collective-permute-start(bf16[128,2048]{1,0:T(8,128)(2,1)} %choose.6.refs_5_.refs_1_), channel_id=1, source_target_pairs={{0,1},{1,0},{2,3},{3,2},{4,5},{5,4},{6,7},{7,6},{8,9},{9,8},{10,11... | collective-permute-start | bytes 1572872 | tf_op jit(solution)/shard_map/ppermute | solution.py:1141
  117.3 33.0 %collective-permute-start.1 = (bf16[128,2048]{1,0:T(8,128)(2,1)}, bf16[128,2048]{1,0:T(8,128)(2,1)}, u32[]{:S(2)}, u32[]{:S(2)}) collective-permute-start(bf16[128,2048]{1,0:T(8,128)(2,1)} %collective-permute-done.refs_1_.refs_3_), channel_id=1, source_target_pairs={{8,4},{4,0},{9,5},{5,1},{10,6},{6,2},{11,7},{7,3},{24,20},{20,16},... | collective-permute-start | bytes 1572872 | tf_op jit(solution)/shard_map/ppermute | solution.py:1169
  119.2 31.1 %collective-permute-start.4 = (bf16[128,2048]{1,0:T(8,128)(2,1)}, bf16[128,2048]{1,0:T(8,128)(2,1)}, u32[]{:S(2)}, u32[]{:S(2)}) collective-permute-start(bf16[128,2048]{1,0:T(8,128)(2,1)} %collective-permute-done.3.refs_2_), channel_id=1, source_target_pairs={{4,8},{8,12},{5,9},{9,13},{6,10},{10,14},{7,11},{11,15},{20,24},{2... | collective-permute-start | bytes 1572872 | tf_op jit(solution)/shard_map/ppermute | solution.py:1169
  153.8 31.9 %collective-permute-start.2 = (bf16[128,2048]{1,0:T(8,128)(2,1)}, bf16[128,2048]{1,0:T(8,128)(2,1)}, u32[]{:S(2)}, u32[]{:S(2)}) collective-permute-start(bf16[128,2048]{1,0:T(8,128)(2,1)} %collective-permute-done.1.refs_1_.refs_2_), channel_id=1, source_target_pairs={{4,0},{5,1},{6,2},{7,3},{20,16},{21,17},{22,18},{23,19}} | collective-permute-start | bytes 1572872 | tf_op jit(solution)/shard_map/ppermute | solution.py:1169
  155.9 29.8 %collective-permute-start.5 = (bf16[128,2048]{1,0:T(8,128)(2,1)}, bf16[128,2048]{1,0:T(8,128)(2,1)}, u32[]{:S(2)}, u32[]{:S(2)}) collective-permute-start(bf16[128,2048]{1,0:T(8,128)(2,1)} %collective-permute-done.4.refs_2_.refs_3_), channel_id=1, source_target_pairs={{8,12},{9,13},{10,14},{11,15},{24,28},{25,29},{26,30},{27,31}} | collective-permute-start | bytes 1572872 | tf_op jit(solution)/shard_map/ppermute | solution.py:1169
  158.3 33.0 %collective-permute-start.17 = (bf16[128,2048]{1,0:T(8,128)(2,1)}, bf16[128,2048]{1,0:T(8,128)(2,1)}, u32[]{:S(2)}, u32[]{:S(2)}) collective-permute-start(bf16[128,2048]{1,0:T(8,128)(2,1)} %choose.7.refs_8_.refs_1_), channel_id=1, source_target_pairs={{0,2},{2,0},{1,3},{3,1},{4,6},{6,4},{5,7},{7,5},{8,10},{10,8},{9,1... | collective-permute-start | bytes 1572872 | tf_op jit(solution)/shard_map/ppermute | solution.py:1141
  254.2 30.9 %all-to-all-start.1 = ((bf16[16,128,128]{1,2,0:T(8,128)(2,1)}), bf16[16,128,128]{1,2,0:T(8,128)(2,1)S(1)}, u32[]{:S(2)}, u32[]{:S(2)}) async-start(bf16[16,128,128]{1,2,0:T(8,128)(2,1)} %copy.136), calls=%async_computation.1 | async-start | bytes 1048576 | tf_op jit(solution)/shard_map/all_to_all | solution.py:1425
  260.5 354.2 %reduce-scatter.2.cloned.1.call-start = ((), (), s32[]{:S(2)}) async-start(), calls=%async_computation.8 | async-start | bytes 8912896 | tf_op jit(solution)/shard_map/reduce_scatter | solution.py:1156
  312.1 29.5 %collective-permute-start.25 = (bf16[128,2048]{1,0:T(8,128)(2,1)S(1)}, bf16[128,2048]{1,0:T(8,128)(2,1)}, u32[]{:S(2)}, u32[]{:S(2)}) collective-permute-start(bf16[128,2048]{1,0:T(8,128)(2,1)S(1)} %collective-permute-done.24.refs_1_.refs_3_), channel_id=1, source_target_pairs={{8,4},{4,0},{9,5},{5,1},{10,6},{6,2},{11,7},{7,3},{24,20},{20,16},... | collective-permute-start | bytes 1572872 | tf_op jit(solution)/shard_map/ppermute | solution.py:1169
  347.3 27.2 %collective-permute-start.40 = (bf16[128,2048]{1,0:T(8,128)(2,1)S(1)}, bf16[128,2048]{1,0:T(8,128)(2,1)S(1)}, u32[]{:S(2)}, u32[]{:S(2)}) collective-permute-start(bf16[128,2048]{1,0:T(8,128)(2,1)S(1)} %choose.10.refs_7_.refs_1_), channel_id=1, source_target_pairs={{0,2},{2,0},{1,3},{3,1},{4,6},{6,4},{5,7},{7,5},{8,10},{10,8},{9,1... | collective-permute-start | bytes 1572872 | tf_op jit(solution)/shard_map/ppermute | solution.py:1141
  490.0 217.1 %all-gather.12.cloned.1.call-start = ((), (), s32[]{:S(2)}) async-start(), calls=%async_computation.10 | async-start | bytes 8912896 | tf_op jit(solution)/shard_map/all_gather | solution.py:1152
  506.3 28.6 %collective-permute-start.48 = (bf16[128,2048]{1,0:T(8,128)(2,1)}, bf16[128,2048]{1,0:T(8,128)(2,1)S(1)}, u32[]{:S(2)}, u32[]{:S(2)}) collective-permute-start(bf16[128,2048]{1,0:T(8,128)(2,1)} %copy-done.76), channel_id=1, source_target_pairs={{0,2},{2,0},{1,3},{3,1},{4,6},{6,4},{5,7},{7,5},{8,10},{10,8},{9,1... | collective-permute-start | bytes 1572872 | tf_op jit(solution)/shard_map/ppermute | solution.py:1141
  526.1 37.0 %collective-permute-start.52 = (bf16[128,2048]{1,0:T(8,128)(2,1)S(1)}, bf16[128,2048]{1,0:T(8,128)(2,1)S(1)}, u32[]{:S(2)}, u32[]{:S(2)}) collective-permute-start(bf16[128,2048]{1,0:T(8,128)(2,1)S(1)} %get-tuple-element.154.refs_3_), channel_id=1, source_target_pairs={{0,4},{4,8},{1,5},{5,9},{2,6},{6,10},{3,7},{7,11},{16,20},{20,24},... | collective-permute-start | bytes 1572872 | tf_op jit(solution)/shard_map/ppermute | solution.py:1169
  530.4 34.7 %collective-permute-start.53 = (bf16[128,2048]{1,0:T(8,128)(2,1)S(1)}, bf16[128,2048]{1,0:T(8,128)(2,1)S(1)}, u32[]{:S(2)}, u32[]{:S(2)}) collective-permute-start(bf16[128,2048]{1,0:T(8,128)(2,1)S(1)} %get-tuple-element.155), channel_id=1, source_target_pairs={{12,8},{8,4},{13,9},{9,5},{14,10},{10,6},{15,11},{11,7},{28,24},{2... | collective-permute-start | bytes 1572872 | tf_op jit(solution)/shard_map/ppermute | solution.py:1169
  531.9 75.6 %collective-permute-start.47 = (bf16[128,2048]{1,0:T(8,128)(2,1)}, bf16[128,2048]{1,0:T(8,128)(2,1)}, u32[]{:S(2)}, u32[]{:S(2)}) collective-permute-start(bf16[128,2048]{1,0:T(8,128)(2,1)} %sum_blocks.19.refs_2_), channel_id=1, source_target_pairs={{0,2},{2,0},{1,3},{3,1},{4,6},{6,4},{5,7},{7,5},{8,10},{10,8},{9,1... | collective-permute-start | bytes 1572872 | tf_op jit(solution)/shard_map/ppermute | solution.py:1141
  566.3 41.1 %collective-permute-start.54 = (bf16[128,2048]{1,0:T(8,128)(2,1)}, bf16[128,2048]{1,0:T(8,128)(2,1)S(1)}, u32[]{:S(2)}, u32[]{:S(2)}) collective-permute-start(bf16[128,2048]{1,0:T(8,128)(2,1)} %get-tuple-element.156.refs_2_), channel_id=1, source_target_pairs={{0,4},{4,8},{8,12},{1,5},{5,9},{9,13},{2,6},{6,10},{10,14},{3,7},{... | collective-permute-start | bytes 1572872 | tf_op jit(solution)/shard_map/ppermute | solution.py:1169
  569.9 38.4 %collective-permute-start.55 = (bf16[128,2048]{1,0:T(8,128)(2,1)}, bf16[128,2048]{1,0:T(8,128)(2,1)S(1)}, u32[]{:S(2)}, u32[]{:S(2)}) collective-permute-start(bf16[128,2048]{1,0:T(8,128)(2,1)} %get-tuple-element.157), channel_id=1, source_target_pairs={{12,8},{8,4},{4,0},{13,9},{9,5},{5,1},{14,10},{10,6},{6,2},{15,11}... | collective-permute-start | bytes 1572872 | tf_op jit(solution)/shard_map/ppermute | solution.py:1169
  578.9 290.9 %all-gather.14.cloned.1.call-start = ((), (), s32[]{:S(2)}) async-start(), calls=%async_computation.11 | async-start | bytes 9469952 | tf_op jit(solution)/shard_map/all_gather | solution.py:1152
  686.7 29.4 %collective-permute-start.69 = (bf16[128,2048]{1,0:T(8,128)(2,1)}, bf16[128,2048]{1,0:T(8,128)(2,1)}, u32[]{:S(2)}, u32[]{:S(2)}) collective-permute-start(bf16[128,2048]{1,0:T(8,128)(2,1)} %sum_blocks.25.refs_2_), channel_id=1, source_target_pairs={{0,2},{2,0},{1,3},{3,1},{4,6},{6,4},{5,7},{7,5},{8,10},{10,8},{9,1... | collective-permute-start | bytes 1572872 | tf_op jit(solution)/shard_map/ppermute | solution.py:1141
  699.8 27.3 %collective-permute-start.70 = (bf16[128,2048]{1,0:T(8,128)(2,1)}, bf16[128,2048]{1,0:T(8,128)(2,1)}, u32[]{:S(2)}, u32[]{:S(2)}) collective-permute-start(bf16[128,2048]{1,0:T(8,128)(2,1)} %sum_blocks.28.refs_2_.refs_4_), channel_id=1, source_target_pairs={{0,4},{1,5},{2,6},{3,7},{16,20},{17,21},{18,22},{19,23}} | collective-permute-start | bytes 1572872 | tf_op jit(solution)/shard_map/ppermute | solution.py:1169
  704.9 76.8 %collective-permute-start.76 = (bf16[1024,384]{1,0:T(8,128)(2,1)}, bf16[1024,384]{1,0:T(8,128)(2,1)}, u32[]{:S(2)}, u32[]{:S(2)}) collective-permute-start(bf16[1024,384]{1,0:T(8,128)(2,1)} %dynamic-slice_convert_fusion), channel_id=1, source_target_pairs={{0,16},{16,0},{1,17},{17,1},{2,18},{18,2},{3,19},{19,3},{4,20},{20... | collective-permute-start | bytes 2359304 | tf_op jit(solution)/shard_map/ppermute | solution.py:1141
  705.6 58.1 %collective-permute-start.66 = (bf16[128,2048]{1,0:T(8,128)(2,1)}, bf16[128,2048]{1,0:T(8,128)(2,1)}, u32[]{:S(2)}, u32[]{:S(2)}) collective-permute-start(bf16[128,2048]{1,0:T(8,128)(2,1)} %copy-done.77), channel_id=1, source_target_pairs={{0,2},{2,0},{1,3},{3,1},{4,6},{6,4},{5,7},{7,5},{8,10},{10,8},{9,1... | collective-permute-start | bytes 1572872 | tf_op jit(solution)/shard_map/ppermute | solution.py:1141
  728.9 36.5 %collective-permute-start.72 = (bf16[128,2048]{1,0:T(8,128)(2,1)S(1)}, bf16[128,2048]{1,0:T(8,128)(2,1)S(1)}, u32[]{:S(2)}, u32[]{:S(2)}) collective-permute-start(bf16[128,2048]{1,0:T(8,128)(2,1)S(1)} %get-tuple-element.176.refs_6_), channel_id=1, source_target_pairs={{0,4},{4,8},{1,5},{5,9},{2,6},{6,10},{3,7},{7,11},{16,20},{20,24},... | collective-permute-start | bytes 1572872 | tf_op jit(solution)/shard_map/ppermute | solution.py:1169
  733.3 36.4 %collective-permute-start.73 = (bf16[128,2048]{1,0:T(8,128)(2,1)S(1)}, bf16[128,2048]{1,0:T(8,128)(2,1)S(1)}, u32[]{:S(2)}, u32[]{:S(2)}) collective-permute-start(bf16[128,2048]{1,0:T(8,128)(2,1)S(1)} %get-tuple-element.178), channel_id=1, source_target_pairs={{12,8},{8,4},{13,9},{9,5},{14,10},{10,6},{15,11},{11,7},{28,24},{2... | collective-permute-start | bytes 1572872 | tf_op jit(solution)/shard_map/ppermute | solution.py:1169
  734.8 85.9 %collective-permute-start.65 = (bf16[128,2048]{1,0:T(8,128)(2,1)S(1)}, bf16[128,2048]{1,0:T(8,128)(2,1)}, u32[]{:S(2)}, u32[]{:S(2)}) collective-permute-start(bf16[128,2048]{1,0:T(8,128)(2,1)S(1)} %copy-done.80), channel_id=1, source_target_pairs={{0,2},{2,0},{1,3},{3,1},{4,6},{6,4},{5,7},{7,5},{8,10},{10,8},{9,1... | collective-permute-start | bytes 1572872 | tf_op jit(solution)/shard_map/ppermute | solution.py:1141
  771.0 49.7 %collective-permute-start.74 = (bf16[128,2048]{1,0:T(8,128)(2,1)}, bf16[128,2048]{1,0:T(8,128)(2,1)}, u32[]{:S(2)}, u32[]{:S(2)}) collective-permute-start(bf16[128,2048]{1,0:T(8,128)(2,1)} %get-tuple-element.179.refs_13_), channel_id=1, source_target_pairs={{0,4},{4,8},{8,12},{1,5},{5,9},{9,13},{2,6},{6,10},{10,14},{3,7},{... | collective-permute-start | bytes 1572872 | tf_op jit(solution)/shard_map/ppermute | solution.py:1169
  772.9 47.7 %collective-permute-start.75 = (bf16[128,2048]{1,0:T(8,128)(2,1)}, bf16[128,2048]{1,0:T(8,128)(2,1)}, u32[]{:S(2)}, u32[]{:S(2)}) collective-permute-start(bf16[128,2048]{1,0:T(8,128)(2,1)} %get-tuple-element.180), channel_id=1, source_target_pairs={{12,8},{8,4},{4,0},{13,9},{9,5},{5,1},{14,10},{10,6},{6,2},{15,11}... | collective-permute-start | bytes 1572872 | tf_op jit(solution)/shard_map/ppermute | solution.py:1169
  833.5 27.0 %all-to-all-start.4 = ((bf16[16,80,384]{2,1,0:T(8,128)(2,1)}), bf16[16,80,384]{2,1,0:T(8,128)(2,1)S(1)}, u32[]{:S(2)}, u32[]{:S(2)}) async-start(bf16[16,80,384]{2,1,0:T(8,128)(2,1)} %maximum_maximum_fusion), calls=%async_computation.5 | async-start | bytes 1966080 | tf_op jit(solution)/shard_map/all_to_all | solution.py:1567
  (181 other events, 1830.9 us)
Sparse Core Ops, SparseCore 0:
  17.7 87.6 all-gather.5
  107.6 96.0 all-gather.7
  206.4 79.2 all-gather.9
  490.1 116.5 reduce-scatter.1
  608.7 79.2 all-gather.11
  690.1 104.3 all-gather.13

commit v3 on v2

--- a/solution.py
+++ b/solution.py
@@ -489,7 +489,7 @@
 ALL = ("grp", "z", "x", "core")
 PAIR = 2 * TOK_DEV
 SLOTS = 2 * CAP
-COST = 0.01
+COST = 0.1
 SIDES = {16: (4, 2, 2)}
 
 
@@ -529,26 +529,59 @@
     return pl.BlockSpec(dims, lambda *_: (0,) * len(dims))
 
 
+class Order:
+    marks = []
+
+    @classmethod
+    def mark_of(cls, array):
+        for known, mark in cls.marks:
+            if known is array:
+                return mark
+        return array
+
+
+MARK = (8, 128)
+
+
 def ordered(kernel, after, specs, **settings):
-    after = [array for array in after if not any(array is other for other in specs.pop("kept", ()))]
+    after = [Order.mark_of(array) for array in after]
     inputs = len(specs["in_specs"])
     prefetch = specs.pop("num_scalar_prefetch", 0)
     extra = len(after)
+    single = not isinstance(specs["out_specs"], list)
+    outputs = [specs["out_specs"]] if single else specs["out_specs"]
+    shapes = settings.pop("out_shape")
+    shapes = [shapes] if single else list(shapes)
+    last = prefetch + inputs + extra + len(outputs)
 
     def body(*refs):
-        kept = refs[: prefetch + inputs] + refs[prefetch + inputs + extra :]
-        kernel(*kept)
+        refs[last][...] = jnp.zeros(MARK, F32)
+        kernel(*refs[: prefetch + inputs], *refs[prefetch + inputs + extra : last], *refs[last + 1 :])
 
     specs["in_specs"] = list(specs["in_specs"]) + [pl.BlockSpec(memory_space=pl.ANY)] * extra
+    specs["out_specs"] = outputs + [pl.BlockSpec(MARK, lambda *_: (0, 0))]
     call = pl.pallas_call(
         body,
         grid_spec=pltpu.PrefetchScalarGridSpec(num_scalar_prefetch=prefetch, **specs),
+        out_shape=shapes + [jax.ShapeDtypeStruct(MARK, F32)],
         **settings,
     )
-    return lambda *args: call(*args, *after)
+
+    def run(*args):
+        *results, mark = call(*args, *after)
+        Order.marks.extend((result, mark) for result in results)
+        return results[0] if single else results
+
+    return run
 
 
 ANYWHERE = pl.BlockSpec(memory_space=pl.ANY)
+
+
+def in_hbm(dims, kind):
+    return pltpu.HBM(dims, kind)
+
+
 BLOCK_SHAPE = (TOK_DEV, D)
 
 
@@ -578,7 +611,6 @@
             grid=(1,),
             in_specs=[whole(TOK_DEV, D), whole(TOK_DEV, D), whole(D, 3 * HD), whole(1, D)]
             + [ANYWHERE] * len(kept),
-            kept=kept,
             out_specs=[
                 pl.BlockSpec((PAIR, D), lambda i, s: (s[0], 0)),
                 pl.BlockSpec((PAIR, 3 * HD), lambda i, s: (s[0], 0)),
@@ -586,8 +618,8 @@
             ],
         ),
         out_shape=[
-            jax.ShapeDtypeStruct((seq, D), BF16),
-            jax.ShapeDtypeStruct((seq, 3 * HD), F32),
+            in_hbm((seq, D), BF16),
+            in_hbm((seq, 3 * HD), F32),
             jax.ShapeDtypeStruct((2, seq), F32),
         ],
         input_output_aliases={5 + i: i for i in range(len(kept))},
@@ -630,11 +662,19 @@
 def attend(qkv, stat, gain_q, gain_k, cosine, sine):
     rows = qkv.shape[0]
     shape = lambda kind: jax.ShapeDtypeStruct((rows, HD), kind)
-    return pl.pallas_call(
+    return ordered(
         attend_kernel,
+        (),
+        dict(
+            grid=(1,),
+            in_specs=[
+                whole(rows, 3 * HD), whole(2, rows), whole(1, HD), whole(1, HD), whole(rows, HD), whole(rows, HD),
+            ],
+            out_specs=[whole(rows, HD)] * 5 + [whole(1, rows)],
+            scratch_shapes=[pltpu.VMEM((HD, rows), BF16)],
+        ),
         out_shape=[shape(BF16), shape(BF16), shape(BF16), shape(F32), shape(BF16),
                    jax.ShapeDtypeStruct((1, rows), F32)],
-        scratch_shapes=[pltpu.VMEM((HD, rows), BF16)],
         compiler_params=params(48),
         cost_estimate=cost(8 * rows * rows * HD, 10 * rows * 384),
         name="attend",
@@ -681,14 +721,22 @@
     gains_ref[1:2, :] = gain_k
 
 
-def attend_back(q, k, v, grad, out, lse, qkv, stat, gain_q, gain_k, cosine, sine):
+def attend_back(q, k, v, grad, out, lse, qkv, stat, gain_q, gain_k, cosine, sine, after=()):
     rows = q.shape[0]
     shape = lambda kind: jax.ShapeDtypeStruct((rows, HD), kind)
-    return pl.pallas_call(
+    return ordered(
         attend_back_kernel,
+        after,
+        dict(
+            grid=(1,),
+            in_specs=[whole(rows, HD)] * 5
+            + [whole(1, rows), whole(rows, 3 * HD), whole(2, rows), whole(1, HD), whole(1, HD)]
+            + [whole(rows, HD)] * 2,
+            out_specs=[whole(rows, HD)] * 3 + [whole(2, rows), whole(2, HD)],
+            scratch_shapes=[pltpu.VMEM((rows, HD), F32), pltpu.VMEM((rows, HD), F32)],
+        ),
         out_shape=[shape(F32), shape(F32), shape(BF16),
                    jax.ShapeDtypeStruct((2, rows), F32), jax.ShapeDtypeStruct((2, HD), F32)],
-        scratch_shapes=[pltpu.VMEM((rows, HD), F32), pltpu.VMEM((rows, HD), F32)],
         compiler_params=params(48),
         cost_estimate=cost(20 * rows * rows * HD, 20 * rows * 384),
         name="attend_back",
@@ -707,16 +755,19 @@
     out_ref[:, 2 * HD :] = dv_ref[...]
 
 
-def finish(dnq, dnk, dv, qkv, stat, means, gain_q, gain_k):
+def finish(dnq, dnk, dv, qkv, stat, means, gain_q, gain_k, after=()):
     rows = dnq.shape[0]
     head = pl.BlockSpec((PAIR, HD), lambda i: (i, 0))
     line = pl.BlockSpec((2, PAIR), lambda i: (0, i))
     full = pl.BlockSpec((PAIR, 3 * HD), lambda i: (i, 0))
-    return pl.pallas_call(
+    return ordered(
         finish_kernel,
+        after,
+        dict(
         grid=(rows // PAIR,),
         in_specs=[head, head, head, full, line, line, whole(1, HD), whole(1, HD)],
         out_specs=full,
+        ),
         out_shape=jax.ShapeDtypeStruct((rows, 3 * HD), BF16),
         compiler_params=params(24),
         cost_estimate=cost(20 * rows * 3 * HD, 12 * rows * 3 * HD),
@@ -725,6 +776,8 @@
 
 
 def sort_cores(core, first, second, own_ref, other_ref, at):
+    at = (0, at)
+
     @pl.when(core == 0)
     def _():
         own_ref[at] = first
@@ -736,32 +789,41 @@
         other_ref[at] = first
 
 
-def normed_part_kernel(place_ref, a_ref, b_ref, w_ref, own_ref, other_ref):
-    for at, g_ref in enumerate((a_ref, b_ref)):
+def normed_part_kernel(
+    place_ref, a_ref, b_ref, w_ref, ya_ref, yb_ref, a_slot, b_slot, own_ref, other_ref
+):
+    core = place_ref[4]
+    here, there = own_ref.at[:, :, :, D:], other_ref.at[:, :, :, D:]
+    for at, (g_ref, y_ref, slot_ref) in enumerate(((a_ref, ya_ref, a_slot), (b_ref, yb_ref, b_slot))):
         out = nt(g_ref[...], w_ref[...]).astype(BF16)
-        sort_cores(place_ref[2], out[:TOK_DEV], out[TOK_DEV:], own_ref, other_ref, at)
-
-
-def normed_part(place, grads, w_head, after=()):
-    blocks = jax.ShapeDtypeStruct((2, TOK_DEV, D), BF16)
+        sort_cores(
+            core, out[:TOK_DEV], out[TOK_DEV:], own_ref.at[:, :, :, :D], other_ref.at[:, :, :, :D], at
+        )
+        first, second = combine_chip(y_ref, slot_ref)
+        sort_cores(core, first, second, here, there, at)
+
+
+def normed_part(place, grads, w_head, y_rows, slots, after=()):
+    blocks = jax.ShapeDtypeStruct((2, 2, TOK_DEV, 2 * D), BF16)
     return ordered(
         normed_part_kernel,
         after,
         dict(
             num_scalar_prefetch=1,
-            grid=(1,),
+            grid=(2,),
             in_specs=[
-                pl.BlockSpec((PAIR, 3 * HD), lambda i, s: (s[0], 0)),
-                pl.BlockSpec((PAIR, 3 * HD), lambda i, s: (s[1], 0)),
+                pl.BlockSpec((PAIR, 3 * HD), lambda i, s: (s[2 * i], 0)),
+                pl.BlockSpec((PAIR, 3 * HD), lambda i, s: (s[2 * i + 1], 0)),
                 whole(D, 3 * HD),
-            ],
-            out_specs=[whole(2, TOK_DEV, D)] * 2,
+            ]
+            + chip_specs(y_rows, slots),
+            out_specs=[pl.BlockSpec((1, 2, TOK_DEV, 2 * D), lambda i, s: (i, 0, 0, 0))] * 2,
         ),
         out_shape=[blocks, blocks],
-        compiler_params=params(24),
-        cost_estimate=cost(4 * PAIR * D * 3 * HD, 8 * PAIR * D),
+        compiler_params=params(32),
+        cost_estimate=cost(8 * PAIR * D * 3 * HD, 24 * PAIR * D),
         name="normed_part",
-    )(place, grads, grads, w_head)
+    )(place, grads, grads, w_head, y_rows, y_rows, slots, slots)
 
 
 def dw_kernel(normed_ref, grad_ref, out_ref):
@@ -803,7 +865,8 @@
 
 
 def dispatch_kernel(place_ref, own_ref, other_ref, own_slot, other_slot, *refs):
-    out_ref, column_ref = refs[-2:]
+    out_ref, column_ref, stack_ref = refs[-3:]
+    stack_ref[0] = own_ref[...]
     core = place_ref[1]
     lanes = pl.ds(pl.multiple_of(place_ref[2] * HD, HD), HD)
     out = nn(pick_matrix(own_slot[0]), own_ref[...])
@@ -830,15 +893,16 @@
                 pl.BlockSpec((1, local, TOK_DEV), lambda i, s: (2 * s[0] + 1 - s[1], 0, 0)),
             ]
             + [ANYWHERE] * len(kept),
-            kept=kept,
             out_specs=[
                 pl.BlockSpec((local, SLOTS, D), lambda i, s: (0, s[0], 0)),
                 pl.BlockSpec((PAIR, HD), lambda i, s: (s[0], 0)),
+                pl.BlockSpec((1, TOK_DEV, D), lambda i, s: (s[0], 0, 0)),
             ],
         ),
         out_shape=[
-            jax.ShapeDtypeStruct((local, blocks // 2 * SLOTS, D), BF16),
-            jax.ShapeDtypeStruct((blocks * TOK_DEV, HD), BF16),
+            in_hbm((local, blocks // 2 * SLOTS, D), BF16),
+            in_hbm((blocks * TOK_DEV, HD), BF16),
+            in_hbm((blocks // 2, TOK_DEV, D), BF16),
         ],
         input_output_aliases={5 + i: i for i in range(len(kept))},
         compiler_params=params(24),
@@ -847,27 +911,81 @@
     )(place, own, other, slots, slots, *kept)
 
 
+def stack_kernel(place_ref, row_ref, out_ref):
+    out_ref[0] = row_ref[0, 0]
+
+
+def stack_of_core(core, rows, after=()):
+    chips = rows.shape[0]
+    return ordered(
+        stack_kernel,
+        after,
+        dict(
+            num_scalar_prefetch=1,
+            grid=(chips,),
+            in_specs=[pl.BlockSpec((1, 1, TOK_DEV, D), lambda i, s: (i, s[0], 0, 0))],
+            out_specs=pl.BlockSpec((1, TOK_DEV, D), lambda i, s: (i, 0, 0)),
+        ),
+        out_shape=in_hbm((chips, TOK_DEV, D), BF16),
+        compiler_params=params(16),
+        cost_estimate=cost(0, 4 * chips * TOK_DEV * D),
+        name="stack_of_core",
+    )(core.reshape(1), rows)
+
+
+def stack_dispatch_kernel(place_ref, own_ref, other_ref, own_slot, other_slot, out_ref):
+    out = nn(pick_matrix(own_slot[0]), own_ref[0])
+    out = (out + nn(pick_matrix(other_slot[0]), other_ref[0])).astype(BF16)
+    for j in range(out_ref.shape[0]):
+        out_ref[j] = out[j * SLOTS : (j + 1) * SLOTS]
+
+
+def stack_dispatch(places, stacks, slots, after=()):
+    chips = stacks.shape[1]
+    blocks, local, _ = slots.shape
+    row_shape = (None, 1, TOK_DEV, D)
+    return ordered(
+        stack_dispatch_kernel,
+        after,
+        dict(
+            num_scalar_prefetch=1,
+            grid=(chips,),
+            in_specs=[
+                pl.BlockSpec(row_shape, lambda i, s: (2 - 2 * s[chips + 1] + s[chips], i, 0, 0)),
+                pl.BlockSpec(row_shape, lambda i, s: (3 - 2 * s[chips + 1] - s[chips], i, 0, 0)),
+                pl.BlockSpec((1, local, TOK_DEV), lambda i, s: (2 * s[i] + s[chips], 0, 0)),
+                pl.BlockSpec((1, local, TOK_DEV), lambda i, s: (2 * s[i] + 1 - s[chips], 0, 0)),
+            ],
+            out_specs=pl.BlockSpec((local, SLOTS, D), lambda i, s: (0, s[i], 0)),
+        ),
+        out_shape=in_hbm((local, blocks // 2 * SLOTS, D), BF16),
+        compiler_params=params(24),
+        cost_estimate=cost(2 * chips * PAIR * D * local * SLOTS, 4 * chips * PAIR * D),
+        name="stack_dispatch",
+    )(places, stacks, stacks, slots, slots)
+
+
 def plain_dispatch_kernel(row_ref, slot_ref, out_ref):
     out = sum(nn(pick_matrix(slot_ref[i]), row_ref[i]) for i in range(2)).astype(BF16)
     for j in range(out_ref.shape[0]):
         out_ref[j] = out[j * SLOTS : (j + 1) * SLOTS]
 
 
-def plain_dispatch(rows, slots, after=()):
+def plain_dispatch(rows, slots, after=(), part=0, parts=1):
     blocks, local, _ = slots.shape
-    rows = rows.reshape(blocks, TOK_DEV, D)
+    rows = rows.reshape(blocks, parts, TOK_DEV, D)
     return ordered(
         plain_dispatch_kernel,
         after,
         dict(
             grid=(blocks // 2,),
             in_specs=[
-                pl.BlockSpec((2, TOK_DEV, D), lambda i: (i, 0, 0)),
+                pl.BlockSpec((2, None, TOK_DEV, D), lambda i: (i, part, 0, 0)),
                 pl.BlockSpec((2, local, TOK_DEV), lambda i: (i, 0, 0)),
             ],
             out_specs=pl.BlockSpec((local, SLOTS, D), lambda i: (0, i, 0)),
         ),
-        out_shape=jax.ShapeDtypeStruct((local, blocks // 2 * SLOTS, D), BF16),
+        out_shape=in_hbm((local, blocks // 2 * SLOTS, D), BF16),
         compiler_params=params(24),
         cost_estimate=cost(2 * blocks * TOK_DEV * D * local * SLOTS, 4 * blocks * TOK_DEV * D),
         name="plain_dispatch",
@@ -879,83 +997,40 @@
     return [tn(pick_matrix(slot_ref[i]), rows).astype(BF16) for i in range(2)]
 
 
-def combine_kernel(row_ref, slot_ref, out_ref):
-    first, second = combine_chip(row_ref, slot_ref)
-    out_ref[:TOK_DEV] = first
-    out_ref[TOK_DEV:] = second
-
-
-def combine(slot_rows, slots, after=()):
-    blocks, local, _ = slots.shape
-    rows = blocks * TOK_DEV
-    return ordered(
-        combine_kernel,
-        after,
-        dict(
-            grid=(blocks // 2,),
-            in_specs=[
-                pl.BlockSpec((local, SLOTS, D), lambda i: (0, i, 0)),
-                pl.BlockSpec((2, local, TOK_DEV), lambda i: (i, 0, 0)),
-            ],
-            out_specs=pl.BlockSpec((PAIR, D), lambda i: (i, 0)),
-        ),
-        out_shape=jax.ShapeDtypeStruct((rows, D), BF16),
-        compiler_params=params(24),
-        cost_estimate=cost(2 * rows * D * local * SLOTS, 4 * rows * D),
-        name="combine",
-    )(slot_rows, slots)
-
-
 def combine_part_kernel(place_ref, a_ref, b_ref, a_slot, b_slot, own_ref, other_ref):
     for at, (row_ref, slot_ref) in enumerate(((a_ref, a_slot), (b_ref, b_slot))):
         first, second = combine_chip(row_ref, slot_ref)
-        sort_cores(place_ref[2], first, second, own_ref, other_ref, at)
+        sort_cores(place_ref[4], first, second, own_ref, other_ref, at)
+
+
+def chip_specs(slot_rows, slots):
+    local, width = slots.shape[1], slot_rows.shape[2]
+    rows = [
+        pl.BlockSpec((local, SLOTS, width), lambda i, s, n=n: (0, s[2 * i + n], 0)) for n in (0, 1)
+    ]
+    spots = [
+        pl.BlockSpec((2, local, TOK_DEV), lambda i, s, n=n: (s[2 * i + n], 0, 0)) for n in (0, 1)
+    ]
+    return rows + spots
 
 
 def combine_part(place, slot_rows, slots, after=()):
-    local = slots.shape[1]
-    shape = jax.ShapeDtypeStruct((2, TOK_DEV, D), BF16)
-    rows = lambda n: pl.BlockSpec((local, SLOTS, D), lambda i, s: (0, s[n], 0))
-    spots = lambda n: pl.BlockSpec((2, local, TOK_DEV), lambda i, s: (s[n], 0, 0))
+    local, width = slots.shape[1], slot_rows.shape[2]
+    shape = jax.ShapeDtypeStruct((2, 2, TOK_DEV, width), BF16)
     return ordered(
         combine_part_kernel,
         after,
         dict(
             num_scalar_prefetch=1,
-            grid=(1,),
-            in_specs=[rows(0), rows(1), spots(0), spots(1)],
-            out_specs=[whole(2, TOK_DEV, D)] * 2,
+            grid=(2,),
+            in_specs=chip_specs(slot_rows, slots),
+            out_specs=[pl.BlockSpec((1, 2, TOK_DEV, width), lambda i, s: (i, 0, 0, 0))] * 2,
         ),
         out_shape=[shape, shape],
         compiler_params=params(24),
         cost_estimate=cost(4 * PAIR * D * local * SLOTS, 8 * PAIR * D),
         name="combine_part",
     )(place, slot_rows, slot_rows, slots, slots)
-
-
-def spread_kernel(dp_ref, slot_ref, out_ref):
-    for i in range(2):
-        for j, pick in enumerate(picks(slot_ref[i], F32)):
-            out_ref[i, j : j + 1, :] = jnp.sum(pick * dp_ref[j], 0, keepdims=True)
-
-
-def spread_back(dp_slots, slots, after=()):
-    blocks, local, _ = slots.shape
-    return ordered(
-        spread_kernel,
-        after,
-        dict(
-            grid=(blocks // 2,),
-            in_specs=[
-                pl.BlockSpec((local, SLOTS, HD), lambda i: (0, i, 0)),
-                pl.BlockSpec((2, local, TOK_DEV), lambda i: (i, 0, 0)),
-            ],
-            out_specs=pl.BlockSpec((2, local, TOK_DEV), lambda i: (i, 0, 0)),
-        ),
-        out_shape=jax.ShapeDtypeStruct(slots.shape, F32),
-        compiler_params=params(24),
-        name="spread_back",
-    )(dp_slots, slots)
 
 
 def slope_kernel(g_ref, wd_ref, out_ref):
@@ -977,16 +1052,16 @@
             ],
             out_specs=pl.BlockSpec((1, count, chunk), lambda j, f: (j, 0, f)),
         ),
-        out_shape=jax.ShapeDtypeStruct((local, count, hidden), F32),
+        out_shape=in_hbm((local, count, hidden), F32),
         compiler_params=params(24),
         cost_estimate=cost(2 * local * count * hidden * D, 2 * local * hidden * D),
         name="slopes",
     )(grads, w_down)
 
 
-def expert_kernel(first_ref, x_ref, h_ref, wg_ref, wu_ref, wr_ref, *rest, full):
+def expert_kernel(first_ref, x_ref, h_ref, wg_ref, wu_ref, wr_ref, *rest, full, offset):
     if full:
-        (act_ref, dg_ref, du_ref, gate_ref, z_ref, dp_ref, z_s, dp_s) = rest
+        (act_ref, dg_ref, du_ref, gate_ref, z_ref, z_s, dp_s) = rest
     else:
         (act_ref, dg_ref, du_ref, gate_ref) = rest
     step, steps = pl.program_id(1), pl.num_programs(1)
@@ -998,7 +1073,7 @@
         lane = lax.broadcasted_iota(jnp.int32, logits.shape, 1)
         logits = jnp.where(lane < EXPERTS, logits, NEG_FILL)
         powers = jnp.exp(logits - jnp.max(logits, -1, keepdims=True))
-        mine = jnp.where(lane == first_ref[0] + pl.program_id(0), powers, 0.0)
+        mine = jnp.where(lane == first_ref[0] + offset + pl.program_id(0), powers, 0.0)
         gate = jnp.sum(mine, -1, keepdims=True) / jnp.sum(powers, -1, keepdims=True)
         gate_ref[0] = jnp.broadcast_to(gate, gate_ref.shape[1:])
         if full:
@@ -1026,44 +1101,53 @@
 
         @pl.when(step == steps - 1)
         def _():
-            z_ref[0] = z_s[...].astype(BF16)
-            dp_ref[0] = dp_s[...]
-
-
-def experts(first, rows, slope, w_gate, w_up, router, full, after=()):
+            z_ref[0, :, :D] = z_s[...].astype(BF16)
+            lane = lax.broadcasted_iota(jnp.int32, dp_s.shape, 1)
+            mine = first_ref[0] + offset + pl.program_id(0)
+            high = dp_s[...].astype(BF16).astype(F32)
+            parts = jnp.where(lane == mine, high, 0.0)
+            parts = jnp.where(lane == mine + EXPERTS, dp_s[...] - high, parts)
+            z_ref[0, :, D:] = parts.astype(BF16)
+
+
+def experts(first, rows, slope, w_gate, w_up, router, full, only=None, after=()):
     local, count, _ = rows.shape
+    offset, number = (0, local) if only is None else only
     hidden = w_gate.shape[2]
     chunk = hidden // 2
     row_spec = pl.BlockSpec((1, count, D), lambda j, f, s: (j, 0, 0))
     mid_spec = pl.BlockSpec((1, count, chunk), lambda j, f, s: (j, 0, f))
     lane_spec = pl.BlockSpec((1, count, HD), lambda j, f, s: (j, 0, 0))
-    in_w = pl.BlockSpec((1, D, chunk), lambda j, f, s: (j, 0, f))
-    mid_shape = jax.ShapeDtypeStruct((local, count, hidden), BF16)
-    lane_shape = jax.ShapeDtypeStruct((local, count, HD), F32)
+    in_w = pl.BlockSpec((1, D, chunk), lambda j, f, s: (j + offset, 0, f))
+    mid_shape = in_hbm((number, count, hidden), BF16)
+    lane_shape = jax.ShapeDtypeStruct((number, count, HD), F32)
     out_specs = [mid_spec, mid_spec, mid_spec, lane_spec]
     out_shape = [mid_shape, mid_shape, mid_shape, lane_shape]
     scratch = []
     if full:
-        out_specs += [row_spec, lane_spec]
-        out_shape += [jax.ShapeDtypeStruct((local, count, D), BF16), lane_shape]
+        out_specs += [pl.BlockSpec((1, count, D + HD), lambda j, f, s: (j, 0, 0))]
+        out_shape += [in_hbm((number, count, D + HD), BF16)]
         scratch += [pltpu.VMEM((count, D), F32), pltpu.VMEM((count, HD), F32)]
-    unit = 2 * local * count * hidden * D
-    return ordered(
-        functools.partial(expert_kernel, full=full),
+    unit = 2 * number * count * hidden * D
+    return ordered(
+        functools.partial(expert_kernel, full=full, offset=offset),
         after,
         dict(
             num_scalar_prefetch=1,
-            grid=(local, 2),
+            grid=(number, 2),
             in_specs=[
-                row_spec, mid_spec, in_w, in_w,
+                pl.BlockSpec((1, count, D), lambda j, f, s: (j + offset, 0, 0)),
+                pl.BlockSpec((1, count, chunk), lambda j, f, s: (j + offset, 0, f)),
+                in_w,
+                in_w,
                 pl.BlockSpec((D, HD), lambda j, f, s: (0, 0)),
             ],
             out_specs=out_specs,
             scratch_shapes=scratch,
         ),
         out_shape=out_shape,
-        compiler_params=params(40),
-        cost_estimate=cost((4 if full else 2) * unit, 4 * local * hidden * D + 8 * local * count * D),
+        compiler_params=params(56),
+        cost_estimate=cost((4 if full else 2) * unit, 4 * number * hidden * D + 8 * number * count * D),
         name="experts_full" if full else "experts_half",
     )(first, rows, slope, w_gate, w_up, router)
 
@@ -1095,46 +1179,374 @@
 
 
 def weights_kernel(
-    half_ref, xa, xb, dga, dgb, dua, dub, aa, ab, ga, gb, gate_a, gate_b, gate_ref, up_ref, down_ref
+    half_ref, xa, xb, dga, dgb, dua, dub, aa, ab, ga, gb, gate_a, gate_b, *refs
 ):
-    gate_ref[0] = tn(xa[0], dga[0]) + tn(xb[0], dgb[0])
-    up_ref[0] = tn(xa[0], dua[0]) + tn(xb[0], dub[0])
+    gate_ref, up_ref, down_ref = refs[-3:]
+    rows = jnp.concatenate([xa[0], xb[0]], 0)
+    gate_ref[0] = tn(rows, jnp.concatenate([dga[0], dgb[0]], 0))
+    up_ref[0] = tn(rows, jnp.concatenate([dua[0], dub[0]], 0))
     grad_a = (ga[0].astype(F32) * gate_a[0, :, 0:1]).astype(BF16)
     grad_b = (gb[0].astype(F32) * gate_b[0, :, 0:1]).astype(BF16)
-    down_ref[0] = tn(aa[0], grad_a) + tn(ab[0], grad_b)
-
-
-def weight_grads(half, x_pair, dg_pair, du_pair, act_pair, g_pair, gate_pair, after=()):
+    down_ref[0] = tn(
+        jnp.concatenate([aa[0], ab[0]], 0), jnp.concatenate([grad_a, grad_b], 0)
+    )
+
+
+def weight_grads(only, half, x_pair, dg_pair, du_pair, act_pair, g_pair, gate_pair, buffers, after=()):
     local, count, _ = x_pair[0].shape
+    start, number = only
     hidden = dg_pair[0].shape[2]
-    x_spec = pl.BlockSpec((1, count, D // 2), lambda j, f, s: (j, 0, s[0]))
-    d_spec = pl.BlockSpec((1, count, hidden // 2), lambda j, f, s: (j, 0, f))
-    a_spec = pl.BlockSpec((1, count, hidden // 2), lambda j, f, s: (j, 0, s[0]))
-    g_spec = pl.BlockSpec((1, count, D // 2), lambda j, f, s: (j, 0, f))
-    lane_spec = pl.BlockSpec((1, count, HD), lambda j, f, s: (j, 0, 0))
-    unit = 2 * local * count * hidden * D
+    kept = [] if buffers is None else list(buffers)
+    chunk = hidden // 2
+
+    def spec(width, by_half, single):
+        at = 0 if single else start
+        if by_half is None:
+            return pl.BlockSpec((1, count, width), lambda j, f, s: (j + at, 0, 0))
+        if by_half:
+            return pl.BlockSpec((1, count, width), lambda j, f, s: (j + at, 0, s[0]))
+        return pl.BlockSpec((1, count, width), lambda j, f, s: (j + at, 0, f))
+
+    in_specs = [
+        spec(D // 2, True, False), spec(D // 2, True, False),
+        spec(chunk, False, False), spec(chunk, False, True),
+        spec(chunk, False, False), spec(chunk, False, True),
+        spec(chunk, True, False), spec(chunk, True, True),
+        spec(D // 2, False, False), spec(D // 2, False, False),
+        spec(HD, None, False), spec(HD, None, True),
+    ]
+    unit = 2 * number * count * hidden * D
     return ordered(
         weights_kernel,
         after,
         dict(
             num_scalar_prefetch=1,
-            grid=(local, 2),
-            in_specs=[x_spec] * 2 + [d_spec] * 4 + [a_spec] * 2 + [g_spec] * 2 + [lane_spec] * 2,
+            grid=(number, 2),
+            in_specs=in_specs + [ANYWHERE] * len(kept),
             out_specs=[
-                pl.BlockSpec((1, D // 2, hidden // 2), lambda j, f, s: (j, 0, f)),
-                pl.BlockSpec((1, D // 2, hidden // 2), lambda j, f, s: (j, 0, f)),
-                pl.BlockSpec((1, hidden // 2, D // 2), lambda j, f, s: (j, 0, f)),
+                pl.BlockSpec((1, D // 2, chunk), lambda j, f, s: (j + start, 0, f)),
+                pl.BlockSpec((1, D // 2, chunk), lambda j, f, s: (j + start, 0, f)),
+                pl.BlockSpec((1, chunk, D // 2), lambda j, f, s: (j + start, 0, f)),
             ],
         ),
         out_shape=[
-            jax.ShapeDtypeStruct((local, D // 2, hidden), F32),
-            jax.ShapeDtypeStruct((local, D // 2, hidden), F32),
-            jax.ShapeDtypeStruct((local, hidden // 2, D), F32),
+            in_hbm((local, D // 2, hidden), F32),
+            in_hbm((local, D // 2, hidden), F32),
+            in_hbm((local, hidden // 2, D), F32),
         ],
-        compiler_params=params(44),
-        cost_estimate=cost(3 * unit, 6 * local * hidden * D + 8 * local * count * D),
+        input_output_aliases={13 + i: i for i in range(len(kept))},
+        compiler_params=params(56),
+        cost_estimate=cost(3 * unit, 6 * number * hidden * D + 8 * number * count * D),
         name="weight_grads",
-    )(half, *x_pair, *dg_pair, *du_pair, *act_pair, *g_pair, *gate_pair)
+    )(half, *x_pair, *dg_pair, *du_pair, *act_pair, *g_pair, *gate_pair, *kept)
+
+
+def softmax_of(mixed, router):
+    logits = nn(mixed, router)
+    lane = lax.broadcasted_iota(jnp.int32, logits.shape, 1)
+    logits = jnp.where(lane < EXPERTS, logits, NEG_FILL)
+    powers = jnp.exp(logits - jnp.max(logits, -1, keepdims=True))
+    return powers / jnp.sum(powers, -1, keepdims=True)
+
+
+def pair_kernel(group_ref, near_ref, far_ref, out_ref):
+    out_ref[group_ref[0]] = near_ref[...]
+    out_ref[1 - group_ref[0]] = far_ref[...]
+
+
+def pair_up(group, near, far, after=()):
+    return ordered(
+        pair_kernel,
+        after,
+        dict(
+            num_scalar_prefetch=1,
+            grid=(1,),
+            in_specs=[whole(*near.shape)] * 2,
+            out_specs=whole(2, *near.shape),
+        ),
+        out_shape=jax.ShapeDtypeStruct((2,) + near.shape, near.dtype),
+        compiler_params=params(16),
+        name="pair_up",
+    )(group.reshape(1).astype(jnp.int32), near, far)
+
+
+def out_kernel(att_ref, w_ref, tok_ref, gain_ref, hidden_ref, mixed_ref, sums_ref, acc_ref):
+    step, steps = pl.program_id(0), pl.num_programs(0)
+    heads = jnp.concatenate([att_ref[i] for i in range(att_ref.shape[0])], 1)
+    part = nn(heads, w_ref[...].reshape(heads.shape[1], D))
+
+    @pl.when(step == 0)
+    def _():
+        acc_ref[...] = part
+
+    @pl.when(step > 0)
+    def _():
+        acc_ref[...] += part
+
+    @pl.when(step == steps - 1)
+    def _():
+        branch = acc_ref[...]
+        hidden = tok_ref[...].astype(F32) + branch
+        hidden_ref[...] = hidden
+        mixed_ref[...] = (hidden * inv_rms(hidden) * gain_ref[...]).astype(BF16)
+        total = jnp.sum(jnp.sum(branch * branch, -1, keepdims=True), 0, keepdims=True)
+        sums_ref[...] = jnp.broadcast_to(total, sums_ref.shape)
+
+
+def out_rows_spec(weights, heads):
+    members, groups, rows, _ = weights.shape
+    count = heads * HD // rows
+    steps = members // count
+    return pl.BlockSpec((count, None, rows, D), lambda i: (i % steps, i // steps, 0, 0))
+
+
+def project_out(att, weights, tokens, gain_row, after=()):
+    chunk = 4
+    return ordered(
+        out_kernel,
+        after,
+        dict(
+        grid=(HEADS // chunk,),
+        in_specs=[
+            pl.BlockSpec((chunk, TOK_DEV, HD), lambda i, *_: (i, 0, 0)),
+            out_rows_spec(weights, chunk),
+            whole(*BLOCK_SHAPE),
+            whole(1, D),
+        ],
+        out_specs=[whole(*BLOCK_SHAPE), whole(*BLOCK_SHAPE), whole(1, HD)],
+        scratch_shapes=[pltpu.VMEM(BLOCK_SHAPE, F32)],
+        ),
+        out_shape=[
+            jax.ShapeDtypeStruct(BLOCK_SHAPE, F32),
+            jax.ShapeDtypeStruct(BLOCK_SHAPE, BF16),
+            jax.ShapeDtypeStruct((1, HD), F32),
+        ],
+        compiler_params=params(24),
+        cost_estimate=cost(2 * TOK_DEV * D * D, 2 * D * D),
+        name="project_out",
+    )(att, weights, tokens, gain_row)
+
+
+def token_back_kernel(
+    a, b, c, d, e, mixed_ref, hidden_ref, cot_ref, router_ref, gain_ref,
+    grad_ref, wide_ref,
+):
+    probs = softmax_of(mixed_ref[...], router_ref[...])
+    grad = sum(ref[...].astype(F32) for ref in (a, b, c, d, e))
+    dp = grad[:, D : D + HD] + pltpu.roll(grad[:, D : D + HD], EXPERTS, 1)
+    logits = (probs * (dp - jnp.sum(probs * dp, -1, keepdims=True))).astype(BF16)
+    grad = grad[:, :D] + nt(logits, router_ref[...])
+    hidden = hidden_ref[...]
+    inverse = inv_rms(hidden)
+    scaled = grad * gain_ref[...]
+    mean = jnp.mean(scaled * hidden, -1, keepdims=True)
+    result = cot_ref[...].astype(F32) + inverse * (scaled - hidden * inverse * inverse * mean)
+    grad_ref[...] = result
+    wide_ref[:, :D] = result.astype(BF16)
+    wide_ref[:, D : D + HD] = logits
+    wide_ref[:, D + HD :] = jnp.zeros((TOK_DEV, HD), BF16)
+    part = jnp.sum(grad * hidden * inverse, 0, keepdims=True)
+    high = part.astype(BF16).astype(F32)
+    rows = lax.broadcasted_iota(jnp.int32, (2 * HEADS, HD), 0)
+    spread = jnp.zeros((2 * HEADS, HD), F32)
+    for i in range(HEADS):
+        lanes = slice(i * HD, (i + 1) * HD)
+        spread = jnp.where(rows == i, high[:, lanes], spread)
+        spread = jnp.where(rows == HEADS + i, part[:, lanes] - high[:, lanes], spread)
+    wide_ref[: 2 * HEADS, D + HD :] = spread.astype(BF16)
+
+
+def term_specs(terms):
+    specs, arrays = [], []
+    for term in terms:
+        if isinstance(term, tuple):
+            arrays.append(term[0])
+            shape = (None, None) + term[0].shape[2:]
+            specs.append(pl.BlockSpec(shape, lambda i, n=term[1]: n + (0, 0)))
+        else:
+            arrays.append(term)
+            specs.append(whole(*term.shape))
+    return specs, arrays
+
+
+def token_back(terms, mixed, hidden, cotangent, router, gain_row, after=()):
+    specs, arrays = term_specs(terms)
+    return ordered(
+        token_back_kernel,
+        after,
+        dict(
+            grid=(1,),
+            in_specs=specs
+            + [whole(*BLOCK_SHAPE)] * 3
+            + [whole(D, HD), whole(1, D)],
+            out_specs=[whole(*BLOCK_SHAPE), whole(TOK_DEV, D + 2 * HD)],
+        ),
+        out_shape=[
+            jax.ShapeDtypeStruct(BLOCK_SHAPE, F32),
+            jax.ShapeDtypeStruct((TOK_DEV, D + 2 * HD), BF16),
+        ],
+        compiler_params=params(40),
+        cost_estimate=cost(30 * TOK_DEV * D, 20 * TOK_DEV * D),
+        name="token_back",
+    )(*arrays, mixed, hidden, cotangent, router, gain_row)
+
+
+def out_back_kernel(grad_ref, w_ref, out_ref):
+    out = nt(grad_ref[...], w_ref[...].reshape(-1, D)).astype(BF16)
+    for i in range(out_ref.shape[0]):
+        out_ref[i] = out[:, i * HD : (i + 1) * HD]
+
+
+def out_back(wide, weights):
+    chunk = 4
+    return ordered(
+        out_back_kernel,
+        (),
+        dict(
+        grid=(HEADS // chunk,),
+        in_specs=[
+            pl.BlockSpec(BLOCK_SHAPE, lambda i: (0, 0)),
+            out_rows_spec(weights, chunk),
+        ],
+        out_specs=pl.BlockSpec((chunk, TOK_DEV, HD), lambda i: (i, 0, 0)),
+        ),
+        out_shape=jax.ShapeDtypeStruct((HEADS, TOK_DEV, HD), BF16),
+        compiler_params=params(24),
+        cost_estimate=cost(2 * TOK_DEV * D * D, 2 * D * D),
+        name="out_back",
+    )(wide, weights)
+
+
+def tokens_grad_kernel(
+    a, b, c, d, e, tok_ref, gain_ref, grad_ref, hidden_ref, before_ref, out_ref, result_ref, sums_ref
+):
+    total = sum(ref[...].astype(F32) for ref in (a, b, c, d, e))
+    grad, branch = total[:, :D], total[:, D:]
+    inputs = tok_ref[...].astype(F32)
+    inverse = inv_rms(inputs)
+    scaled = grad * gain_ref[...]
+    mean = jnp.mean(scaled * inputs, -1, keepdims=True)
+    result = grad_ref[...] + inverse * (scaled - inputs * inverse * inverse * mean)
+    out_ref[...] = result.astype(BF16)
+    result_ref[...] = (hidden_ref[...] + branch).astype(BF16)
+    lane = lax.broadcasted_iota(jnp.int32, sums_ref.shape, 1)
+    sums = jnp.where(lane == 1, before_ref[...], 0.0)
+    for place, values in ((0, inputs), (2, branch)):
+        square = jnp.sum(jnp.sum(values * values, -1, keepdims=True), 0, keepdims=True)
+        sums = jnp.where(lane == place, square, sums)
+    sums_ref[...] = sums
+
+
+def final_tokens(terms, tokens, gain_row, grad_hidden, hidden, branch_sums, after=()):
+    specs, arrays = term_specs(terms)
+    return ordered(
+        tokens_grad_kernel,
+        after,
+        dict(
+            grid=(1,),
+            in_specs=specs
+            + [whole(*BLOCK_SHAPE), whole(1, D), whole(*BLOCK_SHAPE), whole(*BLOCK_SHAPE), whole(1, HD)],
+            out_specs=[whole(*BLOCK_SHAPE), whole(*BLOCK_SHAPE), whole(1, HD)],
+        ),
+        out_shape=[
+            jax.ShapeDtypeStruct(BLOCK_SHAPE, BF16),
+            jax.ShapeDtypeStruct(BLOCK_SHAPE, BF16),
+            jax.ShapeDtypeStruct((1, HD), F32),
+        ],
+        compiler_params=params(40),
+        cost_estimate=cost(30 * TOK_DEV * D, 20 * TOK_DEV * D),
+        name="final_tokens",
+    )(*arrays, tokens, gain_row, grad_hidden, hidden, branch_sums)
+
+
+def owner_rows_kernel(place_ref, att_ref, mixed_ref, wide_ref, out_ref, moe_ref):
+    step, steps = pl.program_id(0), pl.num_programs(0)
+
+    @pl.when(step == 0)
+    def _():
+        out_ref[...] = jnp.zeros_like(out_ref)
+        moe_ref[...] = jnp.zeros_like(moe_ref)
+
+    out_ref[:, :D] += tn(att_ref[...], wide_ref[:, :D])
+    out_ref[:, D:] += tn(mixed_ref[...], wide_ref[:, D : D + HD])
+    tail = wide_ref[:, D + HD :].astype(F32)
+    rows = lax.broadcasted_iota(jnp.int32, tail.shape, 0) % TOK_DEV
+    mine = (rows == place_ref[0]) | (rows == place_ref[0] + HEADS)
+    moe_ref[...] += jnp.sum(jnp.where(mine, tail, 0.0), 0, keepdims=True)
+
+    @pl.when(step == steps - 1)
+    def _():
+        lane = lax.broadcasted_iota(jnp.int32, (HD, HD), 1)
+        out_ref[:, D:] = jnp.where(lane == EXPERTS, as_column(moe_ref[...]), out_ref[:, D:])
+
+
+def owner_rows(place, att, mixed_columns, wide_all, after=()):
+    rows, width = wide_all.shape
+    chunk = rows // 4
+    return ordered(
+        owner_rows_kernel,
+        after,
+        dict(
+            num_scalar_prefetch=1,
+            grid=(4,),
+            in_specs=[
+                pl.BlockSpec((chunk, HD), lambda i, s: (i, 0)),
+                pl.BlockSpec((chunk, HD), lambda i, s: (i, 0)),
+                pl.BlockSpec((chunk, width), lambda i, s: (i, 0)),
+            ],
+            out_specs=whole(HD, D + HD),
+            scratch_shapes=[pltpu.VMEM((1, HD), F32)],
+        ),
+        out_shape=jax.ShapeDtypeStruct((HD, D + HD), F32),
+        compiler_params=params(24),
+        cost_estimate=cost(2 * rows * D * HD, 2 * rows * D),
+        name="owner_rows",
+    )(place.reshape(1).astype(jnp.int32), att, mixed_columns, wide_all)
+
+
+def unpack_kernel(in_ref, wq_ref, wk_ref, wv_ref, gain_ref, q_ref, k_ref, v_ref, sums_ref):
+    heads = in_ref.shape[0]
+    total = jnp.zeros((q_ref.shape[0], 1), F32)
+    for part, (w_ref, out_ref) in enumerate(((wq_ref, q_ref), (wk_ref, k_ref), (wv_ref, v_ref))):
+        for h in range(heads):
+            piece = in_ref[h, : q_ref.shape[0], part * HD : (part + 1) * HD].astype(F32)
+            lanes = slice(h * HD, (h + 1) * HD)
+            out_ref[:, lanes] = piece
+            total += jnp.sum(w_ref[:, lanes].astype(F32) * piece, -1, keepdims=True)
+    sums_ref[...] = jnp.broadcast_to(total / gain_ref[...], sums_ref.shape)
+
+
+def unpack(arrived, weights, gain, after=()):
+    rows = weights[0].shape[0]
+    shape = jax.ShapeDtypeStruct((rows, D), F32)
+    return ordered(
+        unpack_kernel,
+        after,
+        dict(
+            grid=(1,),
+            in_specs=[whole(*arrived.shape)] + [whole(rows, D)] * 3 + [whole(rows, 1)],
+            out_specs=[whole(rows, D)] * 3 + [whole(rows, HD)],
+        ),
+        out_shape=[shape] * 3 + [jax.ShapeDtypeStruct((rows, HD), F32)],
+        compiler_params=params(24),
+        cost_estimate=cost(6 * rows * D, 20 * rows * D),
+        name="unpack",
+    )(arrived, *weights, gain.astype(F32).reshape(rows, 1))
+
+
+def tie_kernel(in_ref, out_ref):
+    out_ref[...] = in_ref[...]
+
+
+def tie(array, after):
+    return ordered(
+        tie_kernel,
+        after,
+        dict(grid=(1,), in_specs=[whole(*array.shape)], out_specs=whole(*array.shape)),
+        out_shape=jax.ShapeDtypeStruct(array.shape, array.dtype),
+        compiler_params=params(16),
+        name="tie",
+    )(array)
 
 
 def swap(value, axis):
@@ -1146,6 +1558,10 @@
     value = value + swap(value, "x")
     value = value + lax.ppermute(value, "z", [(0, 1), (1, 0), (2, 3), (3, 2)])
     return value + lax.ppermute(value, "z", [(0, 2), (2, 0), (1, 3), (3, 1)])
+
+
+def of_groups(value):
+    return lax.all_gather(value, ("grp", "core"))
 
 
 def gather_rows(value):
@@ -1243,19 +1659,12 @@
 
 
 def sum_blocks(terms, after=(), dtype=BF16):
-    specs, arrays = [], []
-    for term in terms:
-        if isinstance(term, tuple):
-            arrays.append(term[0])
-            specs.append(pl.BlockSpec((None,) + BLOCK_SHAPE, lambda i, n=term[1]: (n, 0, 0)))
-        else:
-            arrays.append(term)
-            specs.append(whole(*BLOCK_SHAPE))
+    specs, arrays = term_specs(terms)
     return ordered(
         sum_kernel,
         after,
-        dict(grid=(1,), in_specs=specs, out_specs=whole(*BLOCK_SHAPE)),
-        out_shape=jax.ShapeDtypeStruct(BLOCK_SHAPE, dtype),
+        dict(grid=(1,), in_specs=specs, out_specs=whole(*arrays[0].shape[-2:])),
+        out_shape=jax.ShapeDtypeStruct(arrays[0].shape[-2:], dtype),
         compiler_params=params(16),
         cost_estimate=cost(len(terms) * TOK_DEV * D, 2 * (len(terms) + 1) * TOK_DEV * D),
         name="sum_blocks",
@@ -1277,15 +1686,15 @@
             pl.when(z == edge)(functools.partial(store, out_ref, near, arrived))
             pl.when(z != edge)(functools.partial(store, out_ref, far, arrived))
 
-    shape = jax.ShapeDtypeStruct(BLOCK_SHAPE, BF16)
+    shape = jax.ShapeDtypeStruct(below.shape, BF16)
     return ordered(
         kernel,
         after,
         dict(
             num_scalar_prefetch=1,
             grid=(1,),
-            in_specs=[whole(*BLOCK_SHAPE)] * 6,
-            out_specs=[whole(*BLOCK_SHAPE)] * 2,
+            in_specs=[whole(*below.shape)] * 6,
+            out_specs=[whole(*below.shape)] * 2,
         ),
         out_shape=[shape, shape],
         compiler_params=params(24),
@@ -1296,33 +1705,35 @@
 
 def reduce_steps(parts, work):
     place = lax.axis_index("z").reshape(1).astype(jnp.int32)
-    own, near = {}, {}
-    last = None
+    last, sources = [], {}
+    for s in (3, 1):
+        own, other = parts(s, last)
+        near = swap(other, "core")
+        last = [own]
+        for i in range(2):
+            sources[s - i] = lambda r, i=i, own=own, near=near: [(own, (i, r)), (near, (i, r))]
+    crossed = {}
+    last = last[0]
     for s in (3, 2, 1, 0):
-        own[s], other = parts(s, [] if last is None else [last])
-        near[s] = swap(other, "core")
-        last = own[s]
-    crossed = {}
-    for s in (3, 2, 1, 0):
-        last = sum_blocks([(own[s], 1), (near[s], 1)], [last])
+        last = sum_blocks(sources[s](1), [last])
         crossed[s] = swap(last, "x")
     last = work(0, last)
     low = {}
-    low[3] = last = sum_blocks([(own[3], 0), (near[3], 0), crossed[3]], [last])
+    low[3] = last = sum_blocks(sources[3](0) + [crossed[3]], [last])
     up3 = shift(low[3], [(0, 1)])
     down3 = shift(low[3], [(3, 2)])
     last = work(1, last)
-    low[2] = last = sum_blocks([(own[2], 0), (near[2], 0), crossed[2]], [last])
+    low[2] = last = sum_blocks(sources[2](0) + [crossed[2]], [last])
     up2, down2 = pass_on(place, low[2], low[3], low[2], low[3], up3, down3)
     last = work(2, up2)
     up2 = shift(up2, [(0, 1), (1, 2)])
     down2 = shift(down2, [(3, 2), (2, 1)])
-    low[1] = last = sum_blocks([(own[1], 0), (near[1], 0), crossed[1]], [last])
+    low[1] = last = sum_blocks(sources[1](0) + [crossed[1]], [last])
     up1, down1 = pass_on(place, low[1], low[2], low[1], low[1], up2, down2)
     last = work(3, up1)
     up1 = shift(up1, [(0, 1), (1, 2), (2, 3)])
     down1 = shift(down1, [(3, 2), (2, 1), (1, 0)])
-    return sum_blocks([(own[0], 0), (near[0], 0), crossed[0], up1, down1], [last], F32)
+    return sources[0](0) + [crossed[0], up1, down1], last
 
 
 def expert_slots(routes_all, first, local):
@@ -1345,6 +1756,7 @@
     tokens, w_query, w_key, w_value, w_output, w_router, attn_gain, query_gain, key_gain,
     moe_gain, w_gate, w_up, w_down, routes, cotangent,
 ):
+    Order.marks.clear()
     group = lax.axis_index("grp")
     place = lax.axis_index(EP)
     members = lax.axis_size(EP)
@@ -1385,16 +1797,7 @@
     gain_q, gain_k = head_gains[1:2], head_gains[2:3]
     attn_row, moe_row = gains[0:1], gains[3:4]
 
-    out_pair = jnp.where(
-        group == 0,
-        jnp.concatenate([w_output, swap(w_output, "grp")]),
-        jnp.concatenate([swap(w_output, "grp"), w_output]),
-    )
-    output_full = jnp.transpose(
-        gather_rows(out_pair).reshape(members, 2, wide, D), (1, 0, 2, 3)
-    ).reshape(D, D)
-    cot_own = gather_rows(cotangent)
-    cot_other = gather_rows(swap(cotangent, "grp"))
+    far_out = swap(w_output, "grp")
 
     slots_own = expert_slots(lax.dynamic_index_in_dim(routes_all, group, 0, False), first, local)
     slots_other = expert_slots(
@@ -1415,30 +1818,24 @@
         kept[0] = project(spot, own, far, w_head, attn_row, kept[0], seq, after)
         return kept[0][2]
 
-    def idle(_, last):
+    def start_work(step, last):
+        if step == 3:
+            kept.append(pair_up(group, w_output, far_out, [last, mine]))
+            return kept[1]
         return last
 
-    gather_steps(tokens, use_tokens, idle)
+    gather_steps(tokens, use_tokens, start_work)
+    output_full = gather_rows(kept[1][None])
+    cot_own = gather_rows(cotangent)
     normed_all, qkv, stat = kept[0]
     stat = total_over_ep(stat)
     q16, k16, v16, attn_float, att_head, lse = attend(qkv, stat, gain_q, gain_k, cosine, sine)
     attended = lax.all_to_all(att_head.reshape(members, TOK_DEV, HD), EP, 0, 0, tiled=True)
-    attended = jnp.transpose(attended, (1, 0, 2)).reshape(TOK_DEV, D)
-    inputs = tokens.astype(F32)
-    branch_attn = nn(attended, output_full)
-    hidden = inputs + branch_attn
-    moe_inv = inv_rms(hidden)
-    mixed = (hidden * moe_inv * moe_row).astype(BF16)
-
-    early = {}
-
-    def early_work(step, last):
-        if step == 1:
-            early["g"] = plain_dispatch(cot_own, slots_own, [last])
-            return early["g"]
-        if step == 2:
-            early["slope"] = slopes(early["g"], w_down, [last])
-            return early["slope"]
+    g_own = plain_dispatch(cot_own, slots_own, [att_head])
+    cot_stack = stack_of_core(core, cot_own.reshape(members // 2, 2, TOK_DEV, D), [g_own])
+    slope_own = slopes(g_own, w_down, [cot_stack])
+    hidden, mixed, branch_sums = project_out(attended, output_full, tokens, moe_row, [slope_own])
+    def early_work(_, last):
         return last
 
     rows = [None]
@@ -1449,150 +1846,118 @@
         return rows[0][0]
 
     gather_steps(mixed, use_mixed, early_work)
-    x_own, mixed_columns = rows[0]
-    mixed_other = gather_rows(swap(mixed, "grp"))
-    g_own, slope_own = early["g"], early["slope"]
-    route_probs = jax.nn.softmax(nn(mixed, router_full), -1)
-    act_a, dg_a, du_a, gate_a, z_rows, dp_slots = experts(
+    x_own, mixed_columns, mixed_stack = rows[0]
+    sides = jnp.stack([core, group.astype(jnp.int32)])
+    cot_near = of_groups(cot_stack)
+    mixed_near = of_groups(mixed_stack)
+    every = jnp.concatenate([jnp.arange(members // 2, dtype=jnp.int32), sides])
+    act_a, dg_a, du_a, gate_a, z_rows = experts(
         first, x_own, slope_own, w_gate, w_up, router_wide, True
     )
 
     def place_of(s):
-        return jnp.stack([chips[s][0], chips[s][1], core])
+        return jnp.stack([chips[s][0], chips[s][1], chips[s - 1][0], chips[s - 1][1], core])
 
     late = {}
 
     def late_work(step, last):
-        if step == 0:
-            dp_part = spread_back(dp_slots, slots_own, [last])
-            late["dp"] = lax.all_to_all(dp_part, EP, 0, 0, tiled=True).reshape(EXPERTS, TOK_DEV).T
-            return dp_part
         if step == 1:
             late["y"] = down(act_a, gate_a, w_down, [last])
             return late["y"]
         if step == 2:
-            return last
-        late["g"] = plain_dispatch(cot_other, slots_other, [last])
-        late["slope"] = slopes(late["g"], w_down, [late["g"]])
-        return late["slope"]
-
-    grad_mixed = reduce_steps(
+            late["g"] = stack_dispatch(every, cot_near, slots_other, [last])
+            return late["g"]
+        if step == 3:
+            late["slope"] = slopes(late["g"], w_down, [last])
+            return late["slope"]
+        return last
+
+    terms, last = reduce_steps(
         lambda s, after: combine_part(place_of(s), z_rows, slots_own, after), late_work
     )
-    dp = late["dp"]
-    branch_part = combine(late["y"], slots_own)
-    branch_moe = reduce_rows(branch_part).astype(F32)
-    output = (hidden + branch_moe).astype(BF16)
-
-    grad_logits = (
-        route_probs * (dp - jnp.sum(route_probs * dp, -1, keepdims=True))
-    ).astype(BF16)
-    grad_mixed = grad_mixed + nt(grad_logits, router_full)
-    grad_hid_norm, moe_gain_part = norm_back(grad_mixed, hidden, moe_inv, moe_row)
-    grad_hidden = cotangent.astype(F32) + grad_hid_norm
-    grad_branch = grad_hidden.astype(BF16)
-    grad_out = nt(grad_branch, output_full).astype(BF16).reshape(TOK_DEV, HEADS, HD)
-    grad_out = jnp.transpose(grad_out, (1, 0, 2))
+    grad_hidden, wide_branch = token_back(
+        terms, mixed, hidden, cotangent, router_wide, moe_row, [last]
+    )
+    grad_out = out_back(wide_branch, output_full)
     grad_att_head = lax.all_to_all(grad_out, EP, 0, 0, tiled=True).reshape(seq, HD)
-
-    wide_branch = jnp.concatenate(
-        [grad_branch, grad_logits, jnp.zeros((TOK_DEV, HD - EXPERTS), BF16)], 1
-    )
     branch_all = gather_rows(wide_branch)
+
+    def expert_other(only, last):
+        late[only] = experts(
+            first, late["x"], late["slope"], w_gate, w_up, router_wide, False, only, [last]
+        )
+        return late[only][3]
+
+    groups = [(0, local // 2), (local // 2, local - local // 2)]
+    late["x"] = stack_dispatch(every, mixed_near, slots_other, [grad_out])
+    last = expert_other(groups[0], late["x"])
+
     dnq, dnk, dv16, means, gain_parts = attend_back(
-        q16, k16, v16, grad_att_head, attn_float, lse, qkv, stat, gain_q, gain_k, cosine, sine
+        q16, k16, v16, grad_att_head, attn_float, lse, qkv, stat, gain_q, gain_k, cosine, sine, [last],
     )
     means = total_over_ep(means)
     qkv_grads = finish(dnq, dnk, dv16, qkv, stat, means, gain_q, gain_k)
     half = group.reshape(1).astype(jnp.int32)
+
+    def expert_grads(only, last):
+        act_b, dg_b, du_b, gate_b = late[only]
+        late["grads"] = weight_grads(
+            only, half, (x_own, late["x"]), (dg_a, dg_b), (du_a, du_b), (act_a, act_b),
+            (g_own, late["g"]), (gate_a, gate_b), late.get("grads"), [last],
+        )
+        return late["grads"][0]
 
     def last_work(step, last):
         if step == 0:
             late["dw"] = dw_product(normed_all, qkv_grads, [last])
             return late["dw"]
         if step == 1:
-            late["x"] = plain_dispatch(mixed_other, slots_other, [last])
-            return late["x"]
+            return expert_other(groups[1], last)
         if step == 2:
-            late["mid"] = experts(
-                first, late["x"], late["slope"], w_gate, w_up, router_wide, False, [last]
-            )
-            return late["mid"][3]
-        act_b, dg_b, du_b, gate_b = late["mid"]
-        late["grads"] = weight_grads(
-            half, (x_own, late["x"]), (dg_a, dg_b), (du_a, du_b), (act_a, act_b),
-            (g_own, late["g"]), (gate_a, gate_b), [last],
-        )
-        return late["grads"][0]
-
-    grad_normed = reduce_steps(
-        lambda s, after: normed_part(place_of(s), qkv_grads, w_head, after), last_work
+            return expert_grads(groups[0], last)
+        return last
+
+    terms, last = reduce_steps(
+        lambda s, after: normed_part(place_of(s), qkv_grads, w_head, late["y"], slots_own, after),
+        last_work,
+    )
+    tokens_grad, output, sums = final_tokens(
+        terms, tokens, attn_row, grad_hidden, hidden, branch_sums, [last]
     )
     dw_head = late["dw"]
+    last = tokens_grad
+    last = expert_grads(groups[1], last)
     gate_grad, up_grad, down_grad = late["grads"]
-    attn_inv = inv_rms(inputs)
-    scaled = grad_normed * attn_row
-    grad_tok = attn_inv * (
-        scaled - inputs * attn_inv * attn_inv * jnp.mean(scaled * inputs, -1, keepdims=True)
-    )
-    tokens_grad = (grad_hidden + grad_tok).astype(BF16)
+    rms_stats = jnp.sqrt(total_over_ep(sums)[:, :3] / (seq * D))
 
     dw_keep = lax.dynamic_slice_in_dim(dw_head, group * (D // 2), D // 2, 0)
     dw_send = lax.dynamic_slice_in_dim(dw_head, (1 - group) * (D // 2), D // 2, 0)
     dw_half = (dw_keep + swap(dw_send.astype(BF16), "grp").astype(F32)).astype(BF16)
     gain_parts = gain_parts + swap(gain_parts, "grp")
-    sums = jnp.stack(
-        [jnp.sum(inputs * inputs), jnp.sum(branch_attn * branch_attn), jnp.sum(branch_moe * branch_moe)]
-    )
-    extra = jnp.concatenate(
-        [gain_parts.reshape(1, 2 * HD), sums[None, :], jnp.zeros((1, HD - 3), F32)], 1
-    )
+    extra = gain_parts.reshape(1, 2 * HD)
     high = extra.astype(BF16)
     low = (extra - high.astype(F32)).astype(BF16)
-    moe_high = moe_gain_part.astype(BF16)
-    moe_low = (moe_gain_part - moe_high.astype(F32)).astype(BF16)
-    moe_rows = jnp.concatenate(
-        [moe_high.reshape(members, 1, HD), moe_low.reshape(members, 1, HD),
-         jnp.zeros((members, 1, HD), BF16)], 2,
-    )
-    extra = jnp.broadcast_to(jnp.stack([high[0], low[0]])[None], (members, 2, 3 * HD))
-    extra = jnp.concatenate([extra, moe_rows, jnp.zeros((members, 13, 3 * HD), BF16)], 1)
+    extra = jnp.pad(jnp.concatenate([high, low], 0), ((0, 14), (0, HD)))
     payload = jnp.concatenate(
         [
             dw_half.reshape(members, wide, 3 * HD),
-            extra,
+            jnp.broadcast_to(extra, (members,) + extra.shape),
         ],
         1,
     )
-    arrived = lax.all_to_all(payload, EP, 0, 0, tiled=True).astype(F32)
-    dense = jnp.transpose(
-        arrived[:, :wide].reshape(HEADS, wide, 3, HD), (2, 1, 0, 3)
-    ).reshape(3, wide, D)
-    extras = arrived[:, wide] + arrived[:, wide + 1]
-    rms_stats = jnp.sqrt(jnp.sum(extras[:, 2 * HD : 2 * HD + 3], 0) / (seq * D)).reshape(1, 3)
+    arrived = lax.all_to_all(payload, EP, 0, 0, tiled=True)
+    *dense, attn_sums = unpack(arrived, (w_query, w_key, w_value), attn_gain, [last])
+    attn_gain_grad = attn_sums[:, 0]
+    extras = arrived[:, wide].astype(F32) + arrived[:, wide + 1].astype(F32)
     flat = group * members + place
     head_row = lax.dynamic_slice(
         extras[:, : 2 * HD].reshape(HEADS, 2, HD // wide, wide),
         (flat // (HD // wide), 0, flat % (HD // wide), 0),
         (1, 2, 1, wide),
     ).reshape(2, wide)
-    attn_gain_grad = (
-        jnp.sum(
-            w_query.astype(F32) * dense[0]
-            + w_key.astype(F32) * dense[1]
-            + w_value.astype(F32) * dense[2],
-            -1,
-        )
-        / attn_gain.astype(F32)
-    )
-
-    moe_sums = jnp.sum(arrived[:, wide + 2], 0)
-    moe_part = (moe_sums[:HD] + moe_sums[HD : 2 * HD]).reshape(2, wide, 1)
-    out_part = tn(att_head, branch_all[:, :D]).reshape(2, wide, D)
-    router_part = tn(mixed_columns, branch_all[:, D : D + EXPERTS]).reshape(2, wide, EXPERTS)
-    out_part = jnp.concatenate(
-        [out_part, router_part, moe_part, jnp.zeros((2, wide, HD - EXPERTS - 1), F32)], 2
-    )
+
+    out_part = owner_rows(place, att_head, mixed_columns, branch_all, [last])
+    out_part = out_part.reshape(2, wide, D + HD)
     out_keep = lax.dynamic_index_in_dim(out_part, group, 0, False)
     out_send = lax.dynamic_index_in_dim(out_part, 1 - group, 0, False).astype(BF16)
     out_sum = (out_keep + swap(out_send, "grp").astype(F32)).astype(BF16)

time: 922 us -> 822 us (0.89)
  waiting for transfers between devices: 237 us -> 169 us
  Pallas kernels: 258 us -> 315 us
  blocking collectives: 69.1 us -> 43.8 us
  local copies, waits for them, and re-layouts: 150 us -> 125 us
  matrix products: 21.1 us -> 0.27 us
  other arithmetic: 32.3 us -> 20.5 us
    pallas_call x65 -> x67, Pallas kernels: 258 us -> 315 us  [run(): *results, mark = call(*args, *after)]
    ppermute x51 -> x47, waiting for transfers between devices: 105 us -> 79 us  [swap(): return lax.ppermute(value, axis, [(0, 1), (1, 0)])]
    all_to_all x2, waiting for transfers between devices: 25.3 us -> 0.01 us  [the longest x1 0.01 us: fast_shards(): lax.all_to_all(grad_out, EP, 0, 0, tiled=True).reshape(seq, HD)]
    all_to_all x1 -> x0, blocking collectives: 20.4 us -> none  [fast_shards(): lax.all_to_all(grad_out, EP, 0, 0, tiled=True).reshape(seq, HD)]
    dot_general x5 -> x0, matrix products: 19.4 us -> none  [the longest x2 8.01 us: nt(): lax.dot_general(left, right, (((1,), (1,)), ((), ())), preferred_element_...]
    all_to_all x1, waiting for transfers between devices: 15.7 us -> 0.01 us  [fast_shards(): lax.all_to_all(att_head.reshape(members, TOK_DEV, HD), EP, 0, 0, tiled=True)]
    unnamed x252 -> x180, local copies, waits for them, and re-layouts: 109 us -> 100 us
    ppermute x51 -> x47, starting transfers between devices: 32.8 us -> 30.7 us  [swap(): return lax.ppermute(value, axis, [(0, 1), (1, 0)])]
  transfers between devices with their start and end apart: 89 -> 86, of which waited for: 34 -> 30; matrix products, arithmetic and copies ran while one was open for 9% -> 6% of each run, Pallas kernels for 28% -> 39%
where the time goes in v3:
time: 822 us; the launch traced here: 811 us
  Pallas kernels  315 us (38%)
  waiting for transfers between devices  169 us (21%)
  local copies, waits for them, and re-layouts  125 us (15%)
  starting transfers between devices  119 us (14%)
  blocking collectives  43.8 us (5%)
  other arithmetic  20.5 us (2%)
  between operations  17.9 us (2%)
    pallas_call x67, Pallas kernels, run(): *results, mark = call(*args, *after)  315 us
    unnamed x180, local copies, waits for them, and re-layouts  100 us
    ppermute x47, waiting for transfers between devices, swap(): return lax.ppermute(value, axis, [(0, 1), (1, 0)])  79 us
    ppermute x24, waiting for transfers between devices, shift(): return lax.ppermute(value, 'z', pairs)  66.6 us
    ppermute x24, starting transfers between devices, shift(): return lax.ppermute(value, 'z', pairs)  60.3 us
    all_to_all x1, blocking collectives, fast_shards(): mine = lax.all_to_all(columns, EP, 0, 0, tiled=True)  43.8 us
    ppermute x47, starting transfers between devices, swap(): return lax.ppermute(value, axis, [(0, 1), (1, 0)])  30.7 us
  transfers between devices with their start and end apart: 86, of which 30 were waited for; matrix products, arithmetic and copies ran while one was open for 6% of the time, Pallas kernels for 39%

profile of v3, /device:TPU:12, one launch (start us, length us, event | category | flops | bytes accessed | tf_op | source)
XLA Modules:
  0.0 811.2 jit_solution(17041519841153892773)
XLA Ops:
  16.8 43.8 %all_to_all.20.refs_4_ = bf16[16,80,384]{2,1,0:T(8,128)(2,1)S(1)} all-to-all(bf16[16,80,384]{2,1,0:T(8,128)(2,1)S(1)} %pad_maximum_fusion.2), channel_id=1, replica_groups=mesh['grp'=2,'z'=4,'x'=2,'core'=2] {'z','x','core'}, dimensions={0} | all-to-all | bytes 1966080 | tf_op jit(solution)/shard_map/all_to_all | solution.py:1782
  71.3 24.4 %collective-permute-done.refs_1_.refs_3_ = bf16[128,2048]{1,0:T(8,128)(2,1)} collective-permute-done((bf16[128,2048]{1,0:T(8,128)(2,1)S(1)}, bf16[128,2048]{1,0:T(8,128)(2,1)}, u32[]{:S(2)}, u32[]{:S(2)}) %collective-permute-start) | collective-permute-done | bytes 524320 | tf_op jit(solution)/shard_map/ppermute | solution.py:1585
  137.4 5.9 collective-permute-done.17.refs_1_
  174.0 11.0 %collective-permute-done.14.refs_1_ = bf16[128,2048]{1,0:T(8,128)(2,1)S(1)} collective-permute-done((bf16[128,2048]{1,0:T(8,128)(2,1)}, bf16[128,2048]{1,0:T(8,128)(2,1)S(1)}, u32[]{:S(2)}, u32[]{:S(2)}) %collective-permute-start.14) | collective-permute-done | bytes 524320 | tf_op jit(solution)/shard_map/ppermute | solution.py:1553
  210.5 10.6 %attend.1 = (bf16[2048,128]{1,0:T(8,128)(2,1)S(1)}, bf16[2048,128]{1,0:T(8,128)(2,1)S(1)}, bf16[2048,128]{1,0:T(8,128)(2,1)S(1)}, f32[2048,128]{1,0:T(8,128)S(1)...) custom-call(f32[2048,384]{1,0:T(8,128)} %get-tuple-element.243.refs_0_.refs_6_.refs_3_, ...), custom_call_target="tpu_custom_call" | custom-call | flops 429496736 | bytes 786432 | tf_op jit(solution)/shard_map/attend/pallas_call | solution.py:571
  227.3 6.4 plain_dispatch.1
  237.2 6.6 all-to-all-start.1
  244.4 8.5 %copy-done.1 = bf16[4,1024,2048]{2,1,0:T(8,128)(2,1)S(1)} copy-done((bf16[4,1024,2048]{2,1,0:T(8,128)(2,1)S(1)}, bf16[4,1024,2048]{2,1,0:T(8,128)(2,1)}, u32[]{:S(2)}) %copy-start.1) | copy-done | bytes 16777240
  257.5 9.1 %slopes.2 = (f32[4,384,1024]{2,1,0:T(8,128)}, f32[8,128]{1,0:T(8,128)S(1)}) custom-call(bf16[4,384,2048]{2,1,0:T(8,128)(2,1)S(1)} %copy-done.20, bf16[4,1024,2048]{2,1,0:T(8,128)(2,1)S(1)} %copy-done.1, f32[8,128]{1,0:T(8,128)S(1)} %get-tuple-element.253.refs_2_), custom_call_target="tpu_custom_call" | custom-call | flops 644245120 | bytes 1677721 | tf_op jit(solution)/shard_map/slopes/pallas_call | solution.py:571
  280.5 8.5 %collective-permute-done.24.refs_1_.refs_3_ = bf16[128,2048]{1,0:T(8,128)(2,1)S(1)} collective-permute-done((bf16[128,2048]{1,0:T(8,128)(2,1)S(1)}, bf16[128,2048]{1,0:T(8,128)(2,1)S(1)}, u32[]{:S(2)}, u32[]{:S(2)}) %collective-permute-start.24) | collective-permute-done | bytes 524320 | tf_op jit(solution)/shard_map/ppermute | solution.py:1585
  318.7 6.2 collective-permute-done.26.refs_1_
  328.5 10.8 %collective-permute-done.37.refs_1_ = bf16[128,2048]{1,0:T(8,128)(2,1)S(1)} collective-permute-done((bf16[128,2048]{1,0:T(8,128)(2,1)S(1)}, bf16[128,2048]{1,0:T(8,128)(2,1)S(1)}, u32[]{:S(2)}, u32[]{:S(2)}) %collective-permute-start.37) | collective-permute-done | bytes 524320 | tf_op jit(solution)/shard_map/ppermute | solution.py:1553
  348.1 40.8 %experts_full.1 = (bf16[4,384,1024]{2,1,0:T(8,128)(2,1)}, bf16[4,384,1024]{2,1,0:T(8,128)(2,1)}, bf16[4,384,1024]{2,1,0:T(8,128)(2,1)}, f32[4,384,128]{2,1,0:T(8...) custom-call(s32[1]{0:T(128)} %bitcast.29.refs_0_, bf16[4,384,2048]{2,1,0:T(8,128)(2,1)} %get-tuple-element.291.refs_1_, ...), custom_call_target="tpu_custom_call" | custom-call | flops 2576980480 | bytes 5872025 | tf_op jit(solution)/shard_map/experts_full/pallas_call | solution.py:571
  411.5 10.1 %collective-permute-done.47.refs_2_ = bf16[128,2176]{1,0:T(8,128)(2,1)S(1)} collective-permute-done((bf16[128,2176]{1,0:T(8,128)(2,1)S(1)}, bf16[128,2176]{1,0:T(8,128)(2,1)S(1)}, u32[]{:S(2)}, u32[]{:S(2)}) %collective-permute-start.47) | collective-permute-done | bytes 557088 | tf_op jit(solution)/shard_map/ppermute | solution.py:1553
  425.7 5.8 copy-done.2
  431.5 9.4 %down.1 = (bf16[4,384,2048]{2,1,0:T(8,128)(2,1)S(1)}, f32[8,128]{1,0:T(8,128)S(1)}) custom-call(bf16[4,384,1024]{2,1,0:T(8,128)(2,1)S(1)} %copy-done.33, f32[4,384,128]{2,1,0:T(8,128)S(1)} %copy-done.41, bf16[4,1024,2048]{2,1,0:T(8,128)(2,1)S(1)} %copy-done.2, f32[8,128]{1,0:T(8,128)S(1)} %get-tuple-element.311.refs_3_), custom_call_target="tpu_custom_call" | custom-call | flops 644245120 | bytes 1677721 | tf_op jit(solution)/shard_map/down/pallas_call | solution.py:571
  453.4 5.8 copy-done.8
  459.3 7.0 stack_dispatch.2
  482.2 9.1 %slopes.3 = (f32[4,384,1024]{2,1,0:T(8,128)}, f32[8,128]{1,0:T(8,128)S(1)}) custom-call(bf16[4,384,2048]{2,1,0:T(8,128)(2,1)S(1)} %copy-done.21, bf16[4,1024,2048]{2,1,0:T(8,128)(2,1)S(1)} %copy-done.3, f32[8,128]{1,0:T(8,128)S(1)} %get-tuple-element.324.refs_2_), custom_call_target="tpu_custom_call" | custom-call | flops 644245120 | bytes 1677721 | tf_op jit(solution)/shard_map/slopes/pallas_call | solution.py:571
  510.4 5.8 copy-done.9
  516.2 7.0 stack_dispatch.3
  523.8 16.0 %experts_half.2 = (bf16[2,384,1024]{2,1,0:T(8,128)(2,1)}, bf16[2,384,1024]{2,1,0:T(8,128)(2,1)}, bf16[2,384,1024]{2,1,0:T(8,128)(2,1)}, f32[2,384,128]{2,1,0:T(8,128)}, f32[8,128]{1,0:T(8,128)}) custom-call(s32[1]{0:T(128)} %bitcast.29.refs_0_, bf16[4,384,2048]{2,1,0:T(8,128)(2,1)} %get-tuple-element.332.refs_1_.refs_2_, ...), custom_call_target="tpu_custom_call" | custom-call | flops 644245120 | bytes 2936012 | tf_op jit(solution)/shard_map/experts_half/pallas_call | solution.py:571
  544.9 10.1 %attend_back.1 = (f32[2048,128]{1,0:T(8,128)S(1)}, f32[2048,128]{1,0:T(8,128)S(1)}, bf16[2048,128]{1,0:T(8,128)(2,1)S(1)}, f32[2,2048]{1,0:T(2,128)S(1)}, f32[2,128]{1,0:T(2,128)S(1)}, /*index=5*/f32[8,128]{1,0:T(8,128)}) custom-call(bf16[2048,128]{1,0:T(8,128)(2,1)S(1)} %copy-done.64, bf16[2048,128]{1,0:T(8,128)(2,1)S(1)} %copy-done.66, ...), custom_call_target="tpu_custom_call" | custom-call | flops 1073741824 | bytes 1572864 | tf_op jit(solution)/shard_map/attend_back/pallas_call | solution.py:571
  574.8 8.0 normed_part.2
  582.7 6.5 normed_part.3
  608.4 8.5 %collective-permute-done.63.refs_2_ = bf16[128,4096]{1,0:T(8,128)(2,1)S(1)} collective-permute-done((bf16[128,4096]{1,0:T(8,128)(2,1)S(1)}, bf16[128,4096]{1,0:T(8,128)(2,1)S(1)}, u32[]{:S(2)}, u32[]{:S(2)}) %collective-permute-start.63) | collective-permute-done | bytes 1048608 | tf_op jit(solution)/shard_map/ppermute | solution.py:1553
  624.6 16.7 %collective-permute-done.71 = f32[2,128]{1,0:T(2,128)S(1)} collective-permute-done((f32[2,128]{1,0:T(2,128)S(1)}, f32[2,128]{1,0:T(2,128)S(1)}, u32[]{:S(2)}, u32[]{:S(2)}) %collective-permute-start.71) | collective-permute-done | bytes 1056 | tf_op jit(solution)/shard_map/ppermute | solution.py:1553
  642.3 16.1 %experts_half.3 = (bf16[2,384,1024]{2,1,0:T(8,128)(2,1)}, bf16[2,384,1024]{2,1,0:T(8,128)(2,1)}, bf16[2,384,1024]{2,1,0:T(8,128)(2,1)}, f32[2,384,128]{2,1,0:T(8,128)}, f32[8,128]{1,0:T(8,128)}) custom-call(s32[1]{0:T(128)} %bitcast.29.refs_0_, bf16[4,384,2048]{2,1,0:T(8,128)(2,1)} %get-tuple-element.332.refs_1_.refs_2_, ...), custom_call_target="tpu_custom_call" | custom-call | flops 644245120 | bytes 2936012 | tf_op jit(solution)/shard_map/experts_half/pallas_call | solution.py:571
  682.7 19.9 %weight_grads.2 = (f32[4,1024,1024]{2,1,0:T(8,128)}, f32[4,1024,1024]{2,1,0:T(8,128)}, f32[4,512,2048]{2,1,0:T(8,128)}, f32[8,128]{1,0:T(8,128)}) custom-call(s32[1]{0:T(128)} %bitcast.28.refs_0_, bf16[4,384,2048]{2,1,0:T(8,128)(2,1)} %get-tuple-element.291.refs_1_, bf16[4,384,2048]{2,1,0:T(8,128)(2,1)} %get-tuple-element.332.refs_1_.refs_2_, ...), custom_call_target="tpu_custom_call" | custom-call | flops 966367616 | bytes 3774873 | tf_op jit(solution)/shard_map/weight_grads/pallas_call | solution.py:571
  721.3 18.4 %collective-permute-done.68.refs_3_ = bf16[128,4096]{1,0:T(8,128)(2,1)S(1)} collective-permute-done((bf16[128,4096]{1,0:T(8,128)(2,1)}, bf16[128,4096]{1,0:T(8,128)(2,1)S(1)}, u32[]{:S(2)}, u32[]{:S(2)}) %collective-permute-start.68) | collective-permute-done | bytes 1048608 | tf_op jit(solution)/shard_map/ppermute | solution.py:1585
  753.1 18.4 %weight_grads.3 = (f32[4,1024,1024]{2,1,0:T(8,128)}, f32[4,1024,1024]{2,1,0:T(8,128)}, f32[4,512,2048]{2,1,0:T(8,128)}, f32[8,128]{1,0:T(8,128)}) custom-call(s32[1]{0:T(128)} %bitcast.28.refs_0_, bf16[4,384,2048]{2,1,0:T(8,128)(2,1)} %get-tuple-element.291.refs_1_, ...), custom_call_target="tpu_custom_call", output_to_operand_aliasing={{0}: (13, {}), {1}: (14, {}), {2}: (15, {})} | custom-call | flops 966367616 | bytes 3774873 | tf_op jit(solution)/shard_map/weight_grads/pallas_call | solution.py:571
  792.3 10.0 %collective-permute-done.73 = bf16[64,2176]{1,0:T(8,128)(2,1)S(1)} collective-permute-done((bf16[64,2176]{1,0:T(8,128)(2,1)S(1)}, bf16[64,2176]{1,0:T(8,128)(2,1)S(1)}, u32[]{:S(2)}, u32[]{:S(2)}) %collective-permute-start.73) | collective-permute-done | bytes 278560 | tf_op jit(solution)/shard_map/ppermute | solution.py:1965
  (496 shorter events, 392.4 us)
Async XLA Ops:
  7.2 216.5 %all-gather.9.cloned.1.call-start = ((), (), s32[]{:S(2)}) async-start(), calls=%async_computation.4 | async-start | bytes 8912896 | tf_op jit(solution)/shard_map/all_gather | solution.py:1568
  7.9 258.6 %all-gather.13.cloned.1.call-start = ((), (), s32[]{:S(2)}) async-start(), calls=%async_computation.6 | async-start | bytes 8912896 | tf_op jit(solution)/shard_map/all_gather | solution.py:1568
  60.6 49.8 %collective-permute-start.7 = (bf16[16,80,384]{2,1,0:T(8,128)(2,1)S(1)}, bf16[16,80,384]{2,1,0:T(8,128)(2,1)S(1)}, u32[]{:S(2)}, u32[]{:S(2)}) collective-permute-start(bf16[16,80,384]{2,1,0:T(8,128)(2,1)S(1)} %all_to_all.20.refs_4_), channel_id=1, source_target_pairs={{0,16},{16,0},{1,17},{17,1},{2,18},{18,2},{3,19},{19,3},{4,20},{20... | collective-permute-start | bytes 2949128 | tf_op jit(solution)/shard_map/ppermute | solution.py:1553
  61.2 34.5 %collective-permute-start = (bf16[128,2048]{1,0:T(8,128)(2,1)S(1)}, bf16[128,2048]{1,0:T(8,128)(2,1)}, u32[]{:S(2)}, u32[]{:S(2)}) collective-permute-start(bf16[128,2048]{1,0:T(8,128)(2,1)S(1)} %copy-done.38), channel_id=1, source_target_pairs={{12,8},{8,4},{4,0},{13,9},{9,5},{5,1},{14,10},{10,6},{6,2},{15,11}... | collective-permute-start | bytes 1572872 | tf_op jit(solution)/shard_map/ppermute | solution.py:1585
  63.3 32.4 %collective-permute-start.3 = (bf16[128,2048]{1,0:T(8,128)(2,1)S(1)}, bf16[128,2048]{1,0:T(8,128)(2,1)}, u32[]{:S(2)}, u32[]{:S(2)}) collective-permute-start(bf16[128,2048]{1,0:T(8,128)(2,1)S(1)} %copy-done.38), channel_id=1, source_target_pairs={{0,4},{4,8},{8,12},{1,5},{5,9},{9,13},{2,6},{6,10},{10,14},{3,7},{... | collective-permute-start | bytes 1572872 | tf_op jit(solution)/shard_map/ppermute | solution.py:1585
  67.0 35.1 %collective-permute-start.8 = (bf16[128,2048]{1,0:T(8,128)(2,1)S(1)}, bf16[128,2048]{1,0:T(8,128)(2,1)}, u32[]{:S(2)}, u32[]{:S(2)}) collective-permute-start(bf16[128,2048]{1,0:T(8,128)(2,1)S(1)} %copy-done.38), channel_id=1, source_target_pairs={{0,2},{2,0},{1,3},{3,1},{4,6},{6,4},{5,7},{7,5},{8,10},{10,8},{9,1... | collective-permute-start | bytes 1572872 | tf_op jit(solution)/shard_map/ppermute | solution.py:1553
  68.3 35.7 %collective-permute-start.10 = (bf16[128,2048]{1,0:T(8,128)(2,1)S(1)}, bf16[128,2048]{1,0:T(8,128)(2,1)S(1)}, u32[]{:S(2)}, u32[]{:S(2)}) collective-permute-start(bf16[128,2048]{1,0:T(8,128)(2,1)S(1)} %copy-done.38), channel_id=1, source_target_pairs={{0,1},{1,0},{2,3},{3,2},{4,5},{5,4},{6,7},{7,6},{8,9},{9,8},{10,11... | collective-permute-start | bytes 1572872 | tf_op jit(solution)/shard_map/ppermute | solution.py:1553
  98.3 24.8 %collective-permute-start.6 = (bf16[128,2048]{1,0:T(8,128)(2,1)}, bf16[128,2048]{1,0:T(8,128)(2,1)}, u32[]{:S(2)}, u32[]{:S(2)}) collective-permute-start(bf16[128,2048]{1,0:T(8,128)(2,1)} %get-tuple-element.208.refs_1_), channel_id=1, source_target_pairs={{0,1},{1,0},{2,3},{3,2},{4,5},{5,4},{6,7},{7,6},{8,9},{9,8},{10,11... | collective-permute-start | bytes 1572872 | tf_op jit(solution)/shard_map/ppermute | solution.py:1553
  102.1 24.4 %collective-permute-start.1 = (bf16[128,2048]{1,0:T(8,128)(2,1)}, bf16[128,2048]{1,0:T(8,128)(2,1)}, u32[]{:S(2)}, u32[]{:S(2)}) collective-permute-start(bf16[128,2048]{1,0:T(8,128)(2,1)} %collective-permute-done.refs_1_.refs_3_), channel_id=1, source_target_pairs={{8,4},{4,0},{9,5},{5,1},{10,6},{6,2},{11,7},{7,3},{24,20},{20,16},... | collective-permute-start | bytes 1572872 | tf_op jit(solution)/shard_map/ppermute | solution.py:1585
  104.8 21.7 %collective-permute-start.4 = (bf16[128,2048]{1,0:T(8,128)(2,1)}, bf16[128,2048]{1,0:T(8,128)(2,1)}, u32[]{:S(2)}, u32[]{:S(2)}) collective-permute-start(bf16[128,2048]{1,0:T(8,128)(2,1)} %collective-permute-done.3.refs_2_), channel_id=1, source_target_pairs={{4,8},{8,12},{5,9},{9,13},{6,10},{10,14},{7,11},{11,15},{20,24},{2... | collective-permute-start | bytes 1572872 | tf_op jit(solution)/shard_map/ppermute | solution.py:1585
  160.2 293.2 %all-gather.15.cloned.1.call-start = ((), (), s32[]{:S(2)}) async-start(), calls=%async_computation.7 | async-start | bytes 20971520 | tf_op jit(solution)/shard_map/all_gather | solution.py:1564
  237.2 29.3 %all-to-all-start.1 = ((bf16[16,128,128]{2,1,0:T(8,128)(2,1)}), bf16[16,128,128]{2,1,0:T(8,128)(2,1)S(1)}, u32[]{:S(2)}, u32[]{:S(2)}) async-start(bf16[16,128,128]{2,1,0:T(8,128)(2,1)} %bitcast.31), calls=%async_computation.1 | async-start | bytes 1048576 | tf_op jit(solution)/shard_map/all_to_all | solution.py:1833
  243.8 266.5 %all-gather.17.cloned.1.call-start = ((), (), s32[]{:S(2)}) async-start(), calls=%async_computation.8 | async-start | bytes 20971520 | tf_op jit(solution)/shard_map/all_gather | solution.py:1564
  346.2 425.9 %all-gather.11.cloned.1.call-start = ((), (), s32[]{:S(2)}) async-start(), calls=%async_computation.5 | async-start | bytes 10027008 | tf_op jit(solution)/shard_map/all_gather | solution.py:1568
  408.1 32.8 %collective-permute-start.46 = (bf16[128,2176]{1,0:T(8,128)(2,1)S(1)}, bf16[128,2176]{1,0:T(8,128)(2,1)S(1)}, u32[]{:S(2)}, u32[]{:S(2)}) collective-permute-start(bf16[128,2176]{1,0:T(8,128)(2,1)S(1)} %get-tuple-element.306), channel_id=1, source_target_pairs={{0,2},{2,0},{1,3},{3,1},{4,6},{6,4},{5,7},{7,5},{8,10},{10,8},{9,1... | collective-permute-start | bytes 1671176 | tf_op jit(solution)/shard_map/ppermute | solution.py:1553
  424.9 41.4 %collective-permute-start.45 = (bf16[128,2176]{1,0:T(8,128)(2,1)}, bf16[128,2176]{1,0:T(8,128)(2,1)}, u32[]{:S(2)}, u32[]{:S(2)}) collective-permute-start(bf16[128,2176]{1,0:T(8,128)(2,1)} %get-tuple-element.304), channel_id=1, source_target_pairs={{0,2},{2,0},{1,3},{3,1},{4,6},{6,4},{5,7},{7,5},{8,10},{10,8},{9,1... | collective-permute-start | bytes 1671176 | tf_op jit(solution)/shard_map/ppermute | solution.py:1553
  444.9 23.2 %collective-permute-start.50 = (bf16[128,2176]{1,0:T(8,128)(2,1)}, bf16[128,2176]{1,0:T(8,128)(2,1)S(1)}, u32[]{:S(2)}, u32[]{:S(2)}) collective-permute-start(bf16[128,2176]{1,0:T(8,128)(2,1)} %get-tuple-element.318), channel_id=1, source_target_pairs={{0,4},{4,8},{1,5},{5,9},{2,6},{6,10},{3,7},{7,11},{16,20},{20,24},... | collective-permute-start | bytes 1671176 | tf_op jit(solution)/shard_map/ppermute | solution.py:1585
  451.8 39.5 %collective-permute-start.44 = (bf16[128,2176]{1,0:T(8,128)(2,1)}, bf16[128,2176]{1,0:T(8,128)(2,1)}, u32[]{:S(2)}, u32[]{:S(2)}) collective-permute-start(bf16[128,2176]{1,0:T(8,128)(2,1)} %get-tuple-element.303), channel_id=1, source_target_pairs={{0,2},{2,0},{1,3},{3,1},{4,6},{6,4},{5,7},{7,5},{8,10},{10,8},{9,1... | collective-permute-start | bytes 1671176 | tf_op jit(solution)/shard_map/ppermute | solution.py:1553
  469.6 21.7 %collective-permute-start.52 = (bf16[128,2176]{1,0:T(8,128)(2,1)S(1)}, bf16[128,2176]{1,0:T(8,128)(2,1)S(1)}, u32[]{:S(2)}, u32[]{:S(2)}) collective-permute-start(bf16[128,2176]{1,0:T(8,128)(2,1)S(1)} %get-tuple-element.320), channel_id=1, source_target_pairs={{0,4},{4,8},{8,12},{1,5},{5,9},{9,13},{2,6},{6,10},{10,14},{3,7},{... | collective-permute-start | bytes 1671176 | tf_op jit(solution)/shard_map/ppermute | solution.py:1585
  505.6 34.2 %all-to-all-start.2 = ((bf16[16,128,128]{2,1,0:T(8,128)(2,1)}), bf16[16,128,128]{2,1,0:T(8,128)(2,1)S(1)}, u32[]{:S(2)}, u32[]{:S(2)}) async-start(bf16[16,128,128]{2,1,0:T(8,128)(2,1)} %copy-done.69), calls=%async_computation.2 | async-start | bytes 1048576 | tf_op jit(solution)/shard_map/all_to_all | solution.py:1882
  590.8 26.1 %collective-permute-start.63 = (bf16[128,4096]{1,0:T(8,128)(2,1)S(1)}, bf16[128,4096]{1,0:T(8,128)(2,1)S(1)}, u32[]{:S(2)}, u32[]{:S(2)}) collective-permute-start(bf16[128,4096]{1,0:T(8,128)(2,1)S(1)} %get-tuple-element.360), channel_id=1, source_target_pairs={{0,2},{2,0},{1,3},{3,1},{4,6},{6,4},{5,7},{7,5},{8,10},{10,8},{9,1... | collective-permute-start | bytes 3145736 | tf_op jit(solution)/shard_map/ppermute | solution.py:1553
  593.0 65.3 %collective-permute-start.62 = (bf16[128,4096]{1,0:T(8,128)(2,1)}, bf16[128,4096]{1,0:T(8,128)(2,1)S(1)}, u32[]{:S(2)}, u32[]{:S(2)}) collective-permute-start(bf16[128,4096]{1,0:T(8,128)(2,1)} %get-tuple-element.359), channel_id=1, source_target_pairs={{0,2},{2,0},{1,3},{3,1},{4,6},{6,4},{5,7},{7,5},{8,10},{10,8},{9,1... | collective-permute-start | bytes 3145736 | tf_op jit(solution)/shard_map/ppermute | solution.py:1553
  617.3 46.8 %collective-permute-start.64 = (bf16[128,4096]{1,0:T(8,128)(2,1)S(1)}, bf16[128,4096]{1,0:T(8,128)(2,1)}, u32[]{:S(2)}, u32[]{:S(2)}) collective-permute-start(bf16[128,4096]{1,0:T(8,128)(2,1)S(1)} %get-tuple-element.367.refs_2_.refs_4_), channel_id=1, source_target_pairs={{0,4},{1,5},{2,6},{3,7},{16,20},{17,21},{18,22},{19,23}} | collective-permute-start | bytes 3145736 | tf_op jit(solution)/shard_map/ppermute | solution.py:1585
  618.6 45.5 %collective-permute-start.65 = (bf16[128,4096]{1,0:T(8,128)(2,1)S(1)}, bf16[128,4096]{1,0:T(8,128)(2,1)}, u32[]{:S(2)}, u32[]{:S(2)}) collective-permute-start(bf16[128,4096]{1,0:T(8,128)(2,1)S(1)} %get-tuple-element.367.refs_2_.refs_4_), channel_id=1, source_target_pairs={{12,8},{13,9},{14,10},{15,11},{28,24},{29,25},{30,26},{31,27}} | collective-permute-start | bytes 3145736 | tf_op jit(solution)/shard_map/ppermute | solution.py:1585
  622.6 50.8 %collective-permute-start.70 = (bf16[1024,384]{1,0:T(8,128)(2,1)}, bf16[1024,384]{1,0:T(8,128)(2,1)}, u32[]{:S(2)}, u32[]{:S(2)}) collective-permute-start(bf16[1024,384]{1,0:T(8,128)(2,1)} %dynamic-slice_convert_fusion), channel_id=1, source_target_pairs={{0,16},{16,0},{1,17},{17,1},{2,18},{18,2},{3,19},{19,3},{4,20},{20... | collective-permute-start | bytes 2359304 | tf_op jit(solution)/shard_map/ppermute | solution.py:1553
  641.4 61.2 %collective-permute-start.61 = (bf16[128,4096]{1,0:T(8,128)(2,1)}, bf16[128,4096]{1,0:T(8,128)(2,1)}, u32[]{:S(2)}, u32[]{:S(2)}) collective-permute-start(bf16[128,4096]{1,0:T(8,128)(2,1)} %copy-done.83), channel_id=1, source_target_pairs={{0,2},{2,0},{1,3},{3,1},{4,6},{6,4},{5,7},{7,5},{8,10},{10,8},{9,1... | collective-permute-start | bytes 3145736 | tf_op jit(solution)/shard_map/ppermute | solution.py:1553
  667.8 39.5 %collective-permute-start.66 = (bf16[128,4096]{1,0:T(8,128)(2,1)}, bf16[128,4096]{1,0:T(8,128)(2,1)S(1)}, u32[]{:S(2)}, u32[]{:S(2)}) collective-permute-start(bf16[128,4096]{1,0:T(8,128)(2,1)} %get-tuple-element.371), channel_id=1, source_target_pairs={{0,4},{4,8},{1,5},{5,9},{2,6},{6,10},{3,7},{7,11},{16,20},{20,24},... | collective-permute-start | bytes 3145736 | tf_op jit(solution)/shard_map/ppermute | solution.py:1585
  672.1 38.8 %collective-permute-start.67 = (bf16[128,4096]{1,0:T(8,128)(2,1)}, bf16[128,4096]{1,0:T(8,128)(2,1)}, u32[]{:S(2)}, u32[]{:S(2)}) collective-permute-start(bf16[128,4096]{1,0:T(8,128)(2,1)} %get-tuple-element.372), channel_id=1, source_target_pairs={{12,8},{8,4},{13,9},{9,5},{14,10},{10,6},{15,11},{11,7},{28,24},{2... | collective-permute-start | bytes 3145736 | tf_op jit(solution)/shard_map/ppermute | solution.py:1585
  675.9 105.4 %all-to-all-start.3 = ((bf16[16,80,384]{2,1,0:T(8,128)(2,1)}), bf16[16,80,384]{2,1,0:T(8,128)(2,1)}, u32[]{:S(2)}, u32[]{:S(2)}) async-start(bf16[16,80,384]{2,1,0:T(8,128)(2,1)} %pad_maximum_fusion.3), calls=%async_computation.3 | async-start | bytes 1966080 | tf_op jit(solution)/shard_map/all_to_all | solution.py:1948
  681.3 40.1 %collective-permute-start.60 = (bf16[128,4096]{1,0:T(8,128)(2,1)}, bf16[128,4096]{1,0:T(8,128)(2,1)}, u32[]{:S(2)}, u32[]{:S(2)}) collective-permute-start(bf16[128,4096]{1,0:T(8,128)(2,1)} %copy-done.82), channel_id=1, source_target_pairs={{0,2},{2,0},{1,3},{3,1},{4,6},{6,4},{5,7},{7,5},{8,10},{10,8},{9,1... | collective-permute-start | bytes 3145736 | tf_op jit(solution)/shard_map/ppermute | solution.py:1553
  715.3 24.4 %collective-permute-start.68 = (bf16[128,4096]{1,0:T(8,128)(2,1)}, bf16[128,4096]{1,0:T(8,128)(2,1)S(1)}, u32[]{:S(2)}, u32[]{:S(2)}) collective-permute-start(bf16[128,4096]{1,0:T(8,128)(2,1)} %get-tuple-element.373), channel_id=1, source_target_pairs={{0,4},{4,8},{8,12},{1,5},{5,9},{9,13},{2,6},{6,10},{10,14},{3,7},{... | collective-permute-start | bytes 3145736 | tf_op jit(solution)/shard_map/ppermute | solution.py:1585
  717.2 25.7 %collective-permute-start.69 = (bf16[128,4096]{1,0:T(8,128)(2,1)}, bf16[128,4096]{1,0:T(8,128)(2,1)}, u32[]{:S(2)}, u32[]{:S(2)}) collective-permute-start(bf16[128,4096]{1,0:T(8,128)(2,1)} %get-tuple-element.374), channel_id=1, source_target_pairs={{12,8},{8,4},{4,0},{13,9},{9,5},{5,1},{14,10},{10,6},{6,2},{15,11}... | collective-permute-start | bytes 3145736 | tf_op jit(solution)/shard_map/ppermute | solution.py:1585
  (143 other events, 1299.0 us)
Sparse Core Ops, SparseCore 0:
  10.2 104.0 all-gather.8
  160.3 77.5 all-gather.12
  239.5 104.3 all-gather.14
  346.3 108.3 all-gather.16
  496.4 94.8 all-gather.10

commit v4 on v3

--- a/solution.py
+++ b/solution.py
@@ -789,22 +789,14 @@
         other_ref[at] = first
 
 
-def normed_part_kernel(
-    place_ref, a_ref, b_ref, w_ref, ya_ref, yb_ref, a_slot, b_slot, own_ref, other_ref
-):
-    core = place_ref[4]
-    here, there = own_ref.at[:, :, :, D:], other_ref.at[:, :, :, D:]
-    for at, (g_ref, y_ref, slot_ref) in enumerate(((a_ref, ya_ref, a_slot), (b_ref, yb_ref, b_slot))):
+def normed_part_kernel(place_ref, a_ref, b_ref, w_ref, own_ref, other_ref):
+    for at, g_ref in enumerate((a_ref, b_ref)):
         out = nt(g_ref[...], w_ref[...]).astype(BF16)
-        sort_cores(
-            core, out[:TOK_DEV], out[TOK_DEV:], own_ref.at[:, :, :, :D], other_ref.at[:, :, :, :D], at
-        )
-        first, second = combine_chip(y_ref, slot_ref)
-        sort_cores(core, first, second, here, there, at)
-
-
-def normed_part(place, grads, w_head, y_rows, slots, after=()):
-    blocks = jax.ShapeDtypeStruct((2, 2, TOK_DEV, 2 * D), BF16)
+        sort_cores(place_ref[4], out[:TOK_DEV], out[TOK_DEV:], own_ref, other_ref, at)
+
+
+def normed_part(place, grads, w_head, after=()):
+    blocks = jax.ShapeDtypeStruct((2, 2, TOK_DEV, D), BF16)
     return ordered(
         normed_part_kernel,
         after,
@@ -815,15 +807,14 @@
                 pl.BlockSpec((PAIR, 3 * HD), lambda i, s: (s[2 * i], 0)),
                 pl.BlockSpec((PAIR, 3 * HD), lambda i, s: (s[2 * i + 1], 0)),
                 whole(D, 3 * HD),
-            ]
-            + chip_specs(y_rows, slots),
-            out_specs=[pl.BlockSpec((1, 2, TOK_DEV, 2 * D), lambda i, s: (i, 0, 0, 0))] * 2,
+            ],
+            out_specs=[pl.BlockSpec((1, 2, TOK_DEV, D), lambda i, s: (i, 0, 0, 0))] * 2,
         ),
         out_shape=[blocks, blocks],
-        compiler_params=params(32),
-        cost_estimate=cost(8 * PAIR * D * 3 * HD, 24 * PAIR * D),
+        compiler_params=params(24),
+        cost_estimate=cost(8 * PAIR * D * 3 * HD, 16 * PAIR * D),
         name="normed_part",
-    )(place, grads, grads, w_head, y_rows, y_rows, slots, slots)
+    )(place, grads, grads, w_head)
 
 
 def dw_kernel(normed_ref, grad_ref, out_ref):
@@ -995,6 +986,33 @@
 def combine_chip(row_ref, slot_ref):
     rows = jnp.concatenate([row_ref[j] for j in range(row_ref.shape[0])], 0)
     return [tn(pick_matrix(slot_ref[i]), rows).astype(BF16) for i in range(2)]
+
+
+def combine_kernel(row_ref, slot_ref, out_ref):
+    first, second = combine_chip(row_ref, slot_ref)
+    out_ref[:TOK_DEV] = first
+    out_ref[TOK_DEV:] = second
+
+
+def combine(slot_rows, slots, after=()):
+    blocks, local, _ = slots.shape
+    rows = blocks * TOK_DEV
+    return ordered(
+        combine_kernel,
+        after,
+        dict(
+            grid=(blocks // 2,),
+            in_specs=[
+                pl.BlockSpec((local, SLOTS, D), lambda i: (0, i, 0)),
+                pl.BlockSpec((2, local, TOK_DEV), lambda i: (i, 0, 0)),
+            ],
+            out_specs=pl.BlockSpec((PAIR, D), lambda i: (i, 0)),
+        ),
+        out_shape=jax.ShapeDtypeStruct((rows, D), BF16),
+        compiler_params=params(24),
+        cost_estimate=cost(2 * rows * D * local * SLOTS, 4 * rows * D),
+        name="combine",
+    )(slot_rows, slots)
 
 
 def combine_part_kernel(place_ref, a_ref, b_ref, a_slot, b_slot, own_ref, other_ref):
@@ -1418,26 +1436,18 @@
 
 
 def tokens_grad_kernel(
-    a, b, c, d, e, tok_ref, gain_ref, grad_ref, hidden_ref, before_ref, out_ref, result_ref, sums_ref
+    a, b, c, d, e, tok_ref, gain_ref, grad_ref, out_ref
 ):
-    total = sum(ref[...].astype(F32) for ref in (a, b, c, d, e))
-    grad, branch = total[:, :D], total[:, D:]
+    grad = sum(ref[...].astype(F32) for ref in (a, b, c, d, e))
     inputs = tok_ref[...].astype(F32)
     inverse = inv_rms(inputs)
     scaled = grad * gain_ref[...]
     mean = jnp.mean(scaled * inputs, -1, keepdims=True)
     result = grad_ref[...] + inverse * (scaled - inputs * inverse * inverse * mean)
     out_ref[...] = result.astype(BF16)
-    result_ref[...] = (hidden_ref[...] + branch).astype(BF16)
-    lane = lax.broadcasted_iota(jnp.int32, sums_ref.shape, 1)
-    sums = jnp.where(lane == 1, before_ref[...], 0.0)
-    for place, values in ((0, inputs), (2, branch)):
-        square = jnp.sum(jnp.sum(values * values, -1, keepdims=True), 0, keepdims=True)
-        sums = jnp.where(lane == place, square, sums)
-    sums_ref[...] = sums
-
-
-def final_tokens(terms, tokens, gain_row, grad_hidden, hidden, branch_sums, after=()):
+
+
+def final_tokens(terms, tokens, gain_row, grad_hidden, after=()):
     specs, arrays = term_specs(terms)
     return ordered(
         tokens_grad_kernel,
@@ -1445,18 +1455,14 @@
         dict(
             grid=(1,),
             in_specs=specs
-            + [whole(*BLOCK_SHAPE), whole(1, D), whole(*BLOCK_SHAPE), whole(*BLOCK_SHAPE), whole(1, HD)],
-            out_specs=[whole(*BLOCK_SHAPE), whole(*BLOCK_SHAPE), whole(1, HD)],
-        ),
-        out_shape=[
-            jax.ShapeDtypeStruct(BLOCK_SHAPE, BF16),
-            jax.ShapeDtypeStruct(BLOCK_SHAPE, BF16),
-            jax.ShapeDtypeStruct((1, HD), F32),
-        ],
+            + [whole(*BLOCK_SHAPE), whole(1, D), whole(*BLOCK_SHAPE)],
+            out_specs=whole(*BLOCK_SHAPE),
+        ),
+        out_shape=jax.ShapeDtypeStruct(BLOCK_SHAPE, BF16),
         compiler_params=params(40),
         cost_estimate=cost(30 * TOK_DEV * D, 20 * TOK_DEV * D),
         name="final_tokens",
-    )(*arrays, tokens, gain_row, grad_hidden, hidden, branch_sums)
+    )(*arrays, tokens, gain_row, grad_hidden)
 
 
 def owner_rows_kernel(place_ref, att_ref, mixed_ref, wide_ref, out_ref, moe_ref):
@@ -1614,40 +1620,42 @@
 def gather_steps(block, use, work):
     z = lax.axis_index("z")
     flags = lambda *tests: jnp.stack([jnp.asarray(test, jnp.int32) for test in tests])
+
+    def use_now(arrived, last):
+        for s, r, own, far in arrived:
+            last = use(s, r, own, far, [last])
+        return last
+
     below1 = shift(block, [(0, 1), (1, 2), (2, 3)])
     above1 = shift(block, [(3, 2), (2, 1), (1, 0)])
     across0 = swap(block, "x")
     far00 = swap(block, "core")
     last = work(0, block)
-    column1 = choose(flags(z == 0, z != 0), [above1, below1], [last])
+    column1 = last = choose(flags(z == 0, z != 0), [above1, below1], [last])
     below2 = shift(below1, [(1, 2), (2, 3)])
     above2 = shift(above1, [(2, 1), (1, 0)])
     across1 = swap(column1, "x")
     far01, far10 = swap(across0, "core"), swap(column1, "core")
-    last = use(0, 0, block, far00, [column1])
-    last = use(0, 1, across0, far01, [last])
-    last = use(1, 0, column1, far10, [last])
+    last = use_now([(0, 0, block, far00), (0, 1, across0, far01), (1, 0, column1, far10)], last)
     last = work(1, last)
-    column2 = choose(
+    column2 = last = choose(
         flags(z == 0, z == 3, (z == 1) | (z == 2)), [above2, below2, above1], [last]
     )
     below3 = shift(below2, [(2, 3)])
     above3 = shift(above2, [(1, 0)])
     across2 = swap(column2, "x")
     far11, far20 = swap(across1, "core"), swap(column2, "core")
-    last = use(1, 1, across1, far11, [column2])
-    last = use(2, 0, column2, far20, [last])
+    last = use_now([(1, 1, across1, far11), (2, 0, column2, far20)], last)
     last = work(2, last)
-    column3 = choose(
+    column3 = last = choose(
         flags(z == 0, z == 1, z == 2, z == 3), [above3, above2, below2, below3], [last]
     )
     across3 = swap(column3, "x")
     far21, far30 = swap(across2, "core"), swap(column3, "core")
-    last = use(2, 1, across2, far21, [column3])
-    last = use(3, 0, column3, far30, [last])
+    last = use_now([(2, 1, across2, far21), (3, 0, column3, far30)], last)
     last = work(3, last)
     far31 = swap(across3, "core")
-    return use(3, 1, across3, far31, [last])
+    return use_now([(3, 1, across3, far31)], last)
 
 
 def sum_kernel(*refs):
@@ -1833,9 +1841,13 @@
     attended = lax.all_to_all(att_head.reshape(members, TOK_DEV, HD), EP, 0, 0, tiled=True)
     g_own = plain_dispatch(cot_own, slots_own, [att_head])
     cot_stack = stack_of_core(core, cot_own.reshape(members // 2, 2, TOK_DEV, D), [g_own])
-    slope_own = slopes(g_own, w_down, [cot_stack])
-    hidden, mixed, branch_sums = project_out(attended, output_full, tokens, moe_row, [slope_own])
-    def early_work(_, last):
+    hidden, mixed, branch_sums = project_out(attended, output_full, tokens, moe_row, [cot_stack])
+    early = {}
+
+    def early_work(step, last):
+        if step == 2:
+            early["slope"] = slopes(g_own, w_down, [last])
+            return early["slope"]
         return last
 
     rows = [None]
@@ -1847,6 +1859,7 @@
 
     gather_steps(mixed, use_mixed, early_work)
     x_own, mixed_columns, mixed_stack = rows[0]
+    slope_own = early["slope"]
     sides = jnp.stack([core, group.astype(jnp.int32)])
     cot_near = of_groups(cot_stack)
     mixed_near = of_groups(mixed_stack)
@@ -1865,7 +1878,8 @@
             late["y"] = down(act_a, gate_a, w_down, [last])
             return late["y"]
         if step == 2:
-            late["g"] = stack_dispatch(every, cot_near, slots_other, [last])
+            late["branch"] = combine(late["y"], slots_own, [last])
+            late["g"] = stack_dispatch(every, cot_near, slots_other, [late["branch"]])
             return late["g"]
         if step == 3:
             late["slope"] = slopes(late["g"], w_down, [last])
@@ -1875,6 +1889,8 @@
     terms, last = reduce_steps(
         lambda s, after: combine_part(place_of(s), z_rows, slots_own, after), late_work
     )
+    branch_moe = reduce_rows(late["branch"]).astype(F32)
+    output = (hidden + branch_moe).astype(BF16)
     grad_hidden, wide_branch = token_back(
         terms, mixed, hidden, cotangent, router_wide, moe_row, [last]
     )
@@ -1918,16 +1934,19 @@
         return last
 
     terms, last = reduce_steps(
-        lambda s, after: normed_part(place_of(s), qkv_grads, w_head, late["y"], slots_own, after),
+        lambda s, after: normed_part(place_of(s), qkv_grads, w_head, after),
         last_work,
     )
-    tokens_grad, output, sums = final_tokens(
-        terms, tokens, attn_row, grad_hidden, hidden, branch_sums, [last]
-    )
+    tokens_grad = final_tokens(terms, tokens, attn_row, grad_hidden, [last])
     dw_head = late["dw"]
     last = tokens_grad
     last = expert_grads(groups[1], last)
     gate_grad, up_grad, down_grad = late["grads"]
+    inputs = tokens.astype(F32)
+    sums = jnp.stack(
+        [jnp.sum(inputs * inputs), branch_sums[0, 0], jnp.sum(branch_moe * branch_moe)]
+    )
+    sums = jnp.pad(sums[None, :], ((0, 0), (0, HD - 3)))
     rms_stats = jnp.sqrt(total_over_ep(sums)[:, :3] / (seq * D))
 
     dw_keep = lax.dynamic_slice_in_dim(dw_head, group * (D // 2), D // 2, 0)

time: 822 us -> 795 us (0.967)
  local copies, waits for them, and re-layouts: 125 us -> 106 us
    unnamed x180 -> x184, local copies, waits for them, and re-layouts: 100 us -> 82.1 us
    all_to_all x1, waiting for transfers between devices: 0.01 us -> 13.1 us  [fast_shards(): lax.all_to_all(att_head.reshape(members, TOK_DEV, HD), EP, 0, 0, tiled=True)]
    ppermute x24, waiting for transfers between devices: 66.6 us -> 54 us  [shift(): return lax.ppermute(value, 'z', pairs)]
    ppermute x47, waiting for transfers between devices: 79 us -> 67.4 us  [swap(): return lax.ppermute(value, axis, [(0, 1), (1, 0)])]
    pallas_call x67 -> x68, Pallas kernels: 315 us -> 311 us  [run(): *results, mark = call(*args, *after)]
  transfers between devices with their start and end apart: 86 -> 87, of which waited for: 30 -> 26; matrix products, arithmetic and copies ran while one was open for 6% -> 6% of each run, Pallas kernels for 39% -> 40%
where the time goes in v4:
time: 795 us; the launch traced here: 784 us
  Pallas kernels  311 us (39%)
  waiting for transfers between devices  161 us (20%)
  starting transfers between devices  116 us (15%)
  local copies, waits for them, and re-layouts  106 us (13%)
  blocking collectives  43.8 us (6%)
  other arithmetic  26.5 us (3%)
  between operations  18.3 us (2%)
    pallas_call x68, Pallas kernels, run(): *results, mark = call(*args, *after)  311 us
    unnamed x184, local copies, waits for them, and re-layouts  82.1 us
    ppermute x47, waiting for transfers between devices, swap(): return lax.ppermute(value, axis, [(0, 1), (1, 0)])  67.4 us
    ppermute x24, starting transfers between devices, shift(): return lax.ppermute(value, 'z', pairs)  59.4 us
    ppermute x24, waiting for transfers between devices, shift(): return lax.ppermute(value, 'z', pairs)  54 us
    all_to_all x1, blocking collectives, fast_shards(): mine = lax.all_to_all(columns, EP, 0, 0, tiled=True)  43.8 us
    ppermute x47, starting transfers between devices, swap(): return lax.ppermute(value, axis, [(0, 1), (1, 0)])  30.3 us
  transfers between devices with their start and end apart: 87, of which 26 were waited for; matrix products, arithmetic and copies ran while one was open for 6% of the time, Pallas kernels for 40%

profile of v4, /device:TPU:12, one launch (start us, length us, event | category | flops | bytes accessed | tf_op | source)
XLA Modules:
  0.0 784.3 jit_solution(915052342353647496)
XLA Ops:
  16.8 43.8 %all_to_all.20.refs_4_ = bf16[16,80,384]{2,1,0:T(8,128)(2,1)S(1)} all-to-all(bf16[16,80,384]{2,1,0:T(8,128)(2,1)S(1)} %pad_maximum_fusion.2), channel_id=1, replica_groups=mesh['grp'=2,'z'=4,'x'=2,'core'=2] {'z','x','core'}, dimensions={0} | all-to-all | bytes 1966080 | tf_op jit(solution)/shard_map/all_to_all | solution.py:1790
  71.3 24.4 %collective-permute-done.refs_1_.refs_3_ = bf16[128,2048]{1,0:T(8,128)(2,1)} collective-permute-done((bf16[128,2048]{1,0:T(8,128)(2,1)S(1)}, bf16[128,2048]{1,0:T(8,128)(2,1)}, u32[]{:S(2)}, u32[]{:S(2)}) %collective-permute-start) | collective-permute-done | bytes 524320 | tf_op jit(solution)/shard_map/ppermute | solution.py:1591
  160.0 5.7 fusion.3
  175.8 9.0 %collective-permute-done.14.refs_1_ = bf16[128,2048]{1,0:T(8,128)(2,1)} collective-permute-done((bf16[128,2048]{1,0:T(8,128)(2,1)}, bf16[128,2048]{1,0:T(8,128)(2,1)}, u32[]{:S(2)}, u32[]{:S(2)}) %collective-permute-start.14) | collective-permute-done | bytes 524320 | tf_op jit(solution)/shard_map/ppermute | solution.py:1559
  211.4 10.6 %attend.1 = (bf16[2048,128]{1,0:T(8,128)(2,1)S(1)}, bf16[2048,128]{1,0:T(8,128)(2,1)S(1)}, bf16[2048,128]{1,0:T(8,128)(2,1)S(1)}, f32[2048,128]{1,0:T(8,128)S(1)...) custom-call(f32[2048,384]{1,0:T(8,128)} %get-tuple-element.243.refs_0_.refs_6_.refs_3_, ...), custom_call_target="tpu_custom_call" | custom-call | flops 429496736 | bytes 786432 | tf_op jit(solution)/shard_map/attend/pallas_call | solution.py:571
  228.7 6.4 plain_dispatch.1
  238.7 7.2 all-to-all-start.1
  246.4 13.1 %all-to-all-done.1.refs_0_ = bf16[16,128,128]{2,1,0:T(8,128)(2,1)S(1)} async-done(((bf16[16,128,128]{2,1,0:T(8,128)(2,1)}), bf16[16,128,128]{2,1,0:T(8,128)(2,1)S(1)}, u32[]{:S(2)}, u32[]{:S(2)}) %all-to-all-start.1) | async-done | bytes 524320 | tf_op jit(solution)/shard_map/all_to_all | solution.py:1841
  275.2 9.1 %collective-permute-done.24.refs_1_.refs_3_ = bf16[128,2048]{1,0:T(8,128)(2,1)S(1)} collective-permute-done((bf16[128,2048]{1,0:T(8,128)(2,1)S(1)}, bf16[128,2048]{1,0:T(8,128)(2,1)S(1)}, u32[]{:S(2)}, u32[]{:S(2)}) %collective-permute-start.24) | collective-permute-done | bytes 524320 | tf_op jit(solution)/shard_map/ppermute | solution.py:1591
  316.2 9.2 %slopes.2 = (f32[4,384,1024]{2,1,0:T(8,128)}, f32[8,128]{1,0:T(8,128)S(1)}) custom-call(bf16[4,384,2048]{2,1,0:T(8,128)(2,1)S(1)} %bitcast.112, bf16[4,1024,2048]{2,1,0:T(8,128)(2,1)S(1)} %bitcast.106, f32[8,128]{1,0:T(8,128)S(1)} %get-tuple-element.274.refs_2_), custom_call_target="tpu_custom_call" | custom-call | flops 644245120 | bytes 1677721 | tf_op jit(solution)/shard_map/slopes/pallas_call | solution.py:571
  327.5 12.5 %collective-permute-done.37.refs_1_ = bf16[128,2048]{1,0:T(8,128)(2,1)S(1)} collective-permute-done((bf16[128,2048]{1,0:T(8,128)(2,1)S(1)}, bf16[128,2048]{1,0:T(8,128)(2,1)S(1)}, u32[]{:S(2)}, u32[]{:S(2)}) %collective-permute-start.37) | collective-permute-done | bytes 524320 | tf_op jit(solution)/shard_map/ppermute | solution.py:1559
  348.7 41.0 %experts_full.1 = (bf16[4,384,1024]{2,1,0:T(8,128)(2,1)}, bf16[4,384,1024]{2,1,0:T(8,128)(2,1)}, bf16[4,384,1024]{2,1,0:T(8,128)(2,1)}, f32[4,384,128]{2,1,0:T(8...) custom-call(s32[1]{0:T(128)} %bitcast.37.refs_0_, bf16[4,384,2048]{2,1,0:T(8,128)(2,1)} %get-tuple-element.289.refs_1_, ...), custom_call_target="tpu_custom_call" | custom-call | flops 2576980480 | bytes 5872025 | tf_op jit(solution)/shard_map/experts_full/pallas_call | solution.py:571
  411.6 10.8 %collective-permute-done.43.refs_2_ = bf16[128,2176]{1,0:T(8,128)(2,1)S(1)} collective-permute-done((bf16[128,2176]{1,0:T(8,128)(2,1)S(1)}, bf16[128,2176]{1,0:T(8,128)(2,1)S(1)}, u32[]{:S(2)}, u32[]{:S(2)}) %collective-permute-start.43) | collective-permute-done | bytes 557088 | tf_op jit(solution)/shard_map/ppermute | solution.py:1559
  425.6 5.9 copy-done.2
  431.6 9.4 %down.1 = (bf16[4,384,2048]{2,1,0:T(8,128)(2,1)S(1)}, f32[8,128]{1,0:T(8,128)S(1)}) custom-call(bf16[4,384,1024]{2,1,0:T(8,128)(2,1)S(1)} %copy-done.31, f32[4,384,128]{2,1,0:T(8,128)S(1)} %copy-done.39, bf16[4,1024,2048]{2,1,0:T(8,128)(2,1)S(1)} %copy-done.2, f32[8,128]{1,0:T(8,128)S(1)} %get-tuple-element.305.refs_3_), custom_call_target="tpu_custom_call" | custom-call | flops 644245120 | bytes 1677721 | tf_op jit(solution)/shard_map/down/pallas_call | solution.py:571
  458.9 6.1 copy-done.6
  465.0 7.0 stack_dispatch.2
  483.3 5.8 copy-done.3
  489.1 9.1 %slopes.3 = (f32[4,384,1024]{2,1,0:T(8,128)}, f32[8,128]{1,0:T(8,128)S(1)}) custom-call(bf16[4,384,2048]{2,1,0:T(8,128)(2,1)S(1)} %copy-done.8, bf16[4,1024,2048]{2,1,0:T(8,128)(2,1)S(1)} %copy-done.3, f32[8,128]{1,0:T(8,128)S(1)} %get-tuple-element.327.refs_2_), custom_call_target="tpu_custom_call" | custom-call | flops 644245120 | bytes 1677721 | tf_op jit(solution)/shard_map/slopes/pallas_call | solution.py:571
  498.2 10.6 %collective-permute-done.53.refs_4_ = bf16[128,2176]{1,0:T(8,128)(2,1)S(1)} collective-permute-done((bf16[128,2176]{1,0:T(8,128)(2,1)S(1)}, bf16[128,2176]{1,0:T(8,128)(2,1)S(1)}, u32[]{:S(2)}, u32[]{:S(2)}) %collective-permute-start.53) | collective-permute-done | bytes 557088 | tf_op jit(solution)/shard_map/ppermute | solution.py:1591
  526.6 5.9 copy-done.7
  532.5 7.0 stack_dispatch.3
  540.0 16.3 %experts_half.2 = (bf16[2,384,1024]{2,1,0:T(8,128)(2,1)}, bf16[2,384,1024]{2,1,0:T(8,128)(2,1)}, bf16[2,384,1024]{2,1,0:T(8,128)(2,1)}, f32[2,384,128]{2,1,0:T(8,128)}, f32[8,128]{1,0:T(8,128)}) custom-call(s32[1]{0:T(128)} %bitcast.37.refs_0_, bf16[4,384,2048]{2,1,0:T(8,128)(2,1)} %get-tuple-element.335.refs_1_.refs_2_, ...), custom_call_target="tpu_custom_call" | custom-call | flops 644245120 | bytes 2936012 | tf_op jit(solution)/shard_map/experts_half/pallas_call | solution.py:571
  560.2 10.2 %attend_back.1 = (f32[2048,128]{1,0:T(8,128)S(1)}, f32[2048,128]{1,0:T(8,128)S(1)}, bf16[2048,128]{1,0:T(8,128)(2,1)S(1)}, f32[2,2048]{1,0:T(2,128)S(1)}, f32[2,128]{1,0:T(2,128)S(1)}, /*index=5*/f32[8,128]{1,0:T(8,128)}) custom-call(bf16[2048,128]{1,0:T(8,128)(2,1)S(1)} %copy-done.61, bf16[2048,128]{1,0:T(8,128)(2,1)S(1)} %copy-done.63, ...), custom_call_target="tpu_custom_call" | custom-call | flops 1073741824 | bytes 1572864 | tf_op jit(solution)/shard_map/attend_back/pallas_call | solution.py:571
  612.4 5.7 dw_product.1
  624.4 16.8 %collective-permute-done.71 = f32[2,128]{1,0:T(2,128)S(1)} collective-permute-done((f32[2,128]{1,0:T(2,128)S(1)}, f32[2,128]{1,0:T(2,128)S(1)}, u32[]{:S(2)}, u32[]{:S(2)}) %collective-permute-start.71) | collective-permute-done | bytes 1056 | tf_op jit(solution)/shard_map/ppermute | solution.py:1559
  642.5 16.2 %experts_half.3 = (bf16[2,384,1024]{2,1,0:T(8,128)(2,1)}, bf16[2,384,1024]{2,1,0:T(8,128)(2,1)}, bf16[2,384,1024]{2,1,0:T(8,128)(2,1)}, f32[2,384,128]{2,1,0:T(8,128)}, f32[8,128]{1,0:T(8,128)}) custom-call(s32[1]{0:T(128)} %bitcast.37.refs_0_, bf16[4,384,2048]{2,1,0:T(8,128)(2,1)} %get-tuple-element.335.refs_1_.refs_2_, ...), custom_call_target="tpu_custom_call" | custom-call | flops 644245120 | bytes 2936012 | tf_op jit(solution)/shard_map/experts_half/pallas_call | solution.py:571
  668.4 19.9 %weight_grads.2 = (f32[4,1024,1024]{2,1,0:T(8,128)}, f32[4,1024,1024]{2,1,0:T(8,128)}, f32[4,512,2048]{2,1,0:T(8,128)}, f32[8,128]{1,0:T(8,128)}) custom-call(s32[1]{0:T(128)} %bitcast.28.refs_0_, bf16[4,384,2048]{2,1,0:T(8,128)(2,1)} %get-tuple-element.289.refs_1_, bf16[4,384,2048]{2,1,0:T(8,128)(2,1)} %get-tuple-element.335.refs_1_.refs_2_, ...), custom_call_target="tpu_custom_call" | custom-call | flops 966367616 | bytes 3774873 | tf_op jit(solution)/shard_map/weight_grads/pallas_call | solution.py:571
  699.8 6.2 all-to-all-start.3
  710.6 6.8 collective-permute-done.69.refs_4_
  722.4 18.4 %weight_grads.3 = (f32[4,1024,1024]{2,1,0:T(8,128)}, f32[4,1024,1024]{2,1,0:T(8,128)}, f32[4,512,2048]{2,1,0:T(8,128)}, f32[8,128]{1,0:T(8,128)}) custom-call(s32[1]{0:T(128)} %bitcast.28.refs_0_, bf16[4,384,2048]{2,1,0:T(8,128)(2,1)} %get-tuple-element.289.refs_1_, ...), custom_call_target="tpu_custom_call", output_to_operand_aliasing={{0}: (13, {}), {1}: (14, {}), {2}: (15, {})} | custom-call | flops 966367616 | bytes 3774873 | tf_op jit(solution)/shard_map/weight_grads/pallas_call | solution.py:571
  768.9 6.1 collective-permute-done.73
  (509 shorter events, 374.0 us)
Async XLA Ops:
  7.2 218.1 %all-gather.9.cloned.1.call-start = ((), (), s32[]{:S(2)}) async-start(), calls=%async_computation.5 | async-start | bytes 8912896 | tf_op jit(solution)/shard_map/all_gather | solution.py:1574
  7.9 252.4 %all-gather.13.cloned.1.call-start = ((), (), s32[]{:S(2)}) async-start(), calls=%async_computation.8 | async-start | bytes 8912896 | tf_op jit(solution)/shard_map/all_gather | solution.py:1574
  60.6 49.8 %collective-permute-start.7 = (bf16[16,80,384]{2,1,0:T(8,128)(2,1)S(1)}, bf16[16,80,384]{2,1,0:T(8,128)(2,1)S(1)}, u32[]{:S(2)}, u32[]{:S(2)}) collective-permute-start(bf16[16,80,384]{2,1,0:T(8,128)(2,1)S(1)} %all_to_all.20.refs_4_), channel_id=1, source_target_pairs={{0,16},{16,0},{1,17},{17,1},{2,18},{18,2},{3,19},{19,3},{4,20},{20... | collective-permute-start | bytes 2949128 | tf_op jit(solution)/shard_map/ppermute | solution.py:1559
  61.2 34.5 %collective-permute-start = (bf16[128,2048]{1,0:T(8,128)(2,1)S(1)}, bf16[128,2048]{1,0:T(8,128)(2,1)}, u32[]{:S(2)}, u32[]{:S(2)}) collective-permute-start(bf16[128,2048]{1,0:T(8,128)(2,1)S(1)} %copy-done.33), channel_id=1, source_target_pairs={{12,8},{8,4},{4,0},{13,9},{9,5},{5,1},{14,10},{10,6},{6,2},{15,11}... | collective-permute-start | bytes 1572872 | tf_op jit(solution)/shard_map/ppermute | solution.py:1591
  63.3 32.4 %collective-permute-start.3 = (bf16[128,2048]{1,0:T(8,128)(2,1)S(1)}, bf16[128,2048]{1,0:T(8,128)(2,1)}, u32[]{:S(2)}, u32[]{:S(2)}) collective-permute-start(bf16[128,2048]{1,0:T(8,128)(2,1)S(1)} %copy-done.33), channel_id=1, source_target_pairs={{0,4},{4,8},{8,12},{1,5},{5,9},{9,13},{2,6},{6,10},{10,14},{3,7},{... | collective-permute-start | bytes 1572872 | tf_op jit(solution)/shard_map/ppermute | solution.py:1591
  67.0 35.1 %collective-permute-start.8 = (bf16[128,2048]{1,0:T(8,128)(2,1)S(1)}, bf16[128,2048]{1,0:T(8,128)(2,1)}, u32[]{:S(2)}, u32[]{:S(2)}) collective-permute-start(bf16[128,2048]{1,0:T(8,128)(2,1)S(1)} %copy-done.33), channel_id=1, source_target_pairs={{0,2},{2,0},{1,3},{3,1},{4,6},{6,4},{5,7},{7,5},{8,10},{10,8},{9,1... | collective-permute-start | bytes 1572872 | tf_op jit(solution)/shard_map/ppermute | solution.py:1559
  68.3 35.7 %collective-permute-start.10 = (bf16[128,2048]{1,0:T(8,128)(2,1)S(1)}, bf16[128,2048]{1,0:T(8,128)(2,1)S(1)}, u32[]{:S(2)}, u32[]{:S(2)}) collective-permute-start(bf16[128,2048]{1,0:T(8,128)(2,1)S(1)} %copy-done.33), channel_id=1, source_target_pairs={{0,1},{1,0},{2,3},{3,2},{4,5},{5,4},{6,7},{7,6},{8,9},{9,8},{10,11... | collective-permute-start | bytes 1572872 | tf_op jit(solution)/shard_map/ppermute | solution.py:1559
  98.3 24.2 %collective-permute-start.6 = (bf16[128,2048]{1,0:T(8,128)(2,1)}, bf16[128,2048]{1,0:T(8,128)(2,1)}, u32[]{:S(2)}, u32[]{:S(2)}) collective-permute-start(bf16[128,2048]{1,0:T(8,128)(2,1)} %get-tuple-element.208.refs_1_), channel_id=1, source_target_pairs={{0,1},{1,0},{2,3},{3,2},{4,5},{5,4},{6,7},{7,6},{8,9},{9,8},{10,11... | collective-permute-start | bytes 1572872 | tf_op jit(solution)/shard_map/ppermute | solution.py:1559
  102.1 23.8 %collective-permute-start.1 = (bf16[128,2048]{1,0:T(8,128)(2,1)}, bf16[128,2048]{1,0:T(8,128)(2,1)}, u32[]{:S(2)}, u32[]{:S(2)}) collective-permute-start(bf16[128,2048]{1,0:T(8,128)(2,1)} %collective-permute-done.refs_1_.refs_3_), channel_id=1, source_target_pairs={{8,4},{4,0},{9,5},{5,1},{10,6},{6,2},{11,7},{7,3},{24,20},{20,16},... | collective-permute-start | bytes 1572872 | tf_op jit(solution)/shard_map/ppermute | solution.py:1591
  104.8 21.1 %collective-permute-start.4 = (bf16[128,2048]{1,0:T(8,128)(2,1)}, bf16[128,2048]{1,0:T(8,128)(2,1)}, u32[]{:S(2)}, u32[]{:S(2)}) collective-permute-start(bf16[128,2048]{1,0:T(8,128)(2,1)} %collective-permute-done.3.refs_2_), channel_id=1, source_target_pairs={{4,8},{8,12},{5,9},{9,13},{6,10},{10,14},{7,11},{11,15},{20,24},{2... | collective-permute-start | bytes 1572872 | tf_op jit(solution)/shard_map/ppermute | solution.py:1591
  159.8 299.1 %all-gather.15.cloned.1.call-start = ((), (), s32[]{:S(2)}) async-start(), calls=%async_computation.9 | async-start | bytes 20971520 | tf_op jit(solution)/shard_map/all_gather | solution.py:1570
  238.7 20.8 %all-to-all-start.1 = ((bf16[16,128,128]{2,1,0:T(8,128)(2,1)}), bf16[16,128,128]{2,1,0:T(8,128)(2,1)S(1)}, u32[]{:S(2)}, u32[]{:S(2)}) async-start(bf16[16,128,128]{2,1,0:T(8,128)(2,1)} %bitcast.29), calls=%async_computation.1 | async-start | bytes 1048576 | tf_op jit(solution)/shard_map/all_to_all | solution.py:1841
  245.9 280.7 %all-gather.17.cloned.1.call-start = ((), (), s32[]{:S(2)}) async-start(), calls=%async_computation.10 | async-start | bytes 20971520 | tf_op jit(solution)/shard_map/all_gather | solution.py:1570
  346.8 359.2 %reduce-scatter.2.cloned.1.call-start = ((), (), s32[]{:S(2)}) async-start(), calls=%async_computation.6 | async-start | bytes 8912896 | tf_op jit(solution)/shard_map/reduce_scatter | solution.py:1578
  409.1 32.0 %collective-permute-start.45 = (bf16[128,2176]{1,0:T(8,128)(2,1)S(1)}, bf16[128,2176]{1,0:T(8,128)(2,1)S(1)}, u32[]{:S(2)}, u32[]{:S(2)}) collective-permute-start(bf16[128,2176]{1,0:T(8,128)(2,1)S(1)} %get-tuple-element.307), channel_id=1, source_target_pairs={{0,2},{2,0},{1,3},{3,1},{4,6},{6,4},{5,7},{7,5},{8,10},{10,8},{9,1... | collective-permute-start | bytes 1671176 | tf_op jit(solution)/shard_map/ppermute | solution.py:1559
  450.7 290.1 %all-gather.11.cloned.1.call-start = ((), (), s32[]{:S(2)}) async-start(), calls=%async_computation.7 | async-start | bytes 10027008 | tf_op jit(solution)/shard_map/all_gather | solution.py:1574
  450.8 21.2 %collective-permute-start.49 = (bf16[128,2176]{1,0:T(8,128)(2,1)}, bf16[128,2176]{1,0:T(8,128)(2,1)}, u32[]{:S(2)}, u32[]{:S(2)}) collective-permute-start(bf16[128,2176]{1,0:T(8,128)(2,1)} %copy-done.80), channel_id=1, source_target_pairs={{0,2},{2,0},{1,3},{3,1},{4,6},{6,4},{5,7},{7,5},{8,10},{10,8},{9,1... | collective-permute-start | bytes 1671176 | tf_op jit(solution)/shard_map/ppermute | solution.py:1559
  451.8 22.0 %collective-permute-start.50 = (bf16[128,2176]{1,0:T(8,128)(2,1)}, bf16[128,2176]{1,0:T(8,128)(2,1)}, u32[]{:S(2)}, u32[]{:S(2)}) collective-permute-start(bf16[128,2176]{1,0:T(8,128)(2,1)} %copy-done.82), channel_id=1, source_target_pairs={{0,4},{4,8},{1,5},{5,9},{2,6},{6,10},{3,7},{7,11},{16,20},{20,24},... | collective-permute-start | bytes 1671176 | tf_op jit(solution)/shard_map/ppermute | solution.py:1591
  458.1 40.1 %collective-permute-start.48 = (bf16[128,2176]{1,0:T(8,128)(2,1)}, bf16[128,2176]{1,0:T(8,128)(2,1)}, u32[]{:S(2)}, u32[]{:S(2)}) collective-permute-start(bf16[128,2176]{1,0:T(8,128)(2,1)} %copy-done.79), channel_id=1, source_target_pairs={{0,2},{2,0},{1,3},{3,1},{4,6},{6,4},{5,7},{7,5},{8,10},{10,8},{9,1... | collective-permute-start | bytes 1671176 | tf_op jit(solution)/shard_map/ppermute | solution.py:1559
  476.6 21.6 %collective-permute-start.52 = (bf16[128,2176]{1,0:T(8,128)(2,1)S(1)}, bf16[128,2176]{1,0:T(8,128)(2,1)S(1)}, u32[]{:S(2)}, u32[]{:S(2)}) collective-permute-start(bf16[128,2176]{1,0:T(8,128)(2,1)S(1)} %get-tuple-element.324), channel_id=1, source_target_pairs={{0,4},{4,8},{8,12},{1,5},{5,9},{9,13},{2,6},{6,10},{10,14},{3,7},{... | collective-permute-start | bytes 1671176 | tf_op jit(solution)/shard_map/ppermute | solution.py:1591
  481.4 27.4 %collective-permute-start.53 = (bf16[128,2176]{1,0:T(8,128)(2,1)S(1)}, bf16[128,2176]{1,0:T(8,128)(2,1)S(1)}, u32[]{:S(2)}, u32[]{:S(2)}) collective-permute-start(bf16[128,2176]{1,0:T(8,128)(2,1)S(1)} %get-tuple-element.325), channel_id=1, source_target_pairs={{12,8},{8,4},{4,0},{13,9},{9,5},{5,1},{14,10},{10,6},{6,2},{15,11}... | collective-permute-start | bytes 1671176 | tf_op jit(solution)/shard_map/ppermute | solution.py:1591
  523.0 33.3 %all-to-all-start.2 = ((bf16[16,128,128]{2,1,0:T(8,128)(2,1)}), bf16[16,128,128]{2,1,0:T(8,128)(2,1)S(1)}, u32[]{:S(2)}, u32[]{:S(2)}) async-start(bf16[16,128,128]{2,1,0:T(8,128)(2,1)} %get-tuple-element.330), calls=%async_computation.3 | async-start | bytes 1048576 | tf_op jit(solution)/shard_map/all_to_all | solution.py:1898
  604.2 54.5 %collective-permute-start.62 = (bf16[128,2048]{1,0:T(8,128)(2,1)}, bf16[128,2048]{1,0:T(8,128)(2,1)}, u32[]{:S(2)}, u32[]{:S(2)}) collective-permute-start(bf16[128,2048]{1,0:T(8,128)(2,1)} %get-tuple-element.361), channel_id=1, source_target_pairs={{0,2},{2,0},{1,3},{3,1},{4,6},{6,4},{5,7},{7,5},{8,10},{10,8},{9,1... | collective-permute-start | bytes 1572872 | tf_op jit(solution)/shard_map/ppermute | solution.py:1559
  618.3 42.8 %collective-permute-start.64 = (bf16[128,2048]{1,0:T(8,128)(2,1)S(1)}, bf16[128,2048]{1,0:T(8,128)(2,1)S(1)}, u32[]{:S(2)}, u32[]{:S(2)}) collective-permute-start(bf16[128,2048]{1,0:T(8,128)(2,1)S(1)} %get-tuple-element.369.refs_2_.refs_4_), channel_id=1, source_target_pairs={{0,4},{1,5},{2,6},{3,7},{16,20},{17,21},{18,22},{19,23}} | collective-permute-start | bytes 1572872 | tf_op jit(solution)/shard_map/ppermute | solution.py:1591
  619.8 41.4 %collective-permute-start.65 = (bf16[128,2048]{1,0:T(8,128)(2,1)S(1)}, bf16[128,2048]{1,0:T(8,128)(2,1)S(1)}, u32[]{:S(2)}, u32[]{:S(2)}) collective-permute-start(bf16[128,2048]{1,0:T(8,128)(2,1)S(1)} %get-tuple-element.369.refs_2_.refs_4_), channel_id=1, source_target_pairs={{12,8},{13,9},{14,10},{15,11},{28,24},{29,25},{30,26},{31,27}} | collective-permute-start | bytes 1572872 | tf_op jit(solution)/shard_map/ppermute | solution.py:1591
  621.4 45.6 %collective-permute-start.70 = (bf16[1024,384]{1,0:T(8,128)(2,1)}, bf16[1024,384]{1,0:T(8,128)(2,1)}, u32[]{:S(2)}, u32[]{:S(2)}) collective-permute-start(bf16[1024,384]{1,0:T(8,128)(2,1)} %dynamic-slice_convert_fusion), channel_id=1, source_target_pairs={{0,16},{16,0},{1,17},{17,1},{2,18},{18,2},{3,19},{19,3},{4,20},{20... | collective-permute-start | bytes 2359304 | tf_op jit(solution)/shard_map/ppermute | solution.py:1559
  641.2 47.1 %collective-permute-start.61 = (bf16[128,2048]{1,0:T(8,128)(2,1)}, bf16[128,2048]{1,0:T(8,128)(2,1)}, u32[]{:S(2)}, u32[]{:S(2)}) collective-permute-start(bf16[128,2048]{1,0:T(8,128)(2,1)} %get-tuple-element.354), channel_id=1, source_target_pairs={{0,2},{2,0},{1,3},{3,1},{4,6},{6,4},{5,7},{7,5},{8,10},{10,8},{9,1... | collective-permute-start | bytes 1572872 | tf_op jit(solution)/shard_map/ppermute | solution.py:1559
  661.4 29.4 %collective-permute-start.66 = (bf16[128,2048]{1,0:T(8,128)(2,1)S(1)}, bf16[128,2048]{1,0:T(8,128)(2,1)S(1)}, u32[]{:S(2)}, u32[]{:S(2)}) collective-permute-start(bf16[128,2048]{1,0:T(8,128)(2,1)S(1)} %get-tuple-element.373), channel_id=1, source_target_pairs={{0,4},{4,8},{1,5},{5,9},{2,6},{6,10},{3,7},{7,11},{16,20},{20,24},... | collective-permute-start | bytes 1572872 | tf_op jit(solution)/shard_map/ppermute | solution.py:1591
  665.0 25.8 %collective-permute-start.67 = (bf16[128,2048]{1,0:T(8,128)(2,1)S(1)}, bf16[128,2048]{1,0:T(8,128)(2,1)S(1)}, u32[]{:S(2)}, u32[]{:S(2)}) collective-permute-start(bf16[128,2048]{1,0:T(8,128)(2,1)S(1)} %get-tuple-element.374), channel_id=1, source_target_pairs={{12,8},{8,4},{13,9},{9,5},{14,10},{10,6},{15,11},{11,7},{28,24},{2... | collective-permute-start | bytes 1572872 | tf_op jit(solution)/shard_map/ppermute | solution.py:1591
  666.3 44.3 %collective-permute-start.60 = (bf16[128,2048]{1,0:T(8,128)(2,1)}, bf16[128,2048]{1,0:T(8,128)(2,1)S(1)}, u32[]{:S(2)}, u32[]{:S(2)}) collective-permute-start(bf16[128,2048]{1,0:T(8,128)(2,1)} %get-tuple-element.353), channel_id=1, source_target_pairs={{0,2},{2,0},{1,3},{3,1},{4,6},{6,4},{5,7},{7,5},{8,10},{10,8},{9,1... | collective-permute-start | bytes 1572872 | tf_op jit(solution)/shard_map/ppermute | solution.py:1559
  699.8 64.1 %all-to-all-start.3 = ((bf16[16,80,384]{2,1,0:T(8,128)(2,1)}), bf16[16,80,384]{2,1,0:T(8,128)(2,1)}, u32[]{:S(2)}, u32[]{:S(2)}) async-start(bf16[16,80,384]{2,1,0:T(8,128)(2,1)} %pad_maximum_fusion.3), calls=%async_computation.4 | async-start | bytes 1966080 | tf_op jit(solution)/shard_map/all_to_all | solution.py:1967
  710.4 39.2 %collective-permute-start.74 = (f32[1,128]{1,0:T(1,128)S(1)}, f32[1,128]{1,0:T(1,128)S(1)}, u32[]{:S(2)}, u32[]{:S(2)}) collective-permute-start(f32[1,128]{1,0:T(1,128)S(1)} %pad.10), channel_id=1, source_target_pairs={{0,1},{1,0},{2,3},{3,2},{4,5},{5,4},{6,7},{7,6},{8,9},{9,8},{10,11... | collective-permute-start | bytes 1544 | tf_op jit(solution)/shard_map/ppermute | solution.py:1559
  (146 other events, 1642.4 us)
Sparse Core Ops, SparseCore 0:
  10.2 104.0 all-gather.8
  159.9 78.2 all-gather.12
  239.7 106.0 all-gather.14
  347.3 105.9 all-gather.16
  457.2 112.7 reduce-scatter.1
  572.1 103.4 all-gather.10

commit v5 on v4

--- a/solution.py
+++ b/solution.py
@@ -1511,11 +1511,12 @@
 
 
 def unpack_kernel(in_ref, wq_ref, wk_ref, wv_ref, gain_ref, q_ref, k_ref, v_ref, sums_ref):
-    heads = in_ref.shape[0]
+    heads = in_ref.shape[0] // 2
     total = jnp.zeros((q_ref.shape[0], 1), F32)
     for part, (w_ref, out_ref) in enumerate(((wq_ref, q_ref), (wk_ref, k_ref), (wv_ref, v_ref))):
         for h in range(heads):
-            piece = in_ref[h, : q_ref.shape[0], part * HD : (part + 1) * HD].astype(F32)
+            spot = (slice(0, q_ref.shape[0]), slice(part * HD, (part + 1) * HD))
+            piece = in_ref[(h,) + spot].astype(F32) + in_ref[(heads + h,) + spot].astype(F32)
             lanes = slice(h * HD, (h + 1) * HD)
             out_ref[:, lanes] = piece
             total += jnp.sum(w_ref[:, lanes].astype(F32) * piece, -1, keepdims=True)
@@ -1924,13 +1925,11 @@
         return late["grads"][0]
 
     def last_work(step, last):
-        if step == 0:
+        if step == 1:
+            return expert_other(groups[1], last)
+        if step == 3:
             late["dw"] = dw_product(normed_all, qkv_grads, [last])
             return late["dw"]
-        if step == 1:
-            return expert_other(groups[1], last)
-        if step == 2:
-            return expert_grads(groups[0], last)
         return last
 
     terms, last = reduce_steps(
@@ -1940,34 +1939,34 @@
     tokens_grad = final_tokens(terms, tokens, attn_row, grad_hidden, [last])
     dw_head = late["dw"]
     last = tokens_grad
-    last = expert_grads(groups[1], last)
+    last = expert_grads(groups[0], last)
+    out_part = owner_rows(place, att_head, mixed_columns, branch_all, [last])
+    last = expert_grads(groups[1], out_part)
     gate_grad, up_grad, down_grad = late["grads"]
     inputs = tokens.astype(F32)
     sums = jnp.stack(
         [jnp.sum(inputs * inputs), branch_sums[0, 0], jnp.sum(branch_moe * branch_moe)]
     )
-    sums = jnp.pad(sums[None, :], ((0, 0), (0, HD - 3)))
-    rms_stats = jnp.sqrt(total_over_ep(sums)[:, :3] / (seq * D))
-
-    dw_keep = lax.dynamic_slice_in_dim(dw_head, group * (D // 2), D // 2, 0)
-    dw_send = lax.dynamic_slice_in_dim(dw_head, (1 - group) * (D // 2), D // 2, 0)
-    dw_half = (dw_keep + swap(dw_send.astype(BF16), "grp").astype(F32)).astype(BF16)
-    gain_parts = gain_parts + swap(gain_parts, "grp")
-    extra = gain_parts.reshape(1, 2 * HD)
+
+    extra = jnp.concatenate([gain_parts.reshape(1, 2 * HD), sums[None, :]], 1)
     high = extra.astype(BF16)
     low = (extra - high.astype(F32)).astype(BF16)
-    extra = jnp.pad(jnp.concatenate([high, low], 0), ((0, 14), (0, HD)))
+    extra = jnp.pad(jnp.concatenate([high, low], 0), ((0, 14), (0, HD - 3)))
+    everyone = 2 * members
     payload = jnp.concatenate(
         [
-            dw_half.reshape(members, wide, 3 * HD),
-            jnp.broadcast_to(extra, (members,) + extra.shape),
+            dw_head.astype(BF16).reshape(everyone, wide, 3 * HD),
+            jnp.broadcast_to(extra, (everyone,) + extra.shape),
         ],
         1,
     )
-    arrived = lax.all_to_all(payload, EP, 0, 0, tiled=True)
+    arrived = lax.all_to_all(payload, ALL, 0, 0, tiled=True)
     *dense, attn_sums = unpack(arrived, (w_query, w_key, w_value), attn_gain, [last])
     attn_gain_grad = attn_sums[:, 0]
     extras = arrived[:, wide].astype(F32) + arrived[:, wide + 1].astype(F32)
+    seq_sums = lax.dynamic_slice(extras, (group * members, 2 * HD), (members, 3))
+    rms_stats = jnp.sqrt(jnp.sum(seq_sums, 0, keepdims=True) / (seq * D))
+    extras = extras[:members] + extras[members:]
     flat = group * members + place
     head_row = lax.dynamic_slice(
         extras[:, : 2 * HD].reshape(HEADS, 2, HD // wide, wide),
@@ -1975,7 +1974,6 @@
         (1, 2, 1, wide),
     ).reshape(2, wide)
 
-    out_part = owner_rows(place, att_head, mixed_columns, branch_all, [last])
     out_part = out_part.reshape(2, wide, D + HD)
     out_keep = lax.dynamic_index_in_dim(out_part, group, 0, False)
     out_send = lax.dynamic_index_in_dim(out_part, 1 - group, 0, False).astype(BF16)

time: 795 us -> 837 us (1.053)
  waiting for transfers between devices: 161 us -> 204 us
    ppermute x24, waiting for transfers between devices: 54 us -> 91.2 us  [shift(): return lax.ppermute(value, 'z', pairs)]
    ppermute x47 -> x43, waiting for transfers between devices: 67.4 us -> 87.4 us  [swap(): return lax.ppermute(value, axis, [(0, 1), (1, 0)])]
    unnamed x184 -> x182, local copies, waits for them, and re-layouts: 82.1 us -> 84.1 us
    ppermute x47 -> x43, starting transfers between devices: 30.3 us -> 30 us  [swap(): return lax.ppermute(value, axis, [(0, 1), (1, 0)])]
  transfers between devices with their start and end apart: 87 -> 81, of which waited for: 26 -> 30; matrix products, arithmetic and copies ran while one was open for 6% -> 6% of each run, Pallas kernels for 40% -> 37%
where the time goes in v5:
time: 837 us; the launch traced here: 824 us
  Pallas kernels  308 us (37%)
  waiting for transfers between devices  204 us (24%)
  starting transfers between devices  116 us (14%)
  local copies, waits for them, and re-layouts  107 us (13%)
  blocking collectives  43.8 us (5%)
  other arithmetic  25.7 us (3%)
  between operations  18.3 us (2%)
    pallas_call x68, Pallas kernels, run(): *results, mark = call(*args, *after)  308 us
    ppermute x24, waiting for transfers between devices, shift(): return lax.ppermute(value, 'z', pairs)  91.2 us
    ppermute x43, waiting for transfers between devices, swap(): return lax.ppermute(value, axis, [(0, 1), (1, 0)])  87.4 us
    unnamed x182, local copies, waits for them, and re-layouts  84.1 us
    ppermute x24, starting transfers between devices, shift(): return lax.ppermute(value, 'z', pairs)  60.6 us
    all_to_all x1, blocking collectives, fast_shards(): mine = lax.all_to_all(columns, EP, 0, 0, tiled=True)  43.8 us
    ppermute x43, starting transfers between devices, swap(): return lax.ppermute(value, axis, [(0, 1), (1, 0)])  30 us
  transfers between devices with their start and end apart: 81, of which 30 were waited for; matrix products, arithmetic and copies ran while one was open for 6% of the time, Pallas kernels for 37%

profile of v5, /device:TPU:12, one launch (start us, length us, event | category | flops | bytes accessed | tf_op | source)
XLA Modules:
  0.0 823.9 jit_solution(3002235355117193483)
XLA Ops:
  16.8 43.8 %all_to_all.20.refs_4_ = bf16[16,80,384]{2,1,0:T(8,128)(2,1)S(1)} all-to-all(bf16[16,80,384]{2,1,0:T(8,128)(2,1)S(1)} %pad_maximum_fusion.3), channel_id=1, replica_groups=mesh['grp'=2,'z'=4,'x'=2,'core'=2] {'z','x','core'}, dimensions={0} | all-to-all | bytes 1966080 | tf_op jit(solution)/shard_map/all_to_all | solution.py:1791
  71.3 24.4 %collective-permute-done.refs_1_.refs_3_ = bf16[128,2048]{1,0:T(8,128)(2,1)} collective-permute-done((bf16[128,2048]{1,0:T(8,128)(2,1)S(1)}, bf16[128,2048]{1,0:T(8,128)(2,1)}, u32[]{:S(2)}, u32[]{:S(2)}) %collective-permute-start) | collective-permute-done | bytes 524320 | tf_op jit(solution)/shard_map/ppermute | solution.py:1592
  159.9 5.7 fusion.3
  175.7 9.1 %collective-permute-done.14.refs_1_ = bf16[128,2048]{1,0:T(8,128)(2,1)} collective-permute-done((bf16[128,2048]{1,0:T(8,128)(2,1)}, bf16[128,2048]{1,0:T(8,128)(2,1)}, u32[]{:S(2)}, u32[]{:S(2)}) %collective-permute-start.14) | collective-permute-done | bytes 524320 | tf_op jit(solution)/shard_map/ppermute | solution.py:1560
  211.5 10.5 %attend.1 = (bf16[2048,128]{1,0:T(8,128)(2,1)S(1)}, bf16[2048,128]{1,0:T(8,128)(2,1)S(1)}, bf16[2048,128]{1,0:T(8,128)(2,1)S(1)}, f32[2048,128]{1,0:T(8,128)S(1)...) custom-call(f32[2048,384]{1,0:T(8,128)} %get-tuple-element.244.refs_0_.refs_6_.refs_3_, ...), custom_call_target="tpu_custom_call" | custom-call | flops 429496736 | bytes 786432 | tf_op jit(solution)/shard_map/attend/pallas_call | solution.py:571
  228.9 6.4 plain_dispatch.1
  238.9 7.2 all-to-all-start.1
  246.6 13.1 %all-to-all-done.1.refs_0_ = bf16[16,128,128]{2,1,0:T(8,128)(2,1)S(1)} async-done(((bf16[16,128,128]{2,1,0:T(8,128)(2,1)}), bf16[16,128,128]{2,1,0:T(8,128)(2,1)S(1)}, u32[]{:S(2)}, u32[]{:S(2)}) %all-to-all-start.1) | async-done | bytes 524320 | tf_op jit(solution)/shard_map/all_to_all | solution.py:1842
  275.4 9.1 %collective-permute-done.24.refs_1_.refs_3_ = bf16[128,2048]{1,0:T(8,128)(2,1)S(1)} collective-permute-done((bf16[128,2048]{1,0:T(8,128)(2,1)S(1)}, bf16[128,2048]{1,0:T(8,128)(2,1)S(1)}, u32[]{:S(2)}, u32[]{:S(2)}) %collective-permute-start.24) | collective-permute-done | bytes 524320 | tf_op jit(solution)/shard_map/ppermute | solution.py:1592
  316.5 9.2 %slopes.2 = (f32[4,384,1024]{2,1,0:T(8,128)}, f32[8,128]{1,0:T(8,128)S(1)}) custom-call(bf16[4,384,2048]{2,1,0:T(8,128)(2,1)S(1)} %bitcast.114, bf16[4,1024,2048]{2,1,0:T(8,128)(2,1)S(1)} %bitcast.108, f32[8,128]{1,0:T(8,128)S(1)} %get-tuple-element.275.refs_2_), custom_call_target="tpu_custom_call" | custom-call | flops 644245120 | bytes 1677721 | tf_op jit(solution)/shard_map/slopes/pallas_call | solution.py:571
  327.7 12.5 %collective-permute-done.37.refs_1_ = bf16[128,2048]{1,0:T(8,128)(2,1)S(1)} collective-permute-done((bf16[128,2048]{1,0:T(8,128)(2,1)S(1)}, bf16[128,2048]{1,0:T(8,128)(2,1)S(1)}, u32[]{:S(2)}, u32[]{:S(2)}) %collective-permute-start.37) | collective-permute-done | bytes 524320 | tf_op jit(solution)/shard_map/ppermute | solution.py:1560
  349.1 41.0 %experts_full.1 = (bf16[4,384,1024]{2,1,0:T(8,128)(2,1)}, bf16[4,384,1024]{2,1,0:T(8,128)(2,1)}, bf16[4,384,1024]{2,1,0:T(8,128)(2,1)}, f32[4,384,128]{2,1,0:T(8...) custom-call(s32[1]{0:T(128)} %bitcast.37.refs_0_, bf16[4,384,2048]{2,1,0:T(8,128)(2,1)} %get-tuple-element.290.refs_1_, ...), custom_call_target="tpu_custom_call" | custom-call | flops 2576980480 | bytes 5872025 | tf_op jit(solution)/shard_map/experts_full/pallas_call | solution.py:571
  411.8 10.8 %collective-permute-done.43.refs_2_ = bf16[128,2176]{1,0:T(8,128)(2,1)S(1)} collective-permute-done((bf16[128,2176]{1,0:T(8,128)(2,1)S(1)}, bf16[128,2176]{1,0:T(8,128)(2,1)S(1)}, u32[]{:S(2)}, u32[]{:S(2)}) %collective-permute-start.43) | collective-permute-done | bytes 557088 | tf_op jit(solution)/shard_map/ppermute | solution.py:1560
  426.0 5.9 copy-done.2
  431.9 9.4 %down.1 = (bf16[4,384,2048]{2,1,0:T(8,128)(2,1)S(1)}, f32[8,128]{1,0:T(8,128)S(1)}) custom-call(bf16[4,384,1024]{2,1,0:T(8,128)(2,1)S(1)} %copy-done.26, f32[4,384,128]{2,1,0:T(8,128)S(1)} %copy-done.35, bf16[4,1024,2048]{2,1,0:T(8,128)(2,1)S(1)} %copy-done.2, f32[8,128]{1,0:T(8,128)S(1)} %get-tuple-element.306.refs_3_), custom_call_target="tpu_custom_call" | custom-call | flops 644245120 | bytes 1677721 | tf_op jit(solution)/shard_map/down/pallas_call | solution.py:571
  459.3 6.1 copy-done.6
  465.4 7.0 stack_dispatch.2
  483.7 5.8 copy-done.3
  489.4 9.1 %slopes.3 = (f32[4,384,1024]{2,1,0:T(8,128)}, f32[8,128]{1,0:T(8,128)S(1)}) custom-call(bf16[4,384,2048]{2,1,0:T(8,128)(2,1)S(1)} %copy-done.8, bf16[4,1024,2048]{2,1,0:T(8,128)(2,1)S(1)} %copy-done.3, f32[8,128]{1,0:T(8,128)S(1)} %get-tuple-element.328.refs_2_), custom_call_target="tpu_custom_call" | custom-call | flops 644245120 | bytes 1677721 | tf_op jit(solution)/shard_map/slopes/pallas_call | solution.py:571
  498.5 8.2 collective-permute-done.53.refs_4_
  524.5 6.0 copy-done.7
  530.5 7.0 stack_dispatch.3
  538.1 16.1 %experts_half.2 = (bf16[2,384,1024]{2,1,0:T(8,128)(2,1)}, bf16[2,384,1024]{2,1,0:T(8,128)(2,1)}, bf16[2,384,1024]{2,1,0:T(8,128)(2,1)}, f32[2,384,128]{2,1,0:T(8,128)}, f32[8,128]{1,0:T(8,128)}) custom-call(s32[1]{0:T(128)} %bitcast.37.refs_0_, bf16[4,384,2048]{2,1,0:T(8,128)(2,1)} %get-tuple-element.336.refs_1_.refs_2_, ...), custom_call_target="tpu_custom_call" | custom-call | flops 644245120 | bytes 2936012 | tf_op jit(solution)/shard_map/experts_half/pallas_call | solution.py:571
  558.1 10.1 %attend_back.1 = (f32[2048,128]{1,0:T(8,128)S(1)}, f32[2048,128]{1,0:T(8,128)S(1)}, bf16[2048,128]{1,0:T(8,128)(2,1)S(1)}, f32[2,2048]{1,0:T(2,128)S(1)}, f32[2,128]{1,0:T(2,128)S(1)}, /*index=5*/f32[8,128]{1,0:T(8,128)}) custom-call(bf16[2048,128]{1,0:T(8,128)(2,1)S(1)} %copy-done.56, bf16[2048,128]{1,0:T(8,128)(2,1)S(1)} %copy-done.58, ...), custom_call_target="tpu_custom_call" | custom-call | flops 1073741824 | bytes 1572864 | tf_op jit(solution)/shard_map/attend_back/pallas_call | solution.py:571
  598.0 9.7 %collective-permute-done.63.refs_2_ = bf16[128,2048]{1,0:T(8,128)(2,1)S(1)} collective-permute-done((bf16[128,2048]{1,0:T(8,128)(2,1)S(1)}, bf16[128,2048]{1,0:T(8,128)(2,1)S(1)}, u32[]{:S(2)}, u32[]{:S(2)}) %collective-permute-start.63) | collective-permute-done | bytes 524320 | tf_op jit(solution)/shard_map/ppermute | solution.py:1560
  613.8 16.0 %experts_half.3 = (bf16[2,384,1024]{2,1,0:T(8,128)(2,1)}, bf16[2,384,1024]{2,1,0:T(8,128)(2,1)}, bf16[2,384,1024]{2,1,0:T(8,128)(2,1)}, f32[2,384,128]{2,1,0:T(8,128)}, f32[8,128]{1,0:T(8,128)}) custom-call(s32[1]{0:T(128)} %bitcast.37.refs_0_, bf16[4,384,2048]{2,1,0:T(8,128)(2,1)} %get-tuple-element.336.refs_1_.refs_2_, ...), custom_call_target="tpu_custom_call" | custom-call | flops 644245120 | bytes 2936012 | tf_op jit(solution)/shard_map/experts_half/pallas_call | solution.py:571
  657.9 12.9 %collective-permute-done.67.refs_6_ = bf16[128,2048]{1,0:T(8,128)(2,1)} collective-permute-done((bf16[128,2048]{1,0:T(8,128)(2,1)}, bf16[128,2048]{1,0:T(8,128)(2,1)}, u32[]{:S(2)}, u32[]{:S(2)}) %collective-permute-start.67) | collective-permute-done | bytes 524320 | tf_op jit(solution)/shard_map/ppermute | solution.py:1592
  697.2 22.6 %collective-permute-done.60.refs_2_ = bf16[128,2048]{1,0:T(8,128)(2,1)S(1)} collective-permute-done((bf16[128,2048]{1,0:T(8,128)(2,1)}, bf16[128,2048]{1,0:T(8,128)(2,1)S(1)}, u32[]{:S(2)}, u32[]{:S(2)}) %collective-permute-start.60) | collective-permute-done | bytes 524320 | tf_op jit(solution)/shard_map/ppermute | solution.py:1560
  719.7 23.4 %collective-permute-done.68.refs_3_ = bf16[128,2048]{1,0:T(8,128)(2,1)} collective-permute-done((bf16[128,2048]{1,0:T(8,128)(2,1)}, bf16[128,2048]{1,0:T(8,128)(2,1)}, u32[]{:S(2)}, u32[]{:S(2)}) %collective-permute-start.68) | collective-permute-done | bytes 524320 | tf_op jit(solution)/shard_map/ppermute | solution.py:1592
  751.5 19.9 %weight_grads.2 = (f32[4,1024,1024]{2,1,0:T(8,128)}, f32[4,1024,1024]{2,1,0:T(8,128)}, f32[4,512,2048]{2,1,0:T(8,128)}, f32[8,128]{1,0:T(8,128)}) custom-call(s32[1]{0:T(128)} %bitcast.28.refs_0_, bf16[4,384,2048]{2,1,0:T(8,128)(2,1)} %get-tuple-element.290.refs_1_, bf16[4,384,2048]{2,1,0:T(8,128)(2,1)} %get-tuple-element.336.refs_1_.refs_2_, ...), custom_call_target="tpu_custom_call" | custom-call | flops 966367616 | bytes 3774873 | tf_op jit(solution)/shard_map/weight_grads/pallas_call | solution.py:571
  782.6 6.9 collective-permute-done.70
  792.1 18.3 %weight_grads.3 = (f32[4,1024,1024]{2,1,0:T(8,128)}, f32[4,1024,1024]{2,1,0:T(8,128)}, f32[4,512,2048]{2,1,0:T(8,128)}, f32[8,128]{1,0:T(8,128)}) custom-call(s32[1]{0:T(128)} %bitcast.28.refs_0_, bf16[4,384,2048]{2,1,0:T(8,128)(2,1)} %get-tuple-element.290.refs_1_, ...), custom_call_target="tpu_custom_call", output_to_operand_aliasing={{0}: (13, {}), {1}: (14, {}), {2}: (15, {})} | custom-call | flops 966367616 | bytes 3774873 | tf_op jit(solution)/shard_map/weight_grads/pallas_call | solution.py:571
  (490 shorter events, 382.3 us)
Async XLA Ops:
  7.2 218.3 %all-gather.9.cloned.1.call-start = ((), (), s32[]{:S(2)}) async-start(), calls=%async_computation.5 | async-start | bytes 8912896 | tf_op jit(solution)/shard_map/all_gather | solution.py:1575
  7.9 252.6 %all-gather.13.cloned.1.call-start = ((), (), s32[]{:S(2)}) async-start(), calls=%async_computation.8 | async-start | bytes 8912896 | tf_op jit(solution)/shard_map/all_gather | solution.py:1575
  60.6 49.7 %collective-permute-start.7 = (bf16[16,80,384]{2,1,0:T(8,128)(2,1)S(1)}, bf16[16,80,384]{2,1,0:T(8,128)(2,1)S(1)}, u32[]{:S(2)}, u32[]{:S(2)}) collective-permute-start(bf16[16,80,384]{2,1,0:T(8,128)(2,1)S(1)} %all_to_all.20.refs_4_), channel_id=1, source_target_pairs={{0,16},{16,0},{1,17},{17,1},{2,18},{18,2},{3,19},{19,3},{4,20},{20... | collective-permute-start | bytes 2949128 | tf_op jit(solution)/shard_map/ppermute | solution.py:1560
  61.2 34.5 %collective-permute-start = (bf16[128,2048]{1,0:T(8,128)(2,1)S(1)}, bf16[128,2048]{1,0:T(8,128)(2,1)}, u32[]{:S(2)}, u32[]{:S(2)}) collective-permute-start(bf16[128,2048]{1,0:T(8,128)(2,1)S(1)} %copy-done.28), channel_id=1, source_target_pairs={{12,8},{8,4},{4,0},{13,9},{9,5},{5,1},{14,10},{10,6},{6,2},{15,11}... | collective-permute-start | bytes 1572872 | tf_op jit(solution)/shard_map/ppermute | solution.py:1592
  63.3 32.4 %collective-permute-start.3 = (bf16[128,2048]{1,0:T(8,128)(2,1)S(1)}, bf16[128,2048]{1,0:T(8,128)(2,1)}, u32[]{:S(2)}, u32[]{:S(2)}) collective-permute-start(bf16[128,2048]{1,0:T(8,128)(2,1)S(1)} %copy-done.28), channel_id=1, source_target_pairs={{0,4},{4,8},{8,12},{1,5},{5,9},{9,13},{2,6},{6,10},{10,14},{3,7},{... | collective-permute-start | bytes 1572872 | tf_op jit(solution)/shard_map/ppermute | solution.py:1592
  67.0 35.1 %collective-permute-start.8 = (bf16[128,2048]{1,0:T(8,128)(2,1)S(1)}, bf16[128,2048]{1,0:T(8,128)(2,1)}, u32[]{:S(2)}, u32[]{:S(2)}) collective-permute-start(bf16[128,2048]{1,0:T(8,128)(2,1)S(1)} %copy-done.28), channel_id=1, source_target_pairs={{0,2},{2,0},{1,3},{3,1},{4,6},{6,4},{5,7},{7,5},{8,10},{10,8},{9,1... | collective-permute-start | bytes 1572872 | tf_op jit(solution)/shard_map/ppermute | solution.py:1560
  68.3 35.7 %collective-permute-start.10 = (bf16[128,2048]{1,0:T(8,128)(2,1)S(1)}, bf16[128,2048]{1,0:T(8,128)(2,1)S(1)}, u32[]{:S(2)}, u32[]{:S(2)}) collective-permute-start(bf16[128,2048]{1,0:T(8,128)(2,1)S(1)} %copy-done.28), channel_id=1, source_target_pairs={{0,1},{1,0},{2,3},{3,2},{4,5},{5,4},{6,7},{7,6},{8,9},{9,8},{10,11... | collective-permute-start | bytes 1572872 | tf_op jit(solution)/shard_map/ppermute | solution.py:1560
  98.3 24.2 %collective-permute-start.6 = (bf16[128,2048]{1,0:T(8,128)(2,1)}, bf16[128,2048]{1,0:T(8,128)(2,1)}, u32[]{:S(2)}, u32[]{:S(2)}) collective-permute-start(bf16[128,2048]{1,0:T(8,128)(2,1)} %get-tuple-element.209.refs_1_), channel_id=1, source_target_pairs={{0,1},{1,0},{2,3},{3,2},{4,5},{5,4},{6,7},{7,6},{8,9},{9,8},{10,11... | collective-permute-start | bytes 1572872 | tf_op jit(solution)/shard_map/ppermute | solution.py:1560
  102.1 23.8 %collective-permute-start.1 = (bf16[128,2048]{1,0:T(8,128)(2,1)}, bf16[128,2048]{1,0:T(8,128)(2,1)}, u32[]{:S(2)}, u32[]{:S(2)}) collective-permute-start(bf16[128,2048]{1,0:T(8,128)(2,1)} %collective-permute-done.refs_1_.refs_3_), channel_id=1, source_target_pairs={{8,4},{4,0},{9,5},{5,1},{10,6},{6,2},{11,7},{7,3},{24,20},{20,16},... | collective-permute-start | bytes 1572872 | tf_op jit(solution)/shard_map/ppermute | solution.py:1592
  104.8 21.1 %collective-permute-start.4 = (bf16[128,2048]{1,0:T(8,128)(2,1)}, bf16[128,2048]{1,0:T(8,128)(2,1)}, u32[]{:S(2)}, u32[]{:S(2)}) collective-permute-start(bf16[128,2048]{1,0:T(8,128)(2,1)} %collective-permute-done.3.refs_2_), channel_id=1, source_target_pairs={{4,8},{8,12},{5,9},{9,13},{6,10},{10,14},{7,11},{11,15},{20,24},{2... | collective-permute-start | bytes 1572872 | tf_op jit(solution)/shard_map/ppermute | solution.py:1592
  159.8 299.6 %all-gather.15.cloned.1.call-start = ((), (), s32[]{:S(2)}) async-start(), calls=%async_computation.9 | async-start | bytes 20971520 | tf_op jit(solution)/shard_map/all_gather | solution.py:1571
  238.9 20.8 %all-to-all-start.1 = ((bf16[16,128,128]{2,1,0:T(8,128)(2,1)}), bf16[16,128,128]{2,1,0:T(8,128)(2,1)S(1)}, u32[]{:S(2)}, u32[]{:S(2)}) async-start(bf16[16,128,128]{2,1,0:T(8,128)(2,1)} %bitcast.29), calls=%async_computation.1 | async-start | bytes 1048576 | tf_op jit(solution)/shard_map/all_to_all | solution.py:1842
  246.1 278.4 %all-gather.17.cloned.1.call-start = ((), (), s32[]{:S(2)}) async-start(), calls=%async_computation.10 | async-start | bytes 20971520 | tf_op jit(solution)/shard_map/all_gather | solution.py:1571
  347.1 297.6 %reduce-scatter.2.cloned.1.call-start = ((), (), s32[]{:S(2)}) async-start(), calls=%async_computation.6 | async-start | bytes 8912896 | tf_op jit(solution)/shard_map/reduce_scatter | solution.py:1579
  409.4 31.9 %collective-permute-start.45 = (bf16[128,2176]{1,0:T(8,128)(2,1)S(1)}, bf16[128,2176]{1,0:T(8,128)(2,1)S(1)}, u32[]{:S(2)}, u32[]{:S(2)}) collective-permute-start(bf16[128,2176]{1,0:T(8,128)(2,1)S(1)} %get-tuple-element.308), channel_id=1, source_target_pairs={{0,2},{2,0},{1,3},{3,1},{4,6},{6,4},{5,7},{7,5},{8,10},{10,8},{9,1... | collective-permute-start | bytes 1671176 | tf_op jit(solution)/shard_map/ppermute | solution.py:1560
  451.1 321.5 %all-gather.11.cloned.1.call-start = ((), (), s32[]{:S(2)}) async-start(), calls=%async_computation.7 | async-start | bytes 10027008 | tf_op jit(solution)/shard_map/all_gather | solution.py:1575
  451.2 21.3 %collective-permute-start.49 = (bf16[128,2176]{1,0:T(8,128)(2,1)}, bf16[128,2176]{1,0:T(8,128)(2,1)}, u32[]{:S(2)}, u32[]{:S(2)}) collective-permute-start(bf16[128,2176]{1,0:T(8,128)(2,1)} %copy-done.76), channel_id=1, source_target_pairs={{0,2},{2,0},{1,3},{3,1},{4,6},{6,4},{5,7},{7,5},{8,10},{10,8},{9,1... | collective-permute-start | bytes 1671176 | tf_op jit(solution)/shard_map/ppermute | solution.py:1560
  452.3 22.0 %collective-permute-start.50 = (bf16[128,2176]{1,0:T(8,128)(2,1)}, bf16[128,2176]{1,0:T(8,128)(2,1)}, u32[]{:S(2)}, u32[]{:S(2)}) collective-permute-start(bf16[128,2176]{1,0:T(8,128)(2,1)} %copy-done.78), channel_id=1, source_target_pairs={{0,4},{4,8},{1,5},{5,9},{2,6},{6,10},{3,7},{7,11},{16,20},{20,24},... | collective-permute-start | bytes 1671176 | tf_op jit(solution)/shard_map/ppermute | solution.py:1592
  458.4 40.1 %collective-permute-start.48 = (bf16[128,2176]{1,0:T(8,128)(2,1)}, bf16[128,2176]{1,0:T(8,128)(2,1)}, u32[]{:S(2)}, u32[]{:S(2)}) collective-permute-start(bf16[128,2176]{1,0:T(8,128)(2,1)} %copy-done.75), channel_id=1, source_target_pairs={{0,2},{2,0},{1,3},{3,1},{4,6},{6,4},{5,7},{7,5},{8,10},{10,8},{9,1... | collective-permute-start | bytes 1671176 | tf_op jit(solution)/shard_map/ppermute | solution.py:1560
  477.1 21.4 %collective-permute-start.52 = (bf16[128,2176]{1,0:T(8,128)(2,1)S(1)}, bf16[128,2176]{1,0:T(8,128)(2,1)S(1)}, u32[]{:S(2)}, u32[]{:S(2)}) collective-permute-start(bf16[128,2176]{1,0:T(8,128)(2,1)S(1)} %get-tuple-element.325), channel_id=1, source_target_pairs={{0,4},{4,8},{8,12},{1,5},{5,9},{9,13},{2,6},{6,10},{10,14},{3,7},{... | collective-permute-start | bytes 1671176 | tf_op jit(solution)/shard_map/ppermute | solution.py:1592
  481.7 25.0 %collective-permute-start.53 = (bf16[128,2176]{1,0:T(8,128)(2,1)S(1)}, bf16[128,2176]{1,0:T(8,128)(2,1)S(1)}, u32[]{:S(2)}, u32[]{:S(2)}) collective-permute-start(bf16[128,2176]{1,0:T(8,128)(2,1)S(1)} %get-tuple-element.326), channel_id=1, source_target_pairs={{12,8},{8,4},{4,0},{13,9},{9,5},{5,1},{14,10},{10,6},{6,2},{15,11}... | collective-permute-start | bytes 1671176 | tf_op jit(solution)/shard_map/ppermute | solution.py:1592
  521.0 33.2 %all-to-all-start.2 = ((bf16[16,128,128]{2,1,0:T(8,128)(2,1)}), bf16[16,128,128]{2,1,0:T(8,128)(2,1)S(1)}, u32[]{:S(2)}, u32[]{:S(2)}) async-start(bf16[16,128,128]{2,1,0:T(8,128)(2,1)} %get-tuple-element.331), calls=%async_computation.3 | async-start | bytes 1048576 | tf_op jit(solution)/shard_map/all_to_all | solution.py:1899
  595.3 34.5 %collective-permute-start.62 = (bf16[128,2048]{1,0:T(8,128)(2,1)}, bf16[128,2048]{1,0:T(8,128)(2,1)S(1)}, u32[]{:S(2)}, u32[]{:S(2)}) collective-permute-start(bf16[128,2048]{1,0:T(8,128)(2,1)} %get-tuple-element.356), channel_id=1, source_target_pairs={{0,2},{2,0},{1,3},{3,1},{4,6},{6,4},{5,7},{7,5},{8,10},{10,8},{9,1... | collective-permute-start | bytes 1572872 | tf_op jit(solution)/shard_map/ppermute | solution.py:1560
  608.7 27.3 %collective-permute-start.64 = (bf16[128,2048]{1,0:T(8,128)(2,1)}, bf16[128,2048]{1,0:T(8,128)(2,1)}, u32[]{:S(2)}, u32[]{:S(2)}) collective-permute-start(bf16[128,2048]{1,0:T(8,128)(2,1)} %get-tuple-element.362.refs_2_.refs_4_), channel_id=1, source_target_pairs={{0,4},{1,5},{2,6},{3,7},{16,20},{17,21},{18,22},{19,23}} | collective-permute-start | bytes 1572872 | tf_op jit(solution)/shard_map/ppermute | solution.py:1592
  610.0 26.0 %collective-permute-start.65 = (bf16[128,2048]{1,0:T(8,128)(2,1)}, bf16[128,2048]{1,0:T(8,128)(2,1)}, u32[]{:S(2)}, u32[]{:S(2)}) collective-permute-start(bf16[128,2048]{1,0:T(8,128)(2,1)} %get-tuple-element.362.refs_2_.refs_4_), channel_id=1, source_target_pairs={{12,8},{13,9},{14,10},{15,11},{28,24},{29,25},{30,26},{31,27}} | collective-permute-start | bytes 1572872 | tf_op jit(solution)/shard_map/ppermute | solution.py:1592
  612.4 37.2 %collective-permute-start.61 = (bf16[128,2048]{1,0:T(8,128)(2,1)}, bf16[128,2048]{1,0:T(8,128)(2,1)}, u32[]{:S(2)}, u32[]{:S(2)}) collective-permute-start(bf16[128,2048]{1,0:T(8,128)(2,1)} %get-tuple-element.355), channel_id=1, source_target_pairs={{0,2},{2,0},{1,3},{3,1},{4,6},{6,4},{5,7},{7,5},{8,10},{10,8},{9,1... | collective-permute-start | bytes 1572872 | tf_op jit(solution)/shard_map/ppermute | solution.py:1560
  643.4 27.4 %collective-permute-start.67 = (bf16[128,2048]{1,0:T(8,128)(2,1)}, bf16[128,2048]{1,0:T(8,128)(2,1)}, u32[]{:S(2)}, u32[]{:S(2)}) collective-permute-start(bf16[128,2048]{1,0:T(8,128)(2,1)} %get-tuple-element.366), channel_id=1, source_target_pairs={{12,8},{8,4},{13,9},{9,5},{14,10},{10,6},{15,11},{11,7},{28,24},{2... | collective-permute-start | bytes 1572872 | tf_op jit(solution)/shard_map/ppermute | solution.py:1592
  684.0 87.4 %all-to-all-start.3 = ((bf16[32,80,384]{2,1,0:T(8,128)(2,1)}), bf16[32,80,384]{2,1,0:T(8,128)(2,1)}, u32[]{:S(2)}, u32[]{:S(2)}) async-start(bf16[32,80,384]{2,1,0:T(8,128)(2,1)} %pad_maximum_fusion), calls=%async_computation.4 | async-start | bytes 3932160 | tf_op jit(solution)/shard_map/all_to_all | solution.py:1963
  688.9 30.9 %collective-permute-start.60 = (bf16[128,2048]{1,0:T(8,128)(2,1)}, bf16[128,2048]{1,0:T(8,128)(2,1)S(1)}, u32[]{:S(2)}, u32[]{:S(2)}) collective-permute-start(bf16[128,2048]{1,0:T(8,128)(2,1)} %copy-done.79), channel_id=1, source_target_pairs={{0,2},{2,0},{1,3},{3,1},{4,6},{6,4},{5,7},{7,5},{8,10},{10,8},{9,1... | collective-permute-start | bytes 1572872 | tf_op jit(solution)/shard_map/ppermute | solution.py:1560
  690.4 52.7 %collective-permute-start.68 = (bf16[128,2048]{1,0:T(8,128)(2,1)}, bf16[128,2048]{1,0:T(8,128)(2,1)}, u32[]{:S(2)}, u32[]{:S(2)}) collective-permute-start(bf16[128,2048]{1,0:T(8,128)(2,1)} %copy-done.81), channel_id=1, source_target_pairs={{0,4},{4,8},{8,12},{1,5},{5,9},{9,13},{2,6},{6,10},{10,14},{3,7},{... | collective-permute-start | bytes 1572872 | tf_op jit(solution)/shard_map/ppermute | solution.py:1592
  693.8 51.2 %collective-permute-start.69 = (bf16[128,2048]{1,0:T(8,128)(2,1)}, bf16[128,2048]{1,0:T(8,128)(2,1)}, u32[]{:S(2)}, u32[]{:S(2)}) collective-permute-start(bf16[128,2048]{1,0:T(8,128)(2,1)} %copy-done.80), channel_id=1, source_target_pairs={{12,8},{8,4},{4,0},{13,9},{9,5},{5,1},{14,10},{10,6},{6,2},{15,11}... | collective-permute-start | bytes 1572872 | tf_op jit(solution)/shard_map/ppermute | solution.py:1592
  789.6 25.1 %collective-permute-start.71 = (bf16[64,2176]{1,0:T(8,128)(2,1)S(1)}, bf16[64,2176]{1,0:T(8,128)(2,1)S(1)}, u32[]{:S(2)}, u32[]{:S(2)}) collective-permute-start(bf16[64,2176]{1,0:T(8,128)(2,1)S(1)} %fusion.2), channel_id=1, source_target_pairs={{0,0},{1,2},{2,4},{3,6},{4,8},{5,10},{6,12},{7,14},{8,16},{9,18},{... | collective-permute-start | bytes 835592 | tf_op jit(solution)/shard_map/ppermute | solution.py:1982
  (139 other events, 1683.8 us)
Sparse Core Ops, SparseCore 0:
  10.2 104.0 all-gather.8
  159.9 78.2 all-gather.12
  239.8 106.2 all-gather.14
  347.5 105.9 all-gather.16
  458.0 112.2 reduce-scatter.1
  572.4 99.6 all-gather.10

commit v6 on v4

--- a/solution.py
+++ b/solution.py
@@ -1940,7 +1940,8 @@
     tokens_grad = final_tokens(terms, tokens, attn_row, grad_hidden, [last])
     dw_head = late["dw"]
     last = tokens_grad
-    last = expert_grads(groups[1], last)
+    out_part = owner_rows(place, att_head, mixed_columns, branch_all, [last])
+    last = expert_grads(groups[1], out_part)
     gate_grad, up_grad, down_grad = late["grads"]
     inputs = tokens.astype(F32)
     sums = jnp.stack(
@@ -1975,7 +1976,6 @@
         (1, 2, 1, wide),
     ).reshape(2, wide)
 
-    out_part = owner_rows(place, att_head, mixed_columns, branch_all, [last])
     out_part = out_part.reshape(2, wide, D + HD)
     out_keep = lax.dynamic_index_in_dim(out_part, group, 0, False)
     out_send = lax.dynamic_index_in_dim(out_part, 1 - group, 0, False).astype(BF16)

time: 795 us -> 811 us (1.020)
  starting transfers between devices: 116 us -> 127 us
  waiting for transfers between devices: 161 us -> 152 us
    ppermute x24, waiting for transfers between devices: 54 us -> 43.7 us  [shift(): return lax.ppermute(value, 'z', pairs)]
    ppermute x47, waiting for transfers between devices: 67.4 us -> 77.4 us  [swap(): return lax.ppermute(value, axis, [(0, 1), (1, 0)])]
    unnamed x184 -> x190, local copies, waits for them, and re-layouts: 82.1 us -> 86.8 us
  transfers between devices with their start and end apart: 87 -> 87, of which waited for: 26 -> 28; matrix products, arithmetic and copies ran while one was open for 6% -> 6% of each run, Pallas kernels for 40% -> 40%
where the time goes in v6:
time: 811 us; the launch traced here: 796 us
  Pallas kernels  317 us (39%)
  waiting for transfers between devices  152 us (19%)
  starting transfers between devices  127 us (16%)
  local copies, waits for them, and re-layouts  111 us (14%)
  blocking collectives  43.8 us (5%)
  other arithmetic  26.1 us (3%)
  between operations  18.2 us (2%)
    pallas_call x68, Pallas kernels, run(): *results, mark = call(*args, *after)  317 us
    unnamed x190, local copies, waits for them, and re-layouts  86.8 us
    ppermute x47, waiting for transfers between devices, swap(): return lax.ppermute(value, axis, [(0, 1), (1, 0)])  77.4 us
    ppermute x24, starting transfers between devices, shift(): return lax.ppermute(value, 'z', pairs)  58.2 us
    all_to_all x1, blocking collectives, fast_shards(): mine = lax.all_to_all(columns, EP, 0, 0, tiled=True)  43.8 us
    ppermute x24, waiting for transfers between devices, shift(): return lax.ppermute(value, 'z', pairs)  43.7 us
    ppermute x47, starting transfers between devices, swap(): return lax.ppermute(value, axis, [(0, 1), (1, 0)])  36.5 us
  transfers between devices with their start and end apart: 87, of which 28 were waited for; matrix products, arithmetic and copies ran while one was open for 6% of the time, Pallas kernels for 40%

profile of v6, /device:TPU:12, one launch (start us, length us, event | category | flops | bytes accessed | tf_op | source)
XLA Modules:
  0.0 795.7 jit_solution(5418304974951570070)
XLA Ops:
  16.8 43.8 %all_to_all.20.refs_4_ = bf16[16,80,384]{2,1,0:T(8,128)(2,1)S(1)} all-to-all(bf16[16,80,384]{2,1,0:T(8,128)(2,1)S(1)} %pad_maximum_fusion.2), channel_id=1, replica_groups=mesh['grp'=2,'z'=4,'x'=2,'core'=2] {'z','x','core'}, dimensions={0} | all-to-all | bytes 1966080 | tf_op jit(solution)/shard_map/all_to_all | solution.py:1790
  72.0 21.5 %collective-permute-done.3.refs_2_ = bf16[128,2048]{1,0:T(8,128)(2,1)} collective-permute-done((bf16[128,2048]{1,0:T(8,128)(2,1)S(1)}, bf16[128,2048]{1,0:T(8,128)(2,1)}, u32[]{:S(2)}, u32[]{:S(2)}) %collective-permute-start.3) | collective-permute-done | bytes 524320 | tf_op jit(solution)/shard_map/ppermute | solution.py:1591
  100.1 5.1 collective-permute-start.4
  157.6 5.7 fusion.3
  172.7 10.0 %collective-permute-done.14.refs_1_ = bf16[128,2048]{1,0:T(8,128)(2,1)} collective-permute-done((bf16[128,2048]{1,0:T(8,128)(2,1)}, bf16[128,2048]{1,0:T(8,128)(2,1)}, u32[]{:S(2)}, u32[]{:S(2)}) %collective-permute-start.14) | collective-permute-done | bytes 524320 | tf_op jit(solution)/shard_map/ppermute | solution.py:1559
  209.3 10.6 %attend.1 = (bf16[2048,128]{1,0:T(8,128)(2,1)S(1)}, bf16[2048,128]{1,0:T(8,128)(2,1)S(1)}, bf16[2048,128]{1,0:T(8,128)(2,1)S(1)}, f32[2048,128]{1,0:T(8,128)S(1)...) custom-call(f32[2048,384]{1,0:T(8,128)} %get-tuple-element.244.refs_0_.refs_6_.refs_3_, ...), custom_call_target="tpu_custom_call" | custom-call | flops 429496736 | bytes 786432 | tf_op jit(solution)/shard_map/attend/pallas_call | solution.py:571
  226.6 6.4 plain_dispatch.1
  236.6 6.7 all-to-all-start.1
  243.9 13.1 %all-to-all-done.1.refs_0_ = bf16[16,128,128]{2,1,0:T(8,128)(2,1)S(1)} async-done(((bf16[16,128,128]{2,1,0:T(8,128)(2,1)}), bf16[16,128,128]{2,1,0:T(8,128)(2,1)S(1)}, u32[]{:S(2)}, u32[]{:S(2)}) %all-to-all-start.1) | async-done | bytes 524320 | tf_op jit(solution)/shard_map/all_to_all | solution.py:1841
  272.9 9.0 %collective-permute-done.27.refs_2_ = bf16[128,2048]{1,0:T(8,128)(2,1)S(1)} collective-permute-done((bf16[128,2048]{1,0:T(8,128)(2,1)S(1)}, bf16[128,2048]{1,0:T(8,128)(2,1)S(1)}, u32[]{:S(2)}, u32[]{:S(2)}) %collective-permute-start.27) | collective-permute-done | bytes 524320 | tf_op jit(solution)/shard_map/ppermute | solution.py:1591
  316.1 9.2 %slopes.2 = (f32[4,384,1024]{2,1,0:T(8,128)}, f32[8,128]{1,0:T(8,128)S(1)}) custom-call(bf16[4,384,2048]{2,1,0:T(8,128)(2,1)S(1)} %bitcast.114, bf16[4,1024,2048]{2,1,0:T(8,128)(2,1)S(1)} %bitcast.108, f32[8,128]{1,0:T(8,128)S(1)} %get-tuple-element.275.refs_2_), custom_call_target="tpu_custom_call" | custom-call | flops 644245120 | bytes 1677721 | tf_op jit(solution)/shard_map/slopes/pallas_call | solution.py:571
  328.1 11.6 %collective-permute-done.37.refs_1_ = bf16[128,2048]{1,0:T(8,128)(2,1)S(1)} collective-permute-done((bf16[128,2048]{1,0:T(8,128)(2,1)S(1)}, bf16[128,2048]{1,0:T(8,128)(2,1)S(1)}, u32[]{:S(2)}, u32[]{:S(2)}) %collective-permute-start.37) | collective-permute-done | bytes 524320 | tf_op jit(solution)/shard_map/ppermute | solution.py:1559
  348.5 40.9 %experts_full.1 = (bf16[4,384,1024]{2,1,0:T(8,128)(2,1)}, bf16[4,384,1024]{2,1,0:T(8,128)(2,1)}, bf16[4,384,1024]{2,1,0:T(8,128)(2,1)}, f32[4,384,128]{2,1,0:T(8...) custom-call(s32[1]{0:T(128)} %bitcast.37.refs_0_, bf16[4,384,2048]{2,1,0:T(8,128)(2,1)} %get-tuple-element.290.refs_1_, ...), custom_call_target="tpu_custom_call" | custom-call | flops 2576980480 | bytes 5872025 | tf_op jit(solution)/shard_map/experts_full/pallas_call | solution.py:571
  411.1 10.8 %collective-permute-done.43.refs_2_ = bf16[128,2176]{1,0:T(8,128)(2,1)S(1)} collective-permute-done((bf16[128,2176]{1,0:T(8,128)(2,1)S(1)}, bf16[128,2176]{1,0:T(8,128)(2,1)S(1)}, u32[]{:S(2)}, u32[]{:S(2)}) %collective-permute-start.43) | collective-permute-done | bytes 557088 | tf_op jit(solution)/shard_map/ppermute | solution.py:1559
  425.2 5.9 copy-done.1
  431.2 9.4 %down.1 = (bf16[4,384,2048]{2,1,0:T(8,128)(2,1)S(1)}, f32[8,128]{1,0:T(8,128)S(1)}) custom-call(bf16[4,384,1024]{2,1,0:T(8,128)(2,1)S(1)} %copy-done.26, f32[4,384,128]{2,1,0:T(8,128)S(1)} %copy-done.34, bf16[4,1024,2048]{2,1,0:T(8,128)(2,1)S(1)} %copy-done.1, f32[8,128]{1,0:T(8,128)S(1)} %get-tuple-element.306.refs_3_), custom_call_target="tpu_custom_call" | custom-call | flops 644245120 | bytes 1677721 | tf_op jit(solution)/shard_map/down/pallas_call | solution.py:571
  455.8 5.8 copy-done.5
  461.6 7.0 stack_dispatch.2
  479.9 5.8 copy-done.2
  485.7 9.1 %slopes.3 = (f32[4,384,1024]{2,1,0:T(8,128)}, f32[8,128]{1,0:T(8,128)S(1)}) custom-call(bf16[4,384,2048]{2,1,0:T(8,128)(2,1)S(1)} %copy-done.7, bf16[4,1024,2048]{2,1,0:T(8,128)(2,1)S(1)} %copy-done.2, f32[8,128]{1,0:T(8,128)S(1)} %get-tuple-element.328.refs_2_), custom_call_target="tpu_custom_call" | custom-call | flops 644245120 | bytes 1677721 | tf_op jit(solution)/shard_map/slopes/pallas_call | solution.py:571
  518.6 6.0 copy-done.6
  524.6 7.0 stack_dispatch.3
  532.3 16.0 %experts_half.2 = (bf16[2,384,1024]{2,1,0:T(8,128)(2,1)}, bf16[2,384,1024]{2,1,0:T(8,128)(2,1)}, bf16[2,384,1024]{2,1,0:T(8,128)(2,1)}, f32[2,384,128]{2,1,0:T(8,128)}, f32[8,128]{1,0:T(8,128)}) custom-call(s32[1]{0:T(128)} %bitcast.37.refs_0_, bf16[4,384,2048]{2,1,0:T(8,128)(2,1)} %get-tuple-element.336.refs_1_.refs_2_, ...), custom_call_target="tpu_custom_call" | custom-call | flops 644245120 | bytes 2936012 | tf_op jit(solution)/shard_map/experts_half/pallas_call | solution.py:571
  552.1 10.1 %attend_back.1 = (f32[2048,128]{1,0:T(8,128)S(1)}, f32[2048,128]{1,0:T(8,128)S(1)}, bf16[2048,128]{1,0:T(8,128)(2,1)S(1)}, f32[2,2048]{1,0:T(2,128)S(1)}, f32[2,128]{1,0:T(2,128)S(1)}, /*index=5*/f32[8,128]{1,0:T(8,128)}) custom-call(bf16[2048,128]{1,0:T(8,128)(2,1)S(1)} %copy-done.57, bf16[2048,128]{1,0:T(8,128)(2,1)S(1)} %copy-done.59, ...), custom_call_target="tpu_custom_call" | custom-call | flops 1073741824 | bytes 1572864 | tf_op jit(solution)/shard_map/attend_back/pallas_call | solution.py:571
  601.2 5.7 dw_product.1
  610.0 8.5 %collective-permute-start.70 = (bf16[1024,384]{1,0:T(8,128)(2,1)}, bf16[1024,384]{1,0:T(8,128)(2,1)}, u32[]{:S(2)}, u32[]{:S(2)}) collective-permute-start(bf16[1024,384]{1,0:T(8,128)(2,1)} %dynamic-slice_convert_fusion), channel_id=1, source_target_pairs={{0,16},{16,0},{1,17},{17,1},{2,18},{18,2},{3,19},{19,3},{4,20},{20... | collective-permute-start | bytes 2359304 | tf_op jit(solution)/shard_map/ppermute | solution.py:1559
  619.9 16.6 %collective-permute-done.71 = f32[2,128]{1,0:T(2,128)S(1)} collective-permute-done((f32[2,128]{1,0:T(2,128)S(1)}, f32[2,128]{1,0:T(2,128)S(1)}, u32[]{:S(2)}, u32[]{:S(2)}) %collective-permute-start.71) | collective-permute-done | bytes 1056 | tf_op jit(solution)/shard_map/ppermute | solution.py:1559
  638.0 6.6 collective-permute-done.63.refs_2_
  652.1 8.2 %all-to-all-start.3 = ((bf16[16,80,384]{2,1,0:T(8,128)(2,1)}), bf16[16,80,384]{2,1,0:T(8,128)(2,1)}, u32[]{:S(2)}, u32[]{:S(2)}) async-start(bf16[16,80,384]{2,1,0:T(8,128)(2,1)} %pad_maximum_fusion.3), calls=%async_computation.4 | async-start | bytes 1966080 | tf_op jit(solution)/shard_map/all_to_all | solution.py:1968
  661.8 16.3 %experts_half.3 = (bf16[2,384,1024]{2,1,0:T(8,128)(2,1)}, bf16[2,384,1024]{2,1,0:T(8,128)(2,1)}, bf16[2,384,1024]{2,1,0:T(8,128)(2,1)}, f32[2,384,128]{2,1,0:T(8,128)}, f32[8,128]{1,0:T(8,128)}) custom-call(s32[1]{0:T(128)} %bitcast.37.refs_0_, bf16[4,384,2048]{2,1,0:T(8,128)(2,1)} %get-tuple-element.336.refs_1_.refs_2_, ...), custom_call_target="tpu_custom_call" | custom-call | flops 644245120 | bytes 2936012 | tf_op jit(solution)/shard_map/experts_half/pallas_call | solution.py:571
  693.8 19.9 %weight_grads.2 = (f32[4,1024,1024]{2,1,0:T(8,128)}, f32[4,1024,1024]{2,1,0:T(8,128)}, f32[4,512,2048]{2,1,0:T(8,128)}, f32[8,128]{1,0:T(8,128)}) custom-call(s32[1]{0:T(128)} %bitcast.28.refs_0_, bf16[4,384,2048]{2,1,0:T(8,128)(2,1)} %get-tuple-element.290.refs_1_, bf16[4,384,2048]{2,1,0:T(8,128)(2,1)} %get-tuple-element.336.refs_1_.refs_2_, ...), custom_call_target="tpu_custom_call" | custom-call | flops 966367616 | bytes 3774873 | tf_op jit(solution)/shard_map/weight_grads/pallas_call | solution.py:571
  764.2 18.2 %weight_grads.3 = (f32[4,1024,1024]{2,1,0:T(8,128)}, f32[4,1024,1024]{2,1,0:T(8,128)}, f32[4,512,2048]{2,1,0:T(8,128)}, f32[8,128]{1,0:T(8,128)}) custom-call(s32[1]{0:T(128)} %bitcast.28.refs_0_, bf16[4,384,2048]{2,1,0:T(8,128)(2,1)} %get-tuple-element.290.refs_1_, ...), custom_call_target="tpu_custom_call", output_to_operand_aliasing={{0}: (13, {}), {1}: (14, {}), {2}: (15, {})} | custom-call | flops 966367616 | bytes 3774873 | tf_op jit(solution)/shard_map/weight_grads/pallas_call | solution.py:571
  (516 shorter events, 390.8 us)
Async XLA Ops:
  7.2 216.1 %all-gather.9.cloned.1.call-start = ((), (), s32[]{:S(2)}) async-start(), calls=%async_computation.5 | async-start | bytes 8912896 | tf_op jit(solution)/shard_map/all_gather | solution.py:1574
  7.9 249.8 %all-gather.13.cloned.1.call-start = ((), (), s32[]{:S(2)}) async-start(), calls=%async_computation.8 | async-start | bytes 8912896 | tf_op jit(solution)/shard_map/all_gather | solution.py:1574
  60.6 46.5 %collective-permute-start.7 = (bf16[16,80,384]{2,1,0:T(8,128)(2,1)S(1)}, bf16[16,80,384]{2,1,0:T(8,128)(2,1)S(1)}, u32[]{:S(2)}, u32[]{:S(2)}) collective-permute-start(bf16[16,80,384]{2,1,0:T(8,128)(2,1)S(1)} %all_to_all.20.refs_4_), channel_id=1, source_target_pairs={{0,16},{16,0},{1,17},{17,1},{2,18},{18,2},{3,19},{19,3},{4,20},{20... | collective-permute-start | bytes 2949128 | tf_op jit(solution)/shard_map/ppermute | solution.py:1559
  61.2 38.9 %collective-permute-start.10 = (bf16[128,2048]{1,0:T(8,128)(2,1)S(1)}, bf16[128,2048]{1,0:T(8,128)(2,1)S(1)}, u32[]{:S(2)}, u32[]{:S(2)}) collective-permute-start(bf16[128,2048]{1,0:T(8,128)(2,1)S(1)} %copy-done.28), channel_id=1, source_target_pairs={{0,1},{1,0},{2,3},{3,2},{4,5},{5,4},{6,7},{7,6},{8,9},{9,8},{10,11... | collective-permute-start | bytes 1572872 | tf_op jit(solution)/shard_map/ppermute | solution.py:1559
  61.2 44.1 %collective-permute-start.8 = (bf16[128,2048]{1,0:T(8,128)(2,1)S(1)}, bf16[128,2048]{1,0:T(8,128)(2,1)}, u32[]{:S(2)}, u32[]{:S(2)}) collective-permute-start(bf16[128,2048]{1,0:T(8,128)(2,1)S(1)} %copy-done.28), channel_id=1, source_target_pairs={{0,2},{2,0},{1,3},{3,1},{4,6},{6,4},{5,7},{7,5},{8,10},{10,8},{9,1... | collective-permute-start | bytes 1572872 | tf_op jit(solution)/shard_map/ppermute | solution.py:1559
  62.4 31.1 %collective-permute-start.3 = (bf16[128,2048]{1,0:T(8,128)(2,1)S(1)}, bf16[128,2048]{1,0:T(8,128)(2,1)}, u32[]{:S(2)}, u32[]{:S(2)}) collective-permute-start(bf16[128,2048]{1,0:T(8,128)(2,1)S(1)} %copy-done.28), channel_id=1, source_target_pairs={{0,4},{4,8},{8,12},{1,5},{5,9},{9,13},{2,6},{6,10},{10,14},{3,7},{... | collective-permute-start | bytes 1572872 | tf_op jit(solution)/shard_map/ppermute | solution.py:1591
  64.3 31.5 %collective-permute-start = (bf16[128,2048]{1,0:T(8,128)(2,1)S(1)}, bf16[128,2048]{1,0:T(8,128)(2,1)}, u32[]{:S(2)}, u32[]{:S(2)}) collective-permute-start(bf16[128,2048]{1,0:T(8,128)(2,1)S(1)} %copy-done.28), channel_id=1, source_target_pairs={{12,8},{8,4},{4,0},{13,9},{9,5},{5,1},{14,10},{10,6},{6,2},{15,11}... | collective-permute-start | bytes 1572872 | tf_op jit(solution)/shard_map/ppermute | solution.py:1591
  100.1 22.6 %collective-permute-start.4 = (bf16[128,2048]{1,0:T(8,128)(2,1)}, bf16[128,2048]{1,0:T(8,128)(2,1)}, u32[]{:S(2)}, u32[]{:S(2)}) collective-permute-start(bf16[128,2048]{1,0:T(8,128)(2,1)} %collective-permute-done.3.refs_2_), channel_id=1, source_target_pairs={{4,8},{8,12},{5,9},{9,13},{6,10},{10,14},{7,11},{11,15},{20,24},{2... | collective-permute-start | bytes 1572872 | tf_op jit(solution)/shard_map/ppermute | solution.py:1591
  112.5 20.6 %collective-permute-start.13 = (bf16[128,2048]{1,0:T(8,128)(2,1)}, bf16[128,2048]{1,0:T(8,128)(2,1)}, u32[]{:S(2)}, u32[]{:S(2)}) collective-permute-start(bf16[128,2048]{1,0:T(8,128)(2,1)} %collective-permute-done.12.refs_1_), channel_id=1, source_target_pairs={{0,1},{1,0},{2,3},{3,2},{4,5},{5,4},{6,7},{7,6},{8,9},{9,8},{10,11... | collective-permute-start | bytes 1572872 | tf_op jit(solution)/shard_map/ppermute | solution.py:1559
  157.4 298.4 %all-gather.15.cloned.1.call-start = ((), (), s32[]{:S(2)}) async-start(), calls=%async_computation.9 | async-start | bytes 20971520 | tf_op jit(solution)/shard_map/all_gather | solution.py:1570
  163.3 19.5 %collective-permute-start.14 = (bf16[128,2048]{1,0:T(8,128)(2,1)}, bf16[128,2048]{1,0:T(8,128)(2,1)}, u32[]{:S(2)}, u32[]{:S(2)}) collective-permute-start(bf16[128,2048]{1,0:T(8,128)(2,1)} %get-tuple-element.230.refs_1_), channel_id=1, source_target_pairs={{0,2},{2,0},{1,3},{3,1},{4,6},{6,4},{5,7},{7,5},{8,10},{10,8},{9,1... | collective-permute-start | bytes 1572872 | tf_op jit(solution)/shard_map/ppermute | solution.py:1559
  236.6 20.3 %all-to-all-start.1 = ((bf16[16,128,128]{2,1,0:T(8,128)(2,1)}), bf16[16,128,128]{2,1,0:T(8,128)(2,1)S(1)}, u32[]{:S(2)}, u32[]{:S(2)}) async-start(bf16[16,128,128]{2,1,0:T(8,128)(2,1)} %bitcast.29), calls=%async_computation.1 | async-start | bytes 1048576 | tf_op jit(solution)/shard_map/all_to_all | solution.py:1841
  243.3 275.3 %all-gather.17.cloned.1.call-start = ((), (), s32[]{:S(2)}) async-start(), calls=%async_computation.10 | async-start | bytes 20971520 | tf_op jit(solution)/shard_map/all_gather | solution.py:1570
  346.6 344.2 %reduce-scatter.2.cloned.1.call-start = ((), (), s32[]{:S(2)}) async-start(), calls=%async_computation.6 | async-start | bytes 8912896 | tf_op jit(solution)/shard_map/reduce_scatter | solution.py:1578
  409.2 31.4 %collective-permute-start.45 = (bf16[128,2176]{1,0:T(8,128)(2,1)S(1)}, bf16[128,2176]{1,0:T(8,128)(2,1)S(1)}, u32[]{:S(2)}, u32[]{:S(2)}) collective-permute-start(bf16[128,2176]{1,0:T(8,128)(2,1)S(1)} %get-tuple-element.308), channel_id=1, source_target_pairs={{0,2},{2,0},{1,3},{3,1},{4,6},{6,4},{5,7},{7,5},{8,10},{10,8},{9,1... | collective-permute-start | bytes 1671176 | tf_op jit(solution)/shard_map/ppermute | solution.py:1559
  450.4 296.7 %all-gather.11.cloned.1.call-start = ((), (), s32[]{:S(2)}) async-start(), calls=%async_computation.7 | async-start | bytes 10027008 | tf_op jit(solution)/shard_map/all_gather | solution.py:1574
  455.4 39.4 %collective-permute-start.48 = (bf16[128,2176]{1,0:T(8,128)(2,1)}, bf16[128,2176]{1,0:T(8,128)(2,1)}, u32[]{:S(2)}, u32[]{:S(2)}) collective-permute-start(bf16[128,2176]{1,0:T(8,128)(2,1)} %copy-done.78), channel_id=1, source_target_pairs={{0,2},{2,0},{1,3},{3,1},{4,6},{6,4},{5,7},{7,5},{8,10},{10,8},{9,1... | collective-permute-start | bytes 1671176 | tf_op jit(solution)/shard_map/ppermute | solution.py:1559
  473.3 21.5 %collective-permute-start.52 = (bf16[128,2176]{1,0:T(8,128)(2,1)S(1)}, bf16[128,2176]{1,0:T(8,128)(2,1)S(1)}, u32[]{:S(2)}, u32[]{:S(2)}) collective-permute-start(bf16[128,2176]{1,0:T(8,128)(2,1)S(1)} %get-tuple-element.325), channel_id=1, source_target_pairs={{0,4},{4,8},{8,12},{1,5},{5,9},{9,13},{2,6},{6,10},{10,14},{3,7},{... | collective-permute-start | bytes 1671176 | tf_op jit(solution)/shard_map/ppermute | solution.py:1591
  477.8 21.9 %collective-permute-start.53 = (bf16[128,2176]{1,0:T(8,128)(2,1)S(1)}, bf16[128,2176]{1,0:T(8,128)(2,1)S(1)}, u32[]{:S(2)}, u32[]{:S(2)}) collective-permute-start(bf16[128,2176]{1,0:T(8,128)(2,1)S(1)} %get-tuple-element.326), channel_id=1, source_target_pairs={{12,8},{8,4},{4,0},{13,9},{9,5},{5,1},{14,10},{10,6},{6,2},{15,11}... | collective-permute-start | bytes 1671176 | tf_op jit(solution)/shard_map/ppermute | solution.py:1591
  514.0 34.2 %all-to-all-start.2 = ((bf16[16,128,128]{2,1,0:T(8,128)(2,1)}), bf16[16,128,128]{2,1,0:T(8,128)(2,1)S(1)}, u32[]{:S(2)}, u32[]{:S(2)}) async-start(bf16[16,128,128]{2,1,0:T(8,128)(2,1)} %get-tuple-element.331), calls=%async_computation.3 | async-start | bytes 1048576 | tf_op jit(solution)/shard_map/all_to_all | solution.py:1898
  610.0 39.7 %collective-permute-start.70 = (bf16[1024,384]{1,0:T(8,128)(2,1)}, bf16[1024,384]{1,0:T(8,128)(2,1)}, u32[]{:S(2)}, u32[]{:S(2)}) collective-permute-start(bf16[1024,384]{1,0:T(8,128)(2,1)} %dynamic-slice_convert_fusion), channel_id=1, source_target_pairs={{0,16},{16,0},{1,17},{17,1},{2,18},{18,2},{3,19},{19,3},{4,20},{20... | collective-permute-start | bytes 2359304 | tf_op jit(solution)/shard_map/ppermute | solution.py:1559
  618.4 26.2 %collective-permute-start.63 = (bf16[128,2048]{1,0:T(8,128)(2,1)}, bf16[128,2048]{1,0:T(8,128)(2,1)S(1)}, u32[]{:S(2)}, u32[]{:S(2)}) collective-permute-start(bf16[128,2048]{1,0:T(8,128)(2,1)} %get-tuple-element.363), channel_id=1, source_target_pairs={{0,2},{2,0},{1,3},{3,1},{4,6},{6,4},{5,7},{7,5},{8,10},{10,8},{9,1... | collective-permute-start | bytes 1572872 | tf_op jit(solution)/shard_map/ppermute | solution.py:1559
  636.5 41.6 %collective-permute-start.62 = (bf16[128,2048]{1,0:T(8,128)(2,1)}, bf16[128,2048]{1,0:T(8,128)(2,1)S(1)}, u32[]{:S(2)}, u32[]{:S(2)}) collective-permute-start(bf16[128,2048]{1,0:T(8,128)(2,1)} %copy-done.83), channel_id=1, source_target_pairs={{0,2},{2,0},{1,3},{3,1},{4,6},{6,4},{5,7},{7,5},{8,10},{10,8},{9,1... | collective-permute-start | bytes 1572872 | tf_op jit(solution)/shard_map/ppermute | solution.py:1559
  647.6 34.8 %collective-permute-start.65 = (bf16[128,2048]{1,0:T(8,128)(2,1)S(1)}, bf16[128,2048]{1,0:T(8,128)(2,1)S(1)}, u32[]{:S(2)}, u32[]{:S(2)}) collective-permute-start(bf16[128,2048]{1,0:T(8,128)(2,1)S(1)} %get-tuple-element.370.refs_2_.refs_4_), channel_id=1, source_target_pairs={{12,8},{13,9},{14,10},{15,11},{28,24},{29,25},{30,26},{31,27}} | collective-permute-start | bytes 1572872 | tf_op jit(solution)/shard_map/ppermute | solution.py:1591
  648.3 34.1 %collective-permute-start.64 = (bf16[128,2048]{1,0:T(8,128)(2,1)S(1)}, bf16[128,2048]{1,0:T(8,128)(2,1)}, u32[]{:S(2)}, u32[]{:S(2)}) collective-permute-start(bf16[128,2048]{1,0:T(8,128)(2,1)S(1)} %get-tuple-element.370.refs_2_.refs_4_), channel_id=1, source_target_pairs={{0,4},{1,5},{2,6},{3,7},{16,20},{17,21},{18,22},{19,23}} | collective-permute-start | bytes 1572872 | tf_op jit(solution)/shard_map/ppermute | solution.py:1591
  652.1 103.5 %all-to-all-start.3 = ((bf16[16,80,384]{2,1,0:T(8,128)(2,1)}), bf16[16,80,384]{2,1,0:T(8,128)(2,1)}, u32[]{:S(2)}, u32[]{:S(2)}) async-start(bf16[16,80,384]{2,1,0:T(8,128)(2,1)} %pad_maximum_fusion.3), calls=%async_computation.4 | async-start | bytes 1966080 | tf_op jit(solution)/shard_map/all_to_all | solution.py:1968
  660.3 53.4 %collective-permute-start.61 = (bf16[128,2048]{1,0:T(8,128)(2,1)}, bf16[128,2048]{1,0:T(8,128)(2,1)}, u32[]{:S(2)}, u32[]{:S(2)}) collective-permute-start(bf16[128,2048]{1,0:T(8,128)(2,1)} %get-tuple-element.355), channel_id=1, source_target_pairs={{0,2},{2,0},{1,3},{3,1},{4,6},{6,4},{5,7},{7,5},{8,10},{10,8},{9,1... | collective-permute-start | bytes 1572872 | tf_op jit(solution)/shard_map/ppermute | solution.py:1559
  685.3 30.9 %collective-permute-start.66 = (bf16[128,2048]{1,0:T(8,128)(2,1)}, bf16[128,2048]{1,0:T(8,128)(2,1)}, u32[]{:S(2)}, u32[]{:S(2)}) collective-permute-start(bf16[128,2048]{1,0:T(8,128)(2,1)} %get-tuple-element.374), channel_id=1, source_target_pairs={{0,4},{4,8},{1,5},{5,9},{2,6},{6,10},{3,7},{7,11},{16,20},{20,24},... | collective-permute-start | bytes 1572872 | tf_op jit(solution)/shard_map/ppermute | solution.py:1591
  688.6 27.6 %collective-permute-start.67 = (bf16[128,2048]{1,0:T(8,128)(2,1)}, bf16[128,2048]{1,0:T(8,128)(2,1)}, u32[]{:S(2)}, u32[]{:S(2)}) collective-permute-start(bf16[128,2048]{1,0:T(8,128)(2,1)} %get-tuple-element.375), channel_id=1, source_target_pairs={{12,8},{8,4},{13,9},{9,5},{14,10},{10,6},{15,11},{11,7},{28,24},{2... | collective-permute-start | bytes 1572872 | tf_op jit(solution)/shard_map/ppermute | solution.py:1591
  693.4 47.3 %collective-permute-start.60 = (bf16[128,2048]{1,0:T(8,128)(2,1)}, bf16[128,2048]{1,0:T(8,128)(2,1)}, u32[]{:S(2)}, u32[]{:S(2)}) collective-permute-start(bf16[128,2048]{1,0:T(8,128)(2,1)} %copy-done.82), channel_id=1, source_target_pairs={{0,2},{2,0},{1,3},{3,1},{4,6},{6,4},{5,7},{7,5},{8,10},{10,8},{9,1... | collective-permute-start | bytes 1572872 | tf_op jit(solution)/shard_map/ppermute | solution.py:1559
  718.6 22.1 %collective-permute-start.68 = (bf16[128,2048]{1,0:T(8,128)(2,1)}, bf16[128,2048]{1,0:T(8,128)(2,1)S(1)}, u32[]{:S(2)}, u32[]{:S(2)}) collective-permute-start(bf16[128,2048]{1,0:T(8,128)(2,1)} %get-tuple-element.376), channel_id=1, source_target_pairs={{0,4},{4,8},{8,12},{1,5},{5,9},{9,13},{2,6},{6,10},{10,14},{3,7},{... | collective-permute-start | bytes 1572872 | tf_op jit(solution)/shard_map/ppermute | solution.py:1591
  761.7 24.7 %collective-permute-start.73 = (bf16[64,2176]{1,0:T(8,128)(2,1)S(1)}, bf16[64,2176]{1,0:T(8,128)(2,1)S(1)}, u32[]{:S(2)}, u32[]{:S(2)}) collective-permute-start(bf16[64,2176]{1,0:T(8,128)(2,1)S(1)} %fusion.2), channel_id=1, source_target_pairs={{0,0},{1,2},{2,4},{3,6},{4,8},{5,10},{6,12},{7,14},{8,16},{9,18},{... | collective-permute-start | bytes 835592 | tf_op jit(solution)/shard_map/ppermute | solution.py:1984
  (149 other events, 1557.1 us)
Sparse Core Ops, SparseCore 0:
  10.2 102.5 all-gather.8
  157.6 79.0 all-gather.12
  238.2 106.0 all-gather.14
  346.7 104.9 all-gather.16
  456.2 113.5 reduce-scatter.1
  571.9 103.9 all-gather.10
